TPU v7x, 32 devices: a whole 2x2x4 slice. The times are simulated.
32 devices in a mesh: store: 16 (over z, y, x), rep: 2 (over core).
Axes of the slice: x: 2, y: 2, z: 4, core: 2. Of those that a mesh axis runs over, the one named last changes fastest.
Arguments:
- features: bfloat16 [32768, 768], P('store'), may hold values from -6 to 6
- owners_near: int32 [16384, 1], P(('store', 'rep')), may hold values from 0 to 15; in each aligned block of 512 rows (0 to 511, 512 to 1023, ...) at most 64 rows name the same one
- slots_near: int32 [16384, 1], P(('store', 'rep')), may hold values from 0 to 2047
- owners_far: int32 [98304, 1], P(('store', 'rep')), may hold values from 0 to 15; in each aligned block of 3072 rows (0 to 3071, 3072 to 6143, ...) at most 384 rows name the same one
- slots_far: int32 [98304, 1], P(('store', 'rep')), may hold values from 0 to 2047
- adjacency_low: int32 [16384, 15], P(('store', 'rep')), may hold values from 0 to 3583
- adjacency_top: int32 [4096, 10], P(('store', 'rep')), may hold values from 0 to 511
- labels: int32 [4096], P(('store', 'rep')), may hold values from 0 to 152
- weights_low: float32 [1536, 1024], replicated, may hold values from -0.15625 to 0.15625
- weights_top: float32 [2048, 153], replicated, may hold values from -0.25 to 0.25
- first_low: float32 [1536, 1024], P(('store', 'rep')), may hold values from -0.00390625 to 0.00390625
- second_low: float32 [1536, 1024], P(('store', 'rep')), may hold values from 1e-09 to 1e-07
- first_top: float32 [2048, 153], P(('store', 'rep')), may hold values from -0.03125 to 0.03125
- second_top: float32 [2048, 153], P(('store', 'rep')), may hold values from 1e-07 to 1e-05
Outputs:
- logits: float32 [4096, 153], P(('store', 'rep'))
- new_low: float32 [1536, 1024], replicated
- new_first_low: float32 [1536, 1024], P(('store', 'rep'))
- new_second_low: float32 [1536, 1024], P(('store', 'rep'))
- new_top: float32 [2048, 153], replicated
- new_first_top: float32 [2048, 153], P(('store', 'rep'))
- new_second_top: float32 [2048, 153], P(('store', 'rep'))
Inputs may be any that keep to these rules, and one draw needn't show every extreme that they name: `owners_near`: within the rows of one trainer, no store index is named more than 64 times, and some index is named exactly that often. `owners_far`: within the rows of one trainer, no store index is named more than 384 times, and some index is named exactly that often.
All inputs are finite; a program needn't handle non-finite values.
Results may differ from a plain program's by a relative error of at most 0.005.
Values may be sent and summed in bfloat16 or wider, within the bound.
No kernel may reach another device: no remote copies, remote signals or barrier semaphores. Data moves between devices by JAX's collectives and lax.ppermute only.
A program may use at most 128 MiB of HBM per device.

v0:
```python
import jax
import jax.numpy as jnp
from jax import lax
from jax.sharding import PartitionSpec as P

beta_one = 0.9
beta_two = 0.999
bias_one = 1.0 - 0.9**10
bias_two = 1.0 - 0.999**10
learn_rate = 0.01
adam_eps = 1e-08


def gelu_tanh(values):
    return jax.nn.gelu(values, approximate=True)


def local_step(fetched, adjacency_low, adjacency_top, labels, low_bf, top_bf, scale):
    near_rows = adjacency_low.shape[0]
    seed_rows = labels.shape[0]
    width = top_bf.shape[0] // 2
    classes_all = top_bf.shape[1]
    gathered = jnp.zeros((near_rows, fetched.shape[1]), jnp.float32)
    for column in range(adjacency_low.shape[1]):
        gathered = gathered + fetched[adjacency_low[:, column]].astype(jnp.float32)
    low_mean = (gathered / adjacency_low.shape[1]).astype(jnp.bfloat16)
    low_input = jnp.concatenate([fetched[:near_rows], low_mean], axis=1)
    pre_hidden = jnp.dot(low_input, low_bf, preferred_element_type=jnp.float32)
    hidden = gelu_tanh(pre_hidden).astype(jnp.bfloat16)
    top_sum = jnp.zeros((seed_rows, width), jnp.float32)
    for column in range(adjacency_top.shape[1]):
        top_sum = top_sum + hidden[adjacency_top[:, column]].astype(jnp.float32)
    top_mean = (top_sum / adjacency_top.shape[1]).astype(jnp.bfloat16)
    top_input = jnp.concatenate([hidden[:seed_rows], top_mean], axis=1)
    logits = jnp.dot(top_input, top_bf, preferred_element_type=jnp.float32)
    powers = jnp.exp(logits)
    chances = powers / jnp.sum(powers, axis=1, keepdims=True)
    targets = (labels[:, None] == jnp.arange(classes_all, dtype=jnp.int32)[None, :]).astype(
        jnp.float32
    )
    dlogits = ((chances - targets) * scale).astype(jnp.bfloat16)
    grad_top = lax.dot_general(
        top_input, dlogits, (((0,), (0,)), ((), ())), preferred_element_type=jnp.float32
    )
    dinput = lax.dot_general(
        dlogits, top_bf, (((1,), (1,)), ((), ())), preferred_element_type=jnp.float32
    )
    dhidden = jnp.zeros((near_rows, width), jnp.float32).at[:seed_rows].add(dinput[:, :width])
    spread = dinput[:, width:] / adjacency_top.shape[1]
    for column in range(adjacency_top.shape[1]):
        dhidden = dhidden.at[adjacency_top[:, column]].add(spread)
    unused, pullback = jax.vjp(gelu_tanh, pre_hidden)
    dpre = pullback(dhidden)[0].astype(jnp.bfloat16)
    grad_low = lax.dot_general(
        low_input, dpre, (((0,), (0,)), ((), ())), preferred_element_type=jnp.float32
    )
    return (logits, grad_low, grad_top)


def adam_update(weight, moment, square, gradient):
    moment_new = beta_one * moment + (1.0 - beta_one) * gradient
    square_new = beta_two * square + (1.0 - beta_two) * gradient * gradient
    update = moment_new / bias_one / (jnp.sqrt(square_new / bias_two) + adam_eps)
    return (weight - learn_rate * update, moment_new, square_new)


def bucket(owners, slots, stores, capacity):
    owner_marks = (owners[:, None] == jnp.arange(stores, dtype=jnp.int32)[None, :]).astype(
        jnp.int32
    )
    places = jnp.sum((jnp.cumsum(owner_marks, axis=0) - owner_marks) * owner_marks, axis=1)
    requests = jnp.zeros((stores, capacity), jnp.int32).at[owners, places].set(slots)
    return (requests, places)


def fetch_rows(owners, slots, capacity, table):
    stores = lax.axis_size("store")
    requests, places = bucket(owners, slots, stores, capacity)
    found = table[lax.all_to_all(requests, "store", split_axis=0, concat_axis=0, tiled=True)]
    arrived = lax.all_to_all(found, "store", split_axis=0, concat_axis=0, tiled=True)
    return arrived[owners, places]


def per_device(
    features,
    owners_near,
    slots_near,
    owners_far,
    slots_far,
    adjacency_low,
    adjacency_top,
    labels,
    weights_low,
    weights_top,
    first_low,
    second_low,
    first_top,
    second_top,
):
    stores = lax.axis_size("store")
    near_owners = owners_near[:, 0]
    far_owners = owners_far[:, 0]
    near_limit = 2 * near_owners.shape[0] // stores
    far_limit = 2 * far_owners.shape[0] // stores
    fetched = jnp.concatenate(
        [
            fetch_rows(near_owners, slots_near[:, 0], near_limit, features),
            fetch_rows(far_owners, slots_far[:, 0], far_limit, features),
        ],
        axis=0,
    )
    members = lax.axis_size(("store", "rep"))
    scale = 1.0 / (labels.shape[0] * members)
    logits, grad_low, grad_top = local_step(
        fetched,
        adjacency_low,
        adjacency_top,
        labels,
        weights_low.astype(jnp.bfloat16),
        weights_top.astype(jnp.bfloat16),
        scale,
    )
    position = lax.axis_index(("store", "rep"))
    rows_low = first_low.shape[0]
    rows_top = first_top.shape[0]
    whole_low, whole_top = lax.psum((grad_low, grad_top), ("store", "rep"))
    share_low = lax.dynamic_slice_in_dim(whole_low, position * rows_low, rows_low, 0)
    share_top = lax.dynamic_slice_in_dim(whole_top, position * rows_top, rows_top, 0)
    own_low = lax.dynamic_slice_in_dim(weights_low, position * rows_low, rows_low, 0)
    own_top = lax.dynamic_slice_in_dim(weights_top, position * rows_top, rows_top, 0)
    part_low, new_first_low, new_second_low = adam_update(own_low, first_low, second_low, share_low)
    part_top, new_first_top, new_second_top = adam_update(own_top, first_top, second_top, share_top)
    new_low, new_top = (
        lax.all_gather(part_low, ("store", "rep"), axis=0, tiled=True),
        lax.all_gather(part_top, ("store", "rep"), axis=0, tiled=True),
    )
    return (logits, new_low, new_first_low, new_second_low, new_top, new_first_top, new_second_top)


def solution(mesh):
    return jax.shard_map(
        per_device,
        mesh=mesh,
        in_specs=(
            P("store", None),
            P(("store", "rep"), None),
            P(("store", "rep"), None),
            P(("store", "rep"), None),
            P(("store", "rep"), None),
            P(("store", "rep"), None),
            P(("store", "rep"), None),
            P(("store", "rep")),
            P(),
            P(),
            P(("store", "rep"), None),
            P(("store", "rep"), None),
            P(("store", "rep"), None),
            P(("store", "rep"), None),
        ),
        out_specs=(
            P(("store", "rep"), None),
            P(),
            P(("store", "rep"), None),
            P(("store", "rep"), None),
            P(),
            P(("store", "rep"), None),
            P(("store", "rep"), None),
        ),
        check_vma=False,
    )
```

profile of v0, /device:TPU:9, one launch (start us, length us, event | category | flops | bytes accessed | tf_op | source)
XLA Modules:
  0.0 949.6 jit_solution(18067817958297243353)
XLA Ops:
  11.5 70.9 %scatter_fusion = s32[16,64]{1,0:T(8,128)} fusion(s32[16,64]{1,0:T(8,128)} %broadcast.218, s32[512]{0:T(512)S(1)} %bitcast.98, s32[512]{0:T(512)} %bitcast.124), kind=kCustom, calls=%fused_computation.29 | custom fusion | bytes 10240 | tf_op jit(solution)/shard_map/scatter | solution.py:72
  82.4 6.3 all-to-all-start
  95.7 12.5 %scatter_custom_fusion.11 = s32[6144]{0:T(1024)} fusion(s32[3072]{0:T(1024)S(1)} %broadcast_select_fusion, s32[3072]{0:T(1024)} %bitcast.125, s32[]{:T(128)} %constant.42.clone.1), kind=kCustom, calls=%fused_computation.108 | custom fusion | bytes 25088
  108.3 6.4 all-to-all-start.2
  120.6 6.4 all-to-all-start.1
  127.0 26.1 %gather_fusion.2 = bf16[6144,768]{1,0:T(8,128)(2,1)} fusion(bf16[2048,768]{1,0:T(8,128)(2,1)S(1)} %copy-done, s32[6144]{0:T(1024)S(1)} %broadcast_clamp_fusion), kind=kCustom, calls=%fused_computation.2 | custom fusion | bytes 18898944 | tf_op jit(solution)/shard_map/gather | solution.py:79
  153.2 9.6 %all-to-all-done.1 = bf16[16,64,768]{2,1,0:T(8,128)(2,1)} async-done(((bf16[16,64,768]{2,1,0:T(8,128)(2,1)}), bf16[16,64,768]{2,1,0:T(8,128)(2,1)}, u32[]{:S(2)}, u32[]{:S(2)}) %all-to-all-start.1) | async-done | bytes 1572896 | tf_op jit(solution)/shard_map/all_to_all | solution.py:80
  162.8 5.4 all-to-all-start.3
  168.7 7.5 gather_fusion.1
  177.1 192.8 %all-to-all-done.3 = bf16[16,384,768]{2,1,0:T(8,128)(2,1)} async-done(((bf16[16,384,768]{2,1,0:T(8,128)(2,1)}), bf16[16,384,768]{2,1,0:T(8,128)(2,1)}, u32[]{:S(2)}, u32[]{:S(2)}) %all-to-all-start.3) | async-done | bytes 9437216 | tf_op jit(solution)/shard_map/all_to_all | solution.py:80
  369.9 58.0 %gather_fusion.3 = bf16[3072,768]{1,0:T(8,128)(2,1)} fusion(bf16[16,384,768]{2,1,0:T(8,128)(2,1)} %all-to-all-done.3, s32[3072]{0:T(1024)S(1)} %bitcast.95), kind=kCustom, calls=%fused_computation.3 | custom fusion | bytes 9461760 | tf_op jit(solution)/shard_map/gather | solution.py:81
  432.7 5.7 gather_fusion.10
  438.4 5.7 gather_fusion.11
  444.0 5.7 gather_fusion.12
  449.7 6.3 gather_fusion.13
  456.0 6.4 gather_fusion.14
  462.4 6.8 gather_fusion.15
  469.2 6.4 gather_fusion.16
  475.5 6.3 gather_fusion.17
  481.9 6.3 gather_fusion.5
  488.2 6.4 gather_fusion.6
  494.6 6.4 gather_fusion.7
  500.9 6.4 gather_fusion.8
  507.3 6.3 gather_fusion.9
  513.6 6.3 gather_fusion.18
  520.0 6.5 gather_fusion.4
  531.8 6.5 multiply_convert_fusion
  605.3 7.3 fusion.9
  612.9 190.9 %all-reduce.4.cloned.1.call-done = (f32[1536,1024]{1,0:T(8,128)}, f32[2048,153]{1,0:T(8,128)}) async-done(((f32[1536,1024]{1,0:T(8,128)}, f32[2048,153]{1,0:T(8,128)}), (f32[1536,1024]{1,0:T(8,128)}, f32[2048,153]{1,0:T(8,128)})) %all-reduce.4.cloned.1.call-update) | async-done | bytes 7544848 | tf_op jit(solution)/shard_map/psum | solution.py:126
  807.4 55.9 %all-gather.5.cloned.1.call-done = f32[2048,153]{1,0:T(8,128)} async-done(((f32[64,153]{1,0:T(8,128)}), f32[2048,153]{1,0:T(8,128)}) %all-gather.5.cloned.1.call-update) | async-done | bytes 1253392 | tf_op jit(solution)/shard_map/all_gather | solution.py:135
  866.0 70.1 %all-gather.3.cloned.1.call-done = f32[1536,1024]{1,0:T(8,128)} async-done(((f32[48,1024]{1,0:T(8,128)}), f32[1536,1024]{1,0:T(8,128)}) %all-gather.3.cloned.1.call-update) | async-done | bytes 6291472 | tf_op jit(solution)/shard_map/all_gather | solution.py:134
  936.1 6.8 copy.50
  (108 shorter events, 102.1 us)
Async XLA Ops:
  7.2 108.3 %copy-start = (bf16[2048,768]{1,0:T(8,128)(2,1)S(1)}, bf16[2048,768]{1,0:T(8,128)(2,1)}, u32[]{:S(2)}) copy-start(bf16[2048,768]{1,0:T(8,128)(2,1)} %param.16) | copy-start | bytes 9437188
  11.5 77.2 %copy-start.7 = (s32[3072,1]{0,1:T(1,128)S(1)}, s32[3072,1]{0,1:T(1,128)}, u32[]{:S(2)}) copy-start(s32[3072,1]{0,1:T(1,128)} %param.19) | copy-start | bytes 36868
  82.4 25.9 %all-to-all-start = ((s32[16,1,64]{2,1,0:T(1,128)}), s32[16,1,64]{2,1,0:T(1,128)}, u32[]{:S(2)}, u32[]{:S(2)}) async-start(s32[16,1,64]{2,1,0:T(1,128)} %bitcast.7), calls=%async_computation | async-start | bytes 16384 | tf_op jit(solution)/shard_map/all_to_all | solution.py:79
  108.3 12.4 %all-to-all-start.2 = ((s32[16,1,384]{2,1,0:T(1,128)}), s32[16,1,384]{2,1,0:T(1,128)S(1)}, u32[]{:S(2)}, u32[]{:S(2)}) async-start(s32[16,1,384]{2,1,0:T(1,128)} %bitcast.16), calls=%async_computation.2 | async-start | bytes 49152 | tf_op jit(solution)/shard_map/all_to_all | solution.py:79
  120.6 42.1 %all-to-all-start.1 = ((bf16[16,64,768]{2,1,0:T(8,128)(2,1)}), bf16[16,64,768]{2,1,0:T(8,128)(2,1)}, u32[]{:S(2)}, u32[]{:S(2)}) async-start(bf16[16,64,768]{2,1,0:T(8,128)(2,1)} %bitcast.99), calls=%async_computation.1 | async-start | bytes 3145728 | tf_op jit(solution)/shard_map/all_to_all | solution.py:80
  162.8 5.6 copy-start.10
  162.8 5.8 copy-start.11
  162.8 207.1 %all-to-all-start.3 = ((bf16[16,384,768]{2,1,0:T(8,128)(2,1)}), bf16[16,384,768]{2,1,0:T(8,128)(2,1)}, u32[]{:S(2)}, u32[]{:S(2)}) async-start(bf16[16,384,768]{2,1,0:T(8,128)(2,1)} %bitcast.96), calls=%async_computation.3 | async-start | bytes 18874368 | tf_op jit(solution)/shard_map/all_to_all | solution.py:80
  168.2 635.7 %all-reduce.4.cloned.1.call-start = ((), (), s32[]{:S(2)}) async-start(), calls=%async_computation.6 | async-start | bytes 16777216 | tf_op jit(solution)/shard_map/psum | solution.py:126
  531.8 6.6 copy-start.3
  552.5 3.7 copy-start.2
  554.1 2.5 copy-start.12
  556.6 2.2 copy-start.4
  612.6 191.2 %copy-start.8 = (f32[64,153]{1,0:T(8,128)S(1)}, f32[64,153]{1,0:T(8,128)}, u32[]{:S(2)}) copy-start(f32[64,153]{1,0:T(8,128)} %param.28) | copy-start | bytes 117508
  612.6 191.2 %copy-start.9 = (f32[64,153]{1,0:T(8,128)S(1)}, f32[64,153]{1,0:T(8,128)}, u32[]{:S(2)}) copy-start(f32[64,153]{1,0:T(8,128)} %param.29) | copy-start | bytes 117508
  612.7 192.8 %copy-start.5 = (f32[48,1024]{1,0:T(8,128)S(1)}, f32[48,1024]{1,0:T(8,128)}, u32[]{:S(2)}) copy-start(f32[48,1024]{1,0:T(8,128)} %param.26) | copy-start | bytes 589828
  612.7 192.8 %copy-start.6 = (f32[48,1024]{1,0:T(8,128)S(1)}, f32[48,1024]{1,0:T(8,128)}, u32[]{:S(2)}) copy-start(f32[48,1024]{1,0:T(8,128)} %param.27) | copy-start | bytes 589828
  612.7 250.6 %all-gather.5.cloned.1.call-start = ((), (), s32[]{:S(2)}) async-start(), calls=%async_computation.5 | async-start | bytes 2162688 | tf_op jit(solution)/shard_map/all_gather | solution.py:135
  805.4 130.7 %all-gather.3.cloned.1.call-start = ((), (), s32[]{:S(2)}) async-start(), calls=%async_computation.4 | async-start | bytes 6488064 | tf_op jit(solution)/shard_map/all_gather | solution.py:134
  936.0 6.8 copy-start.1
Sparse Core Ops, SparseCore 0:
  612.8 190.9 all-reduce.3
  807.2 55.9 all-gather.4
  866.7 69.2 all-gather.2
where the time goes:
time: 959 us; the launch traced here: 950 us
  waiting for transfers between devices  519 us (54%)
  local copies, waits for them, and re-layouts  308 us (32%)
  other arithmetic  66.8 us (7%)
  starting transfers between devices  24.7 us (3%)
  matrix products  16.4 us (2%)
  between operations  14.4 us (2%)
    all_to_all x2, waiting for transfers between devices, fetch_rows(): lax.all_to_all(found, 'store', split_axis=0, concat_axis=0, tiled=True)  202 us
    psum x1, waiting for transfers between devices, per_device(): whole_low, whole_top = lax.psum((grad_low, grad_top), ('store', 'rep'))  191 us
    gather x15, local copies, waits for them, and re-layouts, local_step(): gathered = gathered + fetched[adjacency_low[:, column]].astype(jnp.float32)  93.8 us
    scatter x1, local copies, waits for them, and re-layouts, bucket(): jnp.zeros((stores, capacity), jnp.int32).at[owners, places].set(slots)  70.9 us
    all_gather x1, waiting for transfers between devices, per_device(): lax.all_gather(part_low, ('store', 'rep'), axis=0, tiled=True)  70.1 us
    gather x2, local copies, waits for them, and re-layouts, fetch_rows(): return arrived[owners, places]  65.5 us
    all_gather x1, waiting for transfers between devices, per_device(): lax.all_gather(part_top, ('store', 'rep'), axis=0, tiled=True)  55.9 us
    scatter-add x10, other arithmetic, local_step(): dhidden = dhidden.at[adjacency_top[:, column]].add(spread)  45 us
  transfers between devices with their start and end apart: 7, of which 5 were waited for; matrix products, arithmetic and copies ran while one was open for 7% of the time, Pallas kernels for 0%

commit v1 on v0

v1 whole, which is shorter than its diff:
```python
import functools
import math

import jax
import jax.numpy as jnp
from jax import lax
from jax.experimental import pallas as pl
from jax.experimental.pallas import tpu as pltpu
from jax.sharding import PartitionSpec as P

beta_one = 0.9
beta_two = 0.999
bias_one = 1.0 - 0.9**10
bias_two = 1.0 - 0.999**10
learn_rate = 0.01
adam_eps = 1e-08

PLANE = 4
LANES = 128
MIB = 1024 * 1024

VMEM = pl.BlockSpec(memory_space=pltpu.VMEM)
SMEM = pl.BlockSpec(memory_space=pltpu.SMEM)


def dot(a, b, ca=1, cb=0):
    return lax.dot_general(a, b, (((ca,), (cb,)), ((), ())), preferred_element_type=jnp.float32)


def compose_kernel(nodes, per_plane, groups, adj_ref, table_ref, near_ref, ids_ref):
    fan, near_rows = adj_ref.shape
    his = table_ref.shape[1]
    table = table_ref[...]
    top_part = table // 65536
    mid_part = (table // 256) % 256
    low_part = table % 256
    parts = jnp.concatenate([top_part, mid_part, low_part], axis=0).astype(jnp.float32).astype(jnp.bfloat16)
    row_hi = lax.broadcasted_iota(jnp.int32, (his, near_rows), 0)
    row_lo = lax.broadcasted_iota(jnp.int32, (LANES, near_rows), 0)
    for column in range(fan):
        position = adj_ref[column : column + 1, :]
        marks = jnp.where(row_hi == position // LANES, 1.0, 0.0).astype(jnp.bfloat16)
        found = dot(parts, marks)
        value = found[:LANES] * 65536.0 + found[LANES : 2 * LANES] * 256.0 + found[2 * LANES :]
        value = jnp.where(row_lo == position % LANES, value, 0.0)
        ids_ref[column : column + 1, :] = jnp.sum(value, axis=0, keepdims=True).astype(jnp.int32)
    near = near_ref[...]
    plane = near // per_plane
    row_plane = lax.broadcasted_iota(jnp.int32, (groups, near_rows), 0)
    marks = jnp.where(row_plane == plane, 1.0, 0.0)
    earlier = lax.broadcasted_iota(jnp.int32, (near_rows, near_rows), 0) < lax.broadcasted_iota(
        jnp.int32, (near_rows, near_rows), 1
    )
    counts = dot(marks.astype(jnp.bfloat16), jnp.where(earlier, 1.0, 0.0).astype(jnp.bfloat16))
    rank = jnp.sum(counts * marks, axis=0, keepdims=True).astype(jnp.int32)
    ids_ref[fan : fan + 1, :] = near + rank * nodes


def compose(adjacency, table, near, nodes, per_plane, groups):
    near_rows, fan = adjacency.shape
    return pl.pallas_call(
        functools.partial(compose_kernel, nodes, per_plane, groups),
        out_shape=jax.ShapeDtypeStruct((fan + 1, near_rows), jnp.int32),
        in_specs=[VMEM, VMEM, VMEM],
        out_specs=VMEM,
        compiler_params=pltpu.CompilerParams(vmem_limit_bytes=32 * MIB),
        name="compose_ids",
    )(adjacency.T, table, near)


def partial_kernel(places, fan, near_rows, capacity, *refs):
    index_ref = refs[0]
    piece_refs = refs[1 : 1 + len(places)]
    out_ref, table, sums, kept = refs[1 + len(places) :]
    units = piece_refs[0].shape[1] // LANES
    total = table.shape[0] // 8 - 1
    chunk = 256

    def fill(piece, start):
        def step(i, carry):
            values = piece[pl.ds(pl.multiple_of(i * chunk, chunk), chunk), :].astype(jnp.float32)
            base = (start + i * chunk) * 8
            for unit in range(units):
                table[pl.ds(base + unit, chunk, stride=8), :] = values[
                    :, unit * LANES : (unit + 1) * LANES
                ]
            return carry

        lax.fori_loop(0, piece.shape[0] // chunk, step, 0)

    for piece, start in zip(piece_refs, places):
        fill(piece, start)
    table[total * 8 :, :] = jnp.zeros((8, LANES), jnp.float32)
    trainers = out_ref.shape[0]
    unroll = 8

    for trainer in range(trainers):
        kept[...] = jnp.zeros_like(kept)

        def step(i, carry):
            for u in range(unroll):
                n = i * unroll + u
                rows = [
                    table[pl.ds(pl.multiple_of(index_ref[trainer, j, n], 8), 8), :]
                    for j in range(fan)
                ]
                while len(rows) > 1:
                    rows = [a + b for a, b in zip(rows[0::2], rows[1::2])] + (
                        rows[-1:] if len(rows) % 2 else []
                    )
                sums[pl.ds(pl.multiple_of(n * 8, 8), 8), :] = rows[0]
                source = pl.multiple_of(index_ref[trainer, fan, n], 8)
                target = pl.multiple_of(index_ref[trainer, fan + 1, n], 8)
                kept[pl.ds(target, 8), :] = table[pl.ds(source, 8), :]
            return carry

        lax.fori_loop(0, near_rows // unroll, step, 0)
        for unit in range(units):
            lanes = slice(unit * LANES, (unit + 1) * LANES)
            out_ref[trainer, :near_rows, lanes] = sums[
                pl.ds(unit, near_rows, stride=8), :
            ].astype(jnp.bfloat16)
            out_ref[trainer, near_rows:, lanes] = kept[
                pl.ds(unit, capacity, stride=8), :
            ].astype(jnp.bfloat16)


def partial_sums(index, pieces, places, total, capacity):
    trainers, columns, near_rows = index.shape
    width = pieces[0].shape[1]
    return pl.pallas_call(
        functools.partial(partial_kernel, places, columns - 2, near_rows, capacity),
        out_shape=jax.ShapeDtypeStruct((trainers, near_rows + capacity, width), jnp.bfloat16),
        in_specs=[SMEM] + [VMEM] * len(pieces),
        out_specs=VMEM,
        scratch_shapes=[
            pltpu.VMEM(((total + 1) * 8, LANES), jnp.float32),
            pltpu.VMEM(((near_rows + 1) * 8, LANES), jnp.float32),
            pltpu.VMEM(((capacity + 1) * 8, LANES), jnp.float32),
        ],
        compiler_params=pltpu.CompilerParams(vmem_limit_bytes=60 * MIB),
        name="partial_sums",
    )(index, *pieces)


def trainer_kernel(sizes, scale, *refs):
    groups, rows_low, rows_top, classes, class_pad = sizes
    place_ref, labels_ref, adj_ref, column_ref, wl_ref, wt_ref = refs[:6]
    block_refs = refs[6 : 6 + groups]
    logits_ref, keep_ref, send_ref, li, hidden, slope, top_in, wt = refs[6 + groups :]
    seeds, fan_top = adj_ref.shape
    near_rows, low_width = li.shape
    feat = low_width // 2
    width = hidden.shape[1]
    capacity = block_refs[0].shape[0] - near_rows
    here, mine, rep = place_ref[0], place_ref[1], place_ref[2]
    fan_low = place_ref[3].astype(jnp.float32)

    column = column_ref[...]
    rows_cap = lax.broadcasted_iota(jnp.int32, (capacity, near_rows), 0)
    near = None
    total = None
    for k in range(groups):
        marks = jnp.where(rows_cap + k * capacity == column, 1.0, 0.0).astype(jnp.bfloat16)
        term = dot(marks, block_refs[k][near_rows:, :], 0, 0)
        near = term if near is None else near + term
        part = block_refs[k][:near_rows, :].astype(jnp.float32)
        total = part if total is None else total + part
    li[:, :feat] = near.astype(jnp.bfloat16)
    li[:, feat:] = (total / fan_low).astype(jnp.bfloat16)

    wt[...] = jnp.zeros_like(wt)
    wt[:, :classes] = wt_ref[...].astype(jnp.bfloat16)

    factor = math.sqrt(2.0 / math.pi)
    step = 256
    for c in range(width // step):
        cols = slice(c * step, (c + 1) * step)
        v = dot(li[...], wl_ref[:, cols].astype(jnp.bfloat16))
        square = v * v
        t = jnp.tanh(factor * (v + 0.044715 * v * square))
        half = 0.5 * (1.0 + t)
        hidden[:, cols] = (v * half).astype(jnp.bfloat16)
        slope[:, cols] = half + 0.5 * v * (1.0 - t * t) * factor * (1.0 + 3.0 * 0.044715 * square)

    lane_near = lax.broadcasted_iota(jnp.int32, (seeds, near_rows), 1)
    counts = jnp.zeros((seeds, near_rows), jnp.float32)
    for j in range(fan_top):
        counts = counts + jnp.where(adj_ref[:, j : j + 1] == lane_near, 1.0, 0.0)
    counts = counts.astype(jnp.bfloat16)
    top_in[:, :width] = hidden[:seeds, :]
    top_in[:, width:] = (dot(counts, hidden[...]) / fan_top).astype(jnp.bfloat16)
    logits = dot(top_in[...], wt[...])
    logits_ref[...] = logits[:, :classes]
    lane_class = lax.broadcasted_iota(jnp.int32, (seeds, class_pad), 1)
    powers = jnp.where(lane_class < classes, jnp.exp(logits), 0.0)
    chances = powers / jnp.sum(powers, axis=1, keepdims=True)
    targets = jnp.where(lane_class == labels_ref[...], 1.0, 0.0)
    dlogits = ((chances - targets) * scale).astype(jnp.bfloat16)
    dinput = dot(dlogits, wt[...], 1, 1)
    spread = dinput[:, width:] / fan_top
    high = spread.astype(jnp.bfloat16)
    low = (spread - high.astype(jnp.float32)).astype(jnp.bfloat16)
    dhidden = dot(counts, high, 0, 0) + dot(counts, low, 0, 0)
    hidden[:seeds, :] = ((dhidden[:seeds] + dinput[:, :width]) * slope[:seeds, :]).astype(jnp.bfloat16)
    hidden[seeds:, :] = (dhidden[seeds:] * slope[seeds:, :]).astype(jnp.bfloat16)

    first = rep == 0
    members = low_width // rows_low
    stores = members // 2
    lane_groups = width // class_pad
    sub = rows_top // lane_groups

    def slot(store):
        plane, inner = store // PLANE, store % PLANE
        relative = plane - here
        relative = jnp.where(relative < 0, relative + groups, relative)
        return lax.bitwise_xor(mine, jnp.int32(inner)), relative

    tile = 384
    pair = 2 * rows_low
    for m in range(low_width // tile):
        grad = dot(li[:, m * tile : (m + 1) * tile], hidden[...], 0, 0)
        for s in range(tile // pair):
            even = grad[s * pair : s * pair + rows_low]
            odd = grad[s * pair + rows_low : (s + 1) * pair]
            a, b = slot(m * (tile // pair) + s)
            keep_ref[a, b, :rows_low, :] = jnp.where(first, even, odd)
            send_ref[a, b, :rows_low, :] = jnp.where(first, odd, even).astype(jnp.bfloat16)
    grad = dot(top_in[...], dlogits, 0, 0)
    for s in range(stores):
        even = grad[2 * s * rows_top : (2 * s + 1) * rows_top]
        odd = grad[(2 * s + 1) * rows_top : (2 * s + 2) * rows_top]
        own = jnp.where(first, even, odd)
        other = jnp.where(first, odd, even)
        a, b = slot(s)
        own = jnp.concatenate([own[g * sub : (g + 1) * sub] for g in range(lane_groups)], axis=1)
        other = jnp.concatenate([other[g * sub : (g + 1) * sub] for g in range(lane_groups)], axis=1)
        keep_ref[a, b, rows_low:, :] = own
        send_ref[a, b, rows_low:, :] = other.astype(jnp.bfloat16)


def trainer_step(place, labels, adj_top, column, wl, wt, blocks, sizes, scale):
    groups, rows_low, rows_top, classes, class_pad = sizes
    seeds = adj_top.shape[0]
    low_width, width = wl.shape
    near_rows = column.shape[1]
    rows = rows_low + rows_top * class_pad // width
    return pl.pallas_call(
        functools.partial(trainer_kernel, sizes, scale),
        out_shape=(
            jax.ShapeDtypeStruct((seeds, classes), jnp.float32),
            jax.ShapeDtypeStruct((PLANE, groups, rows, width), jnp.float32),
            jax.ShapeDtypeStruct((PLANE, groups, rows, width), jnp.bfloat16),
        ),
        in_specs=[SMEM] + [VMEM] * (5 + groups),
        out_specs=(VMEM, VMEM, VMEM),
        scratch_shapes=[
            pltpu.VMEM((near_rows, low_width), jnp.bfloat16),
            pltpu.VMEM((near_rows, width), jnp.bfloat16),
            pltpu.VMEM((near_rows, width), jnp.float32),
            pltpu.VMEM((seeds, 2 * width), jnp.bfloat16),
            pltpu.VMEM((2 * width, class_pad), jnp.bfloat16),
        ],
        compiler_params=pltpu.CompilerParams(vmem_limit_bytes=60 * MIB),
        name="trainer_step",
    )(place, labels, adj_top, column, wl, wt, *blocks)


def adam_part(gradient, moment, square):
    moment_new = beta_one * moment + (1.0 - beta_one) * gradient
    square_new = beta_two * square + (1.0 - beta_two) * gradient * gradient
    update = moment_new / bias_one / (jnp.sqrt(square_new / bias_two) + adam_eps)
    return learn_rate * update, moment_new, square_new


def adam_kernel(class_pad, parts, *refs):
    part_refs = refs[:parts]
    ml, sl, mt, st, nml, nsl, nmt, nst, delta = refs[parts:]
    rows_low, width = ml.shape
    rows_top, classes = mt.shape
    lane_groups = width // class_pad
    sub = rows_top // lane_groups
    total = part_refs[0][...]
    for ref in part_refs[1:]:
        total = total + ref[...].astype(jnp.float32)
    step, nml[...], nsl[...] = adam_part(total[:rows_low], ml[...], sl[...])
    top = total[rows_low:]
    pieces = []
    for g in range(lane_groups):
        rows = slice(g * sub, (g + 1) * sub)
        gradient = top[:, g * class_pad : g * class_pad + classes]
        piece, nmt[rows, :], nst[rows, :] = adam_part(gradient, mt[rows, :], st[rows, :])
        pieces.append(
            jnp.concatenate([piece, jnp.zeros((sub, class_pad - classes), jnp.float32)], axis=1)
        )
    whole = jnp.concatenate([step, jnp.concatenate(pieces, axis=1)], axis=0)
    delta[...] = whole.astype(jnp.bfloat16)


def adam_share(parts, ml, sl, mt, st, class_pad):
    rows, width = parts[0].shape
    shape = lambda a: jax.ShapeDtypeStruct(a.shape, jnp.float32)
    return pl.pallas_call(
        functools.partial(adam_kernel, class_pad, len(parts)),
        out_shape=(shape(ml), shape(sl), shape(mt), shape(st), jax.ShapeDtypeStruct((rows, width), jnp.bfloat16)),
        in_specs=[VMEM] * (len(parts) + 4),
        out_specs=(VMEM,) * 5,
        compiler_params=pltpu.CompilerParams(vmem_limit_bytes=32 * MIB),
        name="adam_share",
    )(*parts, ml, sl, mt, st)


def apply_kernel(sizes, place_ref, wl, wt, *refs):
    groups, rows_low, rows_top, classes, class_pad = sizes
    delta_refs, (nl, nt) = refs[: 2 * PLANE], refs[2 * PLANE :]
    here, mine, rep = place_ref[0], place_ref[1], place_ref[2]
    width = wl.shape[2]
    lane_groups = width // class_pad
    sub = rows_top // lane_groups
    for d in range(PLANE):
        for half in range(2):
            for k in range(groups):
                plane = here + k
                plane = jnp.where(plane >= groups, plane - groups, plane)
                store = plane * PLANE + lax.bitwise_xor(mine, jnp.int32(d))
                core = rep if half == 0 else 1 - rep
                position = store * 2 + core
                delta = delta_refs[2 * d + half][k].astype(jnp.float32)
                nl[position] = wl[position] - delta[:rows_low]
                for g in range(lane_groups):
                    rows = slice(g * sub, (g + 1) * sub)
                    nt[position, rows, :] = (
                        wt[position, rows, :]
                        - delta[rows_low:, g * class_pad : g * class_pad + classes]
                    )


def apply_updates(place, wl, wt, deltas, sizes):
    groups, rows_low, rows_top, classes, class_pad = sizes
    low3 = wl.reshape(-1, rows_low, wl.shape[1])
    top3 = wt.reshape(-1, rows_top, wt.shape[1])
    nl, nt = pl.pallas_call(
        functools.partial(apply_kernel, sizes),
        out_shape=(
            jax.ShapeDtypeStruct(low3.shape, jnp.float32),
            jax.ShapeDtypeStruct(top3.shape, jnp.float32),
        ),
        in_specs=[SMEM] + [VMEM] * (2 + len(deltas)),
        out_specs=(VMEM, VMEM),
        compiler_params=pltpu.CompilerParams(vmem_limit_bytes=60 * MIB),
        name="apply_updates",
    )(place, low3, top3, *deltas)
    return nl.reshape(wl.shape), nt.reshape(wt.shape)


def per_device(
    features,
    owners_near,
    slots_near,
    owners_far,
    slots_far,
    adjacency_low,
    adjacency_top,
    labels,
    weights_low,
    weights_top,
    first_low,
    second_low,
    first_top,
    second_top,
):
    stores = lax.axis_size("store")
    groups = stores // PLANE
    members = stores * lax.axis_size("rep")
    index = lax.axis_index("store")
    here, mine, rep = index // PLANE, index % PLANE, lax.axis_index("rep")
    store_rows = features.shape[0]
    half = store_rows // 2
    near_rows, fan = adjacency_low.shape
    far_rows = owners_far.shape[0]
    nodes = stores * store_rows
    per_plane = PLANE * store_rows
    near_limit = 2 * near_rows // stores
    capacity = min(near_rows, PLANE * near_limit)
    classes = weights_top.shape[1]
    class_pad = -(-classes // LANES) * LANES
    rows_low, rows_top = first_low.shape[0], first_top.shape[0]
    sizes = (groups, rows_low, rows_top, classes, class_pad)
    bf16 = jnp.bfloat16

    def across(x, distance):
        return lax.ppermute(x, "store", [(i, i ^ distance) for i in range(stores)])

    def along(x, hops):
        return lax.ppermute(x, "store", [(i, (i + hops * PLANE) % stores) for i in range(stores)])

    def sibling(x):
        return lax.ppermute(x, "rep", [(0, 1), (1, 0)])

    own_half = lax.dynamic_slice_in_dim(features, rep * half, half, 0)
    from_x = across(own_half, 1)
    from_y = across(own_half, 2)
    gid_near = owners_near[:, 0] * store_rows + slots_near[:, 0]
    gid_far = owners_far[:, 0] * store_rows + slots_far[:, 0]
    table = jnp.concatenate([gid_near, gid_far]).reshape(-1, LANES)
    table = jnp.pad(table, ((0, -table.shape[0] % 16), (0, 0))).T
    near_line = gid_near.reshape(1, near_rows)
    ids = compose(adjacency_low, table, near_line, nodes, per_plane, groups)
    ids_all = [ids] + [along(ids, -k) for k in range(1, groups)]
    quarter = half // 2
    corner_a = across(from_x[:quarter], 2)
    corner_b = across(from_y[quarter:], 1)
    parts = [from_x, from_y, corner_a, corner_b]
    pieces = [features, from_x, sibling(from_x), from_y, sibling(from_y)]
    pieces += [corner_a, corner_b, sibling(corner_a), sibling(corner_b)]
    places = [0, store_rows, store_rows + half, 2 * store_rows, 2 * store_rows + half]
    places += [3 * store_rows + quarter * i for i in range(4)]

    def local_rows(ids_of):
        neighbours = ids_of[:fan]
        packed = ids_of[fan : fan + 1]
        rank, near_gid = packed // nodes, packed % nodes
        gid = jnp.concatenate([neighbours, near_gid], axis=0)
        held = gid // per_plane == here
        distance = lax.bitwise_xor((gid // store_rows) % PLANE, mine)
        row = gid % store_rows
        turned = jnp.where(distance == 0, row, (row + rep * half) % store_rows)
        row = jnp.where(held, distance * store_rows + turned, per_plane)
        target = jnp.where(held[fan:], rank, capacity)
        return jnp.concatenate([row, target], axis=0) * 8

    per_call = -(-groups // 4)
    order = list(range(1, groups)) + [0]
    blocks = {}
    for start in range(0, groups, per_call):
        turns = order[start : start + per_call]
        lists = jnp.stack([local_rows(ids_all[k]) for k in turns])
        made = partial_sums(lists, pieces, places, per_plane, capacity)
        for i, k in enumerate(turns):
            blocks[k] = along(made[i], k) if k else made[i]

    packed = ids[fan : fan + 1]
    source = (here - (packed % nodes) // per_plane) % groups
    column = source * capacity + packed // nodes
    place = jnp.stack([here, mine, rep, jnp.int32(fan)]).astype(jnp.int32)
    scale = 1.0 / (labels.shape[0] * members)
    logits, keep, send = trainer_step(
        place,
        labels[:, None],
        adjacency_top,
        column,
        weights_low,
        weights_top,
        [blocks[k] for k in range(groups)],
        sizes,
        scale,
    )
    total = keep + sibling(send).astype(jnp.float32)
    arrived = [across(total[d].astype(bf16), d) for d in range(1, PLANE)]
    total = total[0] + sum(a.astype(jnp.float32) for a in arrived)
    shares = [total[0]] + [along(total[k].astype(bf16), k) for k in range(1, groups)]
    new_first_low, new_second_low, new_first_top, new_second_top, delta = adam_share(
        shares, first_low, second_low, first_top, second_top, class_pad
    )
    lined = jnp.stack([delta] + [along(delta, -k) for k in range(1, groups)])
    sheets = [lined] + [across(lined, d) for d in range(1, PLANE)]
    deltas = []
    for sheet in sheets:
        deltas += [sheet, sibling(sheet)]
    new_low, new_top = apply_updates(place, weights_low, weights_top, deltas, sizes)
    return (logits, new_low, new_first_low, new_second_low, new_top, new_first_top, new_second_top)


def solution(mesh):
    both = P(("store", "rep"), None)
    return jax.shard_map(
        per_device,
        mesh=mesh,
        in_specs=(P("store", None),)
        + (both,) * 6
        + (P(("store", "rep")), P(), P(), both, both, both, both),
        out_specs=(both, P(), both, both, P(), both, both),
        check_vma=False,
    )
```

time: 959 us -> 308 us (0.32)
  waiting for transfers between devices: 519 us -> 134 us
  local copies, waits for them, and re-layouts: 308 us -> 12.1 us
  Pallas kernels: 0 us -> 115 us
  other arithmetic: 66.8 us -> 7.77 us
  matrix products: 16.4 us -> 0 us
  between operations: 14.4 us -> 1 us
  starting transfers between devices: 24.7 us -> 37.5 us
    gather x29 -> x0, local copies, waits for them, and re-layouts: 206 us -> none  [the longest x15 93.8 us: local_step(): gathered = gathered + fetched[adjacency_low[:, column]].astype(jnp.float32)]
    all_to_all x4 -> x0, waiting for transfers between devices: 202 us -> none  [the longest x2 202 us: fetch_rows(): lax.all_to_all(found, 'store', split_axis=0, concat_axis=0, tiled=True)]
    psum x1 -> x0, waiting for transfers between devices: 191 us -> none  [per_device(): whole_low, whole_top = lax.psum((grad_low, grad_top), ('store', 'rep'))]
    ppermute x0 -> x31, waiting for transfers between devices: none -> 134 us  [the longest x10 80.2 us: across(): return lax.ppermute(x, 'store', [(i, i ^ distance) for i in range(stores)])]
    all_gather x2 -> x0, waiting for transfers between devices: 126 us -> none  [the longest x1 70.1 us: per_device(): lax.all_gather(part_low, ('store', 'rep'), axis=0, tiled=True)]
    pallas_call x0 -> x8, Pallas kernels: none -> 115 us  [the longest x4 89.1 us: partial_sums(): pl.pallas_call(functools.partial(partial_kernel, places, columns - 2, nea...]
    scatter x1 -> x0, local copies, waits for them, and re-layouts: 70.9 us -> none  [bucket(): jnp.zeros((stores, capacity), jnp.int32).at[owners, places].set(slots)]
    scatter-add x10 -> x0, other arithmetic: 45 us -> none  [local_step(): dhidden = dhidden.at[adjacency_top[:, column]].add(spread)]
  transfers between devices with their start and end apart: 7 -> 31, of which waited for: 5 -> 17; matrix products, arithmetic and copies ran while one was open for 7% -> 3% of each run, Pallas kernels for 0% -> 22%
where the time goes in v1:
time: 308 us
  waiting for transfers between devices  134 us (44%)
  Pallas kernels  115 us (37%)
  starting transfers between devices  37.5 us (12%)
  local copies, waits for them, and re-layouts  12.1 us (4%)
  other arithmetic  7.77 us (3%)
    pallas_call x4, Pallas kernels, partial_sums(): pl.pallas_call(functools.partial(partial_kernel, places, columns - 2, nea...  89.1 us
    ppermute x10, waiting for transfers between devices, across(): return lax.ppermute(x, 'store', [(i, i ^ distance) for i in range(stores)])  80.2 us
    ppermute x12, waiting for transfers between devices, along(): lax.ppermute(x, 'store', [(i, (i + hops * PLANE) % stores) for i in range...  48.6 us
    ppermute x12, starting transfers between devices, along(): lax.ppermute(x, 'store', [(i, (i + hops * PLANE) % stores) for i in range...  14.8 us
    pallas_call x1, Pallas kernels, trainer_step(): pl.pallas_call(functools.partial(trainer_kernel, sizes, scale), out_shape...  14.4 us
    ppermute x9, starting transfers between devices, sibling(): return lax.ppermute(x, 'rep', [(0, 1), (1, 0)])  12.2 us
    ppermute x10, starting transfers between devices, across(): return lax.ppermute(x, 'store', [(i, i ^ distance) for i in range(stores)])  10.5 us
    pallas_call x1, Pallas kernels, apply_updates(): pl.pallas_call(functools.partial(apply_kernel, sizes), out_shape=(jax.Sha...  8.75 us
  transfers between devices with their start and end apart: 31, of which 17 were waited for; matrix products, arithmetic and copies ran while one was open for 3% of the time, Pallas kernels for 22%

profile of v1, /device:TPU:9, one launch (start us, length us, event | category | flops | bytes accessed | tf_op | source)
XLA Modules:
  0.0 307.8 jit_solution(14201297086066468697)
XLA Ops:
  0.7 2.7 constant_dynamic-slice_fusion
  6.0 1.8 compose_ids.1
  11.7 27.1 %collective-permute-done.2.refs_4_ = bf16[1024,768]{1,0:T(8,128)(2,1)S(1)} collective-permute-done((bf16[1024,768]{1,0:T(8,128)(2,1)}, bf16[1024,768]{1,0:T(8,128)(2,1)S(1)}, u32[]{:S(2)}, u32[]{:S(2)}) %collective-permute-start.2) | collective-permute-done | bytes 1572896 | tf_op jit(solution)/shard_map/ppermute | solution.py:393
  41.5 2.1 collective-permute-start.3
  44.0 12.5 %collective-permute-done.5.refs_7_ = bf16[512,768]{1,0:T(8,128)(2,1)S(1)} collective-permute-done((bf16[512,768]{1,0:T(8,128)(2,1)S(1)}, bf16[512,768]{1,0:T(8,128)(2,1)S(1)}, u32[]{:S(2)}, u32[]{:S(2)}) %collective-permute-start.5) | collective-permute-done | bytes 786464 | tf_op jit(solution)/shard_map/ppermute | solution.py:393
  56.5 2.5 collective-permute-start.7
  64.5 22.3 %partial_sums.5 = bf16[1,768,768]{2,1,0:T(8,128)(2,1)} custom-call(s32[1,17,512]{2,1,0:T(8,128)} %add_multiply_fusion.1.refs_0_, bf16[2048,768]{1,0:T(8,128)(2,1)} %refs_1_.7, bf16[1024,768]{1,0:T(8,128)(2,1)} %copy-done.6, bf16[1024,768]{1,0:T(8,128)(2,1)} %collective-permute-done.1.refs_3_, bf16[1024,768]{1,0:T(8,128)(2,1)} %copy-done.5, ...), custom_call_target="tpu_custom_call" | custom-call | tf_op jit(solution)/shard_map/partial_sums/pallas_call | solution.py:131
  88.1 22.3 %partial_sums.6 = bf16[1,768,768]{2,1,0:T(8,128)(2,1)} custom-call(s32[1,17,512]{2,1,0:T(8,128)} %add_multiply_fusion.2.refs_0_, bf16[2048,768]{1,0:T(8,128)(2,1)} %refs_1_.7, bf16[1024,768]{1,0:T(8,128)(2,1)} %copy-done.6, bf16[1024,768]{1,0:T(8,128)(2,1)} %collective-permute-done.1.refs_3_, bf16[1024,768]{1,0:T(8,128)(2,1)} %copy-done.5, ...), custom_call_target="tpu_custom_call" | custom-call | tf_op jit(solution)/shard_map/partial_sums/pallas_call | solution.py:131
  111.4 22.3 %partial_sums.7 = bf16[1,768,768]{2,1,0:T(8,128)(2,1)} custom-call(s32[1,17,512]{2,1,0:T(8,128)} %add_multiply_fusion.3.refs_0_, bf16[2048,768]{1,0:T(8,128)(2,1)} %refs_1_.7, bf16[1024,768]{1,0:T(8,128)(2,1)} %copy-done.6, bf16[1024,768]{1,0:T(8,128)(2,1)} %collective-permute-done.1.refs_3_, bf16[1024,768]{1,0:T(8,128)(2,1)} %copy-done.5, ...), custom_call_target="tpu_custom_call" | custom-call | tf_op jit(solution)/shard_map/partial_sums/pallas_call | solution.py:131
  136.7 1.8 copy.30.refs_5_
  140.5 22.3 %partial_sums.4 = bf16[1,768,768]{2,1,0:T(8,128)(2,1)} custom-call(s32[1,17,512]{2,1,0:T(8,128)} %add_multiply_fusion.refs_0_, bf16[2048,768]{1,0:T(8,128)(2,1)} %refs_1_.7, bf16[1024,768]{1,0:T(8,128)(2,1)} %copy-done.6, bf16[1024,768]{1,0:T(8,128)(2,1)} %collective-permute-done.1.refs_3_, bf16[1024,768]{1,0:T(8,128)(2,1)} %copy-done.5, ...), custom_call_target="tpu_custom_call" | custom-call | tf_op jit(solution)/shard_map/partial_sums/pallas_call | solution.py:131
  162.8 26.8 %collective-permute-done.11.refs_8_ = bf16[768,768]{1,0:T(8,128)(2,1)} collective-permute-done((bf16[768,768]{1,0:T(8,128)(2,1)}, bf16[768,768]{1,0:T(8,128)(2,1)}, u32[]{:S(2)}, u32[]{:S(2)}) %collective-permute-start.11) | collective-permute-done | bytes 1179680 | tf_op jit(solution)/shard_map/ppermute | solution.py:396
  189.6 2.2 collective-permute-done.13.refs_9_
  191.7 14.4 %trainer_step.1 = (f32[128,153]{1,0:T(8,128)}, f32[4,4,64,1024]{3,2,1,0:T(8,128)}, bf16[4,4,64,1024]{3,2,1,0:T(8,128)(2,1)}) custom-call(s32[4]{0:T(128)} %pad_add_fusion.4.refs_0_.place_ref, s32[128,1]{1,0:T(8,128)} %copy.28.refs_1_, s32[128,10]{1,0:T(8,128)} %copy.29.refs_2_, s32[1,512]{1,0:T(1,128)} %fusion.46.refs_3_, f32[1536,1024]{1,0:T(8,128)} %refs_4_.2, ...), custom_call_target="tpu_custom_call" | custom-call | tf_op jit(solution)/shard_map/trainer_step/pallas_call | solution.py:249
  206.6 4.0 %collective-permute-done.14 = bf16[4,4,64,1024]{3,2,1,0:T(8,128)(2,1)S(1)} collective-permute-done((bf16[4,4,64,1024]{3,2,1,0:T(8,128)(2,1)}, bf16[4,4,64,1024]{3,2,1,0:T(8,128)(2,1)S(1)}, u32[]{:S(2)}, u32[]{:S(2)}) %collective-permute-start.14) | collective-permute-done | bytes 2097184 | tf_op jit(solution)/shard_map/ppermute | solution.py:399
  210.6 3.1 %fusion.54 = (bf16[4,4,64,1024]{3,2,1,0:T(8,128)(2,1)S(1)}, f32[4,4,64,1024]{3,2,1,0:T(8,128)S(1)}) fusion(f32[4,4,64,1024]{3,2,1,0:T(8,128)} %get-tuple-element.18, bf16[4,4,64,1024]{3,2,1,0:T(8,128)(2,1)S(1)} %collective-permute-done.14), kind=kLoop, calls=%fused_computation.168 | loop fusion | flops 3145728 | bytes 12582912 | tf_op jit(solution)/shard_map/convert.5
  214.7 1.6 collective-permute-start.17
  216.6 10.5 %collective-permute-done.15 = bf16[4,64,1024]{2,1,0:T(8,128)(2,1)S(1)} collective-permute-done((bf16[4,64,1024]{2,1,0:T(8,128)(2,1)S(1)}, bf16[4,64,1024]{2,1,0:T(8,128)(2,1)S(1)}, u32[]{:S(2)}, u32[]{:S(2)}) %collective-permute-start.15) | collective-permute-done | bytes 524320 | tf_op jit(solution)/shard_map/ppermute | solution.py:393
  227.1 12.2 %collective-permute-done.17 = bf16[4,64,1024]{2,1,0:T(8,128)(2,1)S(1)} collective-permute-done((bf16[4,64,1024]{2,1,0:T(8,128)(2,1)S(1)}, bf16[4,64,1024]{2,1,0:T(8,128)(2,1)S(1)}, u32[]{:S(2)}, u32[]{:S(2)}) %collective-permute-start.17) | collective-permute-done | bytes 524320 | tf_op jit(solution)/shard_map/ppermute | solution.py:393
  241.2 2.3 collective-permute-start.18
  243.5 1.5 collective-permute-done.20.refs_3_
  245.0 1.5 collective-permute-done.19.refs_2_
  246.5 5.4 %collective-permute-done.18.refs_1_ = bf16[64,1024]{1,0:T(8,128)(2,1)S(1)} collective-permute-done((bf16[64,1024]{1,0:T(8,128)(2,1)S(1)}, bf16[64,1024]{1,0:T(8,128)(2,1)S(1)}, u32[]{:S(2)}, u32[]{:S(2)}) %collective-permute-start.18) | collective-permute-done | bytes 131104 | tf_op jit(solution)/shard_map/ppermute | solution.py:396
  252.8 2.2 collective-permute-start.23
  257.5 7.9 %collective-permute-done.22 = bf16[64,1024]{1,0:T(8,128)(2,1)S(1)} collective-permute-done((bf16[64,1024]{1,0:T(8,128)(2,1)S(1)}, bf16[64,1024]{1,0:T(8,128)(2,1)S(1)}, u32[]{:S(2)}, u32[]{:S(2)}) %collective-permute-start.22) | collective-permute-done | bytes 131104 | tf_op jit(solution)/shard_map/ppermute | solution.py:396
  265.4 2.0 collective-permute-done.21
  270.2 1.8 collective-permute-start.24
  272.0 9.0 %collective-permute-done.29.refs_6_ = bf16[4,64,1024]{2,1,0:T(8,128)(2,1)S(1)} collective-permute-done((bf16[4,64,1024]{2,1,0:T(8,128)(2,1)S(1)}, bf16[4,64,1024]{2,1,0:T(8,128)(2,1)S(1)}, u32[]{:S(2)}, u32[]{:S(2)}) %collective-permute-start.29) | collective-permute-done | bytes 524320 | tf_op jit(solution)/shard_map/ppermute | solution.py:393
  281.0 3.3 %collective-permute-start.30 = (bf16[4,64,1024]{2,1,0:T(8,128)(2,1)S(1)}, bf16[4,64,1024]{2,1,0:T(8,128)(2,1)S(1)}, u32[]{:S(2)}, u32[]{:S(2)}) collective-permute-start(bf16[4,64,1024]{2,1,0:T(8,128)(2,1)S(1)} %collective-permute-done.29.refs_6_), channel_id=1, source_target_pairs={{0,1},{1,0},{2,3},{3,2},{4,5},{5,4},{6,7},{7,6},{8,9},{9,8},{10,11... | collective-permute-start | bytes 1572872 | tf_op jit(solution)/shard_map/ppermute | solution.py:399
  284.3 8.9 %collective-permute-done.27.refs_4_ = bf16[4,64,1024]{2,1,0:T(8,128)(2,1)S(1)} collective-permute-done((bf16[4,64,1024]{2,1,0:T(8,128)(2,1)S(1)}, bf16[4,64,1024]{2,1,0:T(8,128)(2,1)S(1)}, u32[]{:S(2)}, u32[]{:S(2)}) %collective-permute-start.27) | collective-permute-done | bytes 524320 | tf_op jit(solution)/shard_map/ppermute | solution.py:393
  296.3 8.8 %apply_updates.1 = (f32[32,48,1024]{2,1,0:T(8,128)}, f32[32,64,153]{2,1,0:T(8,128)}) custom-call(s32[4]{0:T(128)} %pad_add_fusion.4.refs_0_.place_ref, f32[32,48,1024]{2,1,0:T(8,128)} %bitcast.68, f32[32,64,153]{2,1,0:T(8,128)} %bitcast.69, bf16[4,64,1024]{2,1,0:T(8,128)(2,1)} %copy-done.12, bf16[4,64,1024]{2,1,0:T(8,128)(2,1)} %copy-done.18, ...), custom_call_target="tpu_custom_call" | custom-call | tf_op jit(solution)/shard_map/apply_updates/pallas_call | solution.py:343
  305.1 2.7 copy.33
  (128 shorter events, 35.0 us)
Async XLA Ops:
  3.4 35.5 %collective-permute-start.2 = (bf16[1024,768]{1,0:T(8,128)(2,1)}, bf16[1024,768]{1,0:T(8,128)(2,1)S(1)}, u32[]{:S(2)}, u32[]{:S(2)}) collective-permute-start(bf16[1024,768]{1,0:T(8,128)(2,1)} %constant_dynamic-slice_fusion), channel_id=1, source_target_pairs={{0,4},{2,6},{4,0},{6,2},{8,12},{10,14},{12,8},{14,10},{16,20},{18,... | collective-permute-start | bytes 4718600 | tf_op jit(solution)/shard_map/ppermute | solution.py:393
  4.6 35.6 %collective-permute-start = (bf16[1024,768]{1,0:T(8,128)(2,1)}, bf16[1024,768]{1,0:T(8,128)(2,1)S(1)}, u32[]{:S(2)}, u32[]{:S(2)}) collective-permute-start(bf16[1024,768]{1,0:T(8,128)(2,1)} %constant_dynamic-slice_fusion), channel_id=1, source_target_pairs={{0,2},{2,0},{4,6},{6,4},{8,10},{10,8},{12,14},{14,12},{16,18},{18,... | collective-permute-start | bytes 4718600 | tf_op jit(solution)/shard_map/ppermute | solution.py:393
  7.8 3.8 %collective-permute-start.12 = (s32[16,512]{1,0:T(8,128)S(1)}, s32[16,512]{1,0:T(8,128)S(1)}, u32[]{:S(2)}, u32[]{:S(2)}) collective-permute-start(s32[16,512]{1,0:T(8,128)S(1)} %compose_ids.1), channel_id=1, source_target_pairs={{0,8},{2,10},{4,12},{6,14},{8,16},{10,18},{12,20},{14,22},{16,24},... | collective-permute-start | bytes 98312 | tf_op jit(solution)/shard_map/ppermute | solution.py:396
  9.2 34.5 %collective-permute-start.10 = (s32[16,512]{1,0:T(8,128)S(1)}, s32[16,512]{1,0:T(8,128)S(1)}, u32[]{:S(2)}, u32[]{:S(2)}) collective-permute-start(s32[16,512]{1,0:T(8,128)S(1)} %compose_ids.1), channel_id=1, source_target_pairs={{0,16},{2,18},{4,20},{6,22},{8,24},{10,26},{12,28},{14,30},{16,0},... | collective-permute-start | bytes 98312 | tf_op jit(solution)/shard_map/ppermute | solution.py:396
  10.3 33.5 %collective-permute-start.8 = (s32[16,512]{1,0:T(8,128)S(1)}, s32[16,512]{1,0:T(8,128)S(1)}, u32[]{:S(2)}, u32[]{:S(2)}) collective-permute-start(s32[16,512]{1,0:T(8,128)S(1)} %compose_ids.1), channel_id=1, source_target_pairs={{0,24},{2,26},{4,28},{6,30},{8,0},{10,2},{12,4},{14,6},{16,8},{18,... | collective-permute-start | bytes 98312 | tf_op jit(solution)/shard_map/ppermute | solution.py:396
  38.9 17.6 %collective-permute-start.5 = (bf16[512,768]{1,0:T(8,128)(2,1)S(1)}, bf16[512,768]{1,0:T(8,128)(2,1)S(1)}, u32[]{:S(2)}, u32[]{:S(2)}) collective-permute-start(bf16[512,768]{1,0:T(8,128)(2,1)S(1)} %slice.99), channel_id=1, source_target_pairs={{0,2},{2,0},{4,6},{6,4},{8,10},{10,8},{12,14},{14,12},{16,18},{18,... | collective-permute-start | bytes 2359304 | tf_op jit(solution)/shard_map/ppermute | solution.py:393
  40.2 18.7 %collective-permute-start.4 = (bf16[512,768]{1,0:T(8,128)(2,1)S(1)}, bf16[512,768]{1,0:T(8,128)(2,1)S(1)}, u32[]{:S(2)}, u32[]{:S(2)}) collective-permute-start(bf16[512,768]{1,0:T(8,128)(2,1)S(1)} %slice.98), channel_id=1, source_target_pairs={{0,4},{2,6},{4,0},{6,2},{8,12},{10,14},{12,8},{14,10},{16,20},{18,... | collective-permute-start | bytes 2359304 | tf_op jit(solution)/shard_map/ppermute | solution.py:393
  41.5 20.6 %collective-permute-start.3 = (bf16[1024,768]{1,0:T(8,128)(2,1)S(1)}, bf16[1024,768]{1,0:T(8,128)(2,1)S(1)}, u32[]{:S(2)}, u32[]{:S(2)}) collective-permute-start(bf16[1024,768]{1,0:T(8,128)(2,1)S(1)} %collective-permute-done.2.refs_4_), channel_id=1, source_target_pairs={{0,1},{1,0},{2,3},{3,2},{4,5},{5,4},{6,7},{7,6},{8,9},{9,8},{10,11... | collective-permute-start | bytes 4718600 | tf_op jit(solution)/shard_map/ppermute | solution.py:399
  43.6 20.8 %collective-permute-start.1 = (bf16[1024,768]{1,0:T(8,128)(2,1)S(1)}, bf16[1024,768]{1,0:T(8,128)(2,1)}, u32[]{:S(2)}, u32[]{:S(2)}) collective-permute-start(bf16[1024,768]{1,0:T(8,128)(2,1)S(1)} %collective-permute-done.refs_2_), channel_id=1, source_target_pairs={{0,1},{1,0},{2,3},{3,2},{4,5},{5,4},{6,7},{7,6},{8,9},{9,8},{10,11... | collective-permute-start | bytes 4718600 | tf_op jit(solution)/shard_map/ppermute | solution.py:399
  56.5 5.7 %collective-permute-start.7 = (bf16[512,768]{1,0:T(8,128)(2,1)S(1)}, bf16[512,768]{1,0:T(8,128)(2,1)S(1)}, u32[]{:S(2)}, u32[]{:S(2)}) collective-permute-start(bf16[512,768]{1,0:T(8,128)(2,1)S(1)} %collective-permute-done.5.refs_7_), channel_id=1, source_target_pairs={{0,1},{1,0},{2,3},{3,2},{4,5},{5,4},{6,7},{7,6},{8,9},{9,8},{10,11... | collective-permute-start | bytes 2359304 | tf_op jit(solution)/shard_map/ppermute | solution.py:399
  58.9 4.4 %collective-permute-start.6 = (bf16[512,768]{1,0:T(8,128)(2,1)S(1)}, bf16[512,768]{1,0:T(8,128)(2,1)S(1)}, u32[]{:S(2)}, u32[]{:S(2)}) collective-permute-start(bf16[512,768]{1,0:T(8,128)(2,1)S(1)} %collective-permute-done.4.refs_6_), channel_id=1, source_target_pairs={{0,1},{1,0},{2,3},{3,2},{4,5},{5,4},{6,7},{7,6},{8,9},{9,8},{10,11... | collective-permute-start | bytes 2359304 | tf_op jit(solution)/shard_map/ppermute | solution.py:399
  86.8 76.0 %collective-permute-start.9 = (bf16[768,768]{1,0:T(8,128)(2,1)}, bf16[768,768]{1,0:T(8,128)(2,1)S(1)}, u32[]{:S(2)}, u32[]{:S(2)}) collective-permute-start(bf16[768,768]{1,0:T(8,128)(2,1)} %bitcast.72), channel_id=1, source_target_pairs={{0,8},{2,10},{4,12},{6,14},{8,16},{10,18},{12,20},{14,22},{16,24},... | collective-permute-start | bytes 3538952 | tf_op jit(solution)/shard_map/ppermute | solution.py:396
  110.3 79.2 %collective-permute-start.11 = (bf16[768,768]{1,0:T(8,128)(2,1)}, bf16[768,768]{1,0:T(8,128)(2,1)}, u32[]{:S(2)}, u32[]{:S(2)}) collective-permute-start(bf16[768,768]{1,0:T(8,128)(2,1)} %bitcast.73), channel_id=1, source_target_pairs={{0,16},{2,18},{4,20},{6,22},{8,24},{10,26},{12,28},{14,30},{16,0},... | collective-permute-start | bytes 3538952 | tf_op jit(solution)/shard_map/ppermute | solution.py:396
  133.8 58.0 %collective-permute-start.13 = (bf16[768,768]{1,0:T(8,128)(2,1)}, bf16[768,768]{1,0:T(8,128)(2,1)}, u32[]{:S(2)}, u32[]{:S(2)}) collective-permute-start(bf16[768,768]{1,0:T(8,128)(2,1)} %bitcast.74), channel_id=1, source_target_pairs={{0,24},{2,26},{4,28},{6,30},{8,0},{10,2},{12,4},{14,6},{16,8},{18,... | collective-permute-start | bytes 3538952 | tf_op jit(solution)/shard_map/ppermute | solution.py:396
  206.2 4.5 %collective-permute-start.14 = (bf16[4,4,64,1024]{3,2,1,0:T(8,128)(2,1)}, bf16[4,4,64,1024]{3,2,1,0:T(8,128)(2,1)S(1)}, u32[]{:S(2)}, u32[]{:S(2)}) collective-permute-start(bf16[4,4,64,1024]{3,2,1,0:T(8,128)(2,1)} %get-tuple-element.19), channel_id=1, source_target_pairs={{0,1},{1,0},{2,3},{3,2},{4,5},{5,4},{6,7},{7,6},{8,9},{9,8},{10,11... | collective-permute-start | bytes 6291464 | tf_op jit(solution)/shard_map/ppermute | solution.py:399
  213.9 13.2 %collective-permute-start.15 = (bf16[4,64,1024]{2,1,0:T(8,128)(2,1)S(1)}, bf16[4,64,1024]{2,1,0:T(8,128)(2,1)S(1)}, u32[]{:S(2)}, u32[]{:S(2)}) collective-permute-start(bf16[4,64,1024]{2,1,0:T(8,128)(2,1)S(1)} %get-tuple-element.63), channel_id=1, source_target_pairs={{0,2},{2,0},{4,6},{6,4},{8,10},{10,8},{12,14},{14,12},{16,18},{18,... | collective-permute-start | bytes 1572872 | tf_op jit(solution)/shard_map/ppermute | solution.py:393
  214.7 24.6 %collective-permute-start.17 = (bf16[4,64,1024]{2,1,0:T(8,128)(2,1)S(1)}, bf16[4,64,1024]{2,1,0:T(8,128)(2,1)S(1)}, u32[]{:S(2)}, u32[]{:S(2)}) collective-permute-start(bf16[4,64,1024]{2,1,0:T(8,128)(2,1)S(1)} %get-tuple-element.64), channel_id=1, source_target_pairs={{0,6},{2,4},{4,2},{6,0},{8,14},{10,12},{12,10},{14,8},{16,22},{18,... | collective-permute-start | bytes 1572872 | tf_op jit(solution)/shard_map/ppermute | solution.py:393
  216.3 23.0 %collective-permute-start.16 = (bf16[4,64,1024]{2,1,0:T(8,128)(2,1)S(1)}, bf16[4,64,1024]{2,1,0:T(8,128)(2,1)S(1)}, u32[]{:S(2)}, u32[]{:S(2)}) collective-permute-start(bf16[4,64,1024]{2,1,0:T(8,128)(2,1)S(1)} %get-tuple-element.65), channel_id=1, source_target_pairs={{0,4},{2,6},{4,0},{6,2},{8,12},{10,14},{12,8},{14,10},{16,20},{18,... | collective-permute-start | bytes 1572872 | tf_op jit(solution)/shard_map/ppermute | solution.py:393
  239.7 54.3 %copy-start.20 = (f32[128,153]{1,0:T(8,128)S(1)}, f32[128,153]{1,0:T(8,128)}, u32[]{:S(2)}) copy-start(f32[128,153]{1,0:T(8,128)} %get-tuple-element.34) | copy-start | bytes 235012
  239.7 5.3 %collective-permute-start.20 = (bf16[64,1024]{1,0:T(8,128)(2,1)S(1)}, bf16[64,1024]{1,0:T(8,128)(2,1)S(1)}, u32[]{:S(2)}, u32[]{:S(2)}) collective-permute-start(bf16[64,1024]{1,0:T(8,128)(2,1)S(1)} %get-tuple-element.66), channel_id=1, source_target_pairs={{0,24},{2,26},{4,28},{6,30},{8,0},{10,2},{12,4},{14,6},{16,8},{18,... | collective-permute-start | bytes 393224 | tf_op jit(solution)/shard_map/ppermute | solution.py:396
  239.8 6.7 %collective-permute-start.19 = (bf16[64,1024]{1,0:T(8,128)(2,1)S(1)}, bf16[64,1024]{1,0:T(8,128)(2,1)S(1)}, u32[]{:S(2)}, u32[]{:S(2)}) collective-permute-start(bf16[64,1024]{1,0:T(8,128)(2,1)S(1)} %get-tuple-element.67), channel_id=1, source_target_pairs={{0,16},{2,18},{4,20},{6,22},{8,24},{10,26},{12,28},{14,30},{16,0},... | collective-permute-start | bytes 393224 | tf_op jit(solution)/shard_map/ppermute | solution.py:396
  241.2 10.8 %collective-permute-start.18 = (bf16[64,1024]{1,0:T(8,128)(2,1)S(1)}, bf16[64,1024]{1,0:T(8,128)(2,1)S(1)}, u32[]{:S(2)}, u32[]{:S(2)}) collective-permute-start(bf16[64,1024]{1,0:T(8,128)(2,1)S(1)} %get-tuple-element.68), channel_id=1, source_target_pairs={{0,8},{2,10},{4,12},{6,14},{8,16},{10,18},{12,20},{14,22},{16,24},... | collective-permute-start | bytes 393224 | tf_op jit(solution)/shard_map/ppermute | solution.py:396
  252.8 4.7 %collective-permute-start.23 = (bf16[64,1024]{1,0:T(8,128)(2,1)S(1)}, bf16[64,1024]{1,0:T(8,128)(2,1)S(1)}, u32[]{:S(2)}, u32[]{:S(2)}) collective-permute-start(bf16[64,1024]{1,0:T(8,128)(2,1)S(1)} %get-tuple-element.20), channel_id=1, source_target_pairs={{0,8},{2,10},{4,12},{6,14},{8,16},{10,18},{12,20},{14,22},{16,24},... | collective-permute-start | bytes 393224 | tf_op jit(solution)/shard_map/ppermute | solution.py:396
  255.0 10.4 %collective-permute-start.22 = (bf16[64,1024]{1,0:T(8,128)(2,1)S(1)}, bf16[64,1024]{1,0:T(8,128)(2,1)S(1)}, u32[]{:S(2)}, u32[]{:S(2)}) collective-permute-start(bf16[64,1024]{1,0:T(8,128)(2,1)S(1)} %get-tuple-element.20), channel_id=1, source_target_pairs={{0,16},{2,18},{4,20},{6,22},{8,24},{10,26},{12,28},{14,30},{16,0},... | collective-permute-start | bytes 393224 | tf_op jit(solution)/shard_map/ppermute | solution.py:396
  255.9 11.5 %collective-permute-start.21 = (bf16[64,1024]{1,0:T(8,128)(2,1)S(1)}, bf16[64,1024]{1,0:T(8,128)(2,1)S(1)}, u32[]{:S(2)}, u32[]{:S(2)}) collective-permute-start(bf16[64,1024]{1,0:T(8,128)(2,1)S(1)} %get-tuple-element.20), channel_id=1, source_target_pairs={{0,24},{2,26},{4,28},{6,30},{8,0},{10,2},{12,4},{14,6},{16,8},{18,... | collective-permute-start | bytes 393224 | tf_op jit(solution)/shard_map/ppermute | solution.py:396
  267.5 13.5 %collective-permute-start.29 = (bf16[4,64,1024]{2,1,0:T(8,128)(2,1)S(1)}, bf16[4,64,1024]{2,1,0:T(8,128)(2,1)S(1)}, u32[]{:S(2)}, u32[]{:S(2)}) collective-permute-start(bf16[4,64,1024]{2,1,0:T(8,128)(2,1)S(1)} %pad_maximum_fusion.refs_0_), channel_id=1, source_target_pairs={{0,6},{2,4},{4,2},{6,0},{8,14},{10,12},{12,10},{14,8},{16,22},{18,... | collective-permute-start | bytes 1572872 | tf_op jit(solution)/shard_map/ppermute | solution.py:393
  268.3 24.9 %collective-permute-start.27 = (bf16[4,64,1024]{2,1,0:T(8,128)(2,1)S(1)}, bf16[4,64,1024]{2,1,0:T(8,128)(2,1)S(1)}, u32[]{:S(2)}, u32[]{:S(2)}) collective-permute-start(bf16[4,64,1024]{2,1,0:T(8,128)(2,1)S(1)} %pad_maximum_fusion.refs_0_), channel_id=1, source_target_pairs={{0,4},{2,6},{4,0},{6,2},{8,12},{10,14},{12,8},{14,10},{16,20},{18,... | collective-permute-start | bytes 1572872 | tf_op jit(solution)/shard_map/ppermute | solution.py:393
  269.0 24.9 %collective-permute-start.25 = (bf16[4,64,1024]{2,1,0:T(8,128)(2,1)S(1)}, bf16[4,64,1024]{2,1,0:T(8,128)(2,1)S(1)}, u32[]{:S(2)}, u32[]{:S(2)}) collective-permute-start(bf16[4,64,1024]{2,1,0:T(8,128)(2,1)S(1)} %pad_maximum_fusion.refs_0_), channel_id=1, source_target_pairs={{0,2},{2,0},{4,6},{6,4},{8,10},{10,8},{12,14},{14,12},{16,18},{18,... | collective-permute-start | bytes 1572872 | tf_op jit(solution)/shard_map/ppermute | solution.py:393
  270.2 24.5 %collective-permute-start.24 = (bf16[4,64,1024]{2,1,0:T(8,128)(2,1)S(1)}, bf16[4,64,1024]{2,1,0:T(8,128)(2,1)S(1)}, u32[]{:S(2)}, u32[]{:S(2)}) collective-permute-start(bf16[4,64,1024]{2,1,0:T(8,128)(2,1)S(1)} %pad_maximum_fusion.refs_0_), channel_id=1, source_target_pairs={{0,1},{1,0},{2,3},{3,2},{4,5},{5,4},{6,7},{7,6},{8,9},{9,8},{10,11... | collective-permute-start | bytes 1572872 | tf_op jit(solution)/shard_map/ppermute | solution.py:399
  281.0 13.8 %collective-permute-start.30 = (bf16[4,64,1024]{2,1,0:T(8,128)(2,1)S(1)}, bf16[4,64,1024]{2,1,0:T(8,128)(2,1)S(1)}, u32[]{:S(2)}, u32[]{:S(2)}) collective-permute-start(bf16[4,64,1024]{2,1,0:T(8,128)(2,1)S(1)} %collective-permute-done.29.refs_6_), channel_id=1, source_target_pairs={{0,1},{1,0},{2,3},{3,2},{4,5},{5,4},{6,7},{7,6},{8,9},{9,8},{10,11... | collective-permute-start | bytes 1572872 | tf_op jit(solution)/shard_map/ppermute | solution.py:399
  293.2 2.3 collective-permute-start.28
  293.9 2.4 collective-permute-start.26
  (26 other events, 299.9 us)

commit v2 on v1

--- a/solution.py
+++ b/solution.py
@@ -27,14 +27,14 @@
     return lax.dot_general(a, b, (((ca,), (cb,)), ((), ())), preferred_element_type=jnp.float32)
 
 
-def compose_kernel(nodes, per_plane, groups, adj_ref, table_ref, near_ref, ids_ref):
+def compose_kernel(store_rows, stores, capacity, place_ref, adj_ref, table_ref, near_ref, ids_ref, request_ref, column_ref):
     fan, near_rows = adj_ref.shape
     his = table_ref.shape[1]
+    groups = stores // PLANE
+    here, mine = place_ref[0], place_ref[1]
     table = table_ref[...]
-    top_part = table // 65536
-    mid_part = (table // 256) % 256
-    low_part = table % 256
-    parts = jnp.concatenate([top_part, mid_part, low_part], axis=0).astype(jnp.float32).astype(jnp.bfloat16)
+    parts = jnp.concatenate([table // 65536, (table // 256) % 256, table % 256], axis=0)
+    parts = parts.astype(jnp.float32).astype(jnp.bfloat16)
     row_hi = lax.broadcasted_iota(jnp.int32, (his, near_rows), 0)
     row_lo = lax.broadcasted_iota(jnp.int32, (LANES, near_rows), 0)
     for column in range(fan):
@@ -45,40 +45,160 @@
         value = jnp.where(row_lo == position % LANES, value, 0.0)
         ids_ref[column : column + 1, :] = jnp.sum(value, axis=0, keepdims=True).astype(jnp.int32)
     near = near_ref[...]
-    plane = near // per_plane
-    row_plane = lax.broadcasted_iota(jnp.int32, (groups, near_rows), 0)
-    marks = jnp.where(row_plane == plane, 1.0, 0.0)
+    owner, slot = near // store_rows, near % store_rows
+    row_owner = lax.broadcasted_iota(jnp.int32, (stores, near_rows), 0)
+    marks = jnp.where(row_owner == owner, 1.0, 0.0)
     earlier = lax.broadcasted_iota(jnp.int32, (near_rows, near_rows), 0) < lax.broadcasted_iota(
         jnp.int32, (near_rows, near_rows), 1
     )
     counts = dot(marks.astype(jnp.bfloat16), jnp.where(earlier, 1.0, 0.0).astype(jnp.bfloat16))
     rank = jnp.sum(counts * marks, axis=0, keepdims=True).astype(jnp.int32)
-    ids_ref[fan : fan + 1, :] = near + rank * nodes
-
-
-def compose(adjacency, table, near, nodes, per_plane, groups):
+    wanted = lax.broadcasted_iota(jnp.int32, (stores * capacity, near_rows), 0)
+    marks = jnp.where(wanted == owner * capacity + rank, 1.0, 0.0).astype(jnp.bfloat16)
+    line = lax.broadcasted_iota(jnp.int32, (8, near_rows), 0)
+    halves = jnp.where(line == 0, slot // 256, jnp.where(line == 1, slot % 256, 0))
+    found = dot(halves.astype(jnp.float32).astype(jnp.bfloat16), marks, 1, 1)
+    request_ref[...] = (found[0:1] * 256.0 + found[1:2]).astype(jnp.int32)
+    hops = here - owner // PLANE
+    hops = jnp.where(hops < 0, hops + groups, hops)
+    distance = lax.bitwise_xor(owner % PLANE, mine)
+    column_ref[...] = (distance * groups + hops) * capacity + rank
+
+
+def compose(place, adjacency, table, near, store_rows, stores, capacity):
     near_rows, fan = adjacency.shape
     return pl.pallas_call(
-        functools.partial(compose_kernel, nodes, per_plane, groups),
-        out_shape=jax.ShapeDtypeStruct((fan + 1, near_rows), jnp.int32),
-        in_specs=[VMEM, VMEM, VMEM],
+        functools.partial(compose_kernel, store_rows, stores, capacity),
+        out_shape=(
+            jax.ShapeDtypeStruct((fan, near_rows), jnp.int32),
+            jax.ShapeDtypeStruct((1, stores * capacity), jnp.int32),
+            jax.ShapeDtypeStruct((1, near_rows), jnp.int32),
+        ),
+        in_specs=[SMEM, VMEM, VMEM, VMEM],
+        out_specs=(VMEM, VMEM, VMEM),
+        compiler_params=pltpu.CompilerParams(vmem_limit_bytes=32 * MIB),
+        name="compose_ids",
+    )(place, adjacency.T, table, near)
+
+
+def near_kernel(groups, place_ref, request_ref, features_ref, out_ref):
+    here, mine = place_ref[0], place_ref[1]
+    store_rows = features_ref.shape[0]
+    capacity = request_ref.shape[1]
+    slots = lax.broadcasted_iota(jnp.int32, (store_rows, PLANE * capacity), 0)
+    for k in range(groups):
+        plane = here + k
+        plane = jnp.where(plane >= groups, plane - groups, plane)
+        lines = []
+        for d in range(PLANE):
+            trainer = plane * PLANE + lax.bitwise_xor(mine, jnp.int32(d))
+            lines.append(request_ref[pl.ds(trainer, 1), :])
+        marks = jnp.where(slots == jnp.concatenate(lines, axis=1), 1.0, 0.0).astype(jnp.bfloat16)
+        out_ref[k] = dot(marks, features_ref[...], 0, 0).astype(jnp.bfloat16)
+
+
+def near_rows_held(place, requests, features, groups):
+    capacity = requests.shape[1]
+    return pl.pallas_call(
+        functools.partial(near_kernel, groups),
+        out_shape=jax.ShapeDtypeStruct((groups, PLANE * capacity, features.shape[1]), jnp.bfloat16),
+        in_specs=[SMEM, VMEM, VMEM],
         out_specs=VMEM,
         compiler_params=pltpu.CompilerParams(vmem_limit_bytes=32 * MIB),
-        name="compose_ids",
-    )(adjacency.T, table, near)
-
-
-def partial_kernel(places, fan, near_rows, capacity, *refs):
+        name="near_rows",
+    )(place, requests, features)
+
+
+def sort_pairs(count):
+    pairs = []
+    size = 1
+    while size < count:
+        step = size
+        while step >= 1:
+            for start in range(step % size, count - step, 2 * step):
+                for i in range(min(step, count - start - step)):
+                    a, b = start + i, start + i + step
+                    if a // (2 * size) == b // (2 * size):
+                        pairs.append((a, b))
+            step //= 2
+        size *= 2
+    return pairs
+
+
+def list_kernel(store_rows, groups, first, block, place_ref, *refs):
+    ids_refs, out_ref = refs[:-1], refs[-1]
+    here, mine, rep = place_ref[0], place_ref[1], place_ref[2]
+    fan, near_rows = ids_refs[0].shape
+    per_plane = PLANE * store_rows
+    lanes = lax.broadcasted_iota(jnp.int32, (near_rows, near_rows), 0) // block
+    spots = lax.broadcasted_iota(jnp.int32, (near_rows, near_rows), 1)
+    blocks = jnp.where(lanes == spots, 1.0, 0.0).astype(jnp.bfloat16)
+    for k, ids_ref in enumerate(ids_refs):
+        gid = ids_ref[...]
+        owner, row = gid // store_rows, gid % store_rows
+        distance = lax.bitwise_xor(owner % PLANE, mine)
+        turned = row + rep * (store_rows // 2)
+        turned = jnp.where(turned >= store_rows, turned - store_rows, turned)
+        row = distance * store_rows + jnp.where(distance == 0, row, turned)
+        row = jnp.where(owner // PLANE == here, row, per_plane)
+        rows = [row[j : j + 1] for j in range(fan)]
+        for a, b in sort_pairs(fan):
+            rows[a], rows[b] = jnp.minimum(rows[a], rows[b]), jnp.maximum(rows[a], rows[b])
+        for j in range(fan):
+            out_ref[k, j : j + 1, :] = rows[j] * 8
+        if first < fan:
+            more = jnp.where(rows[first] < per_plane, 1.0, 0.0).astype(jnp.bfloat16)
+            more = dot(jnp.broadcast_to(more, (8, near_rows)), blocks)
+            out_ref[k, fan : fan + 1, :] = more[0:1].astype(jnp.int32)
+        else:
+            out_ref[k, fan : fan + 1, :] = jnp.zeros((1, near_rows), jnp.int32)
+
+
+def row_lists(place, ids_all, store_rows, first, block):
+    fan, near_rows = ids_all[0].shape
+    groups = len(ids_all)
+    return pl.pallas_call(
+        functools.partial(list_kernel, store_rows, groups, first, block),
+        out_shape=jax.ShapeDtypeStruct((groups, fan + 1, near_rows), jnp.int32),
+        in_specs=[SMEM] + [VMEM] * groups,
+        out_specs=VMEM,
+        compiler_params=pltpu.CompilerParams(vmem_limit_bytes=32 * MIB),
+        name="row_lists",
+    )(place, *ids_all)
+
+
+def partial_kernel(places, turns, first, block, *refs):
     index_ref = refs[0]
     piece_refs = refs[1 : 1 + len(places)]
-    out_ref, table, sums, kept = refs[1 + len(places) :]
+    out_ref, table, sums = refs[1 + len(places) : 4 + len(places)]
+    buffers = refs[4 + len(places) : -1]
+    arrived = refs[-1]
+    fan, near_rows = index_ref.shape[1] - 1, index_ref.shape[2]
     units = piece_refs[0].shape[1] // LANES
     total = table.shape[0] // 8 - 1
     chunk = 256
 
-    def fill(piece, start):
-        def step(i, carry):
-            values = piece[pl.ds(pl.multiple_of(i * chunk, chunk), chunk), :].astype(jnp.float32)
+    def row(at):
+        return table[pl.ds(pl.multiple_of(at, 8), 8), :]
+
+    def tree(rows):
+        while len(rows) > 1:
+            odd = rows[-1:] if len(rows) % 2 else []
+            rows = [a + b for a, b in zip(rows[0::2], rows[1::2])] + odd
+        return rows[0]
+
+    copies = [
+        pltpu.make_async_copy(piece, buffer, arrived.at[i])
+        for i, (piece, buffer) in enumerate(zip(piece_refs, buffers))
+    ]
+    for copy in copies:
+        copy.start()
+    table[total * 8 :, :] = jnp.zeros((8, LANES), jnp.float32)
+    for copy, buffer, start in zip(copies, buffers, places):
+        copy.wait()
+
+        def fill(i, carry):
+            values = buffer[pl.ds(pl.multiple_of(i * chunk, chunk), chunk), :].astype(jnp.float32)
             base = (start + i * chunk) * 8
             for unit in range(units):
                 table[pl.ds(base + unit, chunk, stride=8), :] = values[
@@ -86,58 +206,54 @@
                 ]
             return carry
 
-        lax.fori_loop(0, piece.shape[0] // chunk, step, 0)
-
-    for piece, start in zip(piece_refs, places):
-        fill(piece, start)
-    table[total * 8 :, :] = jnp.zeros((8, LANES), jnp.float32)
-    trainers = out_ref.shape[0]
-    unroll = 8
-
-    for trainer in range(trainers):
-        kept[...] = jnp.zeros_like(kept)
+        lax.fori_loop(0, buffer.shape[0] // chunk, fill, 0)
+
+    unroll = 16
+    for at, turn in enumerate(turns):
 
         def step(i, carry):
             for u in range(unroll):
                 n = i * unroll + u
-                rows = [
-                    table[pl.ds(pl.multiple_of(index_ref[trainer, j, n], 8), 8), :]
-                    for j in range(fan)
-                ]
-                while len(rows) > 1:
-                    rows = [a + b for a, b in zip(rows[0::2], rows[1::2])] + (
-                        rows[-1:] if len(rows) % 2 else []
+                sums[pl.ds(pl.multiple_of(n * 8, 8), 8), :] = tree(
+                    [row(index_ref[turn, j, n]) for j in range(first)]
+                )
+            return carry
+
+        lax.fori_loop(0, near_rows // unroll, step, 0)
+
+        def rest(i, carry):
+            @pl.when(index_ref[turn, fan, i] > 0)
+            def _():
+                for u in range(block):
+                    n = i * block + u
+                    spot = pl.ds(pl.multiple_of(n * 8, 8), 8)
+                    sums[spot, :] = sums[spot, :] + tree(
+                        [row(index_ref[turn, j, n]) for j in range(first, fan)]
                     )
-                sums[pl.ds(pl.multiple_of(n * 8, 8), 8), :] = rows[0]
-                source = pl.multiple_of(index_ref[trainer, fan, n], 8)
-                target = pl.multiple_of(index_ref[trainer, fan + 1, n], 8)
-                kept[pl.ds(target, 8), :] = table[pl.ds(source, 8), :]
+
             return carry
 
-        lax.fori_loop(0, near_rows // unroll, step, 0)
+        if first < fan:
+            lax.fori_loop(0, near_rows // block, rest, 0)
         for unit in range(units):
             lanes = slice(unit * LANES, (unit + 1) * LANES)
-            out_ref[trainer, :near_rows, lanes] = sums[
-                pl.ds(unit, near_rows, stride=8), :
-            ].astype(jnp.bfloat16)
-            out_ref[trainer, near_rows:, lanes] = kept[
-                pl.ds(unit, capacity, stride=8), :
-            ].astype(jnp.bfloat16)
-
-
-def partial_sums(index, pieces, places, total, capacity):
-    trainers, columns, near_rows = index.shape
+            out_ref[at, :, lanes] = sums[pl.ds(unit, near_rows, stride=8), :].astype(jnp.bfloat16)
+
+
+def partial_sums(index, pieces, places, turns, total, first, block):
+    near_rows = index.shape[2]
     width = pieces[0].shape[1]
     return pl.pallas_call(
-        functools.partial(partial_kernel, places, columns - 2, near_rows, capacity),
-        out_shape=jax.ShapeDtypeStruct((trainers, near_rows + capacity, width), jnp.bfloat16),
-        in_specs=[SMEM] + [VMEM] * len(pieces),
+        functools.partial(partial_kernel, places, turns, first, block),
+        out_shape=jax.ShapeDtypeStruct((len(turns), near_rows, width), jnp.bfloat16),
+        in_specs=[SMEM] + [pl.BlockSpec(memory_space=pl.ANY)] * len(pieces),
         out_specs=VMEM,
         scratch_shapes=[
             pltpu.VMEM(((total + 1) * 8, LANES), jnp.float32),
             pltpu.VMEM(((near_rows + 1) * 8, LANES), jnp.float32),
-            pltpu.VMEM(((capacity + 1) * 8, LANES), jnp.float32),
-        ],
+        ]
+        + [pltpu.VMEM(piece.shape, piece.dtype) for piece in pieces]
+        + [pltpu.SemaphoreType.DMA((len(pieces),))],
         compiler_params=pltpu.CompilerParams(vmem_limit_bytes=60 * MIB),
         name="partial_sums",
     )(index, *pieces)
@@ -147,25 +263,26 @@
     groups, rows_low, rows_top, classes, class_pad = sizes
     place_ref, labels_ref, adj_ref, column_ref, wl_ref, wt_ref = refs[:6]
     block_refs = refs[6 : 6 + groups]
-    logits_ref, keep_ref, send_ref, li, hidden, slope, top_in, wt = refs[6 + groups :]
+    near_refs = refs[6 + groups : 6 + groups + PLANE]
+    logits_ref, keep_ref, send_ref, li, hidden, slope, top_in, wt = refs[6 + groups + PLANE :]
     seeds, fan_top = adj_ref.shape
     near_rows, low_width = li.shape
     feat = low_width // 2
     width = hidden.shape[1]
-    capacity = block_refs[0].shape[0] - near_rows
+    capacity = near_refs[0].shape[0]
     here, mine, rep = place_ref[0], place_ref[1], place_ref[2]
     fan_low = place_ref[3].astype(jnp.float32)
 
     column = column_ref[...]
     rows_cap = lax.broadcasted_iota(jnp.int32, (capacity, near_rows), 0)
     near = None
-    total = None
-    for k in range(groups):
-        marks = jnp.where(rows_cap + k * capacity == column, 1.0, 0.0).astype(jnp.bfloat16)
-        term = dot(marks, block_refs[k][near_rows:, :], 0, 0)
+    for d in range(PLANE):
+        marks = jnp.where(rows_cap + d * capacity == column, 1.0, 0.0).astype(jnp.bfloat16)
+        term = dot(marks, near_refs[d][...], 0, 0)
         near = term if near is None else near + term
-        part = block_refs[k][:near_rows, :].astype(jnp.float32)
-        total = part if total is None else total + part
+    total = block_refs[0][...].astype(jnp.float32)
+    for k in range(1, groups):
+        total = total + block_refs[k][...].astype(jnp.float32)
     li[:, :feat] = near.astype(jnp.bfloat16)
     li[:, feat:] = (total / fan_low).astype(jnp.bfloat16)
 
@@ -240,7 +357,7 @@
         send_ref[a, b, rows_low:, :] = other.astype(jnp.bfloat16)
 
 
-def trainer_step(place, labels, adj_top, column, wl, wt, blocks, sizes, scale):
+def trainer_step(place, labels, adj_top, column, wl, wt, blocks, nears, sizes, scale):
     groups, rows_low, rows_top, classes, class_pad = sizes
     seeds = adj_top.shape[0]
     low_width, width = wl.shape
@@ -253,7 +370,7 @@
             jax.ShapeDtypeStruct((PLANE, groups, rows, width), jnp.float32),
             jax.ShapeDtypeStruct((PLANE, groups, rows, width), jnp.bfloat16),
         ),
-        in_specs=[SMEM] + [VMEM] * (5 + groups),
+        in_specs=[SMEM] + [VMEM] * (5 + groups + PLANE),
         out_specs=(VMEM, VMEM, VMEM),
         scratch_shapes=[
             pltpu.VMEM((near_rows, low_width), jnp.bfloat16),
@@ -264,7 +381,7 @@
         ],
         compiler_params=pltpu.CompilerParams(vmem_limit_bytes=60 * MIB),
         name="trainer_step",
-    )(place, labels, adj_top, column, wl, wt, *blocks)
+    )(place, labels, adj_top, column, wl, wt, *blocks, *nears)
 
 
 def adam_part(gradient, moment, square):
@@ -315,7 +432,7 @@
     groups, rows_low, rows_top, classes, class_pad = sizes
     delta_refs, (nl, nt) = refs[: 2 * PLANE], refs[2 * PLANE :]
     here, mine, rep = place_ref[0], place_ref[1], place_ref[2]
-    width = wl.shape[2]
+    width = wl.shape[-1]
     lane_groups = width // class_pad
     sub = rows_top // lane_groups
     for d in range(PLANE):
@@ -327,19 +444,26 @@
                 core = rep if half == 0 else 1 - rep
                 position = store * 2 + core
                 delta = delta_refs[2 * d + half][k].astype(jnp.float32)
-                nl[position] = wl[position] - delta[:rows_low]
+                if len(wl.shape) == 2:
+                    rows = pl.ds(pl.multiple_of(position * rows_low, 8), rows_low)
+                    nl[rows, :] = wl[rows, :] - delta[:rows_low]
+                else:
+                    nl[position] = wl[position] - delta[:rows_low]
                 for g in range(lane_groups):
-                    rows = slice(g * sub, (g + 1) * sub)
-                    nt[position, rows, :] = (
-                        wt[position, rows, :]
-                        - delta[rows_low:, g * class_pad : g * class_pad + classes]
-                    )
+                    step = delta[rows_low:, g * class_pad : g * class_pad + classes]
+                    if len(wt.shape) == 2:
+                        rows = pl.ds(pl.multiple_of(position * rows_top + g * sub, 8), sub)
+                        nt[rows, :] = wt[rows, :] - step
+                    else:
+                        rows = slice(g * sub, (g + 1) * sub)
+                        nt[position, rows, :] = wt[position, rows, :] - step
 
 
 def apply_updates(place, wl, wt, deltas, sizes):
     groups, rows_low, rows_top, classes, class_pad = sizes
-    low3 = wl.reshape(-1, rows_low, wl.shape[1])
-    top3 = wt.reshape(-1, rows_top, wt.shape[1])
+    sub = rows_top * class_pad // wl.shape[1]
+    low3 = wl if rows_low % 8 == 0 else wl.reshape(-1, rows_low, wl.shape[1])
+    top3 = wt if sub % 8 == 0 else wt.reshape(-1, rows_top, wt.shape[1])
     nl, nt = pl.pallas_call(
         functools.partial(apply_kernel, sizes),
         out_shape=(
@@ -378,16 +502,13 @@
     store_rows = features.shape[0]
     half = store_rows // 2
     near_rows, fan = adjacency_low.shape
-    far_rows = owners_far.shape[0]
-    nodes = stores * store_rows
-    per_plane = PLANE * store_rows
-    near_limit = 2 * near_rows // stores
-    capacity = min(near_rows, PLANE * near_limit)
+    capacity = 2 * near_rows // stores
     classes = weights_top.shape[1]
     class_pad = -(-classes // LANES) * LANES
     rows_low, rows_top = first_low.shape[0], first_top.shape[0]
     sizes = (groups, rows_low, rows_top, classes, class_pad)
     bf16 = jnp.bfloat16
+    place = jnp.stack([here, mine, rep, jnp.int32(fan)]).astype(jnp.int32)
 
     def across(x, distance):
         return lax.ppermute(x, "store", [(i, i ^ distance) for i in range(stores)])
@@ -398,52 +519,44 @@
     def sibling(x):
         return lax.ppermute(x, "rep", [(0, 1), (1, 0)])
 
-    own_half = lax.dynamic_slice_in_dim(features, rep * half, half, 0)
-    from_x = across(own_half, 1)
-    from_y = across(own_half, 2)
+    quarter = half // 2
+    own_a = lax.dynamic_slice_in_dim(features, rep * half, quarter, 0)
+    own_b = lax.dynamic_slice_in_dim(features, rep * half + quarter, quarter, 0)
+    x_a, y_b = across(own_a, 1), across(own_b, 2)
+    x_b, y_a = across(own_b, 1), across(own_a, 2)
     gid_near = owners_near[:, 0] * store_rows + slots_near[:, 0]
     gid_far = owners_far[:, 0] * store_rows + slots_far[:, 0]
     table = jnp.concatenate([gid_near, gid_far]).reshape(-1, LANES)
     table = jnp.pad(table, ((0, -table.shape[0] % 16), (0, 0))).T
-    near_line = gid_near.reshape(1, near_rows)
-    ids = compose(adjacency_low, table, near_line, nodes, per_plane, groups)
+    ids, requests, column = compose(
+        place, adjacency_low, table, gid_near.reshape(1, near_rows), store_rows, stores, capacity
+    )
     ids_all = [ids] + [along(ids, -k) for k in range(1, groups)]
-    quarter = half // 2
-    corner_a = across(from_x[:quarter], 2)
-    corner_b = across(from_y[quarter:], 1)
-    parts = [from_x, from_y, corner_a, corner_b]
-    pieces = [features, from_x, sibling(from_x), from_y, sibling(from_y)]
-    pieces += [corner_a, corner_b, sibling(corner_a), sibling(corner_b)]
-    places = [0, store_rows, store_rows + half, 2 * store_rows, 2 * store_rows + half]
-    places += [3 * store_rows + quarter * i for i in range(4)]
-
-    def local_rows(ids_of):
-        neighbours = ids_of[:fan]
-        packed = ids_of[fan : fan + 1]
-        rank, near_gid = packed // nodes, packed % nodes
-        gid = jnp.concatenate([neighbours, near_gid], axis=0)
-        held = gid // per_plane == here
-        distance = lax.bitwise_xor((gid // store_rows) % PLANE, mine)
-        row = gid % store_rows
-        turned = jnp.where(distance == 0, row, (row + rep * half) % store_rows)
-        row = jnp.where(held, distance * store_rows + turned, per_plane)
-        target = jnp.where(held[fan:], rank, capacity)
-        return jnp.concatenate([row, target], axis=0) * 8
+    requests = lax.all_to_all(requests.reshape(stores, capacity), "store", 0, 0, tiled=True)
+    held = near_rows_held(place, requests, features, groups)
+    first, block = min(8, fan), 8
+    lists = row_lists(place, ids_all, store_rows, first, block)
+    lined = [held[0]] + [along(held[k], k) for k in range(1, groups)]
+    corner_a, corner_b = across(x_a, 2), across(y_b, 1)
+    pieces, places = [features], [0]
+    for turn, (one, two) in enumerate([(x_a, x_b), (y_a, y_b), (corner_a, corner_b)]):
+        pieces += [one, two, sibling(one), sibling(two)]
+        places += [(turn + 1) * store_rows + quarter * i for i in range(4)]
 
     per_call = -(-groups // 4)
-    order = list(range(1, groups)) + [0]
+    order = [groups // 2] + [k for k in range(1, groups) if k != groups // 2] + [0]
     blocks = {}
     for start in range(0, groups, per_call):
         turns = order[start : start + per_call]
-        lists = jnp.stack([local_rows(ids_all[k]) for k in turns])
-        made = partial_sums(lists, pieces, places, per_plane, capacity)
+        made = partial_sums(lists, pieces, places, turns, PLANE * store_rows, first, block)
         for i, k in enumerate(turns):
             blocks[k] = along(made[i], k) if k else made[i]
 
-    packed = ids[fan : fan + 1]
-    source = (here - (packed % nodes) // per_plane) % groups
-    column = source * capacity + packed // nodes
-    place = jnp.stack([here, mine, rep, jnp.int32(fan)]).astype(jnp.int32)
+    nears = []
+    for d in range(PLANE):
+        sheet = jnp.concatenate([part[d * capacity : (d + 1) * capacity] for part in lined])
+        nears.append(across(sheet, d) if d else sheet)
+
     scale = 1.0 / (labels.shape[0] * members)
     logits, keep, send = trainer_step(
         place,
@@ -453,6 +566,7 @@
         weights_low,
         weights_top,
         [blocks[k] for k in range(groups)],
+        nears,
         sizes,
         scale,
     )

time: 308 us -> 304 us (0.987)
  waiting for transfers between devices: 134 us -> 98.8 us
  starting transfers between devices: 37.5 us -> 69 us
  Pallas kernels: 115 us -> 109 us
  local copies, waits for them, and re-layouts: 12.1 us -> 17.5 us
    ppermute x10 -> x15, waiting for transfers between devices: 80.2 us -> 42.6 us  [across(): return lax.ppermute(x, 'store', [(i, i ^ distance) for i in range(stores)])]
    ppermute x9 -> x11, starting transfers between devices: 12.2 us -> 28.9 us  [sibling(): return lax.ppermute(x, 'rep', [(0, 1), (1, 0)])]
    pallas_call x5 -> x7, Pallas kernels: 91 us -> 84.8 us  [the longest x4 76.5 us: partial_sums(): pl.pallas_call(functools.partial(partial_kernel, places, turns, first, bl...]
    ppermute x10 -> x15, starting transfers between devices: 10.5 us -> 16.1 us  [across(): return lax.ppermute(x, 'store', [(i, i ^ distance) for i in range(stores)])]
    all_to_all x0 -> x1, starting transfers between devices: none -> 4.78 us  [per_device(): lax.all_to_all(requests.reshape(stores, capacity), 'store', 0, 0, tiled=T...]
    concatenate x7 -> x4, other arithmetic: 0.42 us -> 5.03 us  [per_device(): jnp.concatenate([part[d * capacity:(d + 1) * capacity] for part in lined])]
    ppermute x12 -> x15, starting transfers between devices: 14.8 us -> 19.2 us  [along(): lax.ppermute(x, 'store', [(i, (i + hops * PLANE) % stores) for i in range...]
    all_to_all x0 -> x1, waiting for transfers between devices: none -> 3.4 us  [per_device(): lax.all_to_all(requests.reshape(stores, capacity), 'store', 0, 0, tiled=T...]
  transfers between devices with their start and end apart: 31 -> 42, of which waited for: 17 -> 19; matrix products, arithmetic and copies ran while one was open for 3% -> 4% of each run, Pallas kernels for 22% -> 28%
where the time goes in v2:
time: 304 us; the launch traced here: 305 us
  Pallas kernels  109 us (36%)
  waiting for transfers between devices  98.8 us (32%)
  starting transfers between devices  69 us (23%)
  local copies, waits for them, and re-layouts  17.5 us (6%)
  other arithmetic  9.31 us (3%)
    pallas_call x4, Pallas kernels, partial_sums(): pl.pallas_call(functools.partial(partial_kernel, places, turns, first, bl...  76.5 us
    ppermute x15, waiting for transfers between devices, along(): lax.ppermute(x, 'store', [(i, (i + hops * PLANE) % stores) for i in range...  47.2 us
    ppermute x15, waiting for transfers between devices, across(): return lax.ppermute(x, 'store', [(i, i ^ distance) for i in range(stores)])  42.6 us
    ppermute x11, starting transfers between devices, sibling(): return lax.ppermute(x, 'rep', [(0, 1), (1, 0)])  28.9 us
    ppermute x15, starting transfers between devices, along(): lax.ppermute(x, 'store', [(i, (i + hops * PLANE) % stores) for i in range...  19.2 us
    ppermute x15, starting transfers between devices, across(): return lax.ppermute(x, 'store', [(i, i ^ distance) for i in range(stores)])  16.1 us
    pallas_call x1, Pallas kernels, trainer_step(): pl.pallas_call(functools.partial(trainer_kernel, sizes, scale), out_shape...  14.4 us
    unnamed x86, local copies, waits for them, and re-layouts  9.6 us
  transfers between devices with their start and end apart: 42, of which 19 were waited for; matrix products, arithmetic and copies ran while one was open for 4% of the time, Pallas kernels for 28%

profile of v2, /device:TPU:9, one launch (start us, length us, event | category | flops | bytes accessed | tf_op | source)
XLA Modules:
  0.0 304.6 jit_solution(7224499654746251148)
XLA Ops:
  0.7 2.8 constant_dynamic-slice_fusion
  6.2 2.8 compose_ids.1
  11.5 4.8 %all-to-all-start = ((s32[16,1,64]{2,1,0:T(1,128)}), s32[16,1,64]{2,1,0:T(1,128)S(1)}, u32[]{:S(2)}, u32[]{:S(2)}) async-start(s32[16,1,64]{2,1,0:T(1,128)} %bitcast.14), calls=%async_computation | async-start | bytes 16384 | tf_op jit(solution)/shard_map/all_to_all | solution.py:535
  19.8 3.4 %all-to-all-done = s32[16,1,64]{2,1,0:T(1,128)S(1)} async-done(((s32[16,1,64]{2,1,0:T(1,128)}), s32[16,1,64]{2,1,0:T(1,128)S(1)}, u32[]{:S(2)}, u32[]{:S(2)}) %all-to-all-start) | async-done | bytes 4128 | tf_op jit(solution)/shard_map/all_to_all | solution.py:535
  23.2 4.1 %near_rows.1 = bf16[4,256,768]{2,1,0:T(8,128)(2,1)S(1)} custom-call(s32[4]{0:T(128)S(1)} %pad_add_fusion.place_ref.refs_0_, s32[16,64]{1,0:T(8,128)S(1)} %bitcast.56, bf16[2048,768]{1,0:T(8,128)(2,1)S(1)} %copy-done), custom_call_target="tpu_custom_call" | custom-call | tf_op jit(solution)/shard_map/near_rows/pallas_call | solution.py:102
  31.2 4.9 %collective-permute-done.18 = bf16[256,768]{1,0:T(8,128)(2,1)S(1)} collective-permute-done((bf16[256,768]{1,0:T(8,128)(2,1)S(1)}, bf16[256,768]{1,0:T(8,128)(2,1)S(1)}, u32[]{:S(2)}, u32[]{:S(2)}) %collective-permute-start.18) | collective-permute-done | bytes 393248 | tf_op jit(solution)/shard_map/ppermute | solution.py:517
  37.3 12.5 %collective-permute-done.20 = bf16[256,768]{1,0:T(8,128)(2,1)S(1)} collective-permute-done((bf16[256,768]{1,0:T(8,128)(2,1)S(1)}, bf16[256,768]{1,0:T(8,128)(2,1)S(1)}, u32[]{:S(2)}, u32[]{:S(2)}) %collective-permute-start.20) | collective-permute-done | bytes 393248 | tf_op jit(solution)/shard_map/ppermute | solution.py:517
  52.1 8.4 %collective-permute-done.19 = bf16[256,768]{1,0:T(8,128)(2,1)S(1)} collective-permute-done((bf16[256,768]{1,0:T(8,128)(2,1)S(1)}, bf16[256,768]{1,0:T(8,128)(2,1)S(1)}, u32[]{:S(2)}, u32[]{:S(2)}) %collective-permute-start.19) | collective-permute-done | bytes 393248 | tf_op jit(solution)/shard_map/ppermute | solution.py:517
  60.5 2.8 collective-permute-start.10
  66.9 4.2 %collective-permute-start.5 = (bf16[512,768]{1,0:T(8,128)(2,1)}, bf16[512,768]{1,0:T(8,128)(2,1)S(1)}, u32[]{:S(2)}, u32[]{:S(2)}) collective-permute-start(bf16[512,768]{1,0:T(8,128)(2,1)} %collective-permute-done.3.refs_2_), channel_id=1, source_target_pairs={{0,1},{1,0},{2,3},{3,2},{4,5},{5,4},{6,7},{7,6},{8,9},{9,8},{10,11... | collective-permute-start | bytes 2359304 | tf_op jit(solution)/shard_map/ppermute | solution.py:520
  71.1 4.2 %collective-permute-start.6 = (bf16[512,768]{1,0:T(8,128)(2,1)S(1)}, bf16[512,768]{1,0:T(8,128)(2,1)S(1)}, u32[]{:S(2)}, u32[]{:S(2)}) collective-permute-start(bf16[512,768]{1,0:T(8,128)(2,1)S(1)} %collective-permute-done.4.refs_3_), channel_id=1, source_target_pairs={{0,1},{1,0},{2,3},{3,2},{4,5},{5,4},{6,7},{7,6},{8,9},{9,8},{10,11... | collective-permute-start | bytes 2359304 | tf_op jit(solution)/shard_map/ppermute | solution.py:520
  75.3 4.3 %collective-permute-start.9 = (bf16[512,768]{1,0:T(8,128)(2,1)S(1)}, bf16[512,768]{1,0:T(8,128)(2,1)S(1)}, u32[]{:S(2)}, u32[]{:S(2)}) collective-permute-start(bf16[512,768]{1,0:T(8,128)(2,1)S(1)} %collective-permute-done.7.refs_6_), channel_id=1, source_target_pairs={{0,1},{1,0},{2,3},{3,2},{4,5},{5,4},{6,7},{7,6},{8,9},{9,8},{10,11... | collective-permute-start | bytes 2359304 | tf_op jit(solution)/shard_map/ppermute | solution.py:520
  79.6 3.5 %collective-permute-done.11.refs_10_ = bf16[512,768]{1,0:T(8,128)(2,1)S(1)} collective-permute-done((bf16[512,768]{1,0:T(8,128)(2,1)}, bf16[512,768]{1,0:T(8,128)(2,1)S(1)}, u32[]{:S(2)}, u32[]{:S(2)}) %collective-permute-start.11) | collective-permute-done | bytes 786464 | tf_op jit(solution)/shard_map/ppermute | solution.py:514
  83.1 4.7 %collective-permute-start.13 = (bf16[512,768]{1,0:T(8,128)(2,1)S(1)}, bf16[512,768]{1,0:T(8,128)(2,1)}, u32[]{:S(2)}, u32[]{:S(2)}) collective-permute-start(bf16[512,768]{1,0:T(8,128)(2,1)S(1)} %collective-permute-done.11.refs_10_), channel_id=1, source_target_pairs={{0,1},{1,0},{2,3},{3,2},{4,5},{5,4},{6,7},{7,6},{8,9},{9,8},{10,11... | collective-permute-start | bytes 2359304 | tf_op jit(solution)/shard_map/ppermute | solution.py:520
  93.2 19.4 %partial_sums.5 = bf16[1,512,768]{2,1,0:T(8,128)(2,1)} custom-call(s32[4,16,512]{2,1,0:T(8,128)} %copy-done.1, bf16[2048,768]{1,0:T(8,128)(2,1)} %features_ref.1, bf16[512,768]{1,0:T(8,128)(2,1)} %collective-permute-done.3.refs_2_, bf16[512,768]{1,0:T(8,128)(2,1)} %copy-done.9, bf16[512,768]{1,0:T(8,128)(2,1)} %copy-done.14, bf16[512,768]{1,0:T(8,128)(2,1)} %copy-done.15, ...), custom_call_target="tpu_custom_call" | custom-call | tf_op jit(solution)/shard_map/partial_sums/pallas_call | solution.py:246
  114.4 19.3 %partial_sums.6 = bf16[1,512,768]{2,1,0:T(8,128)(2,1)} custom-call(s32[4,16,512]{2,1,0:T(8,128)} %copy-done.1, bf16[2048,768]{1,0:T(8,128)(2,1)} %features_ref.1, bf16[512,768]{1,0:T(8,128)(2,1)} %collective-permute-done.3.refs_2_, bf16[512,768]{1,0:T(8,128)(2,1)} %copy-done.9, bf16[512,768]{1,0:T(8,128)(2,1)} %copy-done.14, bf16[512,768]{1,0:T(8,128)(2,1)} %copy-done.15, ...), custom_call_target="tpu_custom_call" | custom-call | tf_op jit(solution)/shard_map/partial_sums/pallas_call | solution.py:246
  133.8 19.1 %partial_sums.7 = bf16[1,512,768]{2,1,0:T(8,128)(2,1)} custom-call(s32[4,16,512]{2,1,0:T(8,128)} %copy-done.1, bf16[2048,768]{1,0:T(8,128)(2,1)} %features_ref.1, bf16[512,768]{1,0:T(8,128)(2,1)} %collective-permute-done.3.refs_2_, bf16[512,768]{1,0:T(8,128)(2,1)} %copy-done.9, bf16[512,768]{1,0:T(8,128)(2,1)} %copy-done.14, bf16[512,768]{1,0:T(8,128)(2,1)} %copy-done.15, ...), custom_call_target="tpu_custom_call" | custom-call | tf_op jit(solution)/shard_map/partial_sums/pallas_call | solution.py:246
  155.2 3.0 collective-permute-start.22
  164.5 18.6 %partial_sums.4 = bf16[1,512,768]{2,1,0:T(8,128)(2,1)} custom-call(s32[4,16,512]{2,1,0:T(8,128)} %copy-done.1, bf16[2048,768]{1,0:T(8,128)(2,1)} %features_ref.1, bf16[512,768]{1,0:T(8,128)(2,1)} %collective-permute-done.3.refs_2_, bf16[512,768]{1,0:T(8,128)(2,1)} %copy-done.9, bf16[512,768]{1,0:T(8,128)(2,1)} %copy-done.14, bf16[512,768]{1,0:T(8,128)(2,1)} %copy-done.15, ...), custom_call_target="tpu_custom_call" | custom-call | tf_op jit(solution)/shard_map/partial_sums/pallas_call | solution.py:246
  185.8 14.4 %trainer_step.1 = (f32[128,153]{1,0:T(8,128)}, f32[4,4,64,1024]{3,2,1,0:T(8,128)}, bf16[4,4,64,1024]{3,2,1,0:T(8,128)(2,1)}) custom-call(s32[4]{0:T(128)} %copy-done.7, s32[128,1]{1,0:T(8,128)} %copy.36.refs_1_, s32[128,10]{1,0:T(8,128)} %copy.37.refs_2_, s32[1,512]{1,0:T(1,128)} %copy-done.8, f32[1536,1024]{1,0:T(8,128)} %wl.1, ...), custom_call_target="tpu_custom_call" | custom-call | tf_op jit(solution)/shard_map/trainer_step/pallas_call | solution.py:366
  201.4 4.0 %collective-permute-done.24 = bf16[4,4,64,1024]{3,2,1,0:T(8,128)(2,1)S(1)} collective-permute-done((bf16[4,4,64,1024]{3,2,1,0:T(8,128)(2,1)}, bf16[4,4,64,1024]{3,2,1,0:T(8,128)(2,1)S(1)}, u32[]{:S(2)}, u32[]{:S(2)}) %collective-permute-start.24) | collective-permute-done | bytes 2097184 | tf_op jit(solution)/shard_map/ppermute | solution.py:520
  205.4 3.1 %fusion.3 = (bf16[4,4,64,1024]{3,2,1,0:T(8,128)(2,1)S(1)}, f32[4,4,64,1024]{3,2,1,0:T(8,128)S(1)}) fusion(f32[4,4,64,1024]{3,2,1,0:T(8,128)} %get-tuple-element.24, bf16[4,4,64,1024]{3,2,1,0:T(8,128)(2,1)S(1)} %collective-permute-done.24), kind=kLoop, calls=%fused_computation.30 | loop fusion | flops 3145728 | bytes 12582912 | tf_op jit(solution)/shard_map/convert.5
  211.5 10.4 %collective-permute-done.25 = bf16[4,64,1024]{2,1,0:T(8,128)(2,1)S(1)} collective-permute-done((bf16[4,64,1024]{2,1,0:T(8,128)(2,1)S(1)}, bf16[4,64,1024]{2,1,0:T(8,128)(2,1)S(1)}, u32[]{:S(2)}, u32[]{:S(2)}) %collective-permute-start.25) | collective-permute-done | bytes 524320 | tf_op jit(solution)/shard_map/ppermute | solution.py:514
  221.8 12.6 %collective-permute-done.27 = bf16[4,64,1024]{2,1,0:T(8,128)(2,1)S(1)} collective-permute-done((bf16[4,64,1024]{2,1,0:T(8,128)(2,1)S(1)}, bf16[4,64,1024]{2,1,0:T(8,128)(2,1)S(1)}, u32[]{:S(2)}, u32[]{:S(2)}) %collective-permute-start.27) | collective-permute-done | bytes 524320 | tf_op jit(solution)/shard_map/ppermute | solution.py:514
  240.6 4.1 %collective-permute-done.29.refs_2_ = bf16[64,1024]{1,0:T(8,128)(2,1)S(1)} collective-permute-done((bf16[64,1024]{1,0:T(8,128)(2,1)S(1)}, bf16[64,1024]{1,0:T(8,128)(2,1)S(1)}, u32[]{:S(2)}, u32[]{:S(2)}) %collective-permute-start.29) | collective-permute-done | bytes 131104 | tf_op jit(solution)/shard_map/ppermute | solution.py:517
  244.8 4.3 %collective-permute-done.28.refs_1_ = bf16[64,1024]{1,0:T(8,128)(2,1)S(1)} collective-permute-done((bf16[64,1024]{1,0:T(8,128)(2,1)S(1)}, bf16[64,1024]{1,0:T(8,128)(2,1)S(1)}, u32[]{:S(2)}, u32[]{:S(2)}) %collective-permute-start.28) | collective-permute-done | bytes 131104 | tf_op jit(solution)/shard_map/ppermute | solution.py:517
  254.5 8.0 %collective-permute-done.32 = bf16[64,1024]{1,0:T(8,128)(2,1)S(1)} collective-permute-done((bf16[64,1024]{1,0:T(8,128)(2,1)S(1)}, bf16[64,1024]{1,0:T(8,128)(2,1)S(1)}, u32[]{:S(2)}, u32[]{:S(2)}) %collective-permute-start.32) | collective-permute-done | bytes 131104 | tf_op jit(solution)/shard_map/ppermute | solution.py:517
  269.4 8.0 %collective-permute-done.39.refs_6_ = bf16[4,64,1024]{2,1,0:T(8,128)(2,1)S(1)} collective-permute-done((bf16[4,64,1024]{2,1,0:T(8,128)(2,1)S(1)}, bf16[4,64,1024]{2,1,0:T(8,128)(2,1)S(1)}, u32[]{:S(2)}, u32[]{:S(2)}) %collective-permute-start.39) | collective-permute-done | bytes 524320 | tf_op jit(solution)/shard_map/ppermute | solution.py:514
  277.4 4.3 %collective-permute-start.40 = (bf16[4,64,1024]{2,1,0:T(8,128)(2,1)S(1)}, bf16[4,64,1024]{2,1,0:T(8,128)(2,1)S(1)}, u32[]{:S(2)}, u32[]{:S(2)}) collective-permute-start(bf16[4,64,1024]{2,1,0:T(8,128)(2,1)S(1)} %collective-permute-done.39.refs_6_), channel_id=1, source_target_pairs={{0,1},{1,0},{2,3},{3,2},{4,5},{5,4},{6,7},{7,6},{8,9},{9,8},{10,11... | collective-permute-start | bytes 1572872 | tf_op jit(solution)/shard_map/ppermute | solution.py:520
  281.7 8.1 %collective-permute-done.37.refs_4_ = bf16[4,64,1024]{2,1,0:T(8,128)(2,1)S(1)} collective-permute-done((bf16[4,64,1024]{2,1,0:T(8,128)(2,1)S(1)}, bf16[4,64,1024]{2,1,0:T(8,128)(2,1)S(1)}, u32[]{:S(2)}, u32[]{:S(2)}) %collective-permute-start.37) | collective-permute-done | bytes 524320 | tf_op jit(solution)/shard_map/ppermute | solution.py:514
  293.1 8.9 %apply_updates.1 = (f32[1536,1024]{1,0:T(8,128)}, f32[2048,153]{1,0:T(8,128)}) custom-call(s32[4]{0:T(128)} %copy-done.7, f32[1536,1024]{1,0:T(8,128)} %wl.1, f32[2048,153]{1,0:T(8,128)} %copy.38.refs_5_.wt, bf16[4,64,1024]{2,1,0:T(8,128)(2,1)} %copy-done.18, bf16[4,64,1024]{2,1,0:T(8,128)(2,1)} %copy-done.25, bf16[4,64,1024]{2,1,0:T(8,128)(2,1)} %copy-done.24, ...), custom_call_target="tpu_custom_call" | custom-call | tf_op jit(solution)/shard_map/apply_updates/pallas_call | solution.py:467
  301.9 2.7 copy.41
  (174 shorter events, 63.8 us)
Async XLA Ops:
  3.5 47.5 %collective-permute-start.8 = (bf16[512,768]{1,0:T(8,128)(2,1)}, bf16[512,768]{1,0:T(8,128)(2,1)}, u32[]{:S(2)}, u32[]{:S(2)}) collective-permute-start(bf16[512,768]{1,0:T(8,128)(2,1)} %get-tuple-element.58), channel_id=1, source_target_pairs={{0,4},{2,6},{4,0},{6,2},{8,12},{10,14},{12,8},{14,10},{16,20},{18,... | collective-permute-start | bytes 2359304 | tf_op jit(solution)/shard_map/ppermute | solution.py:514
  4.7 58.6 %collective-permute-start.3 = (bf16[512,768]{1,0:T(8,128)(2,1)}, bf16[512,768]{1,0:T(8,128)(2,1)}, u32[]{:S(2)}, u32[]{:S(2)}) collective-permute-start(bf16[512,768]{1,0:T(8,128)(2,1)} %get-tuple-element.59), channel_id=1, source_target_pairs={{0,2},{2,0},{4,6},{6,4},{8,10},{10,8},{12,14},{14,12},{16,18},{18,... | collective-permute-start | bytes 2359304 | tf_op jit(solution)/shard_map/ppermute | solution.py:514
  11.5 11.7 %all-to-all-start = ((s32[16,1,64]{2,1,0:T(1,128)}), s32[16,1,64]{2,1,0:T(1,128)S(1)}, u32[]{:S(2)}, u32[]{:S(2)}) async-start(s32[16,1,64]{2,1,0:T(1,128)} %bitcast.14), calls=%async_computation | async-start | bytes 16384 | tf_op jit(solution)/shard_map/all_to_all | solution.py:535
  16.2 11.1 %collective-permute-start.2 = (s32[15,512]{1,0:T(8,128)S(1)}, s32[15,512]{1,0:T(8,128)S(1)}, u32[]{:S(2)}, u32[]{:S(2)}) collective-permute-start(s32[15,512]{1,0:T(8,128)S(1)} %get-tuple-element.21.refs_0_), channel_id=1, source_target_pairs={{0,8},{2,10},{4,12},{6,14},{8,16},{10,18},{12,20},{14,22},{16,24},... | collective-permute-start | bytes 92168 | tf_op jit(solution)/shard_map/ppermute | solution.py:517
  17.4 11.3 %collective-permute-start.1 = (s32[15,512]{1,0:T(8,128)S(1)}, s32[15,512]{1,0:T(8,128)S(1)}, u32[]{:S(2)}, u32[]{:S(2)}) collective-permute-start(s32[15,512]{1,0:T(8,128)S(1)} %get-tuple-element.21.refs_0_), channel_id=1, source_target_pairs={{0,16},{2,18},{4,20},{6,22},{8,24},{10,26},{12,28},{14,30},{16,0},... | collective-permute-start | bytes 92168 | tf_op jit(solution)/shard_map/ppermute | solution.py:517
  28.7 21.2 %collective-permute-start.20 = (bf16[256,768]{1,0:T(8,128)(2,1)S(1)}, bf16[256,768]{1,0:T(8,128)(2,1)S(1)}, u32[]{:S(2)}, u32[]{:S(2)}) collective-permute-start(bf16[256,768]{1,0:T(8,128)(2,1)S(1)} %get-tuple-element.68), channel_id=1, source_target_pairs={{0,24},{2,26},{4,28},{6,30},{8,0},{10,2},{12,4},{14,6},{16,8},{18,... | collective-permute-start | bytes 1179656 | tf_op jit(solution)/shard_map/ppermute | solution.py:517
  28.9 31.6 %collective-permute-start.19 = (bf16[256,768]{1,0:T(8,128)(2,1)S(1)}, bf16[256,768]{1,0:T(8,128)(2,1)S(1)}, u32[]{:S(2)}, u32[]{:S(2)}) collective-permute-start(bf16[256,768]{1,0:T(8,128)(2,1)S(1)} %get-tuple-element.69), channel_id=1, source_target_pairs={{0,16},{2,18},{4,20},{6,22},{8,24},{10,26},{12,28},{14,30},{16,0},... | collective-permute-start | bytes 1179656 | tf_op jit(solution)/shard_map/ppermute | solution.py:517
  36.1 30.8 %collective-permute-start.4 = (bf16[512,768]{1,0:T(8,128)(2,1)}, bf16[512,768]{1,0:T(8,128)(2,1)S(1)}, u32[]{:S(2)}, u32[]{:S(2)}) collective-permute-start(bf16[512,768]{1,0:T(8,128)(2,1)} %get-tuple-element.58), channel_id=1, source_target_pairs={{0,2},{2,0},{4,6},{6,4},{8,10},{10,8},{12,14},{14,12},{16,18},{18,... | collective-permute-start | bytes 2359304 | tf_op jit(solution)/shard_map/ppermute | solution.py:514
  49.9 21.2 %collective-permute-start.7 = (bf16[512,768]{1,0:T(8,128)(2,1)}, bf16[512,768]{1,0:T(8,128)(2,1)S(1)}, u32[]{:S(2)}, u32[]{:S(2)}) collective-permute-start(bf16[512,768]{1,0:T(8,128)(2,1)} %get-tuple-element.59), channel_id=1, source_target_pairs={{0,4},{2,6},{4,0},{6,2},{8,12},{10,14},{12,8},{14,10},{16,20},{18,... | collective-permute-start | bytes 2359304 | tf_op jit(solution)/shard_map/ppermute | solution.py:514
  50.9 24.3 %collective-permute-start.12 = (bf16[512,768]{1,0:T(8,128)(2,1)}, bf16[512,768]{1,0:T(8,128)(2,1)S(1)}, u32[]{:S(2)}, u32[]{:S(2)}) collective-permute-start(bf16[512,768]{1,0:T(8,128)(2,1)} %collective-permute-done.8.refs_7_), channel_id=1, source_target_pairs={{0,2},{2,0},{4,6},{6,4},{8,10},{10,8},{12,14},{14,12},{16,18},{18,... | collective-permute-start | bytes 2359304 | tf_op jit(solution)/shard_map/ppermute | solution.py:514
  60.5 19.0 %collective-permute-start.10 = (bf16[512,768]{1,0:T(8,128)(2,1)}, bf16[512,768]{1,0:T(8,128)(2,1)S(1)}, u32[]{:S(2)}, u32[]{:S(2)}) collective-permute-start(bf16[512,768]{1,0:T(8,128)(2,1)} %collective-permute-done.8.refs_7_), channel_id=1, source_target_pairs={{0,1},{1,0},{2,3},{3,2},{4,5},{5,4},{6,7},{7,6},{8,9},{9,8},{10,11... | collective-permute-start | bytes 2359304 | tf_op jit(solution)/shard_map/ppermute | solution.py:520
  63.3 19.8 %collective-permute-start.11 = (bf16[512,768]{1,0:T(8,128)(2,1)}, bf16[512,768]{1,0:T(8,128)(2,1)S(1)}, u32[]{:S(2)}, u32[]{:S(2)}) collective-permute-start(bf16[512,768]{1,0:T(8,128)(2,1)} %collective-permute-done.3.refs_2_), channel_id=1, source_target_pairs={{0,4},{2,6},{4,0},{6,2},{8,12},{10,14},{12,8},{14,10},{16,20},{18,... | collective-permute-start | bytes 2359304 | tf_op jit(solution)/shard_map/ppermute | solution.py:514
  66.9 24.2 %collective-permute-start.5 = (bf16[512,768]{1,0:T(8,128)(2,1)}, bf16[512,768]{1,0:T(8,128)(2,1)S(1)}, u32[]{:S(2)}, u32[]{:S(2)}) collective-permute-start(bf16[512,768]{1,0:T(8,128)(2,1)} %collective-permute-done.3.refs_2_), channel_id=1, source_target_pairs={{0,1},{1,0},{2,3},{3,2},{4,5},{5,4},{6,7},{7,6},{8,9},{9,8},{10,11... | collective-permute-start | bytes 2359304 | tf_op jit(solution)/shard_map/ppermute | solution.py:520
  71.1 19.7 %collective-permute-start.6 = (bf16[512,768]{1,0:T(8,128)(2,1)S(1)}, bf16[512,768]{1,0:T(8,128)(2,1)S(1)}, u32[]{:S(2)}, u32[]{:S(2)}) collective-permute-start(bf16[512,768]{1,0:T(8,128)(2,1)S(1)} %collective-permute-done.4.refs_3_), channel_id=1, source_target_pairs={{0,1},{1,0},{2,3},{3,2},{4,5},{5,4},{6,7},{7,6},{8,9},{9,8},{10,11... | collective-permute-start | bytes 2359304 | tf_op jit(solution)/shard_map/ppermute | solution.py:520
  75.3 15.8 %collective-permute-start.9 = (bf16[512,768]{1,0:T(8,128)(2,1)S(1)}, bf16[512,768]{1,0:T(8,128)(2,1)S(1)}, u32[]{:S(2)}, u32[]{:S(2)}) collective-permute-start(bf16[512,768]{1,0:T(8,128)(2,1)S(1)} %collective-permute-done.7.refs_6_), channel_id=1, source_target_pairs={{0,1},{1,0},{2,3},{3,2},{4,5},{5,4},{6,7},{7,6},{8,9},{9,8},{10,11... | collective-permute-start | bytes 2359304 | tf_op jit(solution)/shard_map/ppermute | solution.py:520
  79.5 11.6 %collective-permute-start.14 = (bf16[512,768]{1,0:T(8,128)(2,1)S(1)}, bf16[512,768]{1,0:T(8,128)(2,1)S(1)}, u32[]{:S(2)}, u32[]{:S(2)}) collective-permute-start(bf16[512,768]{1,0:T(8,128)(2,1)S(1)} %collective-permute-done.12.refs_11_), channel_id=1, source_target_pairs={{0,1},{1,0},{2,3},{3,2},{4,5},{5,4},{6,7},{7,6},{8,9},{9,8},{10,11... | collective-permute-start | bytes 2359304 | tf_op jit(solution)/shard_map/ppermute | solution.py:520
  90.8 68.2 %collective-permute-start.21 = (bf16[256,768]{1,0:T(8,128)(2,1)}, bf16[256,768]{1,0:T(8,128)(2,1)S(1)}, u32[]{:S(2)}, u32[]{:S(2)}) collective-permute-start(bf16[256,768]{1,0:T(8,128)(2,1)} %pad_maximum_fusion.2), channel_id=1, source_target_pairs={{0,2},{2,0},{4,6},{6,4},{8,10},{10,8},{12,14},{14,12},{16,18},{18,... | collective-permute-start | bytes 1179656 | tf_op jit(solution)/shard_map/ppermute | solution.py:514
  112.6 70.6 %collective-permute-start.15 = (bf16[512,768]{1,0:T(8,128)(2,1)}, bf16[512,768]{1,0:T(8,128)(2,1)S(1)}, u32[]{:S(2)}, u32[]{:S(2)}) collective-permute-start(bf16[512,768]{1,0:T(8,128)(2,1)} %bitcast.61), channel_id=1, source_target_pairs={{0,8},{2,10},{4,12},{6,14},{8,16},{10,18},{12,20},{14,22},{16,24},... | collective-permute-start | bytes 2359304 | tf_op jit(solution)/shard_map/ppermute | solution.py:517
  133.8 51.1 %collective-permute-start.16 = (bf16[512,768]{1,0:T(8,128)(2,1)}, bf16[512,768]{1,0:T(8,128)(2,1)S(1)}, u32[]{:S(2)}, u32[]{:S(2)}) collective-permute-start(bf16[512,768]{1,0:T(8,128)(2,1)} %bitcast.62), channel_id=1, source_target_pairs={{0,16},{2,18},{4,20},{6,22},{8,24},{10,26},{12,28},{14,30},{16,0},... | collective-permute-start | bytes 2359304 | tf_op jit(solution)/shard_map/ppermute | solution.py:517
  153.0 32.5 %collective-permute-start.17 = (bf16[512,768]{1,0:T(8,128)(2,1)}, bf16[512,768]{1,0:T(8,128)(2,1)}, u32[]{:S(2)}, u32[]{:S(2)}) collective-permute-start(bf16[512,768]{1,0:T(8,128)(2,1)} %bitcast.63), channel_id=1, source_target_pairs={{0,24},{2,26},{4,28},{6,30},{8,0},{10,2},{12,4},{14,6},{16,8},{18,... | collective-permute-start | bytes 2359304 | tf_op jit(solution)/shard_map/ppermute | solution.py:517
  155.2 28.0 %collective-permute-start.22 = (bf16[256,768]{1,0:T(8,128)(2,1)}, bf16[256,768]{1,0:T(8,128)(2,1)}, u32[]{:S(2)}, u32[]{:S(2)}) collective-permute-start(bf16[256,768]{1,0:T(8,128)(2,1)} %pad_maximum_fusion.3), channel_id=1, source_target_pairs={{0,4},{2,6},{4,0},{6,2},{8,12},{10,14},{12,8},{14,10},{16,20},{18,... | collective-permute-start | bytes 1179656 | tf_op jit(solution)/shard_map/ppermute | solution.py:514
  159.0 24.1 %collective-permute-start.23 = (bf16[256,768]{1,0:T(8,128)(2,1)}, bf16[256,768]{1,0:T(8,128)(2,1)}, u32[]{:S(2)}, u32[]{:S(2)}) collective-permute-start(bf16[256,768]{1,0:T(8,128)(2,1)} %pad_maximum_fusion.4), channel_id=1, source_target_pairs={{0,6},{2,4},{4,2},{6,0},{8,14},{10,12},{12,10},{14,8},{16,22},{18,... | collective-permute-start | bytes 1179656 | tf_op jit(solution)/shard_map/ppermute | solution.py:514
  208.6 13.2 %collective-permute-start.25 = (bf16[4,64,1024]{2,1,0:T(8,128)(2,1)S(1)}, bf16[4,64,1024]{2,1,0:T(8,128)(2,1)S(1)}, u32[]{:S(2)}, u32[]{:S(2)}) collective-permute-start(bf16[4,64,1024]{2,1,0:T(8,128)(2,1)S(1)} %get-tuple-element.60), channel_id=1, source_target_pairs={{0,2},{2,0},{4,6},{6,4},{8,10},{10,8},{12,14},{14,12},{16,18},{18,... | collective-permute-start | bytes 1572872 | tf_op jit(solution)/shard_map/ppermute | solution.py:514
  209.8 24.6 %collective-permute-start.27 = (bf16[4,64,1024]{2,1,0:T(8,128)(2,1)S(1)}, bf16[4,64,1024]{2,1,0:T(8,128)(2,1)S(1)}, u32[]{:S(2)}, u32[]{:S(2)}) collective-permute-start(bf16[4,64,1024]{2,1,0:T(8,128)(2,1)S(1)} %get-tuple-element.61), channel_id=1, source_target_pairs={{0,6},{2,4},{4,2},{6,0},{8,14},{10,12},{12,10},{14,8},{16,22},{18,... | collective-permute-start | bytes 1572872 | tf_op jit(solution)/shard_map/ppermute | solution.py:514
  211.5 23.0 %collective-permute-start.26 = (bf16[4,64,1024]{2,1,0:T(8,128)(2,1)S(1)}, bf16[4,64,1024]{2,1,0:T(8,128)(2,1)S(1)}, u32[]{:S(2)}, u32[]{:S(2)}) collective-permute-start(bf16[4,64,1024]{2,1,0:T(8,128)(2,1)S(1)} %get-tuple-element.62), channel_id=1, source_target_pairs={{0,4},{2,6},{4,0},{6,2},{8,12},{10,14},{12,8},{14,10},{16,20},{18,... | collective-permute-start | bytes 1572872 | tf_op jit(solution)/shard_map/ppermute | solution.py:514
  238.3 10.8 %collective-permute-start.28 = (bf16[64,1024]{1,0:T(8,128)(2,1)S(1)}, bf16[64,1024]{1,0:T(8,128)(2,1)S(1)}, u32[]{:S(2)}, u32[]{:S(2)}) collective-permute-start(bf16[64,1024]{1,0:T(8,128)(2,1)S(1)} %get-tuple-element.72), channel_id=1, source_target_pairs={{0,8},{2,10},{4,12},{6,14},{8,16},{10,18},{12,20},{14,22},{16,24},... | collective-permute-start | bytes 393224 | tf_op jit(solution)/shard_map/ppermute | solution.py:517
  253.8 10.5 %collective-permute-start.31 = (bf16[64,1024]{1,0:T(8,128)(2,1)S(1)}, bf16[64,1024]{1,0:T(8,128)(2,1)S(1)}, u32[]{:S(2)}, u32[]{:S(2)}) collective-permute-start(bf16[64,1024]{1,0:T(8,128)(2,1)S(1)} %get-tuple-element.26), channel_id=1, source_target_pairs={{0,24},{2,26},{4,28},{6,30},{8,0},{10,2},{12,4},{14,6},{16,8},{18,... | collective-permute-start | bytes 393224 | tf_op jit(solution)/shard_map/ppermute | solution.py:517
  264.4 13.0 %collective-permute-start.39 = (bf16[4,64,1024]{2,1,0:T(8,128)(2,1)S(1)}, bf16[4,64,1024]{2,1,0:T(8,128)(2,1)S(1)}, u32[]{:S(2)}, u32[]{:S(2)}) collective-permute-start(bf16[4,64,1024]{2,1,0:T(8,128)(2,1)S(1)} %pad_maximum_fusion.refs_0_), channel_id=1, source_target_pairs={{0,6},{2,4},{4,2},{6,0},{8,14},{10,12},{12,10},{14,8},{16,22},{18,... | collective-permute-start | bytes 1572872 | tf_op jit(solution)/shard_map/ppermute | solution.py:514
  265.0 24.7 %collective-permute-start.37 = (bf16[4,64,1024]{2,1,0:T(8,128)(2,1)S(1)}, bf16[4,64,1024]{2,1,0:T(8,128)(2,1)S(1)}, u32[]{:S(2)}, u32[]{:S(2)}) collective-permute-start(bf16[4,64,1024]{2,1,0:T(8,128)(2,1)S(1)} %pad_maximum_fusion.refs_0_), channel_id=1, source_target_pairs={{0,4},{2,6},{4,0},{6,2},{8,12},{10,14},{12,8},{14,10},{16,20},{18,... | collective-permute-start | bytes 1572872 | tf_op jit(solution)/shard_map/ppermute | solution.py:514
  265.7 24.9 %collective-permute-start.35 = (bf16[4,64,1024]{2,1,0:T(8,128)(2,1)S(1)}, bf16[4,64,1024]{2,1,0:T(8,128)(2,1)S(1)}, u32[]{:S(2)}, u32[]{:S(2)}) collective-permute-start(bf16[4,64,1024]{2,1,0:T(8,128)(2,1)S(1)} %pad_maximum_fusion.refs_0_), channel_id=1, source_target_pairs={{0,2},{2,0},{4,6},{6,4},{8,10},{10,8},{12,14},{14,12},{16,18},{18,... | collective-permute-start | bytes 1572872 | tf_op jit(solution)/shard_map/ppermute | solution.py:514
  267.1 24.4 %collective-permute-start.34 = (bf16[4,64,1024]{2,1,0:T(8,128)(2,1)S(1)}, bf16[4,64,1024]{2,1,0:T(8,128)(2,1)S(1)}, u32[]{:S(2)}, u32[]{:S(2)}) collective-permute-start(bf16[4,64,1024]{2,1,0:T(8,128)(2,1)S(1)} %pad_maximum_fusion.refs_0_), channel_id=1, source_target_pairs={{0,1},{1,0},{2,3},{3,2},{4,5},{5,4},{6,7},{7,6},{8,9},{9,8},{10,11... | collective-permute-start | bytes 1572872 | tf_op jit(solution)/shard_map/ppermute | solution.py:520
  277.4 14.1 %collective-permute-start.40 = (bf16[4,64,1024]{2,1,0:T(8,128)(2,1)S(1)}, bf16[4,64,1024]{2,1,0:T(8,128)(2,1)S(1)}, u32[]{:S(2)}, u32[]{:S(2)}) collective-permute-start(bf16[4,64,1024]{2,1,0:T(8,128)(2,1)S(1)} %collective-permute-done.39.refs_6_), channel_id=1, source_target_pairs={{0,1},{1,0},{2,3},{3,2},{4,5},{5,4},{6,7},{7,6},{8,9},{9,8},{10,11... | collective-permute-start | bytes 1572872 | tf_op jit(solution)/shard_map/ppermute | solution.py:520
  (51 other events, 622.7 us)

commit v3 on v2

--- a/solution.py
+++ b/solution.py
@@ -126,48 +126,46 @@
 
 
 def list_kernel(store_rows, groups, first, block, place_ref, *refs):
-    ids_refs, out_ref = refs[:-1], refs[-1]
-    here, mine, rep = place_ref[0], place_ref[1], place_ref[2]
-    fan, near_rows = ids_refs[0].shape
+    ids_refs, out_refs = refs[:groups], refs[groups:]
+    here, mine = place_ref[0], place_ref[1]
+    cores, fan, near_rows = ids_refs[0].shape
     per_plane = PLANE * store_rows
     lanes = lax.broadcasted_iota(jnp.int32, (near_rows, near_rows), 0) // block
     spots = lax.broadcasted_iota(jnp.int32, (near_rows, near_rows), 1)
     blocks = jnp.where(lanes == spots, 1.0, 0.0).astype(jnp.bfloat16)
-    for k, ids_ref in enumerate(ids_refs):
-        gid = ids_ref[...]
-        owner, row = gid // store_rows, gid % store_rows
-        distance = lax.bitwise_xor(owner % PLANE, mine)
-        turned = row + rep * (store_rows // 2)
-        turned = jnp.where(turned >= store_rows, turned - store_rows, turned)
-        row = distance * store_rows + jnp.where(distance == 0, row, turned)
-        row = jnp.where(owner // PLANE == here, row, per_plane)
-        rows = [row[j : j + 1] for j in range(fan)]
-        for a, b in sort_pairs(fan):
-            rows[a], rows[b] = jnp.minimum(rows[a], rows[b]), jnp.maximum(rows[a], rows[b])
-        for j in range(fan):
-            out_ref[k, j : j + 1, :] = rows[j] * 8
-        if first < fan:
-            more = jnp.where(rows[first] < per_plane, 1.0, 0.0).astype(jnp.bfloat16)
-            more = dot(jnp.broadcast_to(more, (8, near_rows)), blocks)
-            out_ref[k, fan : fan + 1, :] = more[0:1].astype(jnp.int32)
-        else:
-            out_ref[k, fan : fan + 1, :] = jnp.zeros((1, near_rows), jnp.int32)
+    for ids_ref, out_ref in zip(ids_refs, out_refs):
+        for core in range(cores):
+            gid = ids_ref[core]
+            owner, row = gid // store_rows, gid % store_rows
+            row = lax.bitwise_xor(owner % PLANE, mine) * store_rows + row
+            row = jnp.where(owner // PLANE == here, row, per_plane)
+            rows = [row[j : j + 1] for j in range(fan)]
+            for a, b in sort_pairs(fan):
+                rows[a], rows[b] = jnp.minimum(rows[a], rows[b]), jnp.maximum(rows[a], rows[b])
+            for j in range(fan):
+                out_ref[core, j : j + 1, :] = rows[j] * 8
+            if first < fan:
+                more = jnp.where(rows[first] < per_plane, 1.0, 0.0).astype(jnp.bfloat16)
+                more = dot(jnp.broadcast_to(more, (8, near_rows)), blocks)
+                out_ref[core, fan : fan + 1, :] = more[0:1].astype(jnp.int32)
+            else:
+                out_ref[core, fan : fan + 1, :] = jnp.zeros((1, near_rows), jnp.int32)
 
 
 def row_lists(place, ids_all, store_rows, first, block):
-    fan, near_rows = ids_all[0].shape
+    cores, fan, near_rows = ids_all[0].shape
     groups = len(ids_all)
     return pl.pallas_call(
         functools.partial(list_kernel, store_rows, groups, first, block),
-        out_shape=jax.ShapeDtypeStruct((groups, fan + 1, near_rows), jnp.int32),
+        out_shape=(jax.ShapeDtypeStruct((cores, fan + 1, near_rows), jnp.int32),) * groups,
         in_specs=[SMEM] + [VMEM] * groups,
-        out_specs=VMEM,
+        out_specs=(VMEM,) * groups,
         compiler_params=pltpu.CompilerParams(vmem_limit_bytes=32 * MIB),
         name="row_lists",
     )(place, *ids_all)
 
 
-def partial_kernel(places, turns, first, block, *refs):
+def partial_kernel(places, first, block, *refs):
     index_ref = refs[0]
     piece_refs = refs[1 : 1 + len(places)]
     out_ref, table, sums = refs[1 + len(places) : 4 + len(places)]
@@ -209,7 +207,7 @@
         lax.fori_loop(0, buffer.shape[0] // chunk, fill, 0)
 
     unroll = 16
-    for at, turn in enumerate(turns):
+    for turn in range(index_ref.shape[0]):
 
         def step(i, carry):
             for u in range(unroll):
@@ -237,15 +235,15 @@
             lax.fori_loop(0, near_rows // block, rest, 0)
         for unit in range(units):
             lanes = slice(unit * LANES, (unit + 1) * LANES)
-            out_ref[at, :, lanes] = sums[pl.ds(unit, near_rows, stride=8), :].astype(jnp.bfloat16)
-
-
-def partial_sums(index, pieces, places, turns, total, first, block):
-    near_rows = index.shape[2]
+            out_ref[turn, :, lanes] = sums[pl.ds(unit, near_rows, stride=8), :].astype(jnp.bfloat16)
+
+
+def partial_sums(index, pieces, places, total, first, block):
+    trainers, unused, near_rows = index.shape
     width = pieces[0].shape[1]
     return pl.pallas_call(
-        functools.partial(partial_kernel, places, turns, first, block),
-        out_shape=jax.ShapeDtypeStruct((len(turns), near_rows, width), jnp.bfloat16),
+        functools.partial(partial_kernel, places, first, block),
+        out_shape=jax.ShapeDtypeStruct((trainers, near_rows, width), jnp.bfloat16),
         in_specs=[SMEM] + [pl.BlockSpec(memory_space=pl.ANY)] * len(pieces),
         out_specs=VMEM,
         scratch_shapes=[
@@ -262,16 +260,14 @@
 def trainer_kernel(sizes, scale, *refs):
     groups, rows_low, rows_top, classes, class_pad = sizes
     place_ref, labels_ref, adj_ref, column_ref, wl_ref, wt_ref = refs[:6]
-    block_refs = refs[6 : 6 + groups]
-    near_refs = refs[6 + groups : 6 + groups + PLANE]
-    logits_ref, keep_ref, send_ref, li, hidden, slope, top_in, wt = refs[6 + groups + PLANE :]
+    mean_refs, near_refs = refs[6:8], refs[8 : 8 + PLANE]
+    logits_ref, keep_ref, send_ref, li, hidden, slope, top_in, wt = refs[8 + PLANE :]
     seeds, fan_top = adj_ref.shape
     near_rows, low_width = li.shape
     feat = low_width // 2
     width = hidden.shape[1]
     capacity = near_refs[0].shape[0]
     here, mine, rep = place_ref[0], place_ref[1], place_ref[2]
-    fan_low = place_ref[3].astype(jnp.float32)
 
     column = column_ref[...]
     rows_cap = lax.broadcasted_iota(jnp.int32, (capacity, near_rows), 0)
@@ -280,11 +276,11 @@
         marks = jnp.where(rows_cap + d * capacity == column, 1.0, 0.0).astype(jnp.bfloat16)
         term = dot(marks, near_refs[d][...], 0, 0)
         near = term if near is None else near + term
-    total = block_refs[0][...].astype(jnp.float32)
-    for k in range(1, groups):
-        total = total + block_refs[k][...].astype(jnp.float32)
     li[:, :feat] = near.astype(jnp.bfloat16)
-    li[:, feat:] = (total / fan_low).astype(jnp.bfloat16)
+    share = feat // 2
+    for turn, mean_ref in enumerate(mean_refs):
+        core = rep if turn == 0 else 1 - rep
+        li[:, pl.ds(pl.multiple_of(feat + core * share, LANES), share)] = mean_ref[...]
 
     wt[...] = jnp.zeros_like(wt)
     wt[:, :classes] = wt_ref[...].astype(jnp.bfloat16)
@@ -357,7 +353,7 @@
         send_ref[a, b, rows_low:, :] = other.astype(jnp.bfloat16)
 
 
-def trainer_step(place, labels, adj_top, column, wl, wt, blocks, nears, sizes, scale):
+def trainer_step(place, labels, adj_top, column, wl, wt, means, nears, sizes, scale):
     groups, rows_low, rows_top, classes, class_pad = sizes
     seeds = adj_top.shape[0]
     low_width, width = wl.shape
@@ -370,7 +366,7 @@
             jax.ShapeDtypeStruct((PLANE, groups, rows, width), jnp.float32),
             jax.ShapeDtypeStruct((PLANE, groups, rows, width), jnp.bfloat16),
         ),
-        in_specs=[SMEM] + [VMEM] * (5 + groups + PLANE),
+        in_specs=[SMEM] + [VMEM] * (7 + PLANE),
         out_specs=(VMEM, VMEM, VMEM),
         scratch_shapes=[
             pltpu.VMEM((near_rows, low_width), jnp.bfloat16),
@@ -381,7 +377,7 @@
         ],
         compiler_params=pltpu.CompilerParams(vmem_limit_bytes=60 * MIB),
         name="trainer_step",
-    )(place, labels, adj_top, column, wl, wt, *blocks, *nears)
+    )(place, labels, adj_top, column, wl, wt, *means, *nears)
 
 
 def adam_part(gradient, moment, square):
@@ -508,7 +504,7 @@
     rows_low, rows_top = first_low.shape[0], first_top.shape[0]
     sizes = (groups, rows_low, rows_top, classes, class_pad)
     bf16 = jnp.bfloat16
-    place = jnp.stack([here, mine, rep, jnp.int32(fan)]).astype(jnp.int32)
+    place = jnp.stack([here, mine, rep]).astype(jnp.int32)
 
     def across(x, distance):
         return lax.ppermute(x, "store", [(i, i ^ distance) for i in range(stores)])
@@ -519,11 +515,9 @@
     def sibling(x):
         return lax.ppermute(x, "rep", [(0, 1), (1, 0)])
 
-    quarter = half // 2
-    own_a = lax.dynamic_slice_in_dim(features, rep * half, quarter, 0)
-    own_b = lax.dynamic_slice_in_dim(features, rep * half + quarter, quarter, 0)
-    x_a, y_b = across(own_a, 1), across(own_b, 2)
-    x_b, y_a = across(own_b, 1), across(own_a, 2)
+    share = features.shape[1] // 2
+    own = lax.dynamic_slice_in_dim(features, rep * share, share, 1)
+    from_x, from_y = across(own, 1), across(own, 2)
     gid_near = owners_near[:, 0] * store_rows + slots_near[:, 0]
     gid_far = owners_far[:, 0] * store_rows + slots_far[:, 0]
     table = jnp.concatenate([gid_near, gid_far]).reshape(-1, LANES)
@@ -531,26 +525,23 @@
     ids, requests, column = compose(
         place, adjacency_low, table, gid_near.reshape(1, near_rows), store_rows, stores, capacity
     )
-    ids_all = [ids] + [along(ids, -k) for k in range(1, groups)]
+    pair = jnp.stack([ids, sibling(ids)])
+    ids_all = [pair] + [along(pair, -k) for k in range(1, groups)]
     requests = lax.all_to_all(requests.reshape(stores, capacity), "store", 0, 0, tiled=True)
     held = near_rows_held(place, requests, features, groups)
     first, block = min(8, fan), 8
     lists = row_lists(place, ids_all, store_rows, first, block)
     lined = [held[0]] + [along(held[k], k) for k in range(1, groups)]
-    corner_a, corner_b = across(x_a, 2), across(y_b, 1)
-    pieces, places = [features], [0]
-    for turn, (one, two) in enumerate([(x_a, x_b), (y_a, y_b), (corner_a, corner_b)]):
-        pieces += [one, two, sibling(one), sibling(two)]
-        places += [(turn + 1) * store_rows + quarter * i for i in range(4)]
-
-    per_call = -(-groups // 4)
-    order = [groups // 2] + [k for k in range(1, groups) if k != groups // 2] + [0]
-    blocks = {}
-    for start in range(0, groups, per_call):
-        turns = order[start : start + per_call]
-        made = partial_sums(lists, pieces, places, turns, PLANE * store_rows, first, block)
-        for i, k in enumerate(turns):
-            blocks[k] = along(made[i], k) if k else made[i]
+    corner_a, corner_b = across(from_x[:half], 2), across(from_y[half:], 1)
+    pieces = [own, from_x, from_y, corner_a, corner_b]
+    places = [0, store_rows, 2 * store_rows, 3 * store_rows, 3 * store_rows + half]
+
+    total = 0.0
+    for k in [groups // 2] + [k for k in range(1, groups) if k != groups // 2] + [0]:
+        made = partial_sums(lists[k], pieces, places, PLANE * store_rows, first, block)
+        total = total + (along(made, k) if k else made).astype(jnp.float32)
+    means = (total / fan).astype(bf16)
+    means = [means[0], sibling(means[1])]
 
     nears = []
     for d in range(PLANE):
@@ -565,7 +556,7 @@
         column,
         weights_low,
         weights_top,
-        [blocks[k] for k in range(groups)],
+        means,
         nears,
         sizes,
         scale,

time: 304 us -> 316 us (1.039)
  local copies, waits for them, and re-layouts: 17.5 us -> 24.7 us
  Pallas kernels: 109 us -> 115 us
  waiting for transfers between devices: 98.8 us -> 95.6 us
    all_to_all x1, waiting for transfers between devices: 3.4 us -> 22 us  [per_device(): lax.all_to_all(requests.reshape(stores, capacity), 'store', 0, 0, tiled=T...]
    ppermute x15, waiting for transfers between devices: 47.2 us -> 29 us  [along(): lax.ppermute(x, 'store', [(i, (i + hops * PLANE) % stores) for i in range...]
    pallas_call x4, Pallas kernels: 76.5 us -> 81.5 us  [partial_sums(): pl.pallas_call(functools.partial(partial_kernel, places, first, block), o...]
    ppermute x15 -> x13, starting transfers between devices: 16.1 us -> 13 us  [across(): return lax.ppermute(x, 'store', [(i, i ^ distance) for i in range(stores)])]
    ppermute x15 -> x13, waiting for transfers between devices: 42.6 us -> 39.6 us  [across(): return lax.ppermute(x, 'store', [(i, i ^ distance) for i in range(stores)])]
    unnamed x86 -> x74, local copies, waits for them, and re-layouts: 9.6 us -> 11.1 us
    ppermute x11 -> x7, starting transfers between devices: 28.9 us -> 29.9 us  [sibling(): return lax.ppermute(x, 'rep', [(0, 1), (1, 0)])]
  transfers between devices with their start and end apart: 42 -> 36, of which waited for: 19 -> 17; matrix products, arithmetic and copies ran while one was open for 4% -> 6% of each run, Pallas kernels for 28% -> 29%
where the time goes in v3:
time: 316 us; the launch traced here: 314 us
  Pallas kernels  115 us (36%)
  waiting for transfers between devices  95.6 us (30%)
  starting transfers between devices  68.5 us (22%)
  local copies, waits for them, and re-layouts  24.7 us (8%)
  other arithmetic  9.25 us (3%)
    pallas_call x4, Pallas kernels, partial_sums(): pl.pallas_call(functools.partial(partial_kernel, places, first, block), o...  81.5 us
    ppermute x13, waiting for transfers between devices, across(): return lax.ppermute(x, 'store', [(i, i ^ distance) for i in range(stores)])  39.6 us
    ppermute x7, starting transfers between devices, sibling(): return lax.ppermute(x, 'rep', [(0, 1), (1, 0)])  29.9 us
    ppermute x15, waiting for transfers between devices, along(): lax.ppermute(x, 'store', [(i, (i + hops * PLANE) % stores) for i in range...  29 us
    all_to_all x1, waiting for transfers between devices, per_device(): lax.all_to_all(requests.reshape(stores, capacity), 'store', 0, 0, tiled=T...  22 us
    ppermute x15, starting transfers between devices, along(): lax.ppermute(x, 'store', [(i, (i + hops * PLANE) % stores) for i in range...  20.8 us
    pallas_call x1, Pallas kernels, trainer_step(): pl.pallas_call(functools.partial(trainer_kernel, sizes, scale), out_shape...  14.1 us
    ppermute x13, starting transfers between devices, across(): return lax.ppermute(x, 'store', [(i, i ^ distance) for i in range(stores)])  13 us
  transfers between devices with their start and end apart: 36, of which 17 were waited for; matrix products, arithmetic and copies ran while one was open for 6% of the time, Pallas kernels for 29%

profile of v3, /device:TPU:9, one launch (start us, length us, event | category | flops | bytes accessed | tf_op | source)
XLA Modules:
  0.0 313.6 jit_solution(743944171283174731)
XLA Ops:
  0.7 2.9 constant_dynamic-slice_fusion.refs_1_
  6.3 2.8 compose_ids.1
  11.5 4.8 %all-to-all-start = ((s32[16,1,64]{2,1,0:T(1,128)}), s32[16,1,64]{2,1,0:T(1,128)S(1)}, u32[]{:S(2)}, u32[]{:S(2)}) async-start(s32[16,1,64]{2,1,0:T(1,128)} %bitcast.14), calls=%async_computation | async-start | bytes 16384 | tf_op jit(solution)/shard_map/all_to_all | solution.py:530
  16.3 1.8 collective-permute-start
  18.1 22.0 %all-to-all-done = s32[16,1,64]{2,1,0:T(1,128)S(1)} async-done(((s32[16,1,64]{2,1,0:T(1,128)}), s32[16,1,64]{2,1,0:T(1,128)S(1)}, u32[]{:S(2)}, u32[]{:S(2)}) %all-to-all-start) | async-done | bytes 4128 | tf_op jit(solution)/shard_map/all_to_all | solution.py:530
  40.1 4.1 %near_rows.1 = bf16[4,256,768]{2,1,0:T(8,128)(2,1)S(1)} custom-call(s32[3]{0:T(128)S(1)} %pad_add_fusion.1.place_ref.refs_0_, s32[16,64]{1,0:T(8,128)S(1)} %bitcast.58, bf16[2048,768]{1,0:T(8,128)(2,1)S(1)} %copy-done), custom_call_target="tpu_custom_call" | custom-call | tf_op jit(solution)/shard_map/near_rows/pallas_call | solution.py:102
  53.4 5.7 %collective-permute-done.3.refs_3_ = s32[2,15,512]{2,1,0:T(8,128)S(1)} collective-permute-done((s32[2,15,512]{2,1,0:T(8,128)S(1)}, s32[2,15,512]{2,1,0:T(8,128)S(1)}, u32[]{:S(2)}, u32[]{:S(2)}) %collective-permute-start.3) | collective-permute-done | bytes 61472 | tf_op jit(solution)/shard_map/ppermute | solution.py:513
  59.1 2.1 collective-permute-start.14
  61.2 5.7 %collective-permute-start.1 = (s32[2,15,512]{2,1,0:T(8,128)S(1)}, s32[2,15,512]{2,1,0:T(8,128)S(1)}, u32[]{:S(2)}, u32[]{:S(2)}) collective-permute-start(s32[2,15,512]{2,1,0:T(8,128)S(1)} %pad_add_fusion.refs_0_), channel_id=1, source_target_pairs={{0,24},{2,26},{4,28},{6,30},{8,0},{10,2},{12,4},{14,6},{16,8},{18,... | collective-permute-start | bytes 184328 | tf_op jit(solution)/shard_map/ppermute | solution.py:513
  67.6 3.0 collective-permute-done.1.refs_1_
  71.2 2.3 row_lists.1
  77.2 20.3 %partial_sums.4 = bf16[2,512,384]{2,1,0:T(8,128)(2,1)} custom-call(s32[2,16,512]{2,1,0:T(8,128)} %copy-done.6, bf16[2048,384]{1,0:T(8,128)(2,1)} %constant_dynamic-slice_fusion.refs_1_, bf16[2048,384]{1,0:T(8,128)(2,1)} %collective-permute-done.4.refs_2_, bf16[2048,384]{1,0:T(8,128)(2,1)} %collective-permute-done.5.refs_3_, bf16[1024,384]{1,0:T(8,128)(2,1)} %copy-done.13, ...), custom_call_target="tpu_custom_call" | custom-call | tf_op jit(solution)/shard_map/partial_sums/pallas_call | solution.py:244
  99.0 20.3 %partial_sums.5 = bf16[2,512,384]{2,1,0:T(8,128)(2,1)} custom-call(s32[2,16,512]{2,1,0:T(8,128)} %copy-done.5, bf16[2048,384]{1,0:T(8,128)(2,1)} %constant_dynamic-slice_fusion.refs_1_, bf16[2048,384]{1,0:T(8,128)(2,1)} %collective-permute-done.4.refs_2_, bf16[2048,384]{1,0:T(8,128)(2,1)} %collective-permute-done.5.refs_3_, bf16[1024,384]{1,0:T(8,128)(2,1)} %copy-done.13, ...), custom_call_target="tpu_custom_call" | custom-call | tf_op jit(solution)/shard_map/partial_sums/pallas_call | solution.py:244
  119.6 20.5 %partial_sums.6 = bf16[2,512,384]{2,1,0:T(8,128)(2,1)} custom-call(s32[2,16,512]{2,1,0:T(8,128)} %copy-done.4, bf16[2048,384]{1,0:T(8,128)(2,1)} %constant_dynamic-slice_fusion.refs_1_, bf16[2048,384]{1,0:T(8,128)(2,1)} %collective-permute-done.4.refs_2_, bf16[2048,384]{1,0:T(8,128)(2,1)} %collective-permute-done.5.refs_3_, bf16[1024,384]{1,0:T(8,128)(2,1)} %copy-done.13, ...), custom_call_target="tpu_custom_call" | custom-call | tf_op jit(solution)/shard_map/partial_sums/pallas_call | solution.py:244
  148.4 20.5 %partial_sums.7 = bf16[2,512,384]{2,1,0:T(8,128)(2,1)} custom-call(s32[2,16,512]{2,1,0:T(8,128)} %copy-done.3, bf16[2048,384]{1,0:T(8,128)(2,1)} %constant_dynamic-slice_fusion.refs_1_, bf16[2048,384]{1,0:T(8,128)(2,1)} %collective-permute-done.4.refs_2_, bf16[2048,384]{1,0:T(8,128)(2,1)} %collective-permute-done.5.refs_3_, bf16[1024,384]{1,0:T(8,128)(2,1)} %copy-done.13, ...), custom_call_target="tpu_custom_call" | custom-call | tf_op jit(solution)/shard_map/partial_sums/pallas_call | solution.py:244
  170.1 1.8 multiply_convert_fusion
  172.7 19.1 %collective-permute-start.11 = (bf16[512,384]{1,0:T(8,128)(2,1)S(1)}, bf16[512,384]{1,0:T(8,128)(2,1)S(1)}, u32[]{:S(2)}, u32[]{:S(2)}) collective-permute-start(bf16[512,384]{1,0:T(8,128)(2,1)S(1)} %get-tuple-element.76), channel_id=1, source_target_pairs={{0,1},{1,0},{2,3},{3,2},{4,5},{5,4},{6,7},{7,6},{8,9},{9,8},{10,11... | collective-permute-start | bytes 1179656 | tf_op jit(solution)/shard_map/ppermute | solution.py:516
  196.8 14.1 %trainer_step.1 = (f32[128,153]{1,0:T(8,128)}, f32[4,4,64,1024]{3,2,1,0:T(8,128)}, bf16[4,4,64,1024]{3,2,1,0:T(8,128)(2,1)}) custom-call(s32[3]{0:T(128)} %copy-done.10, s32[128,1]{1,0:T(8,128)} %copy.36.refs_1_, s32[128,10]{1,0:T(8,128)} %copy.37.refs_2_, s32[1,512]{1,0:T(1,128)} %copy-done.11, f32[1536,1024]{1,0:T(8,128)} %wl.1, ...), custom_call_target="tpu_custom_call" | custom-call | tf_op jit(solution)/shard_map/trainer_step/pallas_call | solution.py:362
  211.7 4.0 %collective-permute-done.18 = bf16[4,4,64,1024]{3,2,1,0:T(8,128)(2,1)S(1)} collective-permute-done((bf16[4,4,64,1024]{3,2,1,0:T(8,128)(2,1)}, bf16[4,4,64,1024]{3,2,1,0:T(8,128)(2,1)S(1)}, u32[]{:S(2)}, u32[]{:S(2)}) %collective-permute-start.18) | collective-permute-done | bytes 2097184 | tf_op jit(solution)/shard_map/ppermute | solution.py:516
  215.7 3.1 fusion.3
  221.9 10.6 %collective-permute-done.19 = bf16[4,64,1024]{2,1,0:T(8,128)(2,1)S(1)} collective-permute-done((bf16[4,64,1024]{2,1,0:T(8,128)(2,1)S(1)}, bf16[4,64,1024]{2,1,0:T(8,128)(2,1)S(1)}, u32[]{:S(2)}, u32[]{:S(2)}) %collective-permute-start.19) | collective-permute-done | bytes 524320 | tf_op jit(solution)/shard_map/ppermute | solution.py:510
  232.4 12.3 %collective-permute-done.21 = bf16[4,64,1024]{2,1,0:T(8,128)(2,1)S(1)} collective-permute-done((bf16[4,64,1024]{2,1,0:T(8,128)(2,1)S(1)}, bf16[4,64,1024]{2,1,0:T(8,128)(2,1)S(1)}, u32[]{:S(2)}, u32[]{:S(2)}) %collective-permute-start.21) | collective-permute-done | bytes 524320 | tf_op jit(solution)/shard_map/ppermute | solution.py:510
  250.0 6.0 %collective-permute-done.23.refs_2_ = bf16[64,1024]{1,0:T(8,128)(2,1)S(1)} collective-permute-done((bf16[64,1024]{1,0:T(8,128)(2,1)S(1)}, bf16[64,1024]{1,0:T(8,128)(2,1)S(1)}, u32[]{:S(2)}, u32[]{:S(2)}) %collective-permute-start.23) | collective-permute-done | bytes 131104 | tf_op jit(solution)/shard_map/ppermute | solution.py:513
  255.9 2.8 collective-permute-done.22.refs_1_
  259.6 2.2 collective-permute-start.27
  264.7 7.9 %collective-permute-done.26 = bf16[64,1024]{1,0:T(8,128)(2,1)S(1)} collective-permute-done((bf16[64,1024]{1,0:T(8,128)(2,1)S(1)}, bf16[64,1024]{1,0:T(8,128)(2,1)S(1)}, u32[]{:S(2)}, u32[]{:S(2)}) %collective-permute-start.26) | collective-permute-done | bytes 131104 | tf_op jit(solution)/shard_map/ppermute | solution.py:513
  276.1 2.2 collective-permute-start.28
  278.4 8.1 %collective-permute-done.33.refs_6_ = bf16[4,64,1024]{2,1,0:T(8,128)(2,1)S(1)} collective-permute-done((bf16[4,64,1024]{2,1,0:T(8,128)(2,1)S(1)}, bf16[4,64,1024]{2,1,0:T(8,128)(2,1)S(1)}, u32[]{:S(2)}, u32[]{:S(2)}) %collective-permute-start.33) | collective-permute-done | bytes 524320 | tf_op jit(solution)/shard_map/ppermute | solution.py:510
  286.4 4.2 %collective-permute-start.34 = (bf16[4,64,1024]{2,1,0:T(8,128)(2,1)S(1)}, bf16[4,64,1024]{2,1,0:T(8,128)(2,1)S(1)}, u32[]{:S(2)}, u32[]{:S(2)}) collective-permute-start(bf16[4,64,1024]{2,1,0:T(8,128)(2,1)S(1)} %collective-permute-done.33.refs_6_), channel_id=1, source_target_pairs={{0,1},{1,0},{2,3},{3,2},{4,5},{5,4},{6,7},{7,6},{8,9},{9,8},{10,11... | collective-permute-start | bytes 1572872 | tf_op jit(solution)/shard_map/ppermute | solution.py:516
  290.6 7.9 %collective-permute-done.31.refs_4_ = bf16[4,64,1024]{2,1,0:T(8,128)(2,1)S(1)} collective-permute-done((bf16[4,64,1024]{2,1,0:T(8,128)(2,1)S(1)}, bf16[4,64,1024]{2,1,0:T(8,128)(2,1)S(1)}, u32[]{:S(2)}, u32[]{:S(2)}) %collective-permute-start.31) | collective-permute-done | bytes 524320 | tf_op jit(solution)/shard_map/ppermute | solution.py:510
  302.1 8.9 %apply_updates.1 = (f32[1536,1024]{1,0:T(8,128)}, f32[2048,153]{1,0:T(8,128)}) custom-call(s32[3]{0:T(128)} %copy-done.10, f32[1536,1024]{1,0:T(8,128)} %wl.1, f32[2048,153]{1,0:T(8,128)} %copy.38.refs_5_.wt, bf16[4,64,1024]{2,1,0:T(8,128)(2,1)} %copy-done.14, bf16[4,64,1024]{2,1,0:T(8,128)(2,1)} %copy-done.19, bf16[4,64,1024]{2,1,0:T(8,128)(2,1)} %copy-done.18, ...), custom_call_target="tpu_custom_call" | custom-call | tf_op jit(solution)/shard_map/apply_updates/pallas_call | solution.py:463
  310.9 2.7 copy.41
  (155 shorter events, 56.0 us)
Async XLA Ops:
  3.6 40.6 %collective-permute-start.5 = (bf16[2048,384]{1,0:T(8,128)(2,1)}, bf16[2048,384]{1,0:T(8,128)(2,1)}, u32[]{:S(2)}, u32[]{:S(2)}) collective-permute-start(bf16[2048,384]{1,0:T(8,128)(2,1)} %constant_dynamic-slice_fusion.refs_1_), channel_id=1, source_target_pairs={{0,4},{2,6},{4,0},{6,2},{8,12},{10,14},{12,8},{14,10},{16,20},{18,... | collective-permute-start | bytes 4718600 | tf_op jit(solution)/shard_map/ppermute | solution.py:510
  4.8 41.9 %collective-permute-start.4 = (bf16[2048,384]{1,0:T(8,128)(2,1)}, bf16[2048,384]{1,0:T(8,128)(2,1)}, u32[]{:S(2)}, u32[]{:S(2)}) collective-permute-start(bf16[2048,384]{1,0:T(8,128)(2,1)} %constant_dynamic-slice_fusion.refs_1_), channel_id=1, source_target_pairs={{0,2},{2,0},{4,6},{6,4},{8,10},{10,8},{12,14},{14,12},{16,18},{18,... | collective-permute-start | bytes 4718600 | tf_op jit(solution)/shard_map/ppermute | solution.py:510
  11.5 28.6 %all-to-all-start = ((s32[16,1,64]{2,1,0:T(1,128)}), s32[16,1,64]{2,1,0:T(1,128)S(1)}, u32[]{:S(2)}, u32[]{:S(2)}) async-start(s32[16,1,64]{2,1,0:T(1,128)} %bitcast.14), calls=%async_computation | async-start | bytes 16384 | tf_op jit(solution)/shard_map/all_to_all | solution.py:530
  16.3 34.8 %collective-permute-start = (s32[15,512]{1,0:T(8,128)S(1)}, s32[15,512]{1,0:T(8,128)S(1)}, u32[]{:S(2)}, u32[]{:S(2)}) collective-permute-start(s32[15,512]{1,0:T(8,128)S(1)} %get-tuple-element.25), channel_id=1, source_target_pairs={{0,1},{1,0},{2,3},{3,2},{4,5},{5,4},{6,7},{7,6},{8,9},{9,8},{10,11... | collective-permute-start | bytes 92168 | tf_op jit(solution)/shard_map/ppermute | solution.py:516
  45.4 30.6 %collective-permute-start.7 = (bf16[1024,384]{1,0:T(8,128)(2,1)S(1)}, bf16[1024,384]{1,0:T(8,128)(2,1)S(1)}, u32[]{:S(2)}, u32[]{:S(2)}) collective-permute-start(bf16[1024,384]{1,0:T(8,128)(2,1)S(1)} %slice.152), channel_id=1, source_target_pairs={{0,2},{2,0},{4,6},{6,4},{8,10},{10,8},{12,14},{14,12},{16,18},{18,... | collective-permute-start | bytes 2359304 | tf_op jit(solution)/shard_map/ppermute | solution.py:510
  47.9 28.1 %collective-permute-start.6 = (bf16[1024,384]{1,0:T(8,128)(2,1)S(1)}, bf16[1024,384]{1,0:T(8,128)(2,1)S(1)}, u32[]{:S(2)}, u32[]{:S(2)}) collective-permute-start(bf16[1024,384]{1,0:T(8,128)(2,1)S(1)} %slice.151), channel_id=1, source_target_pairs={{0,4},{2,6},{4,0},{6,2},{8,12},{10,14},{12,8},{14,10},{16,20},{18,... | collective-permute-start | bytes 2359304 | tf_op jit(solution)/shard_map/ppermute | solution.py:510
  49.8 26.2 %collective-permute-start.12 = (bf16[256,768]{1,0:T(8,128)(2,1)S(1)}, bf16[256,768]{1,0:T(8,128)(2,1)S(1)}, u32[]{:S(2)}, u32[]{:S(2)}) collective-permute-start(bf16[256,768]{1,0:T(8,128)(2,1)S(1)} %get-tuple-element.73), channel_id=1, source_target_pairs={{0,8},{2,10},{4,12},{6,14},{8,16},{10,18},{12,20},{14,22},{16,24},... | collective-permute-start | bytes 1179656 | tf_op jit(solution)/shard_map/ppermute | solution.py:513
  51.1 8.0 %collective-permute-start.3 = (s32[2,15,512]{2,1,0:T(8,128)S(1)}, s32[2,15,512]{2,1,0:T(8,128)S(1)}, u32[]{:S(2)}, u32[]{:S(2)}) collective-permute-start(s32[2,15,512]{2,1,0:T(8,128)S(1)} %pad_add_fusion.refs_0_), channel_id=1, source_target_pairs={{0,8},{2,10},{4,12},{6,14},{8,16},{10,18},{12,20},{14,22},{16,24},... | collective-permute-start | bytes 184328 | tf_op jit(solution)/shard_map/ppermute | solution.py:513
  52.4 8.8 %collective-permute-start.2 = (s32[2,15,512]{2,1,0:T(8,128)S(1)}, s32[2,15,512]{2,1,0:T(8,128)S(1)}, u32[]{:S(2)}, u32[]{:S(2)}) collective-permute-start(s32[2,15,512]{2,1,0:T(8,128)S(1)} %pad_add_fusion.refs_0_), channel_id=1, source_target_pairs={{0,16},{2,18},{4,20},{6,22},{8,24},{10,26},{12,28},{14,30},{16,0},... | collective-permute-start | bytes 184328 | tf_op jit(solution)/shard_map/ppermute | solution.py:513
  59.1 81.9 %collective-permute-start.14 = (bf16[256,768]{1,0:T(8,128)(2,1)}, bf16[256,768]{1,0:T(8,128)(2,1)}, u32[]{:S(2)}, u32[]{:S(2)}) collective-permute-start(bf16[256,768]{1,0:T(8,128)(2,1)} %get-tuple-element.74), channel_id=1, source_target_pairs={{0,24},{2,26},{4,28},{6,30},{8,0},{10,2},{12,4},{14,6},{16,8},{18,... | collective-permute-start | bytes 1179656 | tf_op jit(solution)/shard_map/ppermute | solution.py:513
  61.2 9.4 %collective-permute-start.1 = (s32[2,15,512]{2,1,0:T(8,128)S(1)}, s32[2,15,512]{2,1,0:T(8,128)S(1)}, u32[]{:S(2)}, u32[]{:S(2)}) collective-permute-start(s32[2,15,512]{2,1,0:T(8,128)S(1)} %pad_add_fusion.refs_0_), channel_id=1, source_target_pairs={{0,24},{2,26},{4,28},{6,30},{8,0},{10,2},{12,4},{14,6},{16,8},{18,... | collective-permute-start | bytes 184328 | tf_op jit(solution)/shard_map/ppermute | solution.py:513
  70.6 72.1 %collective-permute-start.13 = (bf16[256,768]{1,0:T(8,128)(2,1)}, bf16[256,768]{1,0:T(8,128)(2,1)}, u32[]{:S(2)}, u32[]{:S(2)}) collective-permute-start(bf16[256,768]{1,0:T(8,128)(2,1)} %get-tuple-element.75), channel_id=1, source_target_pairs={{0,16},{2,18},{4,20},{6,22},{8,24},{10,26},{12,28},{14,30},{16,0},... | collective-permute-start | bytes 1179656 | tf_op jit(solution)/shard_map/ppermute | solution.py:513
  97.5 71.4 %collective-permute-start.8 = (bf16[2,512,384]{2,1,0:T(8,128)(2,1)}, bf16[2,512,384]{2,1,0:T(8,128)(2,1)S(1)}, u32[]{:S(2)}, u32[]{:S(2)}) collective-permute-start(bf16[2,512,384]{2,1,0:T(8,128)(2,1)} %partial_sums.4), channel_id=1, source_target_pairs={{0,16},{2,18},{4,20},{6,22},{8,24},{10,26},{12,28},{14,30},{16,0},... | collective-permute-start | bytes 2359304 | tf_op jit(solution)/shard_map/ppermute | solution.py:513
  119.3 50.8 %collective-permute-start.9 = (bf16[2,512,384]{2,1,0:T(8,128)(2,1)}, bf16[2,512,384]{2,1,0:T(8,128)(2,1)S(1)}, u32[]{:S(2)}, u32[]{:S(2)}) collective-permute-start(bf16[2,512,384]{2,1,0:T(8,128)(2,1)} %partial_sums.5), channel_id=1, source_target_pairs={{0,8},{2,10},{4,12},{6,14},{8,16},{10,18},{12,20},{14,22},{16,24},... | collective-permute-start | bytes 2359304 | tf_op jit(solution)/shard_map/ppermute | solution.py:513
  140.1 30.0 %collective-permute-start.10 = (bf16[2,512,384]{2,1,0:T(8,128)(2,1)}, bf16[2,512,384]{2,1,0:T(8,128)(2,1)}, u32[]{:S(2)}, u32[]{:S(2)}) collective-permute-start(bf16[2,512,384]{2,1,0:T(8,128)(2,1)} %partial_sums.6), channel_id=1, source_target_pairs={{0,24},{2,26},{4,28},{6,30},{8,0},{10,2},{12,4},{14,6},{16,8},{18,... | collective-permute-start | bytes 2359304 | tf_op jit(solution)/shard_map/ppermute | solution.py:513
  145.2 50.7 %collective-permute-start.15 = (bf16[256,768]{1,0:T(8,128)(2,1)}, bf16[256,768]{1,0:T(8,128)(2,1)S(1)}, u32[]{:S(2)}, u32[]{:S(2)}) collective-permute-start(bf16[256,768]{1,0:T(8,128)(2,1)} %pad_maximum_fusion.2), channel_id=1, source_target_pairs={{0,2},{2,0},{4,6},{6,4},{8,10},{10,8},{12,14},{14,12},{16,18},{18,... | collective-permute-start | bytes 1179656 | tf_op jit(solution)/shard_map/ppermute | solution.py:510
  146.4 49.5 %collective-permute-start.16 = (bf16[256,768]{1,0:T(8,128)(2,1)}, bf16[256,768]{1,0:T(8,128)(2,1)}, u32[]{:S(2)}, u32[]{:S(2)}) collective-permute-start(bf16[256,768]{1,0:T(8,128)(2,1)} %pad_maximum_fusion.3), channel_id=1, source_target_pairs={{0,4},{2,6},{4,0},{6,2},{8,12},{10,14},{12,8},{14,10},{16,20},{18,... | collective-permute-start | bytes 1179656 | tf_op jit(solution)/shard_map/ppermute | solution.py:510
  168.9 27.0 %collective-permute-start.17 = (bf16[256,768]{1,0:T(8,128)(2,1)}, bf16[256,768]{1,0:T(8,128)(2,1)}, u32[]{:S(2)}, u32[]{:S(2)}) collective-permute-start(bf16[256,768]{1,0:T(8,128)(2,1)} %pad_maximum_fusion.4), channel_id=1, source_target_pairs={{0,6},{2,4},{4,2},{6,0},{8,14},{10,12},{12,10},{14,8},{16,22},{18,... | collective-permute-start | bytes 1179656 | tf_op jit(solution)/shard_map/ppermute | solution.py:510
  172.7 23.2 %collective-permute-start.11 = (bf16[512,384]{1,0:T(8,128)(2,1)S(1)}, bf16[512,384]{1,0:T(8,128)(2,1)S(1)}, u32[]{:S(2)}, u32[]{:S(2)}) collective-permute-start(bf16[512,384]{1,0:T(8,128)(2,1)S(1)} %get-tuple-element.76), channel_id=1, source_target_pairs={{0,1},{1,0},{2,3},{3,2},{4,5},{5,4},{6,7},{7,6},{8,9},{9,8},{10,11... | collective-permute-start | bytes 1179656 | tf_op jit(solution)/shard_map/ppermute | solution.py:516
  219.0 13.5 %collective-permute-start.19 = (bf16[4,64,1024]{2,1,0:T(8,128)(2,1)S(1)}, bf16[4,64,1024]{2,1,0:T(8,128)(2,1)S(1)}, u32[]{:S(2)}, u32[]{:S(2)}) collective-permute-start(bf16[4,64,1024]{2,1,0:T(8,128)(2,1)S(1)} %get-tuple-element.66), channel_id=1, source_target_pairs={{0,2},{2,0},{4,6},{6,4},{8,10},{10,8},{12,14},{14,12},{16,18},{18,... | collective-permute-start | bytes 1572872 | tf_op jit(solution)/shard_map/ppermute | solution.py:510
  220.6 24.1 %collective-permute-start.21 = (bf16[4,64,1024]{2,1,0:T(8,128)(2,1)S(1)}, bf16[4,64,1024]{2,1,0:T(8,128)(2,1)S(1)}, u32[]{:S(2)}, u32[]{:S(2)}) collective-permute-start(bf16[4,64,1024]{2,1,0:T(8,128)(2,1)S(1)} %get-tuple-element.67), channel_id=1, source_target_pairs={{0,6},{2,4},{4,2},{6,0},{8,14},{10,12},{12,10},{14,8},{16,22},{18,... | collective-permute-start | bytes 1572872 | tf_op jit(solution)/shard_map/ppermute | solution.py:510
  221.5 24.0 %collective-permute-start.20 = (bf16[4,64,1024]{2,1,0:T(8,128)(2,1)S(1)}, bf16[4,64,1024]{2,1,0:T(8,128)(2,1)S(1)}, u32[]{:S(2)}, u32[]{:S(2)}) collective-permute-start(bf16[4,64,1024]{2,1,0:T(8,128)(2,1)S(1)} %get-tuple-element.68), channel_id=1, source_target_pairs={{0,4},{2,6},{4,0},{6,2},{8,12},{10,14},{12,8},{14,10},{16,20},{18,... | collective-permute-start | bytes 1572872 | tf_op jit(solution)/shard_map/ppermute | solution.py:510
  247.4 8.6 %collective-permute-start.23 = (bf16[64,1024]{1,0:T(8,128)(2,1)S(1)}, bf16[64,1024]{1,0:T(8,128)(2,1)S(1)}, u32[]{:S(2)}, u32[]{:S(2)}) collective-permute-start(bf16[64,1024]{1,0:T(8,128)(2,1)S(1)} %get-tuple-element.79), channel_id=1, source_target_pairs={{0,16},{2,18},{4,20},{6,22},{8,24},{10,26},{12,28},{14,30},{16,0},... | collective-permute-start | bytes 393224 | tf_op jit(solution)/shard_map/ppermute | solution.py:513
  247.4 11.4 %collective-permute-start.22 = (bf16[64,1024]{1,0:T(8,128)(2,1)S(1)}, bf16[64,1024]{1,0:T(8,128)(2,1)S(1)}, u32[]{:S(2)}, u32[]{:S(2)}) collective-permute-start(bf16[64,1024]{1,0:T(8,128)(2,1)S(1)} %get-tuple-element.80), channel_id=1, source_target_pairs={{0,8},{2,10},{4,12},{6,14},{8,16},{10,18},{12,20},{14,22},{16,24},... | collective-permute-start | bytes 393224 | tf_op jit(solution)/shard_map/ppermute | solution.py:513
  259.6 5.1 %collective-permute-start.27 = (bf16[64,1024]{1,0:T(8,128)(2,1)S(1)}, bf16[64,1024]{1,0:T(8,128)(2,1)S(1)}, u32[]{:S(2)}, u32[]{:S(2)}) collective-permute-start(bf16[64,1024]{1,0:T(8,128)(2,1)S(1)} %get-tuple-element.34), channel_id=1, source_target_pairs={{0,8},{2,10},{4,12},{6,14},{8,16},{10,18},{12,20},{14,22},{16,24},... | collective-permute-start | bytes 393224 | tf_op jit(solution)/shard_map/ppermute | solution.py:513
  261.8 10.8 %collective-permute-start.26 = (bf16[64,1024]{1,0:T(8,128)(2,1)S(1)}, bf16[64,1024]{1,0:T(8,128)(2,1)S(1)}, u32[]{:S(2)}, u32[]{:S(2)}) collective-permute-start(bf16[64,1024]{1,0:T(8,128)(2,1)S(1)} %get-tuple-element.34), channel_id=1, source_target_pairs={{0,16},{2,18},{4,20},{6,22},{8,24},{10,26},{12,28},{14,30},{16,0},... | collective-permute-start | bytes 393224 | tf_op jit(solution)/shard_map/ppermute | solution.py:513
  261.9 11.5 %collective-permute-start.25 = (bf16[64,1024]{1,0:T(8,128)(2,1)S(1)}, bf16[64,1024]{1,0:T(8,128)(2,1)S(1)}, u32[]{:S(2)}, u32[]{:S(2)}) collective-permute-start(bf16[64,1024]{1,0:T(8,128)(2,1)S(1)} %get-tuple-element.34), channel_id=1, source_target_pairs={{0,24},{2,26},{4,28},{6,30},{8,0},{10,2},{12,4},{14,6},{16,8},{18,... | collective-permute-start | bytes 393224 | tf_op jit(solution)/shard_map/ppermute | solution.py:513
  273.4 13.1 %collective-permute-start.33 = (bf16[4,64,1024]{2,1,0:T(8,128)(2,1)S(1)}, bf16[4,64,1024]{2,1,0:T(8,128)(2,1)S(1)}, u32[]{:S(2)}, u32[]{:S(2)}) collective-permute-start(bf16[4,64,1024]{2,1,0:T(8,128)(2,1)S(1)} %pad_maximum_fusion.refs_0_), channel_id=1, source_target_pairs={{0,6},{2,4},{4,2},{6,0},{8,14},{10,12},{12,10},{14,8},{16,22},{18,... | collective-permute-start | bytes 1572872 | tf_op jit(solution)/shard_map/ppermute | solution.py:510
  274.0 24.6 %collective-permute-start.31 = (bf16[4,64,1024]{2,1,0:T(8,128)(2,1)S(1)}, bf16[4,64,1024]{2,1,0:T(8,128)(2,1)S(1)}, u32[]{:S(2)}, u32[]{:S(2)}) collective-permute-start(bf16[4,64,1024]{2,1,0:T(8,128)(2,1)S(1)} %pad_maximum_fusion.refs_0_), channel_id=1, source_target_pairs={{0,4},{2,6},{4,0},{6,2},{8,12},{10,14},{12,8},{14,10},{16,20},{18,... | collective-permute-start | bytes 1572872 | tf_op jit(solution)/shard_map/ppermute | solution.py:510
  275.3 24.3 %collective-permute-start.29 = (bf16[4,64,1024]{2,1,0:T(8,128)(2,1)S(1)}, bf16[4,64,1024]{2,1,0:T(8,128)(2,1)S(1)}, u32[]{:S(2)}, u32[]{:S(2)}) collective-permute-start(bf16[4,64,1024]{2,1,0:T(8,128)(2,1)S(1)} %pad_maximum_fusion.refs_0_), channel_id=1, source_target_pairs={{0,2},{2,0},{4,6},{6,4},{8,10},{10,8},{12,14},{14,12},{16,18},{18,... | collective-permute-start | bytes 1572872 | tf_op jit(solution)/shard_map/ppermute | solution.py:510
  276.1 24.9 %collective-permute-start.28 = (bf16[4,64,1024]{2,1,0:T(8,128)(2,1)S(1)}, bf16[4,64,1024]{2,1,0:T(8,128)(2,1)S(1)}, u32[]{:S(2)}, u32[]{:S(2)}) collective-permute-start(bf16[4,64,1024]{2,1,0:T(8,128)(2,1)S(1)} %pad_maximum_fusion.refs_0_), channel_id=1, source_target_pairs={{0,1},{1,0},{2,3},{3,2},{4,5},{5,4},{6,7},{7,6},{8,9},{9,8},{10,11... | collective-permute-start | bytes 1572872 | tf_op jit(solution)/shard_map/ppermute | solution.py:516
  286.4 14.6 %collective-permute-start.34 = (bf16[4,64,1024]{2,1,0:T(8,128)(2,1)S(1)}, bf16[4,64,1024]{2,1,0:T(8,128)(2,1)S(1)}, u32[]{:S(2)}, u32[]{:S(2)}) collective-permute-start(bf16[4,64,1024]{2,1,0:T(8,128)(2,1)S(1)} %collective-permute-done.33.refs_6_), channel_id=1, source_target_pairs={{0,1},{1,0},{2,3},{3,2},{4,5},{5,4},{6,7},{7,6},{8,9},{9,8},{10,11... | collective-permute-start | bytes 1572872 | tf_op jit(solution)/shard_map/ppermute | solution.py:516
  (39 other events, 465.5 us)

commit v4 on v2

--- a/solution.py
+++ b/solution.py
@@ -27,11 +27,60 @@
     return lax.dot_general(a, b, (((ca,), (cb,)), ((), ())), preferred_element_type=jnp.float32)
 
 
-def compose_kernel(store_rows, stores, capacity, place_ref, adj_ref, table_ref, near_ref, ids_ref, request_ref, column_ref):
+def cut_kernel(first, rows, columns, by_core, place_ref, source_ref, *refs):
+    out_ref, done = refs[-2:]
+    start = pl.multiple_of(place_ref[2] * rows, 16) if by_core else first
+    copy = pltpu.make_async_copy(
+        source_ref.at[pl.ds(start, rows), columns[0] : columns[1]], out_ref, done
+    )
+    copy.start()
+    copy.wait()
+
+
+def cut(place, source, first, rows, columns, after, by_core=False):
+    anywhere = pl.BlockSpec(memory_space=pl.ANY)
+    return pl.pallas_call(
+        functools.partial(cut_kernel, first, rows, columns, by_core),
+        out_shape=jax.ShapeDtypeStruct((rows, columns[1] - columns[0]), source.dtype),
+        in_specs=[SMEM] + [anywhere] * (1 + len(after)),
+        out_specs=anywhere,
+        scratch_shapes=[pltpu.SemaphoreType.DMA],
+        name="cut_block",
+    )(place, source, *after)
+
+
+def pack_kernel(count, *refs):
+    out_ref, done = refs[-2:]
+    copies, start = [], 0
+    for i, ref in enumerate(refs[:count]):
+        rows = ref.shape[0]
+        copies.append(
+            pltpu.make_async_copy(ref, out_ref.at[start : start + rows, :], done.at[i])
+        )
+        start += rows
+    for copy in copies:
+        copy.start()
+    for copy in copies:
+        copy.wait()
+
+
+def pack(arrays, after):
+    anywhere = pl.BlockSpec(memory_space=pl.ANY)
+    rows = sum(array.shape[0] for array in arrays)
+    return pl.pallas_call(
+        functools.partial(pack_kernel, len(arrays)),
+        out_shape=jax.ShapeDtypeStruct((rows, arrays[0].shape[1]), arrays[0].dtype),
+        in_specs=[anywhere] * (len(arrays) + len(after)),
+        out_specs=anywhere,
+        scratch_shapes=[pltpu.SemaphoreType.DMA((len(arrays),))],
+        name="pack_blocks",
+    )(*arrays, *after)
+
+
+def compose_kernel(store_rows, groups, capacity, place_ref, adj_ref, table_ref, near_ref, ids_ref, column_ref):
     fan, near_rows = adj_ref.shape
     his = table_ref.shape[1]
-    groups = stores // PLANE
-    here, mine = place_ref[0], place_ref[1]
+    here = place_ref[0]
     table = table_ref[...]
     parts = jnp.concatenate([table // 65536, (table // 256) % 256, table % 256], axis=0)
     parts = parts.astype(jnp.float32).astype(jnp.bfloat16)
@@ -45,68 +94,42 @@
         value = jnp.where(row_lo == position % LANES, value, 0.0)
         ids_ref[column : column + 1, :] = jnp.sum(value, axis=0, keepdims=True).astype(jnp.int32)
     near = near_ref[...]
-    owner, slot = near // store_rows, near % store_rows
-    row_owner = lax.broadcasted_iota(jnp.int32, (stores, near_rows), 0)
-    marks = jnp.where(row_owner == owner, 1.0, 0.0)
+    per_plane = PLANE * store_rows
+    plane, row = near // per_plane, near % per_plane + 1
+    row_plane = lax.broadcasted_iota(jnp.int32, (groups, near_rows), 0)
+    marks = jnp.where(row_plane == plane, 1.0, 0.0)
     earlier = lax.broadcasted_iota(jnp.int32, (near_rows, near_rows), 0) < lax.broadcasted_iota(
         jnp.int32, (near_rows, near_rows), 1
     )
     counts = dot(marks.astype(jnp.bfloat16), jnp.where(earlier, 1.0, 0.0).astype(jnp.bfloat16))
     rank = jnp.sum(counts * marks, axis=0, keepdims=True).astype(jnp.int32)
-    wanted = lax.broadcasted_iota(jnp.int32, (stores * capacity, near_rows), 0)
-    marks = jnp.where(wanted == owner * capacity + rank, 1.0, 0.0).astype(jnp.bfloat16)
+    wanted = lax.broadcasted_iota(jnp.int32, (groups * capacity, near_rows), 0)
+    marks = jnp.where(wanted == plane * capacity + rank, 1.0, 0.0).astype(jnp.bfloat16)
     line = lax.broadcasted_iota(jnp.int32, (8, near_rows), 0)
-    halves = jnp.where(line == 0, slot // 256, jnp.where(line == 1, slot % 256, 0))
+    halves = jnp.where(line == 0, row // 256, jnp.where(line == 1, row % 256, 0))
     found = dot(halves.astype(jnp.float32).astype(jnp.bfloat16), marks, 1, 1)
-    request_ref[...] = (found[0:1] * 256.0 + found[1:2]).astype(jnp.int32)
-    hops = here - owner // PLANE
+    found = (found[0:1] * 256.0 + found[1:2]).astype(jnp.int32)
+    for line in range(groups * capacity // near_rows):
+        ids_ref[fan + line : fan + line + 1, :] = found[:, line * near_rows : (line + 1) * near_rows]
+    hops = here - plane
     hops = jnp.where(hops < 0, hops + groups, hops)
-    distance = lax.bitwise_xor(owner % PLANE, mine)
-    column_ref[...] = (distance * groups + hops) * capacity + rank
-
-
-def compose(place, adjacency, table, near, store_rows, stores, capacity):
+    column_ref[...] = hops * capacity + rank
+
+
+def compose(place, adjacency, table, near, store_rows, groups, capacity):
     near_rows, fan = adjacency.shape
+    rows = fan + groups * capacity // near_rows
     return pl.pallas_call(
-        functools.partial(compose_kernel, store_rows, stores, capacity),
+        functools.partial(compose_kernel, store_rows, groups, capacity),
         out_shape=(
-            jax.ShapeDtypeStruct((fan, near_rows), jnp.int32),
-            jax.ShapeDtypeStruct((1, stores * capacity), jnp.int32),
+            jax.ShapeDtypeStruct((rows, near_rows), jnp.int32),
             jax.ShapeDtypeStruct((1, near_rows), jnp.int32),
         ),
         in_specs=[SMEM, VMEM, VMEM, VMEM],
-        out_specs=(VMEM, VMEM, VMEM),
+        out_specs=(VMEM, VMEM),
         compiler_params=pltpu.CompilerParams(vmem_limit_bytes=32 * MIB),
         name="compose_ids",
     )(place, adjacency.T, table, near)
-
-
-def near_kernel(groups, place_ref, request_ref, features_ref, out_ref):
-    here, mine = place_ref[0], place_ref[1]
-    store_rows = features_ref.shape[0]
-    capacity = request_ref.shape[1]
-    slots = lax.broadcasted_iota(jnp.int32, (store_rows, PLANE * capacity), 0)
-    for k in range(groups):
-        plane = here + k
-        plane = jnp.where(plane >= groups, plane - groups, plane)
-        lines = []
-        for d in range(PLANE):
-            trainer = plane * PLANE + lax.bitwise_xor(mine, jnp.int32(d))
-            lines.append(request_ref[pl.ds(trainer, 1), :])
-        marks = jnp.where(slots == jnp.concatenate(lines, axis=1), 1.0, 0.0).astype(jnp.bfloat16)
-        out_ref[k] = dot(marks, features_ref[...], 0, 0).astype(jnp.bfloat16)
-
-
-def near_rows_held(place, requests, features, groups):
-    capacity = requests.shape[1]
-    return pl.pallas_call(
-        functools.partial(near_kernel, groups),
-        out_shape=jax.ShapeDtypeStruct((groups, PLANE * capacity, features.shape[1]), jnp.bfloat16),
-        in_specs=[SMEM, VMEM, VMEM],
-        out_specs=VMEM,
-        compiler_params=pltpu.CompilerParams(vmem_limit_bytes=32 * MIB),
-        name="near_rows",
-    )(place, requests, features)
 
 
 def sort_pairs(count):
@@ -125,56 +148,88 @@
     return pairs
 
 
-def list_kernel(store_rows, groups, first, block, place_ref, *refs):
-    ids_refs, out_ref = refs[:-1], refs[-1]
+def depths_of(fan):
+    return [d for d in (2, 3, 4, 5, 6, 8) if d < fan] + [fan]
+
+
+def list_kernel(store_rows, fan, capacity, block, place_ref, *refs):
+    groups = len(refs) // 2
+    ids_refs, out_refs = refs[:groups], refs[groups:]
     here, mine, rep = place_ref[0], place_ref[1], place_ref[2]
-    fan, near_rows = ids_refs[0].shape
+    near_rows = ids_refs[0].shape[1]
     per_plane = PLANE * store_rows
-    lanes = lax.broadcasted_iota(jnp.int32, (near_rows, near_rows), 0) // block
-    spots = lax.broadcasted_iota(jnp.int32, (near_rows, near_rows), 1)
-    blocks = jnp.where(lanes == spots, 1.0, 0.0).astype(jnp.bfloat16)
-    for k, ids_ref in enumerate(ids_refs):
-        gid = ids_ref[...]
-        owner, row = gid // store_rows, gid % store_rows
-        distance = lax.bitwise_xor(owner % PLANE, mine)
-        turned = row + rep * (store_rows // 2)
-        turned = jnp.where(turned >= store_rows, turned - store_rows, turned)
-        row = distance * store_rows + jnp.where(distance == 0, row, turned)
-        row = jnp.where(owner // PLANE == here, row, per_plane)
+    sub = lax.broadcasted_iota(jnp.int32, (near_rows, near_rows), 0)
+    lane = lax.broadcasted_iota(jnp.int32, (near_rows, near_rows), 1)
+    before = jnp.where(sub < lane, 1.0, 0.0).astype(jnp.bfloat16)
+    nodes = lax.broadcasted_iota(jnp.int32, (1, near_rows), 1)
+    classes = lax.broadcasted_iota(jnp.int32, (fan + 1, near_rows), 0)
+
+    def turn(row):
+        half = store_rows // 2
+        distance, slot = lax.bitwise_xor(row // store_rows, mine), row % store_rows
+        core, inner = slot // half, slot % half
+        other = jnp.where(core == rep, 0, (PLANE - 1) * half)
+        return jnp.where(distance == 0, slot, (distance + 1) * half + other + inner)
+
+    for ids_ref, out_ref in zip(ids_refs, out_refs):
+        gid = ids_ref[:fan, :]
+        held = gid // per_plane == here
+        row = jnp.where(held, turn(gid % per_plane), per_plane)
+        count = jnp.sum(jnp.where(held, 1, 0), axis=0, keepdims=True)
         rows = [row[j : j + 1] for j in range(fan)]
         for a, b in sort_pairs(fan):
             rows[a], rows[b] = jnp.minimum(rows[a], rows[b]), jnp.maximum(rows[a], rows[b])
-        for j in range(fan):
-            out_ref[k, j : j + 1, :] = rows[j] * 8
-        if first < fan:
-            more = jnp.where(rows[first] < per_plane, 1.0, 0.0).astype(jnp.bfloat16)
-            more = dot(jnp.broadcast_to(more, (8, near_rows)), blocks)
-            out_ref[k, fan : fan + 1, :] = more[0:1].astype(jnp.int32)
-        else:
-            out_ref[k, fan : fan + 1, :] = jnp.zeros((1, near_rows), jnp.int32)
-
-
-def row_lists(place, ids_all, store_rows, first, block):
-    fan, near_rows = ids_all[0].shape
+        marks = jnp.where(classes == count, 1.0, 0.0)
+        rank = dot(marks.astype(jnp.bfloat16), before)
+        sizes = jnp.sum(marks, axis=1, keepdims=True)
+        larger = jnp.zeros((1, 1), jnp.float32)
+        place = jnp.zeros((1, near_rows), jnp.float32)
+        ends = {}
+        for c in range(fan, -1, -1):
+            ends[c] = larger
+            place = place + marks[c : c + 1] * (rank[c : c + 1] + larger)
+            larger = larger + sizes[c : c + 1]
+        order = jnp.where(sub == place.astype(jnp.int32), 1.0, 0.0).astype(jnp.bfloat16)
+        lines = jnp.concatenate(rows + [nodes], axis=0)
+        parts = jnp.concatenate([lines // 256, lines % 256], axis=0)
+        found = dot(parts.astype(jnp.float32).astype(jnp.bfloat16), order, 1, 1)
+        found = (found[: fan + 1] * 256.0 + found[fan + 1 :]).astype(jnp.int32)
+        out_ref[: fan + 1, :] = found * 8
+        ahead = jnp.zeros((1, near_rows), jnp.int32)
+        for i, d in enumerate(depths_of(fan)[:-1]):
+            blocks = (ends[d].astype(jnp.int32) + (block - 1)) // block
+            ahead = ahead + jnp.where(nodes == i, blocks, 0)
+        out_ref[fan + 1 : fan + 2, :] = ahead
+        lists = jnp.concatenate(
+            [ids_ref[i : i + 1, :] for i in range(fan, ids_ref.shape[0])], axis=1
+        )
+        own = jnp.zeros((1, capacity), jnp.int32)
+        for g in range(groups):
+            own = own + jnp.where(here == g, lists[:, g * capacity : (g + 1) * capacity], 0)
+        own = jnp.where(own == 0, per_plane, turn(own - 1))
+        out_ref[fan + 2 : fan + 3, :capacity] = own * 8
+
+
+def row_lists(place, ids_all, store_rows, fan, capacity, block):
+    near_rows = ids_all[0].shape[1]
     groups = len(ids_all)
     return pl.pallas_call(
-        functools.partial(list_kernel, store_rows, groups, first, block),
-        out_shape=jax.ShapeDtypeStruct((groups, fan + 1, near_rows), jnp.int32),
+        functools.partial(list_kernel, store_rows, fan, capacity, block),
+        out_shape=(jax.ShapeDtypeStruct((fan + 3, near_rows), jnp.int32),) * groups,
         in_specs=[SMEM] + [VMEM] * groups,
-        out_specs=VMEM,
+        out_specs=(VMEM,) * groups,
         compiler_params=pltpu.CompilerParams(vmem_limit_bytes=32 * MIB),
         name="row_lists",
     )(place, *ids_all)
 
 
-def partial_kernel(places, turns, first, block, *refs):
-    index_ref = refs[0]
-    piece_refs = refs[1 : 1 + len(places)]
-    out_ref, table, sums = refs[1 + len(places) : 4 + len(places)]
-    buffers = refs[4 + len(places) : -1]
+def partial_kernel(count, columns, places, capacity, block, *refs):
+    index_refs, piece_refs = refs[:count], refs[count : count + len(places)]
+    out_ref, table, sums, kept = refs[-5 - len(places) : -1 - len(places)]
+    buffers = refs[-1 - len(places) : -1]
     arrived = refs[-1]
-    fan, near_rows = index_ref.shape[1] - 1, index_ref.shape[2]
-    units = piece_refs[0].shape[1] // LANES
+    fan, near_rows = index_refs[0].shape[0] - 3, index_refs[0].shape[1]
+    units = buffers[0].shape[1] // LANES
     total = table.shape[0] // 8 - 1
     chunk = 256
 
@@ -187,9 +242,10 @@
             rows = [a + b for a, b in zip(rows[0::2], rows[1::2])] + odd
         return rows[0]
 
+    sources = [piece_refs[0].at[:, columns[0] : columns[1]]] + list(piece_refs[1:])
     copies = [
-        pltpu.make_async_copy(piece, buffer, arrived.at[i])
-        for i, (piece, buffer) in enumerate(zip(piece_refs, buffers))
+        pltpu.make_async_copy(source, buffer, arrived.at[i])
+        for i, (source, buffer) in enumerate(zip(sources, buffers))
     ]
     for copy in copies:
         copy.start()
@@ -208,83 +264,92 @@
 
         lax.fori_loop(0, buffer.shape[0] // chunk, fill, 0)
 
-    unroll = 16
-    for at, turn in enumerate(turns):
-
-        def step(i, carry):
-            for u in range(unroll):
-                n = i * unroll + u
-                sums[pl.ds(pl.multiple_of(n * 8, 8), 8), :] = tree(
-                    [row(index_ref[turn, j, n]) for j in range(first)]
-                )
-            return carry
-
-        lax.fori_loop(0, near_rows // unroll, step, 0)
-
-        def rest(i, carry):
-            @pl.when(index_ref[turn, fan, i] > 0)
-            def _():
+    near_unroll = 16
+    for turn, index_ref in enumerate(index_refs):
+        begin = 0
+        depths = depths_of(fan)
+        for at in range(len(depths) - 1, -1, -1):
+            depth = depths[at]
+
+            def step(i, carry):
                 for u in range(block):
                     n = i * block + u
-                    spot = pl.ds(pl.multiple_of(n * 8, 8), 8)
-                    sums[spot, :] = sums[spot, :] + tree(
-                        [row(index_ref[turn, j, n]) for j in range(first, fan)]
-                    )
-
+                    spot = pl.multiple_of(index_ref[fan, n], 8)
+                    sums[pl.ds(spot, 8), :] = tree([row(index_ref[j, n]) for j in range(depth)])
+                return carry
+
+            end = index_ref[fan + 1, at - 1] if at else near_rows // block
+            lax.fori_loop(begin, end, step, 0)
+            begin = end
+
+        def near(i, carry):
+            for u in range(near_unroll):
+                n = i * near_unroll + u
+                kept[pl.ds(pl.multiple_of(n * 8, 8), 8), :] = row(index_ref[fan + 2, n])
             return carry
 
-        if first < fan:
-            lax.fori_loop(0, near_rows // block, rest, 0)
+        lax.fori_loop(0, capacity // near_unroll, near, 0)
         for unit in range(units):
             lanes = slice(unit * LANES, (unit + 1) * LANES)
-            out_ref[at, :, lanes] = sums[pl.ds(unit, near_rows, stride=8), :].astype(jnp.bfloat16)
-
-
-def partial_sums(index, pieces, places, turns, total, first, block):
-    near_rows = index.shape[2]
-    width = pieces[0].shape[1]
+            out_ref[turn, :near_rows, lanes] = sums[
+                pl.ds(unit, near_rows, stride=8), :
+            ].astype(jnp.bfloat16)
+            out_ref[turn, near_rows:, lanes] = kept[
+                pl.ds(unit, capacity, stride=8), :
+            ].astype(jnp.bfloat16)
+
+
+def partial_sums(lists, pieces, places, columns, total, capacity, block, after):
+    near_rows = lists[0].shape[1]
+    width = columns[1] - columns[0]
+    rows = [piece.shape[0] for piece in pieces]
     return pl.pallas_call(
-        functools.partial(partial_kernel, places, turns, first, block),
-        out_shape=jax.ShapeDtypeStruct((len(turns), near_rows, width), jnp.bfloat16),
-        in_specs=[SMEM] + [pl.BlockSpec(memory_space=pl.ANY)] * len(pieces),
+        functools.partial(partial_kernel, len(lists), columns, places, capacity, block),
+        out_shape=jax.ShapeDtypeStruct((len(lists), near_rows + capacity, width), jnp.bfloat16),
+        in_specs=[SMEM] * len(lists) + [pl.BlockSpec(memory_space=pl.ANY)] * (len(pieces) + len(after)),
         out_specs=VMEM,
         scratch_shapes=[
             pltpu.VMEM(((total + 1) * 8, LANES), jnp.float32),
             pltpu.VMEM(((near_rows + 1) * 8, LANES), jnp.float32),
+            pltpu.VMEM(((capacity + 1) * 8, LANES), jnp.float32),
         ]
-        + [pltpu.VMEM(piece.shape, piece.dtype) for piece in pieces]
+        + [pltpu.VMEM((count, width), jnp.bfloat16) for count in rows]
         + [pltpu.SemaphoreType.DMA((len(pieces),))],
-        compiler_params=pltpu.CompilerParams(vmem_limit_bytes=60 * MIB),
+        compiler_params=pltpu.CompilerParams(vmem_limit_bytes=52 * MIB),
         name="partial_sums",
-    )(index, *pieces)
+    )(*lists, *pieces, *after)
 
 
 def trainer_kernel(sizes, scale, *refs):
     groups, rows_low, rows_top, classes, class_pad = sizes
     place_ref, labels_ref, adj_ref, column_ref, wl_ref, wt_ref = refs[:6]
-    block_refs = refs[6 : 6 + groups]
-    near_refs = refs[6 + groups : 6 + groups + PLANE]
-    logits_ref, keep_ref, send_ref, li, hidden, slope, top_in, wt = refs[6 + groups + PLANE :]
+    block_refs = refs[6:-8]
+    logits_ref, keep_ref, send_ref, li, hidden, slope, top_in, wt = refs[-8:]
     seeds, fan_top = adj_ref.shape
     near_rows, low_width = li.shape
     feat = low_width // 2
     width = hidden.shape[1]
-    capacity = near_refs[0].shape[0]
+    capacity = block_refs[0].shape[0] - near_rows
     here, mine, rep = place_ref[0], place_ref[1], place_ref[2]
     fan_low = place_ref[3].astype(jnp.float32)
 
     column = column_ref[...]
     rows_cap = lax.broadcasted_iota(jnp.int32, (capacity, near_rows), 0)
-    near = None
-    for d in range(PLANE):
-        marks = jnp.where(rows_cap + d * capacity == column, 1.0, 0.0).astype(jnp.bfloat16)
-        term = dot(marks, near_refs[d][...], 0, 0)
-        near = term if near is None else near + term
-    total = block_refs[0][...].astype(jnp.float32)
-    for k in range(1, groups):
-        total = total + block_refs[k][...].astype(jnp.float32)
-    li[:, :feat] = near.astype(jnp.bfloat16)
-    li[:, feat:] = (total / fan_low).astype(jnp.bfloat16)
+    marks = [
+        jnp.where(rows_cap + k * capacity == column, 1.0, 0.0).astype(jnp.bfloat16)
+        for k in range(groups)
+    ]
+    for part in range(len(block_refs) // groups):
+        blocks = block_refs[part * groups : (part + 1) * groups]
+        share = blocks[0].shape[1]
+        near = total = None
+        for k in range(groups):
+            term = dot(marks[k], blocks[k][near_rows:, :], 0, 0)
+            near = term if near is None else near + term
+            term = blocks[k][:near_rows, :].astype(jnp.float32)
+            total = term if total is None else total + term
+        li[:, part * share : (part + 1) * share] = near.astype(jnp.bfloat16)
+        li[:, feat + part * share : feat + (part + 1) * share] = (total / fan_low).astype(jnp.bfloat16)
 
     wt[...] = jnp.zeros_like(wt)
     wt[:, :classes] = wt_ref[...].astype(jnp.bfloat16)
@@ -357,7 +422,7 @@
         send_ref[a, b, rows_low:, :] = other.astype(jnp.bfloat16)
 
 
-def trainer_step(place, labels, adj_top, column, wl, wt, blocks, nears, sizes, scale):
+def trainer_step(place, labels, adj_top, column, wl, wt, blocks, sizes, scale):
     groups, rows_low, rows_top, classes, class_pad = sizes
     seeds = adj_top.shape[0]
     low_width, width = wl.shape
@@ -370,7 +435,7 @@
             jax.ShapeDtypeStruct((PLANE, groups, rows, width), jnp.float32),
             jax.ShapeDtypeStruct((PLANE, groups, rows, width), jnp.bfloat16),
         ),
-        in_specs=[SMEM] + [VMEM] * (5 + groups + PLANE),
+        in_specs=[SMEM] + [VMEM] * (5 + len(blocks)),
         out_specs=(VMEM, VMEM, VMEM),
         scratch_shapes=[
             pltpu.VMEM((near_rows, low_width), jnp.bfloat16),
@@ -381,7 +446,7 @@
         ],
         compiler_params=pltpu.CompilerParams(vmem_limit_bytes=60 * MIB),
         name="trainer_step",
-    )(place, labels, adj_top, column, wl, wt, *blocks, *nears)
+    )(place, labels, adj_top, column, wl, wt, *blocks)
 
 
 def adam_part(gradient, moment, square):
@@ -502,7 +567,7 @@
     store_rows = features.shape[0]
     half = store_rows // 2
     near_rows, fan = adjacency_low.shape
-    capacity = 2 * near_rows // stores
+    capacity = min(near_rows, PLANE * (2 * near_rows // stores))
     classes = weights_top.shape[1]
     class_pad = -(-classes // LANES) * LANES
     rows_low, rows_top = first_low.shape[0], first_top.shape[0]
@@ -519,43 +584,50 @@
     def sibling(x):
         return lax.ppermute(x, "rep", [(0, 1), (1, 0)])
 
-    quarter = half // 2
-    own_a = lax.dynamic_slice_in_dim(features, rep * half, quarter, 0)
-    own_b = lax.dynamic_slice_in_dim(features, rep * half + quarter, quarter, 0)
-    x_a, y_b = across(own_a, 1), across(own_b, 2)
-    x_b, y_a = across(own_b, 1), across(own_a, 2)
     gid_near = owners_near[:, 0] * store_rows + slots_near[:, 0]
     gid_far = owners_far[:, 0] * store_rows + slots_far[:, 0]
     table = jnp.concatenate([gid_near, gid_far]).reshape(-1, LANES)
     table = jnp.pad(table, ((0, -table.shape[0] % 16), (0, 0))).T
-    ids, requests, column = compose(
-        place, adjacency_low, table, gid_near.reshape(1, near_rows), store_rows, stores, capacity
+    ids, column = compose(
+        place, adjacency_low, table, gid_near.reshape(1, near_rows), store_rows, groups, capacity
     )
     ids_all = [ids] + [along(ids, -k) for k in range(1, groups)]
-    requests = lax.all_to_all(requests.reshape(stores, capacity), "store", 0, 0, tiled=True)
-    held = near_rows_held(place, requests, features, groups)
-    first, block = min(8, fan), 8
-    lists = row_lists(place, ids_all, store_rows, first, block)
-    lined = [held[0]] + [along(held[k], k) for k in range(1, groups)]
-    corner_a, corner_b = across(x_a, 2), across(y_b, 1)
-    pieces, places = [features], [0]
-    for turn, (one, two) in enumerate([(x_a, x_b), (y_a, y_b), (corner_a, corner_b)]):
-        pieces += [one, two, sibling(one), sibling(two)]
-        places += [(turn + 1) * store_rows + quarter * i for i in range(4)]
-
-    per_call = -(-groups // 4)
-    order = [groups // 2] + [k for k in range(1, groups) if k != groups // 2] + [0]
-    blocks = {}
-    for start in range(0, groups, per_call):
-        turns = order[start : start + per_call]
-        made = partial_sums(lists, pieces, places, turns, PLANE * store_rows, first, block)
-        for i, k in enumerate(turns):
-            blocks[k] = along(made[i], k) if k else made[i]
-
-    nears = []
-    for d in range(PLANE):
-        sheet = jnp.concatenate([part[d * capacity : (d + 1) * capacity] for part in lined])
-        nears.append(across(sheet, d) if d else sheet)
+    block = 16
+    lists = row_lists(place, ids_all, store_rows, fan, capacity, block)
+
+    share = features.shape[1] // 2
+    quarter = half // 2
+    places = [0, store_rows, store_rows + 3 * half]
+    far = groups // 2
+    calls = [[far], [k for k in range(1, groups) if k != far], [0]]
+    blocks, pieces, waits = {}, (), ()
+    first, second = (lists[0],), ()
+    for part in range(2):
+        columns, whole = (part * share, (part + 1) * share), (0, share)
+        own = cut(place, features, 0, half, columns, pieces[1:], True)
+        from_x, from_y = across(own, 1), across(own, 2)
+        corner_a = across(cut(place, from_x, 0, quarter, whole, first), 2)
+        corner_b = across(cut(place, from_y, quarter, quarter, whole, first), 1)
+        brought = pack([from_x, from_y, corner_a, corner_b], second)
+        pieces = (features, brought, sibling(brought))
+        for turns in calls:
+            made = partial_sums(
+                [lists[k] for k in turns],
+                pieces,
+                places,
+                columns,
+                PLANE * store_rows,
+                capacity,
+                block,
+                waits,
+            )
+            waits = (made,)
+            for i, k in enumerate(turns):
+                blocks[part, k] = along(made[i], k) if k else made[i]
+            if turns == calls[0]:
+                first, second = (made,), (blocks[part, far],)
+            if turns == calls[1]:
+                second += (made,)
 
     scale = 1.0 / (labels.shape[0] * members)
     logits, keep, send = trainer_step(
@@ -565,8 +637,7 @@
         column,
         weights_low,
         weights_top,
-        [blocks[k] for k in range(groups)],
-        nears,
+        [blocks[part, k] for part in range(2) for k in range(groups)],
         sizes,
         scale,
     )

time: 304 us -> 538 us (1.77)
  Pallas kernels: 109 us -> 353 us
  starting transfers between devices: 69 us -> 53.8 us
  waiting for transfers between devices: 98.8 us -> 105 us
    pallas_call x7 -> x16, Pallas kernels: 84.8 us -> 328 us  [the longest x2 145 us: pack(): pl.pallas_call(functools.partial(pack_kernel, len(arrays)), out_shape=jax...]
    ppermute x11 -> x7, starting transfers between devices: 28.9 us -> 11 us  [sibling(): return lax.ppermute(x, 'rep', [(0, 1), (1, 0)])]
    ppermute x15 -> x14, waiting for transfers between devices: 42.6 us -> 53.7 us  [across(): return lax.ppermute(x, 'store', [(i, i ^ distance) for i in range(stores)])]
    ppermute x15, starting transfers between devices: 19.2 us -> 28.7 us  [along(): lax.ppermute(x, 'store', [(i, (i + hops * PLANE) % stores) for i in range...]
    unnamed x86 -> x80, local copies, waits for them, and re-layouts: 9.6 us -> 18 us
    ppermute x15, waiting for transfers between devices: 47.2 us -> 41.2 us  [along(): lax.ppermute(x, 'store', [(i, (i + hops * PLANE) % stores) for i in range...]
    ppermute x15 -> x14, starting transfers between devices: 16.1 us -> 14.1 us  [across(): return lax.ppermute(x, 'store', [(i, i ^ distance) for i in range(stores)])]
  transfers between devices with their start and end apart: 42 -> 36, of which waited for: 19 -> 22; matrix products, arithmetic and copies ran while one was open for 4% -> 1% of each run, Pallas kernels for 28% -> 24%
where the time goes in v4:
time: 538 us; the launch traced here: 539 us
  Pallas kernels  353 us (66%)
  waiting for transfers between devices  105 us (20%)
  starting transfers between devices  53.8 us (10%)
  local copies, waits for them, and re-layouts  21.3 us (4%)
    pallas_call x2, Pallas kernels, pack(): pl.pallas_call(functools.partial(pack_kernel, len(arrays)), out_shape=jax...  145 us
    pallas_call x6, Pallas kernels, cut(): pl.pallas_call(functools.partial(cut_kernel, first, rows, columns, by_cor...  106 us
    pallas_call x6, Pallas kernels, partial_sums(): pl.pallas_call(functools.partial(partial_kernel, len(lists), columns, pla...  70.9 us
    ppermute x14, waiting for transfers between devices, across(): return lax.ppermute(x, 'store', [(i, i ^ distance) for i in range(stores)])  53.7 us
    ppermute x15, waiting for transfers between devices, along(): lax.ppermute(x, 'store', [(i, (i + hops * PLANE) % stores) for i in range...  41.2 us
    ppermute x15, starting transfers between devices, along(): lax.ppermute(x, 'store', [(i, (i + hops * PLANE) % stores) for i in range...  28.7 us
    unnamed x80, local copies, waits for them, and re-layouts  18 us
    pallas_call x1, Pallas kernels, trainer_step(): pl.pallas_call(functools.partial(trainer_kernel, sizes, scale), out_shape...  15.6 us
  transfers between devices with their start and end apart: 36, of which 22 were waited for; matrix products, arithmetic and copies ran while one was open for 1% of the time, Pallas kernels for 24%

profile of v4, /device:TPU:9, one launch (start us, length us, event | category | flops | bytes accessed | tf_op | source)
XLA Modules:
  0.0 538.6 jit_solution(8836358284626496130)
XLA Ops:
  1.4 25.7 %cut_block.6 = bf16[1024,384]{1,0:T(8,128)(2,1)} custom-call(s32[4]{0:T(128)} %pad_add_fusion.place_ref.refs_0_, bf16[2048,768]{1,0:T(8,128)(2,1)} %refs_1_.7), custom_call_target="tpu_custom_call" | custom-call | tf_op jit(solution)/shard_map/cut_block/pallas_call | solution.py:42
  46.7 13.7 %cut_block.8 = bf16[512,384]{1,0:T(8,128)(2,1)} custom-call(s32[4]{0:T(128)} %pad_add_fusion.place_ref.refs_0_, bf16[1024,384]{1,0:T(8,128)(2,1)} %copy-done.15, s32[18,512]{1,0:T(8,128)} %copy-done.4), custom_call_target="tpu_custom_call" | custom-call | tf_op jit(solution)/shard_map/cut_block/pallas_call | solution.py:42
  62.5 13.7 %cut_block.7 = bf16[512,384]{1,0:T(8,128)(2,1)} custom-call(s32[4]{0:T(128)} %pad_add_fusion.place_ref.refs_0_, bf16[1024,384]{1,0:T(8,128)(2,1)} %copy-done.16, s32[18,512]{1,0:T(8,128)} %copy-done.4), custom_call_target="tpu_custom_call" | custom-call | tf_op jit(solution)/shard_map/cut_block/pallas_call | solution.py:42
  77.5 7.7 %collective-permute-done.5.refs_2_ = bf16[512,384]{1,0:T(8,128)(2,1)S(1)} collective-permute-done((bf16[512,384]{1,0:T(8,128)(2,1)}, bf16[512,384]{1,0:T(8,128)(2,1)S(1)}, u32[]{:S(2)}, u32[]{:S(2)}) %collective-permute-start.5) | collective-permute-done | bytes 393248 | tf_op jit(solution)/shard_map/ppermute | solution.py:579
  86.0 72.6 %pack_blocks.2.refs_2_.refs_3_.refs_0_ = bf16[3072,384]{1,0:T(8,128)(2,1)} custom-call(bf16[1024,384]{1,0:T(8,128)(2,1)} %copy-done.16, bf16[1024,384]{1,0:T(8,128)(2,1)} %copy-done.15, bf16[512,384]{1,0:T(8,128)(2,1)} %copy-done.30, bf16[512,384]{1,0:T(8,128)(2,1)} %copy-done.28), custom_call_target="tpu_custom_call" | custom-call | tf_op jit(solution)/shard_map/pack_blocks/pallas_call | solution.py:70
  161.5 4.4 collective-permute-done.7.refs_3_.refs_4_.refs_1_
  167.2 25.6 %cut_block.9 = bf16[1024,384]{1,0:T(8,128)(2,1)} custom-call(s32[4]{0:T(128)} %pad_add_fusion.place_ref.refs_0_, bf16[2048,768]{1,0:T(8,128)(2,1)} %refs_1_.7, bf16[3072,384]{1,0:T(8,128)(2,1)} %pack_blocks.2.refs_2_.refs_3_.refs_0_, bf16[3072,384]{1,0:T(8,128)(2,1)} %copy-done.13), custom_call_target="tpu_custom_call" | custom-call | tf_op jit(solution)/shard_map/cut_block/pallas_call | solution.py:42
  194.4 10.6 %partial_sums.6.refs_5_.refs_0_ = bf16[1,768,384]{2,1,0:T(8,128)(2,1)} custom-call(s32[18,512]{1,0:T(8,128)S(1)} %get-tuple-element.28.refs_0_, bf16[2048,768]{1,0:T(8,128)(2,1)} %refs_1_.7, bf16[3072,384]{1,0:T(8,128)(2,1)} %pack_blocks.2.refs_2_.refs_3_.refs_0_, bf16[3072,384]{1,0:T(8,128)(2,1)} %copy-done.13), custom_call_target="tpu_custom_call" | custom-call | tf_op jit(solution)/shard_map/partial_sums/pallas_call | solution.py:306
  205.0 3.7 collective-permute-start.9
  208.7 3.2 collective-permute-done.12.source_ref.refs_1_
  212.7 13.7 %cut_block.11 = bf16[512,384]{1,0:T(8,128)(2,1)} custom-call(s32[4]{0:T(128)} %pad_add_fusion.place_ref.refs_0_, bf16[1024,384]{1,0:T(8,128)(2,1)} %copy-done.17, bf16[1,768,384]{2,1,0:T(8,128)(2,1)} %partial_sums.6.refs_5_.refs_0_), custom_call_target="tpu_custom_call" | custom-call | tf_op jit(solution)/shard_map/cut_block/pallas_call | solution.py:42
  227.7 13.7 %cut_block.10 = bf16[512,384]{1,0:T(8,128)(2,1)} custom-call(s32[4]{0:T(128)} %pad_add_fusion.place_ref.refs_0_, bf16[1024,384]{1,0:T(8,128)(2,1)} %copy-done.18, bf16[1,768,384]{2,1,0:T(8,128)(2,1)} %partial_sums.6.refs_5_.refs_0_), custom_call_target="tpu_custom_call" | custom-call | tf_op jit(solution)/shard_map/cut_block/pallas_call | solution.py:42
  242.7 15.0 %partial_sums.7.refs_4_.refs_5_ = bf16[2,768,384]{2,1,0:T(8,128)(2,1)S(1)} custom-call(s32[18,512]{1,0:T(8,128)S(1)} %get-tuple-element.26.refs_0_, s32[18,512]{1,0:T(8,128)S(1)} %get-tuple-element.27.refs_1_, bf16[2048,768]{1,0:T(8,128)(2,1)} %refs_1_.7, bf16[3072,384]{1,0:T(8,128)(2,1)} %pack_blocks.2.refs_2_.refs_3_.refs_0_, ...), custom_call_target="tpu_custom_call" | custom-call | tf_op jit(solution)/shard_map/partial_sums/pallas_call | solution.py:306
  260.5 72.6 %pack_blocks.3.refs_2_.refs_3_ = bf16[3072,384]{1,0:T(8,128)(2,1)} custom-call(bf16[1024,384]{1,0:T(8,128)(2,1)} %copy-done.18, bf16[1024,384]{1,0:T(8,128)(2,1)} %copy-done.17, bf16[512,384]{1,0:T(8,128)(2,1)} %copy-done.29, bf16[512,384]{1,0:T(8,128)(2,1)} %copy-done.27, bf16[768,384]{1,0:T(8,128)(2,1)} %copy-done.19, bf16[2,768,384]{2,1,0:T(8,128)(2,1)} %copy-done), custom_call_target="tpu_custom_call" | custom-call | tf_op jit(solution)/shard_map/pack_blocks/pallas_call | solution.py:70
  338.2 10.3 %partial_sums.8.refs_4_ = bf16[1,768,384]{2,1,0:T(8,128)(2,1)S(1)} custom-call(s32[18,512]{1,0:T(8,128)S(1)} %copy-done.5, bf16[2048,768]{1,0:T(8,128)(2,1)} %refs_1_.7, bf16[3072,384]{1,0:T(8,128)(2,1)} %pack_blocks.2.refs_2_.refs_3_.refs_0_, bf16[3072,384]{1,0:T(8,128)(2,1)} %copy-done.13, bf16[2,768,384]{2,1,0:T(8,128)(2,1)S(1)} %copy-done.1), custom_call_target="tpu_custom_call" | custom-call | tf_op jit(solution)/shard_map/partial_sums/pallas_call | solution.py:306
  349.9 9.8 %partial_sums.9.refs_5_ = bf16[1,768,384]{2,1,0:T(8,128)(2,1)S(1)} custom-call(s32[18,512]{1,0:T(8,128)S(1)} %get-tuple-element.28.refs_0_, bf16[2048,768]{1,0:T(8,128)(2,1)} %refs_1_.7, bf16[3072,384]{1,0:T(8,128)(2,1)} %pack_blocks.3.refs_2_.refs_3_, bf16[3072,384]{1,0:T(8,128)(2,1)} %copy-done.14, bf16[1,768,384]{2,1,0:T(8,128)(2,1)S(1)} %partial_sums.8.refs_4_), custom_call_target="tpu_custom_call" | custom-call | tf_op jit(solution)/shard_map/partial_sums/pallas_call | solution.py:306
  359.7 8.6 %collective-permute-start.17 = (bf16[768,384]{1,0:T(8,128)(2,1)S(1)}, bf16[768,384]{1,0:T(8,128)(2,1)}, u32[]{:S(2)}, u32[]{:S(2)}) collective-permute-start(bf16[768,384]{1,0:T(8,128)(2,1)S(1)} %bitcast.49), channel_id=1, source_target_pairs={{0,16},{2,18},{4,20},{6,22},{8,24},{10,26},{12,28},{14,30},{16,0},... | collective-permute-start | bytes 1769480 | tf_op jit(solution)/shard_map/ppermute | solution.py:582
  368.3 15.0 %partial_sums.10.refs_4_ = bf16[2,768,384]{2,1,0:T(8,128)(2,1)S(1)} custom-call(s32[18,512]{1,0:T(8,128)S(1)} %get-tuple-element.26.refs_0_, s32[18,512]{1,0:T(8,128)S(1)} %get-tuple-element.27.refs_1_, bf16[2048,768]{1,0:T(8,128)(2,1)} %refs_1_.7, bf16[3072,384]{1,0:T(8,128)(2,1)} %pack_blocks.3.refs_2_.refs_3_, bf16[3072,384]{1,0:T(8,128)(2,1)} %copy-done.14, ...), custom_call_target="tpu_custom_call" | custom-call | tf_op jit(solution)/shard_map/partial_sums/pallas_call | solution.py:306
  389.2 10.3 %partial_sums.11 = bf16[1,768,384]{2,1,0:T(8,128)(2,1)S(1)} custom-call(s32[18,512]{1,0:T(8,128)S(1)} %copy-done.5, bf16[2048,768]{1,0:T(8,128)(2,1)} %refs_1_.7, bf16[3072,384]{1,0:T(8,128)(2,1)} %pack_blocks.3.refs_2_.refs_3_, bf16[3072,384]{1,0:T(8,128)(2,1)} %copy-done.14, bf16[2,768,384]{2,1,0:T(8,128)(2,1)S(1)} %partial_sums.10.refs_4_), custom_call_target="tpu_custom_call" | custom-call | tf_op jit(solution)/shard_map/partial_sums/pallas_call | solution.py:306
  400.4 5.3 collective-permute-done.17.refs_12_
  405.6 12.6 %collective-permute-done.18.refs_13_ = bf16[768,384]{1,0:T(8,128)(2,1)} collective-permute-done((bf16[768,384]{1,0:T(8,128)(2,1)}, bf16[768,384]{1,0:T(8,128)(2,1)}, u32[]{:S(2)}, u32[]{:S(2)}) %collective-permute-start.18) | collective-permute-done | bytes 589856 | tf_op jit(solution)/shard_map/ppermute | solution.py:582
  418.4 15.6 %trainer_step.1 = (f32[128,153]{1,0:T(8,128)}, f32[4,4,64,1024]{3,2,1,0:T(8,128)}, bf16[4,4,64,1024]{3,2,1,0:T(8,128)(2,1)}) custom-call(s32[4]{0:T(128)} %pad_add_fusion.place_ref.refs_0_, s32[128,1]{1,0:T(8,128)} %copy.28.refs_1_, s32[128,10]{1,0:T(8,128)} %copy.29.refs_2_, s32[1,512]{1,0:T(1,128)} %copy-done.12, f32[1536,1024]{1,0:T(8,128)} %wl.1, ...), custom_call_target="tpu_custom_call" | custom-call | tf_op jit(solution)/shard_map/trainer_step/pallas_call | solution.py:431
  434.5 4.0 collective-permute-done.19
  444.8 10.7 %collective-permute-done.20 = bf16[4,64,1024]{2,1,0:T(8,128)(2,1)S(1)} collective-permute-done((bf16[4,64,1024]{2,1,0:T(8,128)(2,1)S(1)}, bf16[4,64,1024]{2,1,0:T(8,128)(2,1)S(1)}, u32[]{:S(2)}, u32[]{:S(2)}) %collective-permute-start.20) | collective-permute-done | bytes 524320 | tf_op jit(solution)/shard_map/ppermute | solution.py:579
  455.5 11.3 %collective-permute-done.22 = bf16[4,64,1024]{2,1,0:T(8,128)(2,1)S(1)} collective-permute-done((bf16[4,64,1024]{2,1,0:T(8,128)(2,1)S(1)}, bf16[4,64,1024]{2,1,0:T(8,128)(2,1)S(1)}, u32[]{:S(2)}, u32[]{:S(2)}) %collective-permute-start.22) | collective-permute-done | bytes 524320 | tf_op jit(solution)/shard_map/ppermute | solution.py:579
  473.6 5.2 collective-permute-done.24.refs_2_
  478.7 3.8 collective-permute-done.23.refs_1_
  487.9 8.2 %collective-permute-done.27 = bf16[64,1024]{1,0:T(8,128)(2,1)S(1)} collective-permute-done((bf16[64,1024]{1,0:T(8,128)(2,1)S(1)}, bf16[64,1024]{1,0:T(8,128)(2,1)S(1)}, u32[]{:S(2)}, u32[]{:S(2)}) %collective-permute-start.27) | collective-permute-done | bytes 131104 | tf_op jit(solution)/shard_map/ppermute | solution.py:582
  502.6 8.7 %collective-permute-done.34.refs_6_ = bf16[4,64,1024]{2,1,0:T(8,128)(2,1)S(1)} collective-permute-done((bf16[4,64,1024]{2,1,0:T(8,128)(2,1)S(1)}, bf16[4,64,1024]{2,1,0:T(8,128)(2,1)S(1)}, u32[]{:S(2)}, u32[]{:S(2)}) %collective-permute-start.34) | collective-permute-done | bytes 524320 | tf_op jit(solution)/shard_map/ppermute | solution.py:579
  511.3 3.6 collective-permute-start.35
  514.9 9.1 %collective-permute-done.32.refs_4_ = bf16[4,64,1024]{2,1,0:T(8,128)(2,1)S(1)} collective-permute-done((bf16[4,64,1024]{2,1,0:T(8,128)(2,1)S(1)}, bf16[4,64,1024]{2,1,0:T(8,128)(2,1)S(1)}, u32[]{:S(2)}, u32[]{:S(2)}) %collective-permute-start.32) | collective-permute-done | bytes 524320 | tf_op jit(solution)/shard_map/ppermute | solution.py:579
  526.9 8.9 %apply_updates.1 = (f32[1536,1024]{1,0:T(8,128)}, f32[2048,153]{1,0:T(8,128)}) custom-call(s32[4]{0:T(128)} %pad_add_fusion.place_ref.refs_0_, f32[1536,1024]{1,0:T(8,128)} %wl.1, f32[2048,153]{1,0:T(8,128)} %copy.30.refs_5_.wt, bf16[4,64,1024]{2,1,0:T(8,128)(2,1)} %copy-done.20, bf16[4,64,1024]{2,1,0:T(8,128)(2,1)} %copy-done.25, ...), custom_call_target="tpu_custom_call" | custom-call | tf_op jit(solution)/shard_map/apply_updates/pallas_call | solution.py:532
  (154 shorter events, 80.8 us)
Async XLA Ops:
  27.1 18.7 %collective-permute-start.4 = (bf16[1024,384]{1,0:T(8,128)(2,1)}, bf16[1024,384]{1,0:T(8,128)(2,1)S(1)}, u32[]{:S(2)}, u32[]{:S(2)}) collective-permute-start(bf16[1024,384]{1,0:T(8,128)(2,1)} %cut_block.6), channel_id=1, source_target_pairs={{0,4},{2,6},{4,0},{6,2},{8,12},{10,14},{12,8},{14,10},{16,20},{18,... | collective-permute-start | bytes 2359304 | tf_op jit(solution)/shard_map/ppermute | solution.py:579
  28.4 33.3 %collective-permute-start.3 = (bf16[1024,384]{1,0:T(8,128)(2,1)}, bf16[1024,384]{1,0:T(8,128)(2,1)S(1)}, u32[]{:S(2)}, u32[]{:S(2)}) collective-permute-start(bf16[1024,384]{1,0:T(8,128)(2,1)} %cut_block.6), channel_id=1, source_target_pairs={{0,2},{2,0},{4,6},{6,4},{8,10},{10,8},{12,14},{14,12},{16,18},{18,... | collective-permute-start | bytes 2359304 | tf_op jit(solution)/shard_map/ppermute | solution.py:579
  35.5 4.6 collective-permute-start
  60.4 17.2 %collective-permute-start.6 = (bf16[512,384]{1,0:T(8,128)(2,1)}, bf16[512,384]{1,0:T(8,128)(2,1)S(1)}, u32[]{:S(2)}, u32[]{:S(2)}) collective-permute-start(bf16[512,384]{1,0:T(8,128)(2,1)} %cut_block.8), channel_id=1, source_target_pairs={{0,2},{2,0},{4,6},{6,4},{8,10},{10,8},{12,14},{14,12},{16,18},{18,... | collective-permute-start | bytes 1179656 | tf_op jit(solution)/shard_map/ppermute | solution.py:579
  76.2 9.1 %collective-permute-start.5 = (bf16[512,384]{1,0:T(8,128)(2,1)}, bf16[512,384]{1,0:T(8,128)(2,1)S(1)}, u32[]{:S(2)}, u32[]{:S(2)}) collective-permute-start(bf16[512,384]{1,0:T(8,128)(2,1)} %cut_block.7), channel_id=1, source_target_pairs={{0,4},{2,6},{4,0},{6,2},{8,12},{10,14},{12,8},{14,10},{16,20},{18,... | collective-permute-start | bytes 1179656 | tf_op jit(solution)/shard_map/ppermute | solution.py:579
  158.6 7.2 %collective-permute-start.7 = (bf16[3072,384]{1,0:T(8,128)(2,1)}, bf16[3072,384]{1,0:T(8,128)(2,1)S(1)}, u32[]{:S(2)}, u32[]{:S(2)}) collective-permute-start(bf16[3072,384]{1,0:T(8,128)(2,1)} %pack_blocks.2.refs_2_.refs_3_.refs_0_), channel_id=1, source_target_pairs={{0,1},{1,0},{2,3},{3,2},{4,5},{5,4},{6,7},{7,6},{8,9},{9,8},{10,11... | collective-permute-start | bytes 7077896 | tf_op jit(solution)/shard_map/ppermute | solution.py:585
  192.8 19.0 %collective-permute-start.12 = (bf16[1024,384]{1,0:T(8,128)(2,1)}, bf16[1024,384]{1,0:T(8,128)(2,1)S(1)}, u32[]{:S(2)}, u32[]{:S(2)}) collective-permute-start(bf16[1024,384]{1,0:T(8,128)(2,1)} %cut_block.9), channel_id=1, source_target_pairs={{0,4},{2,6},{4,0},{6,2},{8,12},{10,14},{12,8},{14,10},{16,20},{18,... | collective-permute-start | bytes 2359304 | tf_op jit(solution)/shard_map/ppermute | solution.py:579
  194.1 32.6 %collective-permute-start.11 = (bf16[1024,384]{1,0:T(8,128)(2,1)}, bf16[1024,384]{1,0:T(8,128)(2,1)S(1)}, u32[]{:S(2)}, u32[]{:S(2)}) collective-permute-start(bf16[1024,384]{1,0:T(8,128)(2,1)} %cut_block.9), channel_id=1, source_target_pairs={{0,2},{2,0},{4,6},{6,4},{8,10},{10,8},{12,14},{14,12},{16,18},{18,... | collective-permute-start | bytes 2359304 | tf_op jit(solution)/shard_map/ppermute | solution.py:579
  205.0 53.6 %collective-permute-start.9 = (bf16[768,384]{1,0:T(8,128)(2,1)}, bf16[768,384]{1,0:T(8,128)(2,1)S(1)}, u32[]{:S(2)}, u32[]{:S(2)}) collective-permute-start(bf16[768,384]{1,0:T(8,128)(2,1)} %bitcast.12), channel_id=1, source_target_pairs={{0,16},{2,18},{4,20},{6,22},{8,24},{10,26},{12,28},{14,30},{16,0},... | collective-permute-start | bytes 1769480 | tf_op jit(solution)/shard_map/ppermute | solution.py:582
  226.4 32.2 %collective-permute-start.14 = (bf16[512,384]{1,0:T(8,128)(2,1)}, bf16[512,384]{1,0:T(8,128)(2,1)S(1)}, u32[]{:S(2)}, u32[]{:S(2)}) collective-permute-start(bf16[512,384]{1,0:T(8,128)(2,1)} %cut_block.11), channel_id=1, source_target_pairs={{0,2},{2,0},{4,6},{6,4},{8,10},{10,8},{12,14},{14,12},{16,18},{18,... | collective-permute-start | bytes 1179656 | tf_op jit(solution)/shard_map/ppermute | solution.py:579
  241.3 17.3 %collective-permute-start.13 = (bf16[512,384]{1,0:T(8,128)(2,1)}, bf16[512,384]{1,0:T(8,128)(2,1)S(1)}, u32[]{:S(2)}, u32[]{:S(2)}) collective-permute-start(bf16[512,384]{1,0:T(8,128)(2,1)} %cut_block.10), channel_id=1, source_target_pairs={{0,4},{2,6},{4,0},{6,2},{8,12},{10,14},{12,8},{14,10},{16,20},{18,... | collective-permute-start | bytes 1179656 | tf_op jit(solution)/shard_map/ppermute | solution.py:579
  333.1 15.4 %collective-permute-start.15 = (bf16[3072,384]{1,0:T(8,128)(2,1)}, bf16[3072,384]{1,0:T(8,128)(2,1)S(1)}, u32[]{:S(2)}, u32[]{:S(2)}) collective-permute-start(bf16[3072,384]{1,0:T(8,128)(2,1)} %pack_blocks.3.refs_2_.refs_3_), channel_id=1, source_target_pairs={{0,1},{1,0},{2,3},{3,2},{4,5},{5,4},{6,7},{7,6},{8,9},{9,8},{10,11... | collective-permute-start | bytes 7077896 | tf_op jit(solution)/shard_map/ppermute | solution.py:585
  335.8 64.5 %collective-permute-start.10 = (bf16[768,384]{1,0:T(8,128)(2,1)}, bf16[768,384]{1,0:T(8,128)(2,1)}, u32[]{:S(2)}, u32[]{:S(2)}) collective-permute-start(bf16[768,384]{1,0:T(8,128)(2,1)} %get-tuple-element.62), channel_id=1, source_target_pairs={{0,24},{2,26},{4,28},{6,30},{8,0},{10,2},{12,4},{14,6},{16,8},{18,... | collective-permute-start | bytes 1769480 | tf_op jit(solution)/shard_map/ppermute | solution.py:582
  335.8 64.5 %collective-permute-start.8 = (bf16[768,384]{1,0:T(8,128)(2,1)}, bf16[768,384]{1,0:T(8,128)(2,1)}, u32[]{:S(2)}, u32[]{:S(2)}) collective-permute-start(bf16[768,384]{1,0:T(8,128)(2,1)} %get-tuple-element.63), channel_id=1, source_target_pairs={{0,8},{2,10},{4,12},{6,14},{8,16},{10,18},{12,20},{14,22},{16,24},... | collective-permute-start | bytes 1769480 | tf_op jit(solution)/shard_map/ppermute | solution.py:582
  359.7 45.9 %collective-permute-start.17 = (bf16[768,384]{1,0:T(8,128)(2,1)S(1)}, bf16[768,384]{1,0:T(8,128)(2,1)}, u32[]{:S(2)}, u32[]{:S(2)}) collective-permute-start(bf16[768,384]{1,0:T(8,128)(2,1)S(1)} %bitcast.49), channel_id=1, source_target_pairs={{0,16},{2,18},{4,20},{6,22},{8,24},{10,26},{12,28},{14,30},{16,0},... | collective-permute-start | bytes 1769480 | tf_op jit(solution)/shard_map/ppermute | solution.py:582
  384.5 33.7 %collective-permute-start.18 = (bf16[768,384]{1,0:T(8,128)(2,1)}, bf16[768,384]{1,0:T(8,128)(2,1)}, u32[]{:S(2)}, u32[]{:S(2)}) collective-permute-start(bf16[768,384]{1,0:T(8,128)(2,1)} %get-tuple-element.60), channel_id=1, source_target_pairs={{0,24},{2,26},{4,28},{6,30},{8,0},{10,2},{12,4},{14,6},{16,8},{18,... | collective-permute-start | bytes 1769480 | tf_op jit(solution)/shard_map/ppermute | solution.py:582
  384.5 33.9 %collective-permute-start.16 = (bf16[768,384]{1,0:T(8,128)(2,1)}, bf16[768,384]{1,0:T(8,128)(2,1)}, u32[]{:S(2)}, u32[]{:S(2)}) collective-permute-start(bf16[768,384]{1,0:T(8,128)(2,1)} %get-tuple-element.61), channel_id=1, source_target_pairs={{0,8},{2,10},{4,12},{6,14},{8,16},{10,18},{12,20},{14,22},{16,24},... | collective-permute-start | bytes 1769480 | tf_op jit(solution)/shard_map/ppermute | solution.py:582
  434.0 4.5 collective-permute-start.19
  441.7 13.8 %collective-permute-start.20 = (bf16[4,64,1024]{2,1,0:T(8,128)(2,1)S(1)}, bf16[4,64,1024]{2,1,0:T(8,128)(2,1)S(1)}, u32[]{:S(2)}, u32[]{:S(2)}) collective-permute-start(bf16[4,64,1024]{2,1,0:T(8,128)(2,1)S(1)} %get-tuple-element.57), channel_id=1, source_target_pairs={{0,2},{2,0},{4,6},{6,4},{8,10},{10,8},{12,14},{14,12},{16,18},{18,... | collective-permute-start | bytes 1572872 | tf_op jit(solution)/shard_map/ppermute | solution.py:579
  443.5 23.2 %collective-permute-start.22 = (bf16[4,64,1024]{2,1,0:T(8,128)(2,1)S(1)}, bf16[4,64,1024]{2,1,0:T(8,128)(2,1)S(1)}, u32[]{:S(2)}, u32[]{:S(2)}) collective-permute-start(bf16[4,64,1024]{2,1,0:T(8,128)(2,1)S(1)} %get-tuple-element.58), channel_id=1, source_target_pairs={{0,6},{2,4},{4,2},{6,0},{8,14},{10,12},{12,10},{14,8},{16,22},{18,... | collective-permute-start | bytes 1572872 | tf_op jit(solution)/shard_map/ppermute | solution.py:579
  443.6 24.0 %collective-permute-start.21 = (bf16[4,64,1024]{2,1,0:T(8,128)(2,1)S(1)}, bf16[4,64,1024]{2,1,0:T(8,128)(2,1)S(1)}, u32[]{:S(2)}, u32[]{:S(2)}) collective-permute-start(bf16[4,64,1024]{2,1,0:T(8,128)(2,1)S(1)} %get-tuple-element.59), channel_id=1, source_target_pairs={{0,4},{2,6},{4,0},{6,2},{8,12},{10,14},{12,8},{14,10},{16,20},{18,... | collective-permute-start | bytes 1572872 | tf_op jit(solution)/shard_map/ppermute | solution.py:579
  468.0 5.5 %collective-permute-start.25 = (bf16[64,1024]{1,0:T(8,128)(2,1)S(1)}, bf16[64,1024]{1,0:T(8,128)(2,1)S(1)}, u32[]{:S(2)}, u32[]{:S(2)}) collective-permute-start(bf16[64,1024]{1,0:T(8,128)(2,1)S(1)} %get-tuple-element.64), channel_id=1, source_target_pairs={{0,24},{2,26},{4,28},{6,30},{8,0},{10,2},{12,4},{14,6},{16,8},{18,... | collective-permute-start | bytes 393224 | tf_op jit(solution)/shard_map/ppermute | solution.py:582
  469.0 9.7 %collective-permute-start.24 = (bf16[64,1024]{1,0:T(8,128)(2,1)S(1)}, bf16[64,1024]{1,0:T(8,128)(2,1)S(1)}, u32[]{:S(2)}, u32[]{:S(2)}) collective-permute-start(bf16[64,1024]{1,0:T(8,128)(2,1)S(1)} %get-tuple-element.65), channel_id=1, source_target_pairs={{0,16},{2,18},{4,20},{6,22},{8,24},{10,26},{12,28},{14,30},{16,0},... | collective-permute-start | bytes 393224 | tf_op jit(solution)/shard_map/ppermute | solution.py:582
  471.5 11.1 %collective-permute-start.23 = (bf16[64,1024]{1,0:T(8,128)(2,1)S(1)}, bf16[64,1024]{1,0:T(8,128)(2,1)S(1)}, u32[]{:S(2)}, u32[]{:S(2)}) collective-permute-start(bf16[64,1024]{1,0:T(8,128)(2,1)S(1)} %get-tuple-element.66), channel_id=1, source_target_pairs={{0,8},{2,10},{4,12},{6,14},{8,16},{10,18},{12,20},{14,22},{16,24},... | collective-permute-start | bytes 393224 | tf_op jit(solution)/shard_map/ppermute | solution.py:582
  483.4 4.5 collective-permute-start.28
  485.6 10.4 %collective-permute-start.27 = (bf16[64,1024]{1,0:T(8,128)(2,1)S(1)}, bf16[64,1024]{1,0:T(8,128)(2,1)S(1)}, u32[]{:S(2)}, u32[]{:S(2)}) collective-permute-start(bf16[64,1024]{1,0:T(8,128)(2,1)S(1)} %get-tuple-element.32), channel_id=1, source_target_pairs={{0,16},{2,18},{4,20},{6,22},{8,24},{10,26},{12,28},{14,30},{16,0},... | collective-permute-start | bytes 393224 | tf_op jit(solution)/shard_map/ppermute | solution.py:582
  486.6 11.3 %collective-permute-start.26 = (bf16[64,1024]{1,0:T(8,128)(2,1)S(1)}, bf16[64,1024]{1,0:T(8,128)(2,1)S(1)}, u32[]{:S(2)}, u32[]{:S(2)}) collective-permute-start(bf16[64,1024]{1,0:T(8,128)(2,1)S(1)} %get-tuple-element.32), channel_id=1, source_target_pairs={{0,24},{2,26},{4,28},{6,30},{8,0},{10,2},{12,4},{14,6},{16,8},{18,... | collective-permute-start | bytes 393224 | tf_op jit(solution)/shard_map/ppermute | solution.py:582
  497.9 13.3 %collective-permute-start.34 = (bf16[4,64,1024]{2,1,0:T(8,128)(2,1)S(1)}, bf16[4,64,1024]{2,1,0:T(8,128)(2,1)S(1)}, u32[]{:S(2)}, u32[]{:S(2)}) collective-permute-start(bf16[4,64,1024]{2,1,0:T(8,128)(2,1)S(1)} %pad_maximum_fusion.refs_0_), channel_id=1, source_target_pairs={{0,6},{2,4},{4,2},{6,0},{8,14},{10,12},{12,10},{14,8},{16,22},{18,... | collective-permute-start | bytes 1572872 | tf_op jit(solution)/shard_map/ppermute | solution.py:579
  499.1 24.9 %collective-permute-start.32 = (bf16[4,64,1024]{2,1,0:T(8,128)(2,1)S(1)}, bf16[4,64,1024]{2,1,0:T(8,128)(2,1)S(1)}, u32[]{:S(2)}, u32[]{:S(2)}) collective-permute-start(bf16[4,64,1024]{2,1,0:T(8,128)(2,1)S(1)} %pad_maximum_fusion.refs_0_), channel_id=1, source_target_pairs={{0,4},{2,6},{4,0},{6,2},{8,12},{10,14},{12,8},{14,10},{16,20},{18,... | collective-permute-start | bytes 1572872 | tf_op jit(solution)/shard_map/ppermute | solution.py:579
  499.4 25.1 %collective-permute-start.30 = (bf16[4,64,1024]{2,1,0:T(8,128)(2,1)S(1)}, bf16[4,64,1024]{2,1,0:T(8,128)(2,1)S(1)}, u32[]{:S(2)}, u32[]{:S(2)}) collective-permute-start(bf16[4,64,1024]{2,1,0:T(8,128)(2,1)S(1)} %pad_maximum_fusion.refs_0_), channel_id=1, source_target_pairs={{0,2},{2,0},{4,6},{6,4},{8,10},{10,8},{12,14},{14,12},{16,18},{18,... | collective-permute-start | bytes 1572872 | tf_op jit(solution)/shard_map/ppermute | solution.py:579
  500.7 24.7 %collective-permute-start.29 = (bf16[4,64,1024]{2,1,0:T(8,128)(2,1)S(1)}, bf16[4,64,1024]{2,1,0:T(8,128)(2,1)S(1)}, u32[]{:S(2)}, u32[]{:S(2)}) collective-permute-start(bf16[4,64,1024]{2,1,0:T(8,128)(2,1)S(1)} %pad_maximum_fusion.refs_0_), channel_id=1, source_target_pairs={{0,1},{1,0},{2,3},{3,2},{4,5},{5,4},{6,7},{7,6},{8,9},{9,8},{10,11... | collective-permute-start | bytes 1572872 | tf_op jit(solution)/shard_map/ppermute | solution.py:585
  511.3 14.0 %collective-permute-start.35 = (bf16[4,64,1024]{2,1,0:T(8,128)(2,1)S(1)}, bf16[4,64,1024]{2,1,0:T(8,128)(2,1)S(1)}, u32[]{:S(2)}, u32[]{:S(2)}) collective-permute-start(bf16[4,64,1024]{2,1,0:T(8,128)(2,1)S(1)} %collective-permute-done.34.refs_6_), channel_id=1, source_target_pairs={{0,1},{1,0},{2,3},{3,2},{4,5},{5,4},{6,7},{7,6},{8,9},{9,8},{10,11... | collective-permute-start | bytes 1572872 | tf_op jit(solution)/shard_map/ppermute | solution.py:585
  (42 other events, 477.8 us)

commit v5 on v4

--- a/solution.py
+++ b/solution.py
@@ -43,7 +43,7 @@
         functools.partial(cut_kernel, first, rows, columns, by_core),
         out_shape=jax.ShapeDtypeStruct((rows, columns[1] - columns[0]), source.dtype),
         in_specs=[SMEM] + [anywhere] * (1 + len(after)),
-        out_specs=anywhere,
+        out_specs=VMEM,
         scratch_shapes=[pltpu.SemaphoreType.DMA],
         name="cut_block",
     )(place, source, *after)
@@ -71,7 +71,7 @@
         functools.partial(pack_kernel, len(arrays)),
         out_shape=jax.ShapeDtypeStruct((rows, arrays[0].shape[1]), arrays[0].dtype),
         in_specs=[anywhere] * (len(arrays) + len(after)),
-        out_specs=anywhere,
+        out_specs=VMEM,
         scratch_shapes=[pltpu.SemaphoreType.DMA((len(arrays),))],
         name="pack_blocks",
     )(*arrays, *after)

time: 538 us -> 305 us (0.57)
  Pallas kernels: 353 us -> 127 us
  starting transfers between devices: 53.8 us -> 47.9 us
    pallas_call x2, Pallas kernels: 145 us -> 6.07 us  [pack(): pl.pallas_call(functools.partial(pack_kernel, len(arrays)), out_shape=jax...]
    pallas_call x6, Pallas kernels: 106 us -> 15.2 us  [cut(): pl.pallas_call(functools.partial(cut_kernel, first, rows, columns, by_cor...]
    ppermute x15, starting transfers between devices: 28.7 us -> 22.8 us  [along(): lax.ppermute(x, 'store', [(i, (i + hops * PLANE) % stores) for i in range...]
  transfers between devices with their start and end apart: 36 -> 36, of which waited for: 22 -> 21; matrix products, arithmetic and copies ran while one was open for 1% -> 2% of each run, Pallas kernels for 24% -> 29%
where the time goes in v5:
time: 305 us
  Pallas kernels  127 us (42%)
  waiting for transfers between devices  104 us (34%)
  starting transfers between devices  47.9 us (16%)
  local copies, waits for them, and re-layouts  21.3 us (7%)
  other arithmetic  4.2 us (1%)
    pallas_call x6, Pallas kernels, partial_sums(): pl.pallas_call(functools.partial(partial_kernel, len(lists), columns, pla...  74.4 us
    ppermute x14, waiting for transfers between devices, across(): return lax.ppermute(x, 'store', [(i, i ^ distance) for i in range(stores)])  52.6 us
    ppermute x15, waiting for transfers between devices, along(): lax.ppermute(x, 'store', [(i, (i + hops * PLANE) % stores) for i in range...  41.6 us
    ppermute x15, starting transfers between devices, along(): lax.ppermute(x, 'store', [(i, (i + hops * PLANE) % stores) for i in range...  22.8 us
    unnamed x80, local copies, waits for them, and re-layouts  18 us
    pallas_call x1, Pallas kernels, trainer_step(): pl.pallas_call(functools.partial(trainer_kernel, sizes, scale), out_shape...  15.6 us
    pallas_call x6, Pallas kernels, cut(): pl.pallas_call(functools.partial(cut_kernel, first, rows, columns, by_cor...  15.2 us
    ppermute x14, starting transfers between devices, across(): return lax.ppermute(x, 'store', [(i, i ^ distance) for i in range(stores)])  13.7 us
  transfers between devices with their start and end apart: 36, of which 21 were waited for; matrix products, arithmetic and copies ran while one was open for 2% of the time, Pallas kernels for 29%

profile of v5, /device:TPU:9, one launch (start us, length us, event | category | flops | bytes accessed | tf_op | source)
XLA Modules:
  0.0 305.4 jit_solution(10170749921390968093)
XLA Ops:
  1.4 2.8 cut_block.6
  6.9 2.8 compose_ids.1
  17.2 2.9 row_lists.1
  32.1 3.5 %collective-permute-done.6.refs_3_ = bf16[512,384]{1,0:T(8,128)(2,1)S(1)} collective-permute-done((bf16[512,384]{1,0:T(8,128)(2,1)}, bf16[512,384]{1,0:T(8,128)(2,1)S(1)}, u32[]{:S(2)}, u32[]{:S(2)}) %collective-permute-start.6) | collective-permute-done | bytes 393248 | tf_op jit(solution)/shard_map/ppermute | solution.py:579
  35.5 4.3 %collective-permute-done.5.refs_2_ = bf16[512,384]{1,0:T(8,128)(2,1)S(1)} collective-permute-done((bf16[512,384]{1,0:T(8,128)(2,1)}, bf16[512,384]{1,0:T(8,128)(2,1)S(1)}, u32[]{:S(2)}, u32[]{:S(2)}) %collective-permute-start.5) | collective-permute-done | bytes 393248 | tf_op jit(solution)/shard_map/ppermute | solution.py:579
  40.6 3.0 pack_blocks.2.refs_2_.refs_3_.refs_0_
  43.6 2.8 collective-permute-start.7
  46.4 4.4 %collective-permute-done.7.refs_3_.refs_4_.refs_1_ = bf16[3072,384]{1,0:T(8,128)(2,1)S(1)} collective-permute-done((bf16[3072,384]{1,0:T(8,128)(2,1)}, bf16[3072,384]{1,0:T(8,128)(2,1)S(1)}, u32[]{:S(2)}, u32[]{:S(2)}) %collective-permute-start.7) | collective-permute-done | bytes 2359328 | tf_op jit(solution)/shard_map/ppermute | solution.py:585
  56.4 11.4 %partial_sums.6.refs_5_.refs_0_ = bf16[1,768,384]{2,1,0:T(8,128)(2,1)} custom-call(s32[18,512]{1,0:T(8,128)S(1)} %get-tuple-element.28.refs_0_, bf16[2048,768]{1,0:T(8,128)(2,1)} %refs_1_.7, bf16[3072,384]{1,0:T(8,128)(2,1)} %pack_blocks.2.refs_2_.refs_3_.refs_0_, bf16[3072,384]{1,0:T(8,128)(2,1)} %copy-done.13), custom_call_target="tpu_custom_call" | custom-call | tf_op jit(solution)/shard_map/partial_sums/pallas_call | solution.py:306
  70.1 3.8 %collective-permute-done.12.source_ref.refs_1_ = bf16[1024,384]{1,0:T(8,128)(2,1)S(1)} collective-permute-done((bf16[1024,384]{1,0:T(8,128)(2,1)}, bf16[1024,384]{1,0:T(8,128)(2,1)S(1)}, u32[]{:S(2)}, u32[]{:S(2)}) %collective-permute-start.12) | collective-permute-done | bytes 786464 | tf_op jit(solution)/shard_map/ppermute | solution.py:579
  82.2 15.5 %partial_sums.7.refs_4_.refs_5_ = bf16[2,768,384]{2,1,0:T(8,128)(2,1)S(1)} custom-call(s32[18,512]{1,0:T(8,128)S(1)} %get-tuple-element.26.refs_0_, s32[18,512]{1,0:T(8,128)S(1)} %get-tuple-element.27.refs_1_, bf16[2048,768]{1,0:T(8,128)(2,1)} %refs_1_.7, bf16[3072,384]{1,0:T(8,128)(2,1)} %pack_blocks.2.refs_2_.refs_3_.refs_0_, ...), custom_call_target="tpu_custom_call" | custom-call | tf_op jit(solution)/shard_map/partial_sums/pallas_call | solution.py:306
  100.6 3.0 pack_blocks.3.refs_2_.refs_3_
  107.8 10.6 %partial_sums.8.refs_4_ = bf16[1,768,384]{2,1,0:T(8,128)(2,1)S(1)} custom-call(s32[18,512]{1,0:T(8,128)S(1)} %copy-done.5, bf16[2048,768]{1,0:T(8,128)(2,1)} %refs_1_.7, bf16[3072,384]{1,0:T(8,128)(2,1)} %pack_blocks.2.refs_2_.refs_3_.refs_0_, bf16[3072,384]{1,0:T(8,128)(2,1)} %copy-done.13, bf16[2,768,384]{2,1,0:T(8,128)(2,1)S(1)} %copy-done.1), custom_call_target="tpu_custom_call" | custom-call | tf_op jit(solution)/shard_map/partial_sums/pallas_call | solution.py:306
  120.0 10.6 %partial_sums.9.refs_5_ = bf16[1,768,384]{2,1,0:T(8,128)(2,1)S(1)} custom-call(s32[18,512]{1,0:T(8,128)S(1)} %get-tuple-element.28.refs_0_, bf16[2048,768]{1,0:T(8,128)(2,1)} %refs_1_.7, bf16[3072,384]{1,0:T(8,128)(2,1)} %pack_blocks.3.refs_2_.refs_3_, bf16[3072,384]{1,0:T(8,128)(2,1)} %copy-done.14, bf16[1,768,384]{2,1,0:T(8,128)(2,1)S(1)} %partial_sums.8.refs_4_), custom_call_target="tpu_custom_call" | custom-call | tf_op jit(solution)/shard_map/partial_sums/pallas_call | solution.py:306
  130.6 5.0 %collective-permute-start.17 = (bf16[768,384]{1,0:T(8,128)(2,1)S(1)}, bf16[768,384]{1,0:T(8,128)(2,1)}, u32[]{:S(2)}, u32[]{:S(2)}) collective-permute-start(bf16[768,384]{1,0:T(8,128)(2,1)S(1)} %bitcast.49), channel_id=1, source_target_pairs={{0,16},{2,18},{4,20},{6,22},{8,24},{10,26},{12,28},{14,30},{16,0},... | collective-permute-start | bytes 1769480 | tf_op jit(solution)/shard_map/ppermute | solution.py:582
  135.6 15.5 %partial_sums.10.refs_4_ = bf16[2,768,384]{2,1,0:T(8,128)(2,1)S(1)} custom-call(s32[18,512]{1,0:T(8,128)S(1)} %get-tuple-element.26.refs_0_, s32[18,512]{1,0:T(8,128)S(1)} %get-tuple-element.27.refs_1_, bf16[2048,768]{1,0:T(8,128)(2,1)} %refs_1_.7, bf16[3072,384]{1,0:T(8,128)(2,1)} %pack_blocks.3.refs_2_.refs_3_, bf16[3072,384]{1,0:T(8,128)(2,1)} %copy-done.14, ...), custom_call_target="tpu_custom_call" | custom-call | tf_op jit(solution)/shard_map/partial_sums/pallas_call | solution.py:306
  157.0 10.7 %partial_sums.11 = bf16[1,768,384]{2,1,0:T(8,128)(2,1)S(1)} custom-call(s32[18,512]{1,0:T(8,128)S(1)} %copy-done.5, bf16[2048,768]{1,0:T(8,128)(2,1)} %refs_1_.7, bf16[3072,384]{1,0:T(8,128)(2,1)} %pack_blocks.3.refs_2_.refs_3_, bf16[3072,384]{1,0:T(8,128)(2,1)} %copy-done.14, bf16[2,768,384]{2,1,0:T(8,128)(2,1)S(1)} %partial_sums.10.refs_4_), custom_call_target="tpu_custom_call" | custom-call | tf_op jit(solution)/shard_map/partial_sums/pallas_call | solution.py:306
  168.5 4.8 %collective-permute-done.17.refs_12_ = bf16[768,384]{1,0:T(8,128)(2,1)} collective-permute-done((bf16[768,384]{1,0:T(8,128)(2,1)S(1)}, bf16[768,384]{1,0:T(8,128)(2,1)}, u32[]{:S(2)}, u32[]{:S(2)}) %collective-permute-start.17) | collective-permute-done | bytes 589856 | tf_op jit(solution)/shard_map/ppermute | solution.py:582
  173.3 13.7 %collective-permute-done.18.refs_13_ = bf16[768,384]{1,0:T(8,128)(2,1)} collective-permute-done((bf16[768,384]{1,0:T(8,128)(2,1)}, bf16[768,384]{1,0:T(8,128)(2,1)}, u32[]{:S(2)}, u32[]{:S(2)}) %collective-permute-start.18) | collective-permute-done | bytes 589856 | tf_op jit(solution)/shard_map/ppermute | solution.py:582
  187.0 15.6 %trainer_step.1 = (f32[128,153]{1,0:T(8,128)}, f32[4,4,64,1024]{3,2,1,0:T(8,128)}, bf16[4,4,64,1024]{3,2,1,0:T(8,128)(2,1)}) custom-call(s32[4]{0:T(128)} %pad_add_fusion.place_ref.refs_0_, s32[128,1]{1,0:T(8,128)} %copy.28.refs_1_, s32[128,10]{1,0:T(8,128)} %copy.29.refs_2_, s32[1,512]{1,0:T(1,128)} %copy-done.12, f32[1536,1024]{1,0:T(8,128)} %wl.1, ...), custom_call_target="tpu_custom_call" | custom-call | tf_op jit(solution)/shard_map/trainer_step/pallas_call | solution.py:431
  203.1 4.0 %collective-permute-done.19 = bf16[4,4,64,1024]{3,2,1,0:T(8,128)(2,1)S(1)} collective-permute-done((bf16[4,4,64,1024]{3,2,1,0:T(8,128)(2,1)}, bf16[4,4,64,1024]{3,2,1,0:T(8,128)(2,1)S(1)}, u32[]{:S(2)}, u32[]{:S(2)}) %collective-permute-start.19) | collective-permute-done | bytes 2097184 | tf_op jit(solution)/shard_map/ppermute | solution.py:585
  207.1 3.1 %fusion.3 = (bf16[4,4,64,1024]{3,2,1,0:T(8,128)(2,1)S(1)}, f32[4,4,64,1024]{3,2,1,0:T(8,128)S(1)}) fusion(f32[4,4,64,1024]{3,2,1,0:T(8,128)} %get-tuple-element.30, bf16[4,4,64,1024]{3,2,1,0:T(8,128)(2,1)S(1)} %collective-permute-done.19), kind=kLoop, calls=%fused_computation.21 | loop fusion | flops 3145728 | bytes 12582912 | tf_op jit(solution)/shard_map/convert.5
  213.1 10.5 %collective-permute-done.20 = bf16[4,64,1024]{2,1,0:T(8,128)(2,1)S(1)} collective-permute-done((bf16[4,64,1024]{2,1,0:T(8,128)(2,1)S(1)}, bf16[4,64,1024]{2,1,0:T(8,128)(2,1)S(1)}, u32[]{:S(2)}, u32[]{:S(2)}) %collective-permute-start.20) | collective-permute-done | bytes 524320 | tf_op jit(solution)/shard_map/ppermute | solution.py:579
  223.5 11.2 %collective-permute-done.22 = bf16[4,64,1024]{2,1,0:T(8,128)(2,1)S(1)} collective-permute-done((bf16[4,64,1024]{2,1,0:T(8,128)(2,1)S(1)}, bf16[4,64,1024]{2,1,0:T(8,128)(2,1)S(1)}, u32[]{:S(2)}, u32[]{:S(2)}) %collective-permute-start.22) | collective-permute-done | bytes 524320 | tf_op jit(solution)/shard_map/ppermute | solution.py:579
  240.5 4.0 %collective-permute-done.24.refs_2_ = bf16[64,1024]{1,0:T(8,128)(2,1)S(1)} collective-permute-done((bf16[64,1024]{1,0:T(8,128)(2,1)S(1)}, bf16[64,1024]{1,0:T(8,128)(2,1)S(1)}, u32[]{:S(2)}, u32[]{:S(2)}) %collective-permute-start.24) | collective-permute-done | bytes 131104 | tf_op jit(solution)/shard_map/ppermute | solution.py:582
  244.6 5.0 %collective-permute-done.23.refs_1_ = bf16[64,1024]{1,0:T(8,128)(2,1)S(1)} collective-permute-done((bf16[64,1024]{1,0:T(8,128)(2,1)S(1)}, bf16[64,1024]{1,0:T(8,128)(2,1)S(1)}, u32[]{:S(2)}, u32[]{:S(2)}) %collective-permute-start.23) | collective-permute-done | bytes 131104 | tf_op jit(solution)/shard_map/ppermute | solution.py:582
  254.9 8.2 %collective-permute-done.27 = bf16[64,1024]{1,0:T(8,128)(2,1)S(1)} collective-permute-done((bf16[64,1024]{1,0:T(8,128)(2,1)S(1)}, bf16[64,1024]{1,0:T(8,128)(2,1)S(1)}, u32[]{:S(2)}, u32[]{:S(2)}) %collective-permute-start.27) | collective-permute-done | bytes 131104 | tf_op jit(solution)/shard_map/ppermute | solution.py:582
  269.6 8.4 %collective-permute-done.34.refs_6_ = bf16[4,64,1024]{2,1,0:T(8,128)(2,1)S(1)} collective-permute-done((bf16[4,64,1024]{2,1,0:T(8,128)(2,1)S(1)}, bf16[4,64,1024]{2,1,0:T(8,128)(2,1)S(1)}, u32[]{:S(2)}, u32[]{:S(2)}) %collective-permute-start.34) | collective-permute-done | bytes 524320 | tf_op jit(solution)/shard_map/ppermute | solution.py:579
  278.0 3.9 %collective-permute-start.35 = (bf16[4,64,1024]{2,1,0:T(8,128)(2,1)S(1)}, bf16[4,64,1024]{2,1,0:T(8,128)(2,1)S(1)}, u32[]{:S(2)}, u32[]{:S(2)}) collective-permute-start(bf16[4,64,1024]{2,1,0:T(8,128)(2,1)S(1)} %collective-permute-done.34.refs_6_), channel_id=1, source_target_pairs={{0,1},{1,0},{2,3},{3,2},{4,5},{5,4},{6,7},{7,6},{8,9},{9,8},{10,11... | collective-permute-start | bytes 1572872 | tf_op jit(solution)/shard_map/ppermute | solution.py:585
  281.9 8.9 %collective-permute-done.32.refs_4_ = bf16[4,64,1024]{2,1,0:T(8,128)(2,1)S(1)} collective-permute-done((bf16[4,64,1024]{2,1,0:T(8,128)(2,1)S(1)}, bf16[4,64,1024]{2,1,0:T(8,128)(2,1)S(1)}, u32[]{:S(2)}, u32[]{:S(2)}) %collective-permute-start.32) | collective-permute-done | bytes 524320 | tf_op jit(solution)/shard_map/ppermute | solution.py:579
  293.8 8.9 %apply_updates.1 = (f32[1536,1024]{1,0:T(8,128)}, f32[2048,153]{1,0:T(8,128)}) custom-call(s32[4]{0:T(128)} %pad_add_fusion.place_ref.refs_0_, f32[1536,1024]{1,0:T(8,128)} %wl.1, f32[2048,153]{1,0:T(8,128)} %copy.30.refs_5_.wt, bf16[4,64,1024]{2,1,0:T(8,128)(2,1)} %copy-done.20, bf16[4,64,1024]{2,1,0:T(8,128)(2,1)} %copy-done.25, ...), custom_call_target="tpu_custom_call" | custom-call | tf_op jit(solution)/shard_map/apply_updates/pallas_call | solution.py:532
  302.8 2.7 copy.33
  (154 shorter events, 78.8 us)
Async XLA Ops:
  4.2 18.7 %collective-permute-start.4 = (bf16[1024,384]{1,0:T(8,128)(2,1)}, bf16[1024,384]{1,0:T(8,128)(2,1)S(1)}, u32[]{:S(2)}, u32[]{:S(2)}) collective-permute-start(bf16[1024,384]{1,0:T(8,128)(2,1)} %cut_block.6), channel_id=1, source_target_pairs={{0,4},{2,6},{4,0},{6,2},{8,12},{10,14},{12,8},{14,10},{16,20},{18,... | collective-permute-start | bytes 2359304 | tf_op jit(solution)/shard_map/ppermute | solution.py:579
  5.5 22.0 %collective-permute-start.3 = (bf16[1024,384]{1,0:T(8,128)(2,1)}, bf16[1024,384]{1,0:T(8,128)(2,1)S(1)}, u32[]{:S(2)}, u32[]{:S(2)}) collective-permute-start(bf16[1024,384]{1,0:T(8,128)(2,1)} %cut_block.6), channel_id=1, source_target_pairs={{0,2},{2,0},{4,6},{6,4},{8,10},{10,8},{12,14},{14,12},{16,18},{18,... | collective-permute-start | bytes 2359304 | tf_op jit(solution)/shard_map/ppermute | solution.py:579
  12.6 4.6 %collective-permute-start = (s32[17,512]{1,0:T(8,128)S(1)}, s32[17,512]{1,0:T(8,128)S(1)}, u32[]{:S(2)}, u32[]{:S(2)}) collective-permute-start(s32[17,512]{1,0:T(8,128)S(1)} %get-tuple-element.24.refs_0_), channel_id=1, source_target_pairs={{0,24},{2,26},{4,28},{6,30},{8,0},{10,2},{12,4},{14,6},{16,8},{18,... | collective-permute-start | bytes 104456 | tf_op jit(solution)/shard_map/ppermute | solution.py:582
  26.2 9.3 %collective-permute-start.6 = (bf16[512,384]{1,0:T(8,128)(2,1)}, bf16[512,384]{1,0:T(8,128)(2,1)S(1)}, u32[]{:S(2)}, u32[]{:S(2)}) collective-permute-start(bf16[512,384]{1,0:T(8,128)(2,1)} %cut_block.8), channel_id=1, source_target_pairs={{0,2},{2,0},{4,6},{6,4},{8,10},{10,8},{12,14},{14,12},{16,18},{18,... | collective-permute-start | bytes 1179656 | tf_op jit(solution)/shard_map/ppermute | solution.py:579
  30.8 9.1 %collective-permute-start.5 = (bf16[512,384]{1,0:T(8,128)(2,1)}, bf16[512,384]{1,0:T(8,128)(2,1)S(1)}, u32[]{:S(2)}, u32[]{:S(2)}) collective-permute-start(bf16[512,384]{1,0:T(8,128)(2,1)} %cut_block.7), channel_id=1, source_target_pairs={{0,4},{2,6},{4,0},{6,2},{8,12},{10,14},{12,8},{14,10},{16,20},{18,... | collective-permute-start | bytes 1179656 | tf_op jit(solution)/shard_map/ppermute | solution.py:579
  43.6 7.2 %collective-permute-start.7 = (bf16[3072,384]{1,0:T(8,128)(2,1)}, bf16[3072,384]{1,0:T(8,128)(2,1)S(1)}, u32[]{:S(2)}, u32[]{:S(2)}) collective-permute-start(bf16[3072,384]{1,0:T(8,128)(2,1)} %pack_blocks.2.refs_2_.refs_3_.refs_0_), channel_id=1, source_target_pairs={{0,1},{1,0},{2,3},{3,2},{4,5},{5,4},{6,7},{7,6},{8,9},{9,8},{10,11... | collective-permute-start | bytes 7077896 | tf_op jit(solution)/shard_map/ppermute | solution.py:585
  54.9 19.0 %collective-permute-start.12 = (bf16[1024,384]{1,0:T(8,128)(2,1)}, bf16[1024,384]{1,0:T(8,128)(2,1)S(1)}, u32[]{:S(2)}, u32[]{:S(2)}) collective-permute-start(bf16[1024,384]{1,0:T(8,128)(2,1)} %cut_block.9), channel_id=1, source_target_pairs={{0,4},{2,6},{4,0},{6,2},{8,12},{10,14},{12,8},{14,10},{16,20},{18,... | collective-permute-start | bytes 2359304 | tf_op jit(solution)/shard_map/ppermute | solution.py:579
  56.2 21.4 %collective-permute-start.11 = (bf16[1024,384]{1,0:T(8,128)(2,1)}, bf16[1024,384]{1,0:T(8,128)(2,1)S(1)}, u32[]{:S(2)}, u32[]{:S(2)}) collective-permute-start(bf16[1024,384]{1,0:T(8,128)(2,1)} %cut_block.9), channel_id=1, source_target_pairs={{0,2},{2,0},{4,6},{6,4},{8,10},{10,8},{12,14},{14,12},{16,18},{18,... | collective-permute-start | bytes 2359304 | tf_op jit(solution)/shard_map/ppermute | solution.py:579
  67.9 30.9 %collective-permute-start.9 = (bf16[768,384]{1,0:T(8,128)(2,1)}, bf16[768,384]{1,0:T(8,128)(2,1)S(1)}, u32[]{:S(2)}, u32[]{:S(2)}) collective-permute-start(bf16[768,384]{1,0:T(8,128)(2,1)} %bitcast.12), channel_id=1, source_target_pairs={{0,16},{2,18},{4,20},{6,22},{8,24},{10,26},{12,28},{14,30},{16,0},... | collective-permute-start | bytes 1769480 | tf_op jit(solution)/shard_map/ppermute | solution.py:582
  77.2 21.5 %collective-permute-start.14 = (bf16[512,384]{1,0:T(8,128)(2,1)}, bf16[512,384]{1,0:T(8,128)(2,1)S(1)}, u32[]{:S(2)}, u32[]{:S(2)}) collective-permute-start(bf16[512,384]{1,0:T(8,128)(2,1)} %cut_block.11), channel_id=1, source_target_pairs={{0,2},{2,0},{4,6},{6,4},{8,10},{10,8},{12,14},{14,12},{16,18},{18,... | collective-permute-start | bytes 1179656 | tf_op jit(solution)/shard_map/ppermute | solution.py:579
  80.9 17.9 %collective-permute-start.13 = (bf16[512,384]{1,0:T(8,128)(2,1)}, bf16[512,384]{1,0:T(8,128)(2,1)S(1)}, u32[]{:S(2)}, u32[]{:S(2)}) collective-permute-start(bf16[512,384]{1,0:T(8,128)(2,1)} %cut_block.10), channel_id=1, source_target_pairs={{0,4},{2,6},{4,0},{6,2},{8,12},{10,14},{12,8},{14,10},{16,20},{18,... | collective-permute-start | bytes 1179656 | tf_op jit(solution)/shard_map/ppermute | solution.py:579
  103.6 14.9 %collective-permute-start.15 = (bf16[3072,384]{1,0:T(8,128)(2,1)}, bf16[3072,384]{1,0:T(8,128)(2,1)S(1)}, u32[]{:S(2)}, u32[]{:S(2)}) collective-permute-start(bf16[3072,384]{1,0:T(8,128)(2,1)} %pack_blocks.3.refs_2_.refs_3_), channel_id=1, source_target_pairs={{0,1},{1,0},{2,3},{3,2},{4,5},{5,4},{6,7},{7,6},{8,9},{9,8},{10,11... | collective-permute-start | bytes 7077896 | tf_op jit(solution)/shard_map/ppermute | solution.py:585
  106.4 62.2 %collective-permute-start.10 = (bf16[768,384]{1,0:T(8,128)(2,1)}, bf16[768,384]{1,0:T(8,128)(2,1)}, u32[]{:S(2)}, u32[]{:S(2)}) collective-permute-start(bf16[768,384]{1,0:T(8,128)(2,1)} %get-tuple-element.62), channel_id=1, source_target_pairs={{0,24},{2,26},{4,28},{6,30},{8,0},{10,2},{12,4},{14,6},{16,8},{18,... | collective-permute-start | bytes 1769480 | tf_op jit(solution)/shard_map/ppermute | solution.py:582
  106.6 61.9 %collective-permute-start.8 = (bf16[768,384]{1,0:T(8,128)(2,1)}, bf16[768,384]{1,0:T(8,128)(2,1)}, u32[]{:S(2)}, u32[]{:S(2)}) collective-permute-start(bf16[768,384]{1,0:T(8,128)(2,1)} %get-tuple-element.63), channel_id=1, source_target_pairs={{0,8},{2,10},{4,12},{6,14},{8,16},{10,18},{12,20},{14,22},{16,24},... | collective-permute-start | bytes 1769480 | tf_op jit(solution)/shard_map/ppermute | solution.py:582
  130.6 42.8 %collective-permute-start.17 = (bf16[768,384]{1,0:T(8,128)(2,1)S(1)}, bf16[768,384]{1,0:T(8,128)(2,1)}, u32[]{:S(2)}, u32[]{:S(2)}) collective-permute-start(bf16[768,384]{1,0:T(8,128)(2,1)S(1)} %bitcast.49), channel_id=1, source_target_pairs={{0,16},{2,18},{4,20},{6,22},{8,24},{10,26},{12,28},{14,30},{16,0},... | collective-permute-start | bytes 1769480 | tf_op jit(solution)/shard_map/ppermute | solution.py:582
  152.3 34.8 %collective-permute-start.18 = (bf16[768,384]{1,0:T(8,128)(2,1)}, bf16[768,384]{1,0:T(8,128)(2,1)}, u32[]{:S(2)}, u32[]{:S(2)}) collective-permute-start(bf16[768,384]{1,0:T(8,128)(2,1)} %get-tuple-element.60), channel_id=1, source_target_pairs={{0,24},{2,26},{4,28},{6,30},{8,0},{10,2},{12,4},{14,6},{16,8},{18,... | collective-permute-start | bytes 1769480 | tf_op jit(solution)/shard_map/ppermute | solution.py:582
  152.3 34.8 %collective-permute-start.16 = (bf16[768,384]{1,0:T(8,128)(2,1)}, bf16[768,384]{1,0:T(8,128)(2,1)}, u32[]{:S(2)}, u32[]{:S(2)}) collective-permute-start(bf16[768,384]{1,0:T(8,128)(2,1)} %get-tuple-element.61), channel_id=1, source_target_pairs={{0,8},{2,10},{4,12},{6,14},{8,16},{10,18},{12,20},{14,22},{16,24},... | collective-permute-start | bytes 1769480 | tf_op jit(solution)/shard_map/ppermute | solution.py:582
  202.6 4.5 %collective-permute-start.19 = (bf16[4,4,64,1024]{3,2,1,0:T(8,128)(2,1)}, bf16[4,4,64,1024]{3,2,1,0:T(8,128)(2,1)S(1)}, u32[]{:S(2)}, u32[]{:S(2)}) collective-permute-start(bf16[4,4,64,1024]{3,2,1,0:T(8,128)(2,1)} %get-tuple-element.31), channel_id=1, source_target_pairs={{0,1},{1,0},{2,3},{3,2},{4,5},{5,4},{6,7},{7,6},{8,9},{9,8},{10,11... | collective-permute-start | bytes 6291464 | tf_op jit(solution)/shard_map/ppermute | solution.py:585
  210.3 13.2 %collective-permute-start.20 = (bf16[4,64,1024]{2,1,0:T(8,128)(2,1)S(1)}, bf16[4,64,1024]{2,1,0:T(8,128)(2,1)S(1)}, u32[]{:S(2)}, u32[]{:S(2)}) collective-permute-start(bf16[4,64,1024]{2,1,0:T(8,128)(2,1)S(1)} %get-tuple-element.57), channel_id=1, source_target_pairs={{0,2},{2,0},{4,6},{6,4},{8,10},{10,8},{12,14},{14,12},{16,18},{18,... | collective-permute-start | bytes 1572872 | tf_op jit(solution)/shard_map/ppermute | solution.py:579
  211.2 23.5 %collective-permute-start.22 = (bf16[4,64,1024]{2,1,0:T(8,128)(2,1)S(1)}, bf16[4,64,1024]{2,1,0:T(8,128)(2,1)S(1)}, u32[]{:S(2)}, u32[]{:S(2)}) collective-permute-start(bf16[4,64,1024]{2,1,0:T(8,128)(2,1)S(1)} %get-tuple-element.58), channel_id=1, source_target_pairs={{0,6},{2,4},{4,2},{6,0},{8,14},{10,12},{12,10},{14,8},{16,22},{18,... | collective-permute-start | bytes 1572872 | tf_op jit(solution)/shard_map/ppermute | solution.py:579
  211.7 23.0 %collective-permute-start.21 = (bf16[4,64,1024]{2,1,0:T(8,128)(2,1)S(1)}, bf16[4,64,1024]{2,1,0:T(8,128)(2,1)S(1)}, u32[]{:S(2)}, u32[]{:S(2)}) collective-permute-start(bf16[4,64,1024]{2,1,0:T(8,128)(2,1)S(1)} %get-tuple-element.59), channel_id=1, source_target_pairs={{0,4},{2,6},{4,0},{6,2},{8,12},{10,14},{12,8},{14,10},{16,20},{18,... | collective-permute-start | bytes 1572872 | tf_op jit(solution)/shard_map/ppermute | solution.py:579
  235.1 5.4 %collective-permute-start.25 = (bf16[64,1024]{1,0:T(8,128)(2,1)S(1)}, bf16[64,1024]{1,0:T(8,128)(2,1)S(1)}, u32[]{:S(2)}, u32[]{:S(2)}) collective-permute-start(bf16[64,1024]{1,0:T(8,128)(2,1)S(1)} %get-tuple-element.64), channel_id=1, source_target_pairs={{0,24},{2,26},{4,28},{6,30},{8,0},{10,2},{12,4},{14,6},{16,8},{18,... | collective-permute-start | bytes 393224 | tf_op jit(solution)/shard_map/ppermute | solution.py:582
  236.3 8.2 %collective-permute-start.24 = (bf16[64,1024]{1,0:T(8,128)(2,1)S(1)}, bf16[64,1024]{1,0:T(8,128)(2,1)S(1)}, u32[]{:S(2)}, u32[]{:S(2)}) collective-permute-start(bf16[64,1024]{1,0:T(8,128)(2,1)S(1)} %get-tuple-element.65), channel_id=1, source_target_pairs={{0,16},{2,18},{4,20},{6,22},{8,24},{10,26},{12,28},{14,30},{16,0},... | collective-permute-start | bytes 393224 | tf_op jit(solution)/shard_map/ppermute | solution.py:582
  238.5 11.1 %collective-permute-start.23 = (bf16[64,1024]{1,0:T(8,128)(2,1)S(1)}, bf16[64,1024]{1,0:T(8,128)(2,1)S(1)}, u32[]{:S(2)}, u32[]{:S(2)}) collective-permute-start(bf16[64,1024]{1,0:T(8,128)(2,1)S(1)} %get-tuple-element.66), channel_id=1, source_target_pairs={{0,8},{2,10},{4,12},{6,14},{8,16},{10,18},{12,20},{14,22},{16,24},... | collective-permute-start | bytes 393224 | tf_op jit(solution)/shard_map/ppermute | solution.py:582
  250.4 4.5 %collective-permute-start.28 = (bf16[64,1024]{1,0:T(8,128)(2,1)S(1)}, bf16[64,1024]{1,0:T(8,128)(2,1)S(1)}, u32[]{:S(2)}, u32[]{:S(2)}) collective-permute-start(bf16[64,1024]{1,0:T(8,128)(2,1)S(1)} %get-tuple-element.32), channel_id=1, source_target_pairs={{0,8},{2,10},{4,12},{6,14},{8,16},{10,18},{12,20},{14,22},{16,24},... | collective-permute-start | bytes 393224 | tf_op jit(solution)/shard_map/ppermute | solution.py:582
  252.6 10.4 %collective-permute-start.27 = (bf16[64,1024]{1,0:T(8,128)(2,1)S(1)}, bf16[64,1024]{1,0:T(8,128)(2,1)S(1)}, u32[]{:S(2)}, u32[]{:S(2)}) collective-permute-start(bf16[64,1024]{1,0:T(8,128)(2,1)S(1)} %get-tuple-element.32), channel_id=1, source_target_pairs={{0,16},{2,18},{4,20},{6,22},{8,24},{10,26},{12,28},{14,30},{16,0},... | collective-permute-start | bytes 393224 | tf_op jit(solution)/shard_map/ppermute | solution.py:582
  253.7 11.0 %collective-permute-start.26 = (bf16[64,1024]{1,0:T(8,128)(2,1)S(1)}, bf16[64,1024]{1,0:T(8,128)(2,1)S(1)}, u32[]{:S(2)}, u32[]{:S(2)}) collective-permute-start(bf16[64,1024]{1,0:T(8,128)(2,1)S(1)} %get-tuple-element.32), channel_id=1, source_target_pairs={{0,24},{2,26},{4,28},{6,30},{8,0},{10,2},{12,4},{14,6},{16,8},{18,... | collective-permute-start | bytes 393224 | tf_op jit(solution)/shard_map/ppermute | solution.py:582
  264.8 13.2 %collective-permute-start.34 = (bf16[4,64,1024]{2,1,0:T(8,128)(2,1)S(1)}, bf16[4,64,1024]{2,1,0:T(8,128)(2,1)S(1)}, u32[]{:S(2)}, u32[]{:S(2)}) collective-permute-start(bf16[4,64,1024]{2,1,0:T(8,128)(2,1)S(1)} %pad_maximum_fusion.refs_0_), channel_id=1, source_target_pairs={{0,6},{2,4},{4,2},{6,0},{8,14},{10,12},{12,10},{14,8},{16,22},{18,... | collective-permute-start | bytes 1572872 | tf_op jit(solution)/shard_map/ppermute | solution.py:579
  266.7 24.2 %collective-permute-start.32 = (bf16[4,64,1024]{2,1,0:T(8,128)(2,1)S(1)}, bf16[4,64,1024]{2,1,0:T(8,128)(2,1)S(1)}, u32[]{:S(2)}, u32[]{:S(2)}) collective-permute-start(bf16[4,64,1024]{2,1,0:T(8,128)(2,1)S(1)} %pad_maximum_fusion.refs_0_), channel_id=1, source_target_pairs={{0,4},{2,6},{4,0},{6,2},{8,12},{10,14},{12,8},{14,10},{16,20},{18,... | collective-permute-start | bytes 1572872 | tf_op jit(solution)/shard_map/ppermute | solution.py:579
  266.9 24.5 %collective-permute-start.30 = (bf16[4,64,1024]{2,1,0:T(8,128)(2,1)S(1)}, bf16[4,64,1024]{2,1,0:T(8,128)(2,1)S(1)}, u32[]{:S(2)}, u32[]{:S(2)}) collective-permute-start(bf16[4,64,1024]{2,1,0:T(8,128)(2,1)S(1)} %pad_maximum_fusion.refs_0_), channel_id=1, source_target_pairs={{0,2},{2,0},{4,6},{6,4},{8,10},{10,8},{12,14},{14,12},{16,18},{18,... | collective-permute-start | bytes 1572872 | tf_op jit(solution)/shard_map/ppermute | solution.py:579
  267.5 24.7 %collective-permute-start.29 = (bf16[4,64,1024]{2,1,0:T(8,128)(2,1)S(1)}, bf16[4,64,1024]{2,1,0:T(8,128)(2,1)S(1)}, u32[]{:S(2)}, u32[]{:S(2)}) collective-permute-start(bf16[4,64,1024]{2,1,0:T(8,128)(2,1)S(1)} %pad_maximum_fusion.refs_0_), channel_id=1, source_target_pairs={{0,1},{1,0},{2,3},{3,2},{4,5},{5,4},{6,7},{7,6},{8,9},{9,8},{10,11... | collective-permute-start | bytes 1572872 | tf_op jit(solution)/shard_map/ppermute | solution.py:585
  278.0 14.2 %collective-permute-start.35 = (bf16[4,64,1024]{2,1,0:T(8,128)(2,1)S(1)}, bf16[4,64,1024]{2,1,0:T(8,128)(2,1)S(1)}, u32[]{:S(2)}, u32[]{:S(2)}) collective-permute-start(bf16[4,64,1024]{2,1,0:T(8,128)(2,1)S(1)} %collective-permute-done.34.refs_6_), channel_id=1, source_target_pairs={{0,1},{1,0},{2,3},{3,2},{4,5},{5,4},{6,7},{7,6},{8,9},{9,8},{10,11... | collective-permute-start | bytes 1572872 | tf_op jit(solution)/shard_map/ppermute | solution.py:585
  (42 other events, 266.9 us)

commit v6 on v5

--- a/solution.py
+++ b/solution.py
@@ -25,56 +25,6 @@
 
 def dot(a, b, ca=1, cb=0):
     return lax.dot_general(a, b, (((ca,), (cb,)), ((), ())), preferred_element_type=jnp.float32)
-
-
-def cut_kernel(first, rows, columns, by_core, place_ref, source_ref, *refs):
-    out_ref, done = refs[-2:]
-    start = pl.multiple_of(place_ref[2] * rows, 16) if by_core else first
-    copy = pltpu.make_async_copy(
-        source_ref.at[pl.ds(start, rows), columns[0] : columns[1]], out_ref, done
-    )
-    copy.start()
-    copy.wait()
-
-
-def cut(place, source, first, rows, columns, after, by_core=False):
-    anywhere = pl.BlockSpec(memory_space=pl.ANY)
-    return pl.pallas_call(
-        functools.partial(cut_kernel, first, rows, columns, by_core),
-        out_shape=jax.ShapeDtypeStruct((rows, columns[1] - columns[0]), source.dtype),
-        in_specs=[SMEM] + [anywhere] * (1 + len(after)),
-        out_specs=VMEM,
-        scratch_shapes=[pltpu.SemaphoreType.DMA],
-        name="cut_block",
-    )(place, source, *after)
-
-
-def pack_kernel(count, *refs):
-    out_ref, done = refs[-2:]
-    copies, start = [], 0
-    for i, ref in enumerate(refs[:count]):
-        rows = ref.shape[0]
-        copies.append(
-            pltpu.make_async_copy(ref, out_ref.at[start : start + rows, :], done.at[i])
-        )
-        start += rows
-    for copy in copies:
-        copy.start()
-    for copy in copies:
-        copy.wait()
-
-
-def pack(arrays, after):
-    anywhere = pl.BlockSpec(memory_space=pl.ANY)
-    rows = sum(array.shape[0] for array in arrays)
-    return pl.pallas_call(
-        functools.partial(pack_kernel, len(arrays)),
-        out_shape=jax.ShapeDtypeStruct((rows, arrays[0].shape[1]), arrays[0].dtype),
-        in_specs=[anywhere] * (len(arrays) + len(after)),
-        out_specs=VMEM,
-        scratch_shapes=[pltpu.SemaphoreType.DMA((len(arrays),))],
-        name="pack_blocks",
-    )(*arrays, *after)
 
 
 def compose_kernel(store_rows, groups, capacity, place_ref, adj_ref, table_ref, near_ref, ids_ref, column_ref):
@@ -165,11 +115,10 @@
     classes = lax.broadcasted_iota(jnp.int32, (fan + 1, near_rows), 0)
 
     def turn(row):
-        half = store_rows // 2
         distance, slot = lax.bitwise_xor(row // store_rows, mine), row % store_rows
-        core, inner = slot // half, slot % half
-        other = jnp.where(core == rep, 0, (PLANE - 1) * half)
-        return jnp.where(distance == 0, slot, (distance + 1) * half + other + inner)
+        turned = slot + rep * (store_rows // 2)
+        turned = jnp.where(turned >= store_rows, turned - store_rows, turned)
+        return distance * store_rows + jnp.where(distance == 0, slot, turned)
 
     for ids_ref, out_ref in zip(ids_refs, out_refs):
         gid = ids_ref[:fan, :]
@@ -223,7 +172,7 @@
     )(place, *ids_all)
 
 
-def partial_kernel(count, columns, places, capacity, block, *refs):
+def partial_kernel(count, places, capacity, block, *refs):
     index_refs, piece_refs = refs[:count], refs[count : count + len(places)]
     out_ref, table, sums, kept = refs[-5 - len(places) : -1 - len(places)]
     buffers = refs[-1 - len(places) : -1]
@@ -242,10 +191,9 @@
             rows = [a + b for a, b in zip(rows[0::2], rows[1::2])] + odd
         return rows[0]
 
-    sources = [piece_refs[0].at[:, columns[0] : columns[1]]] + list(piece_refs[1:])
     copies = [
         pltpu.make_async_copy(source, buffer, arrived.at[i])
-        for i, (source, buffer) in enumerate(zip(sources, buffers))
+        for i, (source, buffer) in enumerate(zip(piece_refs, buffers))
     ]
     for copy in copies:
         copy.start()
@@ -299,32 +247,31 @@
             ].astype(jnp.bfloat16)
 
 
-def partial_sums(lists, pieces, places, columns, total, capacity, block, after):
+def partial_sums(lists, pieces, places, total, capacity, block):
     near_rows = lists[0].shape[1]
-    width = columns[1] - columns[0]
-    rows = [piece.shape[0] for piece in pieces]
+    width = pieces[0].shape[1]
     return pl.pallas_call(
-        functools.partial(partial_kernel, len(lists), columns, places, capacity, block),
+        functools.partial(partial_kernel, len(lists), places, capacity, block),
         out_shape=jax.ShapeDtypeStruct((len(lists), near_rows + capacity, width), jnp.bfloat16),
-        in_specs=[SMEM] * len(lists) + [pl.BlockSpec(memory_space=pl.ANY)] * (len(pieces) + len(after)),
+        in_specs=[SMEM] * len(lists) + [pl.BlockSpec(memory_space=pl.ANY)] * len(pieces),
         out_specs=VMEM,
         scratch_shapes=[
             pltpu.VMEM(((total + 1) * 8, LANES), jnp.float32),
             pltpu.VMEM(((near_rows + 1) * 8, LANES), jnp.float32),
             pltpu.VMEM(((capacity + 1) * 8, LANES), jnp.float32),
         ]
-        + [pltpu.VMEM((count, width), jnp.bfloat16) for count in rows]
+        + [pltpu.VMEM(piece.shape, piece.dtype) for piece in pieces]
         + [pltpu.SemaphoreType.DMA((len(pieces),))],
-        compiler_params=pltpu.CompilerParams(vmem_limit_bytes=52 * MIB),
+        compiler_params=pltpu.CompilerParams(vmem_limit_bytes=60 * MIB),
         name="partial_sums",
-    )(*lists, *pieces, *after)
+    )(*lists, *pieces)
 
 
 def trainer_kernel(sizes, scale, *refs):
     groups, rows_low, rows_top, classes, class_pad = sizes
     place_ref, labels_ref, adj_ref, column_ref, wl_ref, wt_ref = refs[:6]
-    block_refs = refs[6:-8]
-    logits_ref, keep_ref, send_ref, li, hidden, slope, top_in, wt = refs[-8:]
+    block_refs = refs[6:-10]
+    logits_ref, keep_ref, send_ref, li, hidden, slope, top_in, wt, weights, arrived = refs[-10:]
     seeds, fan_top = adj_ref.shape
     near_rows, low_width = li.shape
     feat = low_width // 2
@@ -333,6 +280,8 @@
     here, mine, rep = place_ref[0], place_ref[1], place_ref[2]
     fan_low = place_ref[3].astype(jnp.float32)
 
+    bring = pltpu.make_async_copy(wl_ref, weights, arrived)
+    bring.start()
     column = column_ref[...]
     rows_cap = lax.broadcasted_iota(jnp.int32, (capacity, near_rows), 0)
     marks = [
@@ -354,11 +303,12 @@
     wt[...] = jnp.zeros_like(wt)
     wt[:, :classes] = wt_ref[...].astype(jnp.bfloat16)
 
+    bring.wait()
     factor = math.sqrt(2.0 / math.pi)
     step = 256
     for c in range(width // step):
         cols = slice(c * step, (c + 1) * step)
-        v = dot(li[...], wl_ref[:, cols].astype(jnp.bfloat16))
+        v = dot(li[...], weights[:, cols].astype(jnp.bfloat16))
         square = v * v
         t = jnp.tanh(factor * (v + 0.044715 * v * square))
         half = 0.5 * (1.0 + t)
@@ -435,7 +385,7 @@
             jax.ShapeDtypeStruct((PLANE, groups, rows, width), jnp.float32),
             jax.ShapeDtypeStruct((PLANE, groups, rows, width), jnp.bfloat16),
         ),
-        in_specs=[SMEM] + [VMEM] * (5 + len(blocks)),
+        in_specs=[SMEM] + [VMEM] * 3 + [pl.BlockSpec(memory_space=pl.ANY)] + [VMEM] * (1 + len(blocks)),
         out_specs=(VMEM, VMEM, VMEM),
         scratch_shapes=[
             pltpu.VMEM((near_rows, low_width), jnp.bfloat16),
@@ -443,6 +393,8 @@
             pltpu.VMEM((near_rows, width), jnp.float32),
             pltpu.VMEM((seeds, 2 * width), jnp.bfloat16),
             pltpu.VMEM((2 * width, class_pad), jnp.bfloat16),
+            pltpu.VMEM((low_width, width), jnp.float32),
+            pltpu.SemaphoreType.DMA,
         ],
         compiler_params=pltpu.CompilerParams(vmem_limit_bytes=60 * MIB),
         name="trainer_step",
@@ -496,50 +448,46 @@
 def apply_kernel(sizes, place_ref, wl, wt, *refs):
     groups, rows_low, rows_top, classes, class_pad = sizes
     delta_refs, (nl, nt) = refs[: 2 * PLANE], refs[2 * PLANE :]
-    here, mine, rep = place_ref[0], place_ref[1], place_ref[2]
-    width = wl.shape[-1]
-    lane_groups = width // class_pad
+    here = place_ref[0]
+    lane_groups = wl.shape[-1] // class_pad
     sub = rows_top // lane_groups
-    for d in range(PLANE):
-        for half in range(2):
+    for turn, delta_ref in enumerate(delta_refs):
+
+        @pl.when(pl.program_id(0) == turn)
+        def _():
             for k in range(groups):
                 plane = here + k
                 plane = jnp.where(plane >= groups, plane - groups, plane)
-                store = plane * PLANE + lax.bitwise_xor(mine, jnp.int32(d))
-                core = rep if half == 0 else 1 - rep
-                position = store * 2 + core
-                delta = delta_refs[2 * d + half][k].astype(jnp.float32)
-                if len(wl.shape) == 2:
-                    rows = pl.ds(pl.multiple_of(position * rows_low, 8), rows_low)
-                    nl[rows, :] = wl[rows, :] - delta[:rows_low]
-                else:
-                    nl[position] = wl[position] - delta[:rows_low]
+                delta = delta_ref[k].astype(jnp.float32)
+                nl[plane, 0, 0] = wl[plane, 0, 0] - delta[:rows_low]
                 for g in range(lane_groups):
+                    rows = slice(g * sub, (g + 1) * sub)
                     step = delta[rows_low:, g * class_pad : g * class_pad + classes]
-                    if len(wt.shape) == 2:
-                        rows = pl.ds(pl.multiple_of(position * rows_top + g * sub, 8), sub)
-                        nt[rows, :] = wt[rows, :] - step
-                    else:
-                        rows = slice(g * sub, (g + 1) * sub)
-                        nt[position, rows, :] = wt[position, rows, :] - step
+                    nt[plane, 0, 0, rows, :] = wt[plane, 0, 0, rows, :] - step
 
 
 def apply_updates(place, wl, wt, deltas, sizes):
     groups, rows_low, rows_top, classes, class_pad = sizes
-    sub = rows_top * class_pad // wl.shape[1]
-    low3 = wl if rows_low % 8 == 0 else wl.reshape(-1, rows_low, wl.shape[1])
-    top3 = wt if sub % 8 == 0 else wt.reshape(-1, rows_top, wt.shape[1])
+    low = wl.reshape(groups, PLANE, 2, rows_low, wl.shape[1])
+    top = wt.reshape(groups, PLANE, 2, rows_top, wt.shape[1])
+
+    def spot(turn, place_ref):
+        core = jnp.where(turn % 2 == 0, place_ref[2], 1 - place_ref[2])
+        return (0, lax.bitwise_xor(place_ref[1], turn // 2), core, 0, 0)
+
+    specs = [pl.BlockSpec((groups, 1, 1) + a.shape[3:], spot) for a in (low, top)]
     nl, nt = pl.pallas_call(
         functools.partial(apply_kernel, sizes),
-        out_shape=(
-            jax.ShapeDtypeStruct(low3.shape, jnp.float32),
-            jax.ShapeDtypeStruct(top3.shape, jnp.float32),
+        grid_spec=pltpu.PrefetchScalarGridSpec(
+            num_scalar_prefetch=1,
+            grid=(2 * PLANE,),
+            in_specs=specs + [VMEM] * len(deltas),
+            out_specs=specs,
         ),
-        in_specs=[SMEM] + [VMEM] * (2 + len(deltas)),
-        out_specs=(VMEM, VMEM),
-        compiler_params=pltpu.CompilerParams(vmem_limit_bytes=60 * MIB),
+        out_shape=[jax.ShapeDtypeStruct(a.shape, jnp.float32) for a in (low, top)],
+        compiler_params=pltpu.CompilerParams(vmem_limit_bytes=32 * MIB),
         name="apply_updates",
-    )(place, low3, top3, *deltas)
+    )(place, low, top, *deltas)
     return nl.reshape(wl.shape), nt.reshape(wt.shape)
 
 
@@ -584,6 +532,10 @@
     def sibling(x):
         return lax.ppermute(x, "rep", [(0, 1), (1, 0)])
 
+    quarter = half // 2
+    own = lax.dynamic_slice_in_dim(features, rep * half, half, 0)
+    from_x, from_y = across(own, 1), across(own, 2)
+
     gid_near = owners_near[:, 0] * store_rows + slots_near[:, 0]
     gid_far = owners_far[:, 0] * store_rows + slots_far[:, 0]
     table = jnp.concatenate([gid_near, gid_far]).reshape(-1, LANES)
@@ -595,39 +547,17 @@
     block = 16
     lists = row_lists(place, ids_all, store_rows, fan, capacity, block)
 
-    share = features.shape[1] // 2
-    quarter = half // 2
-    places = [0, store_rows, store_rows + 3 * half]
-    far = groups // 2
-    calls = [[far], [k for k in range(1, groups) if k != far], [0]]
-    blocks, pieces, waits = {}, (), ()
-    first, second = (lists[0],), ()
-    for part in range(2):
-        columns, whole = (part * share, (part + 1) * share), (0, share)
-        own = cut(place, features, 0, half, columns, pieces[1:], True)
-        from_x, from_y = across(own, 1), across(own, 2)
-        corner_a = across(cut(place, from_x, 0, quarter, whole, first), 2)
-        corner_b = across(cut(place, from_y, quarter, quarter, whole, first), 1)
-        brought = pack([from_x, from_y, corner_a, corner_b], second)
-        pieces = (features, brought, sibling(brought))
-        for turns in calls:
-            made = partial_sums(
-                [lists[k] for k in turns],
-                pieces,
-                places,
-                columns,
-                PLANE * store_rows,
-                capacity,
-                block,
-                waits,
-            )
-            waits = (made,)
-            for i, k in enumerate(turns):
-                blocks[part, k] = along(made[i], k) if k else made[i]
-            if turns == calls[0]:
-                first, second = (made,), (blocks[part, far],)
-            if turns == calls[1]:
-                second += (made,)
+    from_x, from_y, lists = lax.optimization_barrier((from_x, from_y, lists))
+    corner_a, corner_b = across(from_x[:quarter], 2), across(from_y[quarter:], 1)
+    pieces = [features, from_x, sibling(from_x), from_y, sibling(from_y)]
+    pieces += [corner_a, corner_b, sibling(corner_a), sibling(corner_b)]
+    places = [0, store_rows, store_rows + half, 2 * store_rows, 2 * store_rows + half]
+    places += [3 * store_rows + quarter * i for i in range(4)]
+
+    blocks = []
+    for k in range(groups):
+        made = partial_sums([lists[k]], pieces, places, PLANE * store_rows, capacity, block)
+        blocks.append(along(made[0], k) if k else made[0])
 
     scale = 1.0 / (labels.shape[0] * members)
     logits, keep, send = trainer_step(
@@ -637,7 +567,7 @@
         column,
         weights_low,
         weights_top,
-        [blocks[part, k] for part in range(2) for k in range(groups)],
+        blocks,
         sizes,
         scale,
     )

time: 305 us -> 305 us (level)
  waiting for transfers between devices: 104 us -> 150 us
  Pallas kernels: 127 us -> 87.4 us
  starting transfers between devices: 47.9 us -> 42.8 us
    pallas_call x15 -> x5, Pallas kernels: 105 us -> 66.4 us  [the longest x4 59.3 us: partial_sums(): pl.pallas_call(functools.partial(partial_kernel, len(lists), places, capa...]
    ppermute x15 -> x12, waiting for transfers between devices: 41.6 us -> 73.6 us  [along(): lax.ppermute(x, 'store', [(i, (i + hops * PLANE) % stores) for i in range...]
    ppermute x14 -> x10, waiting for transfers between devices: 52.6 us -> 69.2 us  [across(): return lax.ppermute(x, 'store', [(i, i ^ distance) for i in range(stores)])]
    ppermute x15 -> x12, starting transfers between devices: 22.8 us -> 17.8 us  [along(): lax.ppermute(x, 'store', [(i, (i + hops * PLANE) % stores) for i in range...]
    unnamed x80 -> x62, local copies, waits for them, and re-layouts: 18 us -> 13.5 us
    ppermute x14 -> x10, starting transfers between devices: 13.7 us -> 9.59 us  [across(): return lax.ppermute(x, 'store', [(i, i ^ distance) for i in range(stores)])]
    ppermute x7 -> x9, starting transfers between devices: 11.5 us -> 15.4 us  [sibling(): return lax.ppermute(x, 'rep', [(0, 1), (1, 0)])]
    ppermute x7 -> x9, waiting for transfers between devices: 9.93 us -> 7.41 us  [sibling(): return lax.ppermute(x, 'rep', [(0, 1), (1, 0)])]
  transfers between devices with their start and end apart: 36 -> 31, of which waited for: 21 -> 21; matrix products, arithmetic and copies ran while one was open for 2% -> 2% of each run, Pallas kernels for 29% -> 17%
where the time goes in v6:
time: 305 us; the launch traced here: 303 us
  waiting for transfers between devices  150 us (49%)
  Pallas kernels  87.4 us (29%)
  starting transfers between devices  42.8 us (14%)
  local copies, waits for them, and re-layouts  18.5 us (6%)
  other arithmetic  3.62 us (1%)
    ppermute x12, waiting for transfers between devices, along(): lax.ppermute(x, 'store', [(i, (i + hops * PLANE) % stores) for i in range...  73.6 us
    ppermute x10, waiting for transfers between devices, across(): return lax.ppermute(x, 'store', [(i, i ^ distance) for i in range(stores)])  69.2 us
    pallas_call x4, Pallas kernels, partial_sums(): pl.pallas_call(functools.partial(partial_kernel, len(lists), places, capa...  59.3 us
    ppermute x12, starting transfers between devices, along(): lax.ppermute(x, 'store', [(i, (i + hops * PLANE) % stores) for i in range...  17.8 us
    ppermute x9, starting transfers between devices, sibling(): return lax.ppermute(x, 'rep', [(0, 1), (1, 0)])  15.4 us
    pallas_call x1, Pallas kernels, trainer_step(): pl.pallas_call(functools.partial(trainer_kernel, sizes, scale), out_shape...  14.5 us
    unnamed x62, local copies, waits for them, and re-layouts  13.5 us
    ppermute x10, starting transfers between devices, across(): return lax.ppermute(x, 'store', [(i, i ^ distance) for i in range(stores)])  9.59 us
  transfers between devices with their start and end apart: 31, of which 21 were waited for; matrix products, arithmetic and copies ran while one was open for 2% of the time, Pallas kernels for 17%

profile of v6, /device:TPU:9, one launch (start us, length us, event | category | flops | bytes accessed | tf_op | source)
XLA Modules:
  0.0 303.4 jit_solution(9267683236225164834)
XLA Ops:
  0.7 2.7 constant_dynamic-slice_fusion
  6.1 2.8 compose_ids.1
  16.0 2.8 row_lists.1
  21.3 17.6 %collective-permute-done.1.refs_4_ = bf16[1024,768]{1,0:T(8,128)(2,1)S(1)} collective-permute-done((bf16[1024,768]{1,0:T(8,128)(2,1)}, bf16[1024,768]{1,0:T(8,128)(2,1)S(1)}, u32[]{:S(2)}, u32[]{:S(2)}) %collective-permute-start.1) | collective-permute-done | bytes 1572896 | tf_op jit(solution)/shard_map/ppermute | solution.py:527
  42.8 2.3 collective-permute-start.5
  45.1 12.1 %collective-permute-done.8.refs_7_ = bf16[512,768]{1,0:T(8,128)(2,1)S(1)} collective-permute-done((bf16[512,768]{1,0:T(8,128)(2,1)S(1)}, bf16[512,768]{1,0:T(8,128)(2,1)S(1)}, u32[]{:S(2)}, u32[]{:S(2)}) %collective-permute-start.8) | collective-permute-done | bytes 786464 | tf_op jit(solution)/shard_map/ppermute | solution.py:527
  57.2 2.8 collective-permute-start.10
  60.0 2.5 collective-permute-start.9
  65.2 14.8 %partial_sums.5 = bf16[1,768,768]{2,1,0:T(8,128)(2,1)} custom-call(s32[18,512]{1,0:T(8,128)} %copy-done.10, bf16[2048,768]{1,0:T(8,128)(2,1)} %refs_1_.7, bf16[1024,768]{1,0:T(8,128)(2,1)} %collective-permute-done.refs_2_, bf16[1024,768]{1,0:T(8,128)(2,1)} %collective-permute-done.5.refs_3_, bf16[1024,768]{1,0:T(8,128)(2,1)} %copy-done.15, ...), custom_call_target="tpu_custom_call" | custom-call | tf_op jit(solution)/shard_map/partial_sums/pallas_call | solution.py:253
  80.1 2.3 collective-permute-start.11
  82.3 15.0 %partial_sums.6 = bf16[1,768,768]{2,1,0:T(8,128)(2,1)} custom-call(s32[18,512]{1,0:T(8,128)} %copy-done.9, bf16[2048,768]{1,0:T(8,128)(2,1)} %refs_1_.7, bf16[1024,768]{1,0:T(8,128)(2,1)} %collective-permute-done.refs_2_, bf16[1024,768]{1,0:T(8,128)(2,1)} %collective-permute-done.5.refs_3_, bf16[1024,768]{1,0:T(8,128)(2,1)} %copy-done.15, ...), custom_call_target="tpu_custom_call" | custom-call | tf_op jit(solution)/shard_map/partial_sums/pallas_call | solution.py:253
  97.4 2.2 collective-permute-start.12
  99.6 14.8 %partial_sums.7 = bf16[1,768,768]{2,1,0:T(8,128)(2,1)} custom-call(s32[18,512]{1,0:T(8,128)} %copy-done.8, bf16[2048,768]{1,0:T(8,128)(2,1)} %refs_1_.7, bf16[1024,768]{1,0:T(8,128)(2,1)} %collective-permute-done.refs_2_, bf16[1024,768]{1,0:T(8,128)(2,1)} %collective-permute-done.5.refs_3_, bf16[1024,768]{1,0:T(8,128)(2,1)} %copy-done.15, ...), custom_call_target="tpu_custom_call" | custom-call | tf_op jit(solution)/shard_map/partial_sums/pallas_call | solution.py:253
  114.4 2.6 collective-permute-start.13
  120.3 14.7 %partial_sums.4 = bf16[1,768,768]{2,1,0:T(8,128)(2,1)} custom-call(s32[18,512]{1,0:T(8,128)} %copy-done.7, bf16[2048,768]{1,0:T(8,128)(2,1)} %refs_1_.7, bf16[1024,768]{1,0:T(8,128)(2,1)} %collective-permute-done.refs_2_, bf16[1024,768]{1,0:T(8,128)(2,1)} %collective-permute-done.5.refs_3_, bf16[1024,768]{1,0:T(8,128)(2,1)} %copy-done.15, ...), custom_call_target="tpu_custom_call" | custom-call | tf_op jit(solution)/shard_map/partial_sums/pallas_call | solution.py:253
  135.1 48.6 %collective-permute-done.12.refs_8_ = bf16[768,768]{1,0:T(8,128)(2,1)} collective-permute-done((bf16[768,768]{1,0:T(8,128)(2,1)}, bf16[768,768]{1,0:T(8,128)(2,1)}, u32[]{:S(2)}, u32[]{:S(2)}) %collective-permute-start.12) | collective-permute-done | bytes 1179680 | tf_op jit(solution)/shard_map/ppermute | solution.py:530
  183.7 2.7 collective-permute-done.13.refs_9_
  186.3 14.5 %trainer_step.1 = (f32[128,153]{1,0:T(8,128)}, f32[4,4,64,1024]{3,2,1,0:T(8,128)}, bf16[4,4,64,1024]{3,2,1,0:T(8,128)(2,1)}) custom-call(s32[4]{0:T(128)} %copy-done.12, s32[128,1]{1,0:T(8,128)} %copy.28.refs_1_, s32[128,10]{1,0:T(8,128)} %copy.29.refs_2_, s32[1,512]{1,0:T(1,128)} %copy-done.14, f32[1536,1024]{1,0:T(8,128)} %refs_4_.2, ...), custom_call_target="tpu_custom_call" | custom-call | tf_op jit(solution)/shard_map/trainer_step/pallas_call | solution.py:381
  201.4 4.0 %collective-permute-done.14 = bf16[4,4,64,1024]{3,2,1,0:T(8,128)(2,1)S(1)} collective-permute-done((bf16[4,4,64,1024]{3,2,1,0:T(8,128)(2,1)}, bf16[4,4,64,1024]{3,2,1,0:T(8,128)(2,1)S(1)}, u32[]{:S(2)}, u32[]{:S(2)}) %collective-permute-start.14) | collective-permute-done | bytes 2097184 | tf_op jit(solution)/shard_map/ppermute | solution.py:533
  205.4 3.1 %fusion.3 = (bf16[4,4,64,1024]{3,2,1,0:T(8,128)(2,1)S(1)}, f32[4,4,64,1024]{3,2,1,0:T(8,128)S(1)}) fusion(f32[4,4,64,1024]{3,2,1,0:T(8,128)} %get-tuple-element.42, bf16[4,4,64,1024]{3,2,1,0:T(8,128)(2,1)S(1)} %collective-permute-done.14), kind=kLoop, calls=%fused_computation.18 | loop fusion | flops 3145728 | bytes 12582912 | tf_op jit(solution)/shard_map/convert.5
  211.3 10.5 %collective-permute-done.15 = bf16[4,64,1024]{2,1,0:T(8,128)(2,1)S(1)} collective-permute-done((bf16[4,64,1024]{2,1,0:T(8,128)(2,1)S(1)}, bf16[4,64,1024]{2,1,0:T(8,128)(2,1)S(1)}, u32[]{:S(2)}, u32[]{:S(2)}) %collective-permute-start.15) | collective-permute-done | bytes 524320 | tf_op jit(solution)/shard_map/ppermute | solution.py:527
  221.8 11.1 %collective-permute-done.17 = bf16[4,64,1024]{2,1,0:T(8,128)(2,1)S(1)} collective-permute-done((bf16[4,64,1024]{2,1,0:T(8,128)(2,1)S(1)}, bf16[4,64,1024]{2,1,0:T(8,128)(2,1)S(1)}, u32[]{:S(2)}, u32[]{:S(2)}) %collective-permute-start.17) | collective-permute-done | bytes 524320 | tf_op jit(solution)/shard_map/ppermute | solution.py:527
  234.4 2.3 collective-permute-start.18
  239.7 5.4 %collective-permute-done.18.refs_1_ = bf16[64,1024]{1,0:T(8,128)(2,1)S(1)} collective-permute-done((bf16[64,1024]{1,0:T(8,128)(2,1)S(1)}, bf16[64,1024]{1,0:T(8,128)(2,1)S(1)}, u32[]{:S(2)}, u32[]{:S(2)}) %collective-permute-start.18) | collective-permute-done | bytes 131104 | tf_op jit(solution)/shard_map/ppermute | solution.py:530
  251.2 7.6 %collective-permute-done.22 = bf16[64,1024]{1,0:T(8,128)(2,1)S(1)} collective-permute-done((bf16[64,1024]{1,0:T(8,128)(2,1)S(1)}, bf16[64,1024]{1,0:T(8,128)(2,1)S(1)}, u32[]{:S(2)}, u32[]{:S(2)}) %collective-permute-start.22) | collective-permute-done | bytes 131104 | tf_op jit(solution)/shard_map/ppermute | solution.py:530
  260.2 2.3 collective-permute-start.29
  265.2 8.1 %collective-permute-done.29.refs_6_ = bf16[4,64,1024]{2,1,0:T(8,128)(2,1)S(1)} collective-permute-done((bf16[4,64,1024]{2,1,0:T(8,128)(2,1)S(1)}, bf16[4,64,1024]{2,1,0:T(8,128)(2,1)S(1)}, u32[]{:S(2)}, u32[]{:S(2)}) %collective-permute-start.29) | collective-permute-done | bytes 524320 | tf_op jit(solution)/shard_map/ppermute | solution.py:527
  273.3 4.2 %collective-permute-start.30 = (bf16[4,64,1024]{2,1,0:T(8,128)(2,1)S(1)}, bf16[4,64,1024]{2,1,0:T(8,128)(2,1)}, u32[]{:S(2)}, u32[]{:S(2)}) collective-permute-start(bf16[4,64,1024]{2,1,0:T(8,128)(2,1)S(1)} %collective-permute-done.29.refs_6_), channel_id=1, source_target_pairs={{0,1},{1,0},{2,3},{3,2},{4,5},{5,4},{6,7},{7,6},{8,9},{9,8},{10,11... | collective-permute-start | bytes 1572872 | tf_op jit(solution)/shard_map/ppermute | solution.py:533
  277.5 8.9 %collective-permute-done.27.refs_4_ = bf16[4,64,1024]{2,1,0:T(8,128)(2,1)} collective-permute-done((bf16[4,64,1024]{2,1,0:T(8,128)(2,1)S(1)}, bf16[4,64,1024]{2,1,0:T(8,128)(2,1)}, u32[]{:S(2)}, u32[]{:S(2)}) %collective-permute-start.27) | collective-permute-done | bytes 524320 | tf_op jit(solution)/shard_map/ppermute | solution.py:527
  289.5 2.8 copy-done
  292.3 7.1 %apply_updates.1 = (f32[4,4,2,48,1024]{4,3,2,1,0:T(8,128)}, f32[4,4,2,64,153]{4,3,2,1,0:T(8,128)S(1)}) custom-call(s32[4]{0:T(128)S(1)} %copy-done.13, f32[4,4,2,48,1024]{4,3,2,1,0:T(8,128)S(1)} %bitcast.43, f32[4,4,2,64,153]{4,3,2,1,0:T(8,128)S(1)} %bitcast.44, bf16[4,64,1024]{2,1,0:T(8,128)(2,1)S(1)} %pad_maximum_fusion.refs_0_, ...), custom_call_target="tpu_custom_call" | custom-call | tf_op jit(solution)/shard_map/apply_updates/pallas_call | solution.py:479
  300.7 2.7 copy.33
  (117 shorter events, 44.6 us)
Async XLA Ops:
  3.4 35.6 %collective-permute-start.1 = (bf16[1024,768]{1,0:T(8,128)(2,1)}, bf16[1024,768]{1,0:T(8,128)(2,1)S(1)}, u32[]{:S(2)}, u32[]{:S(2)}) collective-permute-start(bf16[1024,768]{1,0:T(8,128)(2,1)} %constant_dynamic-slice_fusion), channel_id=1, source_target_pairs={{0,4},{2,6},{4,0},{6,2},{8,12},{10,14},{12,8},{14,10},{16,20},{18,... | collective-permute-start | bytes 4718600 | tf_op jit(solution)/shard_map/ppermute | solution.py:527
  4.6 35.3 %collective-permute-start = (bf16[1024,768]{1,0:T(8,128)(2,1)}, bf16[1024,768]{1,0:T(8,128)(2,1)}, u32[]{:S(2)}, u32[]{:S(2)}) collective-permute-start(bf16[1024,768]{1,0:T(8,128)(2,1)} %constant_dynamic-slice_fusion), channel_id=1, source_target_pairs={{0,2},{2,0},{4,6},{6,4},{8,10},{10,8},{12,14},{14,12},{16,18},{18,... | collective-permute-start | bytes 4718600 | tf_op jit(solution)/shard_map/ppermute | solution.py:527
  6.1 74.0 %copy-start.12 = (s32[4]{0:T(128)}, s32[4]{0:T(128)S(1)}, u32[]{:S(2)}) copy-start(s32[4]{0:T(128)S(1)} %pad_add_fusion.place_ref.refs_0_) | copy-start | bytes 52
  8.9 3.8 %collective-permute-start.4 = (s32[17,512]{1,0:T(8,128)S(1)}, s32[17,512]{1,0:T(8,128)S(1)}, u32[]{:S(2)}, u32[]{:S(2)}) collective-permute-start(s32[17,512]{1,0:T(8,128)S(1)} %get-tuple-element.30.refs_0_), channel_id=1, source_target_pairs={{0,8},{2,10},{4,12},{6,14},{8,16},{10,18},{12,20},{14,22},{16,24},... | collective-permute-start | bytes 104456 | tf_op jit(solution)/shard_map/ppermute | solution.py:530
  10.3 4.1 %collective-permute-start.3 = (s32[17,512]{1,0:T(8,128)S(1)}, s32[17,512]{1,0:T(8,128)S(1)}, u32[]{:S(2)}, u32[]{:S(2)}) collective-permute-start(s32[17,512]{1,0:T(8,128)S(1)} %get-tuple-element.30.refs_0_), channel_id=1, source_target_pairs={{0,16},{2,18},{4,20},{6,22},{8,24},{10,26},{12,28},{14,30},{16,0},... | collective-permute-start | bytes 104456 | tf_op jit(solution)/shard_map/ppermute | solution.py:530
  11.4 4.6 %collective-permute-start.2 = (s32[17,512]{1,0:T(8,128)S(1)}, s32[17,512]{1,0:T(8,128)S(1)}, u32[]{:S(2)}, u32[]{:S(2)}) collective-permute-start(s32[17,512]{1,0:T(8,128)S(1)} %get-tuple-element.30.refs_0_), channel_id=1, source_target_pairs={{0,24},{2,26},{4,28},{6,30},{8,0},{10,2},{12,4},{14,6},{16,8},{18,... | collective-permute-start | bytes 104456 | tf_op jit(solution)/shard_map/ppermute | solution.py:530
  39.9 17.2 %collective-permute-start.8 = (bf16[512,768]{1,0:T(8,128)(2,1)S(1)}, bf16[512,768]{1,0:T(8,128)(2,1)S(1)}, u32[]{:S(2)}, u32[]{:S(2)}) collective-permute-start(bf16[512,768]{1,0:T(8,128)(2,1)S(1)} %slice.37), channel_id=1, source_target_pairs={{0,2},{2,0},{4,6},{6,4},{8,10},{10,8},{12,14},{14,12},{16,18},{18,... | collective-permute-start | bytes 2359304 | tf_op jit(solution)/shard_map/ppermute | solution.py:527
  42.4 17.6 %collective-permute-start.7 = (bf16[512,768]{1,0:T(8,128)(2,1)S(1)}, bf16[512,768]{1,0:T(8,128)(2,1)S(1)}, u32[]{:S(2)}, u32[]{:S(2)}) collective-permute-start(bf16[512,768]{1,0:T(8,128)(2,1)S(1)} %slice.36), channel_id=1, source_target_pairs={{0,4},{2,6},{4,0},{6,2},{8,12},{10,14},{12,8},{14,10},{16,20},{18,... | collective-permute-start | bytes 2359304 | tf_op jit(solution)/shard_map/ppermute | solution.py:527
  42.8 21.6 %collective-permute-start.5 = (bf16[1024,768]{1,0:T(8,128)(2,1)}, bf16[1024,768]{1,0:T(8,128)(2,1)}, u32[]{:S(2)}, u32[]{:S(2)}) collective-permute-start(bf16[1024,768]{1,0:T(8,128)(2,1)} %collective-permute-done.refs_2_), channel_id=1, source_target_pairs={{0,1},{1,0},{2,3},{3,2},{4,5},{5,4},{6,7},{7,6},{8,9},{9,8},{10,11... | collective-permute-start | bytes 4718600 | tf_op jit(solution)/shard_map/ppermute | solution.py:533
  45.1 20.1 %collective-permute-start.6 = (bf16[1024,768]{1,0:T(8,128)(2,1)S(1)}, bf16[1024,768]{1,0:T(8,128)(2,1)}, u32[]{:S(2)}, u32[]{:S(2)}) collective-permute-start(bf16[1024,768]{1,0:T(8,128)(2,1)S(1)} %collective-permute-done.1.refs_4_), channel_id=1, source_target_pairs={{0,1},{1,0},{2,3},{3,2},{4,5},{5,4},{6,7},{7,6},{8,9},{9,8},{10,11... | collective-permute-start | bytes 4718600 | tf_op jit(solution)/shard_map/ppermute | solution.py:533
  57.2 5.3 %collective-permute-start.10 = (bf16[512,768]{1,0:T(8,128)(2,1)S(1)}, bf16[512,768]{1,0:T(8,128)(2,1)S(1)}, u32[]{:S(2)}, u32[]{:S(2)}) collective-permute-start(bf16[512,768]{1,0:T(8,128)(2,1)S(1)} %collective-permute-done.8.refs_7_), channel_id=1, source_target_pairs={{0,1},{1,0},{2,3},{3,2},{4,5},{5,4},{6,7},{7,6},{8,9},{9,8},{10,11... | collective-permute-start | bytes 2359304 | tf_op jit(solution)/shard_map/ppermute | solution.py:533
  60.0 4.4 %collective-permute-start.9 = (bf16[512,768]{1,0:T(8,128)(2,1)S(1)}, bf16[512,768]{1,0:T(8,128)(2,1)S(1)}, u32[]{:S(2)}, u32[]{:S(2)}) collective-permute-start(bf16[512,768]{1,0:T(8,128)(2,1)S(1)} %collective-permute-done.7.refs_6_), channel_id=1, source_target_pairs={{0,1},{1,0},{2,3},{3,2},{4,5},{5,4},{6,7},{7,6},{8,9},{9,8},{10,11... | collective-permute-start | bytes 2359304 | tf_op jit(solution)/shard_map/ppermute | solution.py:533
  80.1 55.0 %collective-permute-start.11 = (bf16[768,768]{1,0:T(8,128)(2,1)}, bf16[768,768]{1,0:T(8,128)(2,1)S(1)}, u32[]{:S(2)}, u32[]{:S(2)}) collective-permute-start(bf16[768,768]{1,0:T(8,128)(2,1)} %bitcast.51), channel_id=1, source_target_pairs={{0,8},{2,10},{4,12},{6,14},{8,16},{10,18},{12,20},{14,22},{16,24},... | collective-permute-start | bytes 3538952 | tf_op jit(solution)/shard_map/ppermute | solution.py:530
  97.4 86.3 %collective-permute-start.12 = (bf16[768,768]{1,0:T(8,128)(2,1)}, bf16[768,768]{1,0:T(8,128)(2,1)}, u32[]{:S(2)}, u32[]{:S(2)}) collective-permute-start(bf16[768,768]{1,0:T(8,128)(2,1)} %bitcast.52), channel_id=1, source_target_pairs={{0,16},{2,18},{4,20},{6,22},{8,24},{10,26},{12,28},{14,30},{16,0},... | collective-permute-start | bytes 3538952 | tf_op jit(solution)/shard_map/ppermute | solution.py:530
  114.4 71.9 %collective-permute-start.13 = (bf16[768,768]{1,0:T(8,128)(2,1)}, bf16[768,768]{1,0:T(8,128)(2,1)}, u32[]{:S(2)}, u32[]{:S(2)}) collective-permute-start(bf16[768,768]{1,0:T(8,128)(2,1)} %bitcast.53), channel_id=1, source_target_pairs={{0,24},{2,26},{4,28},{6,30},{8,0},{10,2},{12,4},{14,6},{16,8},{18,... | collective-permute-start | bytes 3538952 | tf_op jit(solution)/shard_map/ppermute | solution.py:530
  200.9 4.5 %collective-permute-start.14 = (bf16[4,4,64,1024]{3,2,1,0:T(8,128)(2,1)}, bf16[4,4,64,1024]{3,2,1,0:T(8,128)(2,1)S(1)}, u32[]{:S(2)}, u32[]{:S(2)}) collective-permute-start(bf16[4,4,64,1024]{3,2,1,0:T(8,128)(2,1)} %get-tuple-element.43), channel_id=1, source_target_pairs={{0,1},{1,0},{2,3},{3,2},{4,5},{5,4},{6,7},{7,6},{8,9},{9,8},{10,11... | collective-permute-start | bytes 6291464 | tf_op jit(solution)/shard_map/ppermute | solution.py:533
  208.6 13.2 %collective-permute-start.15 = (bf16[4,64,1024]{2,1,0:T(8,128)(2,1)S(1)}, bf16[4,64,1024]{2,1,0:T(8,128)(2,1)S(1)}, u32[]{:S(2)}, u32[]{:S(2)}) collective-permute-start(bf16[4,64,1024]{2,1,0:T(8,128)(2,1)S(1)} %get-tuple-element.69), channel_id=1, source_target_pairs={{0,2},{2,0},{4,6},{6,4},{8,10},{10,8},{12,14},{14,12},{16,18},{18,... | collective-permute-start | bytes 1572872 | tf_op jit(solution)/shard_map/ppermute | solution.py:527
  208.7 24.2 %collective-permute-start.17 = (bf16[4,64,1024]{2,1,0:T(8,128)(2,1)S(1)}, bf16[4,64,1024]{2,1,0:T(8,128)(2,1)S(1)}, u32[]{:S(2)}, u32[]{:S(2)}) collective-permute-start(bf16[4,64,1024]{2,1,0:T(8,128)(2,1)S(1)} %get-tuple-element.70), channel_id=1, source_target_pairs={{0,6},{2,4},{4,2},{6,0},{8,14},{10,12},{12,10},{14,8},{16,22},{18,... | collective-permute-start | bytes 1572872 | tf_op jit(solution)/shard_map/ppermute | solution.py:527
  210.0 23.0 %collective-permute-start.16 = (bf16[4,64,1024]{2,1,0:T(8,128)(2,1)S(1)}, bf16[4,64,1024]{2,1,0:T(8,128)(2,1)S(1)}, u32[]{:S(2)}, u32[]{:S(2)}) collective-permute-start(bf16[4,64,1024]{2,1,0:T(8,128)(2,1)S(1)} %get-tuple-element.71), channel_id=1, source_target_pairs={{0,4},{2,6},{4,0},{6,2},{8,12},{10,14},{12,8},{14,10},{16,20},{18,... | collective-permute-start | bytes 1572872 | tf_op jit(solution)/shard_map/ppermute | solution.py:527
  233.4 5.3 %collective-permute-start.20 = (bf16[64,1024]{1,0:T(8,128)(2,1)S(1)}, bf16[64,1024]{1,0:T(8,128)(2,1)S(1)}, u32[]{:S(2)}, u32[]{:S(2)}) collective-permute-start(bf16[64,1024]{1,0:T(8,128)(2,1)S(1)} %get-tuple-element.72), channel_id=1, source_target_pairs={{0,24},{2,26},{4,28},{6,30},{8,0},{10,2},{12,4},{14,6},{16,8},{18,... | collective-permute-start | bytes 393224 | tf_op jit(solution)/shard_map/ppermute | solution.py:530
  233.4 6.3 %collective-permute-start.19 = (bf16[64,1024]{1,0:T(8,128)(2,1)S(1)}, bf16[64,1024]{1,0:T(8,128)(2,1)S(1)}, u32[]{:S(2)}, u32[]{:S(2)}) collective-permute-start(bf16[64,1024]{1,0:T(8,128)(2,1)S(1)} %get-tuple-element.73), channel_id=1, source_target_pairs={{0,16},{2,18},{4,20},{6,22},{8,24},{10,26},{12,28},{14,30},{16,0},... | collective-permute-start | bytes 393224 | tf_op jit(solution)/shard_map/ppermute | solution.py:530
  234.4 10.8 %collective-permute-start.18 = (bf16[64,1024]{1,0:T(8,128)(2,1)S(1)}, bf16[64,1024]{1,0:T(8,128)(2,1)S(1)}, u32[]{:S(2)}, u32[]{:S(2)}) collective-permute-start(bf16[64,1024]{1,0:T(8,128)(2,1)S(1)} %get-tuple-element.74), channel_id=1, source_target_pairs={{0,8},{2,10},{4,12},{6,14},{8,16},{10,18},{12,20},{14,22},{16,24},... | collective-permute-start | bytes 393224 | tf_op jit(solution)/shard_map/ppermute | solution.py:530
  246.0 5.2 %collective-permute-start.23 = (bf16[64,1024]{1,0:T(8,128)(2,1)S(1)}, bf16[64,1024]{1,0:T(8,128)(2,1)S(1)}, u32[]{:S(2)}, u32[]{:S(2)}) collective-permute-start(bf16[64,1024]{1,0:T(8,128)(2,1)S(1)} %get-tuple-element.44), channel_id=1, source_target_pairs={{0,8},{2,10},{4,12},{6,14},{8,16},{10,18},{12,20},{14,22},{16,24},... | collective-permute-start | bytes 393224 | tf_op jit(solution)/shard_map/ppermute | solution.py:530
  248.2 10.6 %collective-permute-start.22 = (bf16[64,1024]{1,0:T(8,128)(2,1)S(1)}, bf16[64,1024]{1,0:T(8,128)(2,1)S(1)}, u32[]{:S(2)}, u32[]{:S(2)}) collective-permute-start(bf16[64,1024]{1,0:T(8,128)(2,1)S(1)} %get-tuple-element.44), channel_id=1, source_target_pairs={{0,16},{2,18},{4,20},{6,22},{8,24},{10,26},{12,28},{14,30},{16,0},... | collective-permute-start | bytes 393224 | tf_op jit(solution)/shard_map/ppermute | solution.py:530
  249.5 10.7 %collective-permute-start.21 = (bf16[64,1024]{1,0:T(8,128)(2,1)S(1)}, bf16[64,1024]{1,0:T(8,128)(2,1)S(1)}, u32[]{:S(2)}, u32[]{:S(2)}) collective-permute-start(bf16[64,1024]{1,0:T(8,128)(2,1)S(1)} %get-tuple-element.44), channel_id=1, source_target_pairs={{0,24},{2,26},{4,28},{6,30},{8,0},{10,2},{12,4},{14,6},{16,8},{18,... | collective-permute-start | bytes 393224 | tf_op jit(solution)/shard_map/ppermute | solution.py:530
  260.2 13.0 %collective-permute-start.29 = (bf16[4,64,1024]{2,1,0:T(8,128)(2,1)S(1)}, bf16[4,64,1024]{2,1,0:T(8,128)(2,1)S(1)}, u32[]{:S(2)}, u32[]{:S(2)}) collective-permute-start(bf16[4,64,1024]{2,1,0:T(8,128)(2,1)S(1)} %pad_maximum_fusion.refs_0_), channel_id=1, source_target_pairs={{0,6},{2,4},{4,2},{6,0},{8,14},{10,12},{12,10},{14,8},{16,22},{18,... | collective-permute-start | bytes 1572872 | tf_op jit(solution)/shard_map/ppermute | solution.py:527
  262.5 23.9 %collective-permute-start.27 = (bf16[4,64,1024]{2,1,0:T(8,128)(2,1)S(1)}, bf16[4,64,1024]{2,1,0:T(8,128)(2,1)}, u32[]{:S(2)}, u32[]{:S(2)}) collective-permute-start(bf16[4,64,1024]{2,1,0:T(8,128)(2,1)S(1)} %pad_maximum_fusion.refs_0_), channel_id=1, source_target_pairs={{0,4},{2,6},{4,0},{6,2},{8,12},{10,14},{12,8},{14,10},{16,20},{18,... | collective-permute-start | bytes 1572872 | tf_op jit(solution)/shard_map/ppermute | solution.py:527
  262.5 24.4 %collective-permute-start.25 = (bf16[4,64,1024]{2,1,0:T(8,128)(2,1)S(1)}, bf16[4,64,1024]{2,1,0:T(8,128)(2,1)}, u32[]{:S(2)}, u32[]{:S(2)}) collective-permute-start(bf16[4,64,1024]{2,1,0:T(8,128)(2,1)S(1)} %pad_maximum_fusion.refs_0_), channel_id=1, source_target_pairs={{0,2},{2,0},{4,6},{6,4},{8,10},{10,8},{12,14},{14,12},{16,18},{18,... | collective-permute-start | bytes 1572872 | tf_op jit(solution)/shard_map/ppermute | solution.py:527
  263.0 25.0 %collective-permute-start.24 = (bf16[4,64,1024]{2,1,0:T(8,128)(2,1)S(1)}, bf16[4,64,1024]{2,1,0:T(8,128)(2,1)}, u32[]{:S(2)}, u32[]{:S(2)}) collective-permute-start(bf16[4,64,1024]{2,1,0:T(8,128)(2,1)S(1)} %pad_maximum_fusion.refs_0_), channel_id=1, source_target_pairs={{0,1},{1,0},{2,3},{3,2},{4,5},{5,4},{6,7},{7,6},{8,9},{9,8},{10,11... | collective-permute-start | bytes 1572872 | tf_op jit(solution)/shard_map/ppermute | solution.py:533
  273.3 14.7 %collective-permute-start.30 = (bf16[4,64,1024]{2,1,0:T(8,128)(2,1)S(1)}, bf16[4,64,1024]{2,1,0:T(8,128)(2,1)}, u32[]{:S(2)}, u32[]{:S(2)}) collective-permute-start(bf16[4,64,1024]{2,1,0:T(8,128)(2,1)S(1)} %collective-permute-done.29.refs_6_), channel_id=1, source_target_pairs={{0,1},{1,0},{2,3},{3,2},{4,5},{5,4},{6,7},{7,6},{8,9},{9,8},{10,11... | collective-permute-start | bytes 1572872 | tf_op jit(solution)/shard_map/ppermute | solution.py:533
  286.4 2.4 collective-permute-start.28
  286.9 2.6 collective-permute-start.26
  (28 other events, 410.2 us)

commit v7 on v6

--- a/solution.py
+++ b/solution.py
@@ -61,9 +61,7 @@
     found = (found[0:1] * 256.0 + found[1:2]).astype(jnp.int32)
     for line in range(groups * capacity // near_rows):
         ids_ref[fan + line : fan + line + 1, :] = found[:, line * near_rows : (line + 1) * near_rows]
-    hops = here - plane
-    hops = jnp.where(hops < 0, hops + groups, hops)
-    column_ref[...] = hops * capacity + rank
+    column_ref[...] = lax.bitwise_xor(plane, here) * capacity + rank
 
 
 def compose(place, adjacency, table, near, store_rows, groups, capacity):
@@ -172,9 +170,11 @@
     )(place, *ids_all)
 
 
-def partial_kernel(count, places, capacity, block, *refs):
+def partial_kernel(count, joined, places, capacity, block, *refs):
     index_refs, piece_refs = refs[:count], refs[count : count + len(places)]
-    out_ref, table, sums, kept = refs[-5 - len(places) : -1 - len(places)]
+    sums_ref, near_ref = refs[count + len(places)], refs[-5 - len(places)]
+    near_start = sums_ref.shape[1] - capacity if joined else 0
+    table, sums, kept = refs[-4 - len(places) : -1 - len(places)]
     buffers = refs[-1 - len(places) : -1]
     arrived = refs[-1]
     fan, near_rows = index_refs[0].shape[0] - 3, index_refs[0].shape[1]
@@ -239,22 +239,23 @@
         lax.fori_loop(0, capacity // near_unroll, near, 0)
         for unit in range(units):
             lanes = slice(unit * LANES, (unit + 1) * LANES)
-            out_ref[turn, :near_rows, lanes] = sums[
+            sums_ref[turn, :near_rows, lanes] = sums[
                 pl.ds(unit, near_rows, stride=8), :
             ].astype(jnp.bfloat16)
-            out_ref[turn, near_rows:, lanes] = kept[
+            near_ref[turn, near_start : near_start + capacity, lanes] = kept[
                 pl.ds(unit, capacity, stride=8), :
             ].astype(jnp.bfloat16)
 
 
-def partial_sums(lists, pieces, places, total, capacity, block):
+def partial_sums(lists, pieces, places, total, capacity, block, joined):
     near_rows = lists[0].shape[1]
     width = pieces[0].shape[1]
+    heights = [near_rows + capacity] if joined else [near_rows, capacity]
     return pl.pallas_call(
-        functools.partial(partial_kernel, len(lists), places, capacity, block),
-        out_shape=jax.ShapeDtypeStruct((len(lists), near_rows + capacity, width), jnp.bfloat16),
+        functools.partial(partial_kernel, len(lists), joined, places, capacity, block),
+        out_shape=[jax.ShapeDtypeStruct((len(lists), n, width), jnp.bfloat16) for n in heights],
         in_specs=[SMEM] * len(lists) + [pl.BlockSpec(memory_space=pl.ANY)] * len(pieces),
-        out_specs=VMEM,
+        out_specs=[VMEM] * len(heights),
         scratch_shapes=[
             pltpu.VMEM(((total + 1) * 8, LANES), jnp.float32),
             pltpu.VMEM(((near_rows + 1) * 8, LANES), jnp.float32),
@@ -267,10 +268,11 @@
     )(*lists, *pieces)
 
 
-def trainer_kernel(sizes, scale, *refs):
+def trainer_kernel(sizes, scale, joined, *refs):
     groups, rows_low, rows_top, classes, class_pad = sizes
+    rest = groups - joined
     place_ref, labels_ref, adj_ref, column_ref, wl_ref, wt_ref = refs[:6]
-    block_refs = refs[6:-10]
+    block_refs, sum_refs, near_refs = refs[6 : 6 + joined], refs[6 + joined : -10 - rest], refs[-10 - rest : -10]
     logits_ref, keep_ref, send_ref, li, hidden, slope, top_in, wt, weights, arrived = refs[-10:]
     seeds, fan_top = adj_ref.shape
     near_rows, low_width = li.shape
@@ -284,21 +286,17 @@
     bring.start()
     column = column_ref[...]
     rows_cap = lax.broadcasted_iota(jnp.int32, (capacity, near_rows), 0)
-    marks = [
-        jnp.where(rows_cap + k * capacity == column, 1.0, 0.0).astype(jnp.bfloat16)
-        for k in range(groups)
-    ]
-    for part in range(len(block_refs) // groups):
-        blocks = block_refs[part * groups : (part + 1) * groups]
-        share = blocks[0].shape[1]
-        near = total = None
-        for k in range(groups):
-            term = dot(marks[k], blocks[k][near_rows:, :], 0, 0)
-            near = term if near is None else near + term
-            term = blocks[k][:near_rows, :].astype(jnp.float32)
-            total = term if total is None else total + term
-        li[:, part * share : (part + 1) * share] = near.astype(jnp.bfloat16)
-        li[:, feat + part * share : feat + (part + 1) * share] = (total / fan_low).astype(jnp.bfloat16)
+    near = total = None
+    for k in range(groups):
+        marks = jnp.where(rows_cap + k * capacity == column, 1.0, 0.0).astype(jnp.bfloat16)
+        rows = block_refs[k][near_rows:, :] if k < joined else near_refs[k - joined][...]
+        term = dot(marks, rows, 0, 0)
+        near = term if near is None else near + term
+    for ref in block_refs + sum_refs:
+        term = ref[:near_rows, :].astype(jnp.float32)
+        total = term if total is None else total + term
+    li[:, :feat] = near.astype(jnp.bfloat16)
+    li[:, feat:] = (total / fan_low).astype(jnp.bfloat16)
 
     wt[...] = jnp.zeros_like(wt)
     wt[:, :classes] = wt_ref[...].astype(jnp.bfloat16)
@@ -345,9 +343,7 @@
 
     def slot(store):
         plane, inner = store // PLANE, store % PLANE
-        relative = plane - here
-        relative = jnp.where(relative < 0, relative + groups, relative)
-        return lax.bitwise_xor(mine, jnp.int32(inner)), relative
+        return lax.bitwise_xor(mine, jnp.int32(inner)), lax.bitwise_xor(here, jnp.int32(plane))
 
     tile = 384
     pair = 2 * rows_low
@@ -372,14 +368,14 @@
         send_ref[a, b, rows_low:, :] = other.astype(jnp.bfloat16)
 
 
-def trainer_step(place, labels, adj_top, column, wl, wt, blocks, sizes, scale):
+def trainer_step(place, labels, adj_top, column, wl, wt, joined, blocks, sizes, scale):
     groups, rows_low, rows_top, classes, class_pad = sizes
     seeds = adj_top.shape[0]
     low_width, width = wl.shape
     near_rows = column.shape[1]
     rows = rows_low + rows_top * class_pad // width
     return pl.pallas_call(
-        functools.partial(trainer_kernel, sizes, scale),
+        functools.partial(trainer_kernel, sizes, scale, joined),
         out_shape=(
             jax.ShapeDtypeStruct((seeds, classes), jnp.float32),
             jax.ShapeDtypeStruct((PLANE, groups, rows, width), jnp.float32),
@@ -456,8 +452,7 @@
         @pl.when(pl.program_id(0) == turn)
         def _():
             for k in range(groups):
-                plane = here + k
-                plane = jnp.where(plane >= groups, plane - groups, plane)
+                plane = lax.bitwise_xor(here, jnp.int32(k))
                 delta = delta_ref[k].astype(jnp.float32)
                 nl[plane, 0, 0] = wl[plane, 0, 0] - delta[:rows_low]
                 for g in range(lane_groups):
@@ -526,8 +521,12 @@
     def across(x, distance):
         return lax.ppermute(x, "store", [(i, i ^ distance) for i in range(stores)])
 
-    def along(x, hops):
-        return lax.ppermute(x, "store", [(i, (i + hops * PLANE) % stores) for i in range(stores)])
+    def along(x, distance):
+        return across(x, distance * PLANE)
+
+    def between(x, moves):
+        pairs = [(a * PLANE + i, b * PLANE + i) for a, b in moves for i in range(PLANE)]
+        return lax.ppermute(x, "store", pairs)
 
     def sibling(x):
         return lax.ppermute(x, "rep", [(0, 1), (1, 0)])
@@ -543,7 +542,7 @@
     ids, column = compose(
         place, adjacency_low, table, gid_near.reshape(1, near_rows), store_rows, groups, capacity
     )
-    ids_all = [ids] + [along(ids, -k) for k in range(1, groups)]
+    ids_all = [ids] + [along(ids, k) for k in range(1, groups)]
     block = 16
     lists = row_lists(place, ids_all, store_rows, fan, capacity, block)
 
@@ -554,10 +553,27 @@
     places = [0, store_rows, store_rows + half, 2 * store_rows, 2 * store_rows + half]
     places += [3 * store_rows + quarter * i for i in range(4)]
 
-    blocks = []
-    for k in range(groups):
-        made = partial_sums([lists[k]], pieces, places, PLANE * store_rows, capacity, block)
-        blocks.append(along(made[0], k) if k else made[0])
+    def summed(turns, joined=True):
+        return partial_sums(
+            [lists[k] for k in turns], pieces, places, PLANE * store_rows, capacity, block, joined
+        )
+
+    if groups == 4:
+        sums_far, near_far = summed([3, 2], False)
+        handed = between(sums_far, [(0, 1), (3, 2)])
+        (beside,), (own_block,) = summed([1]), summed([0])
+        near_far = [along(near_far[1], 2), along(near_far[0], 3)]
+        handed, near_far, beside = lax.optimization_barrier((handed, near_far, beside))
+        handed = handed.astype(jnp.float32)
+        for_two = (sums_far[1].astype(jnp.float32) + handed[0]).astype(bf16)
+        for_three = (sums_far[0].astype(jnp.float32) + handed[1]).astype(bf16)
+        sums_far = [between(for_two, [(1, 3), (2, 0)]), between(for_three, [(1, 2), (2, 1)])]
+        joined, blocks = 2, [own_block[0], along(beside[0], 1)] + sums_far + near_far
+    else:
+        joined, blocks = groups, []
+        for k in range(groups):
+            (made,) = summed([k])
+            blocks.append(along(made[0], k) if k else made[0])
 
     scale = 1.0 / (labels.shape[0] * members)
     logits, keep, send = trainer_step(
@@ -567,6 +583,7 @@
         column,
         weights_low,
         weights_top,
+        joined,
         blocks,
         sizes,
         scale,
@@ -578,7 +595,7 @@
     new_first_low, new_second_low, new_first_top, new_second_top, delta = adam_share(
         shares, first_low, second_low, first_top, second_top, class_pad
     )
-    lined = jnp.stack([delta] + [along(delta, -k) for k in range(1, groups)])
+    lined = jnp.stack([delta] + [along(delta, k) for k in range(1, groups)])
     sheets = [lined] + [across(lined, d) for d in range(1, PLANE)]
     deltas = []
     for sheet in sheets:

time: 305 us -> 308 us (level)
  waiting for transfers between devices: 150 us -> 142 us
  starting transfers between devices: 42.8 us -> 49.6 us
  Pallas kernels: 87.4 us -> 82.8 us
  local copies, waits for them, and re-layouts: 18.5 us -> 22.6 us
    ppermute x12 -> x3, waiting for transfers between devices: 73.6 us -> 10.9 us  [between(): return lax.ppermute(x, 'store', pairs)]
    ppermute x10 -> x22, waiting for transfers between devices: 69.2 us -> 124 us  [across(): return lax.ppermute(x, 'store', [(i, i ^ distance) for i in range(stores)])]
    ppermute x10 -> x22, starting transfers between devices: 9.59 us -> 26 us  [across(): return lax.ppermute(x, 'store', [(i, i ^ distance) for i in range(stores)])]
    ppermute x12 -> x3, starting transfers between devices: 17.8 us -> 6.91 us  [between(): return lax.ppermute(x, 'store', pairs)]
    pallas_call x5 -> x4, Pallas kernels: 73.8 us -> 69.2 us  [the longest x3 54.7 us: partial_sums(): pl.pallas_call(functools.partial(partial_kernel, len(lists), joined, plac...]
    unnamed x62 -> x70, local copies, waits for them, and re-layouts: 13.5 us -> 16.5 us
  transfers between devices with their start and end apart: 31 -> 34, of which waited for: 21 -> 18; matrix products, arithmetic and copies ran while one was open for 2% -> 3% of each run, Pallas kernels for 17% -> 13%
where the time goes in v7:
time: 308 us; the launch traced here: 304 us
  waiting for transfers between devices  142 us (46%)
  Pallas kernels  82.8 us (27%)
  starting transfers between devices  49.6 us (16%)
  local copies, waits for them, and re-layouts  22.6 us (7%)
  other arithmetic  5.39 us (2%)
    ppermute x22, waiting for transfers between devices, across(): return lax.ppermute(x, 'store', [(i, i ^ distance) for i in range(stores)])  124 us
    pallas_call x3, Pallas kernels, partial_sums(): pl.pallas_call(functools.partial(partial_kernel, len(lists), joined, plac...  54.7 us
    ppermute x22, starting transfers between devices, across(): return lax.ppermute(x, 'store', [(i, i ^ distance) for i in range(stores)])  26 us
    ppermute x9, starting transfers between devices, sibling(): return lax.ppermute(x, 'rep', [(0, 1), (1, 0)])  16.6 us
    unnamed x70, local copies, waits for them, and re-layouts  16.5 us
    pallas_call x1, Pallas kernels, trainer_step(): pl.pallas_call(functools.partial(trainer_kernel, sizes, scale, joined), o...  14.5 us
    ppermute x3, waiting for transfers between devices, between(): return lax.ppermute(x, 'store', pairs)  10.9 us
    ppermute x9, waiting for transfers between devices, sibling(): return lax.ppermute(x, 'rep', [(0, 1), (1, 0)])  7.78 us
  transfers between devices with their start and end apart: 34, of which 18 were waited for; matrix products, arithmetic and copies ran while one was open for 3% of the time, Pallas kernels for 13%

profile of v7, /device:TPU:9, one launch (start us, length us, event | category | flops | bytes accessed | tf_op | source)
XLA Modules:
  0.0 303.7 jit_solution(6793765711760692956)
XLA Ops:
  0.7 2.7 constant_dynamic-slice_fusion
  6.1 2.8 compose_ids.1
  15.5 2.8 row_lists.1
  20.7 18.2 %collective-permute-done.1.refs_4_.refs_5_ = bf16[1024,768]{1,0:T(8,128)(2,1)S(1)} collective-permute-done((bf16[1024,768]{1,0:T(8,128)(2,1)}, bf16[1024,768]{1,0:T(8,128)(2,1)S(1)}, u32[]{:S(2)}, u32[]{:S(2)}) %collective-permute-start.1) | collective-permute-done | bytes 1572896 | tf_op jit(solution)/shard_map/ppermute | solution.py:522
  42.8 2.3 collective-permute-start.5
  45.1 12.1 %collective-permute-done.8.refs_7_.refs_8_ = bf16[512,768]{1,0:T(8,128)(2,1)S(1)} collective-permute-done((bf16[512,768]{1,0:T(8,128)(2,1)S(1)}, bf16[512,768]{1,0:T(8,128)(2,1)S(1)}, u32[]{:S(2)}, u32[]{:S(2)}) %collective-permute-start.8) | collective-permute-done | bytes 786464 | tf_op jit(solution)/shard_map/ppermute | solution.py:522
  57.2 2.8 collective-permute-start.10
  60.0 2.5 collective-permute-start.9
  65.3 22.1 %partial_sums.4 = (bf16[2,512,768]{2,1,0:T(8,128)(2,1)}, bf16[2,256,768]{2,1,0:T(8,128)(2,1)}) custom-call(s32[18,512]{1,0:T(8,128)} %copy-done.10, s32[18,512]{1,0:T(8,128)} %copy-done.9, bf16[2048,768]{1,0:T(8,128)(2,1)} %refs_1_.3, bf16[1024,768]{1,0:T(8,128)(2,1)} %collective-permute-done.refs_2_.refs_3_, ...), custom_call_target="tpu_custom_call" | custom-call | tf_op jit(solution)/shard_map/partial_sums/pallas_call | solution.py:254
  90.0 4.2 %collective-permute-start.12 = (bf16[256,768]{1,0:T(8,128)(2,1)S(1)}, bf16[256,768]{1,0:T(8,128)(2,1)S(1)}, u32[]{:S(2)}, u32[]{:S(2)}) collective-permute-start(bf16[256,768]{1,0:T(8,128)(2,1)S(1)} %get-tuple-element.87), channel_id=1, source_target_pairs={{0,16},{2,18},{4,20},{6,22},{8,24},{10,26},{12,28},{14,30},{16,0},... | collective-permute-start | bytes 1179656 | tf_op jit(solution)/shard_map/ppermute | solution.py:522
  94.2 16.2 %partial_sums.5 = bf16[1,768,768]{2,1,0:T(8,128)(2,1)} custom-call(s32[18,512]{1,0:T(8,128)} %copy-done.8, bf16[2048,768]{1,0:T(8,128)(2,1)} %refs_1_.3, bf16[1024,768]{1,0:T(8,128)(2,1)} %collective-permute-done.refs_2_.refs_3_, bf16[1024,768]{1,0:T(8,128)(2,1)} %collective-permute-done.5.refs_3_.refs_4_, bf16[1024,768]{1,0:T(8,128)(2,1)} %copy-done.15, ...), custom_call_target="tpu_custom_call" | custom-call | tf_op jit(solution)/shard_map/partial_sums/pallas_call | solution.py:254
  110.4 31.1 %collective-permute-done.12.refs_10_ = bf16[256,768]{1,0:T(8,128)(2,1)S(1)} collective-permute-done((bf16[256,768]{1,0:T(8,128)(2,1)S(1)}, bf16[256,768]{1,0:T(8,128)(2,1)S(1)}, u32[]{:S(2)}, u32[]{:S(2)}) %collective-permute-start.12) | collective-permute-done | bytes 393248 | tf_op jit(solution)/shard_map/ppermute | solution.py:522
  145.2 3.4 %collective-permute-start.16 = (bf16[512,768]{1,0:T(8,128)(2,1)}, bf16[512,768]{1,0:T(8,128)(2,1)S(1)}, u32[]{:S(2)}, u32[]{:S(2)}) collective-permute-start(bf16[512,768]{1,0:T(8,128)(2,1)} %get-tuple-element.81), channel_id=1, source_target_pairs={{8,16},{10,18},{12,20},{14,22},{16,8},{18,10},{20,12},{22,14},{9,1... | collective-permute-start | bytes 2359304 | tf_op jit(solution)/shard_map/ppermute | solution.py:529
  148.7 2.2 collective-permute-start.15
  154.1 16.4 %partial_sums.3 = bf16[1,768,768]{2,1,0:T(8,128)(2,1)} custom-call(s32[18,512]{1,0:T(8,128)} %copy-done.7, bf16[2048,768]{1,0:T(8,128)(2,1)} %refs_1_.3, bf16[1024,768]{1,0:T(8,128)(2,1)} %collective-permute-done.refs_2_.refs_3_, bf16[1024,768]{1,0:T(8,128)(2,1)} %collective-permute-done.5.refs_3_.refs_4_, bf16[1024,768]{1,0:T(8,128)(2,1)} %copy-done.15, ...), custom_call_target="tpu_custom_call" | custom-call | tf_op jit(solution)/shard_map/partial_sums/pallas_call | solution.py:254
  170.5 10.9 %collective-permute-done.15.refs_8_ = bf16[512,768]{1,0:T(8,128)(2,1)} collective-permute-done((bf16[512,768]{1,0:T(8,128)(2,1)}, bf16[512,768]{1,0:T(8,128)(2,1)}, u32[]{:S(2)}, u32[]{:S(2)}) %collective-permute-start.15) | collective-permute-done | bytes 786464 | tf_op jit(solution)/shard_map/ppermute | solution.py:529
  184.5 14.5 %trainer_step.1 = (f32[128,153]{1,0:T(8,128)}, f32[4,4,64,1024]{3,2,1,0:T(8,128)}, bf16[4,4,64,1024]{3,2,1,0:T(8,128)(2,1)}) custom-call(s32[4]{0:T(128)} %copy-done.12, s32[128,1]{1,0:T(8,128)} %copy.28.refs_1_, s32[128,10]{1,0:T(8,128)} %copy.29.refs_2_, s32[1,512]{1,0:T(1,128)} %copy-done.14, f32[1536,1024]{1,0:T(8,128)} %refs_4_.2, ...), custom_call_target="tpu_custom_call" | custom-call | tf_op jit(solution)/shard_map/trainer_step/pallas_call | solution.py:377
  198.9 2.3 collective-permute-start.17
  201.2 4.0 %collective-permute-done.17 = bf16[4,4,64,1024]{3,2,1,0:T(8,128)(2,1)S(1)} collective-permute-done((bf16[4,4,64,1024]{3,2,1,0:T(8,128)(2,1)}, bf16[4,4,64,1024]{3,2,1,0:T(8,128)(2,1)S(1)}, u32[]{:S(2)}, u32[]{:S(2)}) %collective-permute-start.17) | collective-permute-done | bytes 2097184 | tf_op jit(solution)/shard_map/ppermute | solution.py:532
  205.2 3.1 %fusion.7 = (bf16[4,4,64,1024]{3,2,1,0:T(8,128)(2,1)S(1)}, f32[4,4,64,1024]{3,2,1,0:T(8,128)S(1)}) fusion(f32[4,4,64,1024]{3,2,1,0:T(8,128)} %get-tuple-element.54, bf16[4,4,64,1024]{3,2,1,0:T(8,128)(2,1)S(1)} %collective-permute-done.17), kind=kLoop, calls=%fused_computation.26 | loop fusion | flops 3145728 | bytes 12582912 | tf_op jit(solution)/shard_map/convert.5
  211.2 10.5 %collective-permute-done.18 = bf16[4,64,1024]{2,1,0:T(8,128)(2,1)S(1)} collective-permute-done((bf16[4,64,1024]{2,1,0:T(8,128)(2,1)S(1)}, bf16[4,64,1024]{2,1,0:T(8,128)(2,1)S(1)}, u32[]{:S(2)}, u32[]{:S(2)}) %collective-permute-start.18) | collective-permute-done | bytes 524320 | tf_op jit(solution)/shard_map/ppermute | solution.py:522
  221.7 11.7 %collective-permute-done.20 = bf16[4,64,1024]{2,1,0:T(8,128)(2,1)S(1)} collective-permute-done((bf16[4,64,1024]{2,1,0:T(8,128)(2,1)S(1)}, bf16[4,64,1024]{2,1,0:T(8,128)(2,1)S(1)}, u32[]{:S(2)}, u32[]{:S(2)}) %collective-permute-start.20) | collective-permute-done | bytes 524320 | tf_op jit(solution)/shard_map/ppermute | solution.py:522
  235.1 3.0 collective-permute-start.22
  238.1 8.6 %collective-permute-done.22.refs_2_ = bf16[64,1024]{1,0:T(8,128)(2,1)S(1)} collective-permute-done((bf16[64,1024]{1,0:T(8,128)(2,1)S(1)}, bf16[64,1024]{1,0:T(8,128)(2,1)S(1)}, u32[]{:S(2)}, u32[]{:S(2)}) %collective-permute-start.22) | collective-permute-done | bytes 131104 | tf_op jit(solution)/shard_map/ppermute | solution.py:522
  248.0 4.0 %collective-permute-start.25 = (bf16[64,1024]{1,0:T(8,128)(2,1)S(1)}, bf16[64,1024]{1,0:T(8,128)(2,1)S(1)}, u32[]{:S(2)}, u32[]{:S(2)}) collective-permute-start(bf16[64,1024]{1,0:T(8,128)(2,1)S(1)} %get-tuple-element.56), channel_id=1, source_target_pairs={{0,16},{2,18},{4,20},{6,22},{8,24},{10,26},{12,28},{14,30},{16,0},... | collective-permute-start | bytes 393224 | tf_op jit(solution)/shard_map/ppermute | solution.py:522
  252.0 8.4 %collective-permute-done.25 = bf16[64,1024]{1,0:T(8,128)(2,1)S(1)} collective-permute-done((bf16[64,1024]{1,0:T(8,128)(2,1)S(1)}, bf16[64,1024]{1,0:T(8,128)(2,1)S(1)}, u32[]{:S(2)}, u32[]{:S(2)}) %collective-permute-start.25) | collective-permute-done | bytes 131104 | tf_op jit(solution)/shard_map/ppermute | solution.py:522
  265.4 8.2 %collective-permute-done.32.refs_6_ = bf16[4,64,1024]{2,1,0:T(8,128)(2,1)S(1)} collective-permute-done((bf16[4,64,1024]{2,1,0:T(8,128)(2,1)S(1)}, bf16[4,64,1024]{2,1,0:T(8,128)(2,1)S(1)}, u32[]{:S(2)}, u32[]{:S(2)}) %collective-permute-start.32) | collective-permute-done | bytes 524320 | tf_op jit(solution)/shard_map/ppermute | solution.py:522
  273.6 4.1 %collective-permute-start.33 = (bf16[4,64,1024]{2,1,0:T(8,128)(2,1)S(1)}, bf16[4,64,1024]{2,1,0:T(8,128)(2,1)}, u32[]{:S(2)}, u32[]{:S(2)}) collective-permute-start(bf16[4,64,1024]{2,1,0:T(8,128)(2,1)S(1)} %collective-permute-done.32.refs_6_), channel_id=1, source_target_pairs={{0,1},{1,0},{2,3},{3,2},{4,5},{5,4},{6,7},{7,6},{8,9},{9,8},{10,11... | collective-permute-start | bytes 1572872 | tf_op jit(solution)/shard_map/ppermute | solution.py:532
  277.7 9.0 %collective-permute-done.30.refs_4_ = bf16[4,64,1024]{2,1,0:T(8,128)(2,1)} collective-permute-done((bf16[4,64,1024]{2,1,0:T(8,128)(2,1)S(1)}, bf16[4,64,1024]{2,1,0:T(8,128)(2,1)}, u32[]{:S(2)}, u32[]{:S(2)}) %collective-permute-start.30) | collective-permute-done | bytes 524320 | tf_op jit(solution)/shard_map/ppermute | solution.py:522
  289.8 2.8 copy-done
  292.6 7.1 %apply_updates.1 = (f32[4,4,2,48,1024]{4,3,2,1,0:T(8,128)}, f32[4,4,2,64,153]{4,3,2,1,0:T(8,128)S(1)}) custom-call(s32[4]{0:T(128)S(1)} %copy-done.13, f32[4,4,2,48,1024]{4,3,2,1,0:T(8,128)S(1)} %bitcast.49, f32[4,4,2,64,153]{4,3,2,1,0:T(8,128)S(1)} %bitcast.50, bf16[4,64,1024]{2,1,0:T(8,128)(2,1)S(1)} %pad_maximum_fusion.refs_0_, ...), custom_call_target="tpu_custom_call" | custom-call | tf_op jit(solution)/shard_map/apply_updates/pallas_call | solution.py:474
  301.0 2.7 copy.33
  (133 shorter events, 46.2 us)
Async XLA Ops:
  3.4 35.6 %collective-permute-start.1 = (bf16[1024,768]{1,0:T(8,128)(2,1)}, bf16[1024,768]{1,0:T(8,128)(2,1)S(1)}, u32[]{:S(2)}, u32[]{:S(2)}) collective-permute-start(bf16[1024,768]{1,0:T(8,128)(2,1)} %constant_dynamic-slice_fusion), channel_id=1, source_target_pairs={{0,4},{2,6},{4,0},{6,2},{8,12},{10,14},{12,8},{14,10},{16,20},{18,... | collective-permute-start | bytes 4718600 | tf_op jit(solution)/shard_map/ppermute | solution.py:522
  4.6 35.3 %collective-permute-start = (bf16[1024,768]{1,0:T(8,128)(2,1)}, bf16[1024,768]{1,0:T(8,128)(2,1)}, u32[]{:S(2)}, u32[]{:S(2)}) collective-permute-start(bf16[1024,768]{1,0:T(8,128)(2,1)} %constant_dynamic-slice_fusion), channel_id=1, source_target_pairs={{0,2},{2,0},{4,6},{6,4},{8,10},{10,8},{12,14},{14,12},{16,18},{18,... | collective-permute-start | bytes 4718600 | tf_op jit(solution)/shard_map/ppermute | solution.py:522
  8.9 3.6 %collective-permute-start.4 = (s32[17,512]{1,0:T(8,128)S(1)}, s32[17,512]{1,0:T(8,128)S(1)}, u32[]{:S(2)}, u32[]{:S(2)}) collective-permute-start(s32[17,512]{1,0:T(8,128)S(1)} %get-tuple-element.36.refs_0_), channel_id=1, source_target_pairs={{0,24},{2,26},{4,28},{6,30},{8,16},{10,18},{12,20},{14,22},{16,8},... | collective-permute-start | bytes 104456 | tf_op jit(solution)/shard_map/ppermute | solution.py:522
  10.3 4.1 %collective-permute-start.3 = (s32[17,512]{1,0:T(8,128)S(1)}, s32[17,512]{1,0:T(8,128)S(1)}, u32[]{:S(2)}, u32[]{:S(2)}) collective-permute-start(s32[17,512]{1,0:T(8,128)S(1)} %get-tuple-element.36.refs_0_), channel_id=1, source_target_pairs={{0,16},{2,18},{4,20},{6,22},{8,24},{10,26},{12,28},{14,30},{16,0},... | collective-permute-start | bytes 104456 | tf_op jit(solution)/shard_map/ppermute | solution.py:522
  11.4 4.1 %collective-permute-start.2 = (s32[17,512]{1,0:T(8,128)S(1)}, s32[17,512]{1,0:T(8,128)S(1)}, u32[]{:S(2)}, u32[]{:S(2)}) collective-permute-start(s32[17,512]{1,0:T(8,128)S(1)} %get-tuple-element.36.refs_0_), channel_id=1, source_target_pairs={{0,8},{2,10},{4,12},{6,14},{8,0},{10,2},{12,4},{14,6},{16,24},{18,... | collective-permute-start | bytes 104456 | tf_op jit(solution)/shard_map/ppermute | solution.py:522
  39.9 17.2 %collective-permute-start.8 = (bf16[512,768]{1,0:T(8,128)(2,1)S(1)}, bf16[512,768]{1,0:T(8,128)(2,1)S(1)}, u32[]{:S(2)}, u32[]{:S(2)}) collective-permute-start(bf16[512,768]{1,0:T(8,128)(2,1)S(1)} %slice.55), channel_id=1, source_target_pairs={{0,2},{2,0},{4,6},{6,4},{8,10},{10,8},{12,14},{14,12},{16,18},{18,... | collective-permute-start | bytes 2359304 | tf_op jit(solution)/shard_map/ppermute | solution.py:522
  42.4 17.6 %collective-permute-start.7 = (bf16[512,768]{1,0:T(8,128)(2,1)S(1)}, bf16[512,768]{1,0:T(8,128)(2,1)S(1)}, u32[]{:S(2)}, u32[]{:S(2)}) collective-permute-start(bf16[512,768]{1,0:T(8,128)(2,1)S(1)} %slice.54), channel_id=1, source_target_pairs={{0,4},{2,6},{4,0},{6,2},{8,12},{10,14},{12,8},{14,10},{16,20},{18,... | collective-permute-start | bytes 2359304 | tf_op jit(solution)/shard_map/ppermute | solution.py:522
  42.8 21.6 %collective-permute-start.5 = (bf16[1024,768]{1,0:T(8,128)(2,1)}, bf16[1024,768]{1,0:T(8,128)(2,1)}, u32[]{:S(2)}, u32[]{:S(2)}) collective-permute-start(bf16[1024,768]{1,0:T(8,128)(2,1)} %collective-permute-done.refs_2_.refs_3_), channel_id=1, source_target_pairs={{0,1},{1,0},{2,3},{3,2},{4,5},{5,4},{6,7},{7,6},{8,9},{9,8},{10,11... | collective-permute-start | bytes 4718600 | tf_op jit(solution)/shard_map/ppermute | solution.py:532
  45.1 20.1 %collective-permute-start.6 = (bf16[1024,768]{1,0:T(8,128)(2,1)S(1)}, bf16[1024,768]{1,0:T(8,128)(2,1)}, u32[]{:S(2)}, u32[]{:S(2)}) collective-permute-start(bf16[1024,768]{1,0:T(8,128)(2,1)S(1)} %collective-permute-done.1.refs_4_.refs_5_), channel_id=1, source_target_pairs={{0,1},{1,0},{2,3},{3,2},{4,5},{5,4},{6,7},{7,6},{8,9},{9,8},{10,11... | collective-permute-start | bytes 4718600 | tf_op jit(solution)/shard_map/ppermute | solution.py:532
  57.2 5.3 %collective-permute-start.10 = (bf16[512,768]{1,0:T(8,128)(2,1)S(1)}, bf16[512,768]{1,0:T(8,128)(2,1)S(1)}, u32[]{:S(2)}, u32[]{:S(2)}) collective-permute-start(bf16[512,768]{1,0:T(8,128)(2,1)S(1)} %collective-permute-done.8.refs_7_.refs_8_), channel_id=1, source_target_pairs={{0,1},{1,0},{2,3},{3,2},{4,5},{5,4},{6,7},{7,6},{8,9},{9,8},{10,11... | collective-permute-start | bytes 2359304 | tf_op jit(solution)/shard_map/ppermute | solution.py:532
  60.0 4.4 %collective-permute-start.9 = (bf16[512,768]{1,0:T(8,128)(2,1)S(1)}, bf16[512,768]{1,0:T(8,128)(2,1)S(1)}, u32[]{:S(2)}, u32[]{:S(2)}) collective-permute-start(bf16[512,768]{1,0:T(8,128)(2,1)S(1)} %collective-permute-done.7.refs_6_.refs_7_), channel_id=1, source_target_pairs={{0,1},{1,0},{2,3},{3,2},{4,5},{5,4},{6,7},{7,6},{8,9},{9,8},{10,11... | collective-permute-start | bytes 2359304 | tf_op jit(solution)/shard_map/ppermute | solution.py:532
  87.4 54.1 %collective-permute-start.11 = (bf16[2,512,768]{2,1,0:T(8,128)(2,1)}, bf16[2,512,768]{2,1,0:T(8,128)(2,1)S(1)}, u32[]{:S(2)}, u32[]{:S(2)}) collective-permute-start(bf16[2,512,768]{2,1,0:T(8,128)(2,1)} %get-tuple-element.46), channel_id=1, source_target_pairs={{0,8},{2,10},{4,12},{6,14},{24,16},{26,18},{28,20},{30,22},{1,9},{... | collective-permute-start | bytes 4718600 | tf_op jit(solution)/shard_map/ppermute | solution.py:529
  89.9 20.5 %collective-permute-start.13 = (bf16[256,768]{1,0:T(8,128)(2,1)S(1)}, bf16[256,768]{1,0:T(8,128)(2,1)S(1)}, u32[]{:S(2)}, u32[]{:S(2)}) collective-permute-start(bf16[256,768]{1,0:T(8,128)(2,1)S(1)} %get-tuple-element.86), channel_id=1, source_target_pairs={{0,24},{2,26},{4,28},{6,30},{8,16},{10,18},{12,20},{14,22},{16,8},... | collective-permute-start | bytes 1179656 | tf_op jit(solution)/shard_map/ppermute | solution.py:522
  90.0 51.5 %collective-permute-start.12 = (bf16[256,768]{1,0:T(8,128)(2,1)S(1)}, bf16[256,768]{1,0:T(8,128)(2,1)S(1)}, u32[]{:S(2)}, u32[]{:S(2)}) collective-permute-start(bf16[256,768]{1,0:T(8,128)(2,1)S(1)} %get-tuple-element.87), channel_id=1, source_target_pairs={{0,16},{2,18},{4,20},{6,22},{8,24},{10,26},{12,28},{14,30},{16,0},... | collective-permute-start | bytes 1179656 | tf_op jit(solution)/shard_map/ppermute | solution.py:522
  142.3 41.1 %collective-permute-start.14 = (bf16[768,768]{1,0:T(8,128)(2,1)}, bf16[768,768]{1,0:T(8,128)(2,1)S(1)}, u32[]{:S(2)}, u32[]{:S(2)}) collective-permute-start(bf16[768,768]{1,0:T(8,128)(2,1)} %bitcast.57), channel_id=1, source_target_pairs={{0,8},{2,10},{4,12},{6,14},{8,0},{10,2},{12,4},{14,6},{16,24},{18,... | collective-permute-start | bytes 3538952 | tf_op jit(solution)/shard_map/ppermute | solution.py:522
  145.2 25.2 %collective-permute-start.16 = (bf16[512,768]{1,0:T(8,128)(2,1)}, bf16[512,768]{1,0:T(8,128)(2,1)S(1)}, u32[]{:S(2)}, u32[]{:S(2)}) collective-permute-start(bf16[512,768]{1,0:T(8,128)(2,1)} %get-tuple-element.81), channel_id=1, source_target_pairs={{8,16},{10,18},{12,20},{14,22},{16,8},{18,10},{20,12},{22,14},{9,1... | collective-permute-start | bytes 2359304 | tf_op jit(solution)/shard_map/ppermute | solution.py:529
  148.7 32.7 %collective-permute-start.15 = (bf16[512,768]{1,0:T(8,128)(2,1)}, bf16[512,768]{1,0:T(8,128)(2,1)}, u32[]{:S(2)}, u32[]{:S(2)}) collective-permute-start(bf16[512,768]{1,0:T(8,128)(2,1)} %get-tuple-element.82), channel_id=1, source_target_pairs={{8,24},{10,26},{12,28},{14,30},{16,0},{18,2},{20,4},{22,6},{9,25},... | collective-permute-start | bytes 2359304 | tf_op jit(solution)/shard_map/ppermute | solution.py:529
  198.9 6.3 %collective-permute-start.17 = (bf16[4,4,64,1024]{3,2,1,0:T(8,128)(2,1)}, bf16[4,4,64,1024]{3,2,1,0:T(8,128)(2,1)S(1)}, u32[]{:S(2)}, u32[]{:S(2)}) collective-permute-start(bf16[4,4,64,1024]{3,2,1,0:T(8,128)(2,1)} %get-tuple-element.55), channel_id=1, source_target_pairs={{0,1},{1,0},{2,3},{3,2},{4,5},{5,4},{6,7},{7,6},{8,9},{9,8},{10,11... | collective-permute-start | bytes 6291464 | tf_op jit(solution)/shard_map/ppermute | solution.py:532
  208.5 13.2 %collective-permute-start.18 = (bf16[4,64,1024]{2,1,0:T(8,128)(2,1)S(1)}, bf16[4,64,1024]{2,1,0:T(8,128)(2,1)S(1)}, u32[]{:S(2)}, u32[]{:S(2)}) collective-permute-start(bf16[4,64,1024]{2,1,0:T(8,128)(2,1)S(1)} %get-tuple-element.83), channel_id=1, source_target_pairs={{0,2},{2,0},{4,6},{6,4},{8,10},{10,8},{12,14},{14,12},{16,18},{18,... | collective-permute-start | bytes 1572872 | tf_op jit(solution)/shard_map/ppermute | solution.py:522
  209.6 23.8 %collective-permute-start.20 = (bf16[4,64,1024]{2,1,0:T(8,128)(2,1)S(1)}, bf16[4,64,1024]{2,1,0:T(8,128)(2,1)S(1)}, u32[]{:S(2)}, u32[]{:S(2)}) collective-permute-start(bf16[4,64,1024]{2,1,0:T(8,128)(2,1)S(1)} %get-tuple-element.84), channel_id=1, source_target_pairs={{0,6},{2,4},{4,2},{6,0},{8,14},{10,12},{12,10},{14,8},{16,22},{18,... | collective-permute-start | bytes 1572872 | tf_op jit(solution)/shard_map/ppermute | solution.py:522
  210.4 23.0 %collective-permute-start.19 = (bf16[4,64,1024]{2,1,0:T(8,128)(2,1)S(1)}, bf16[4,64,1024]{2,1,0:T(8,128)(2,1)S(1)}, u32[]{:S(2)}, u32[]{:S(2)}) collective-permute-start(bf16[4,64,1024]{2,1,0:T(8,128)(2,1)S(1)} %get-tuple-element.85), channel_id=1, source_target_pairs={{0,4},{2,6},{4,0},{6,2},{8,12},{10,14},{12,8},{14,10},{16,20},{18,... | collective-permute-start | bytes 1572872 | tf_op jit(solution)/shard_map/ppermute | solution.py:522
  233.8 4.3 %collective-permute-start.23 = (bf16[64,1024]{1,0:T(8,128)(2,1)S(1)}, bf16[64,1024]{1,0:T(8,128)(2,1)S(1)}, u32[]{:S(2)}, u32[]{:S(2)}) collective-permute-start(bf16[64,1024]{1,0:T(8,128)(2,1)S(1)} %get-tuple-element.88), channel_id=1, source_target_pairs={{0,24},{2,26},{4,28},{6,30},{8,16},{10,18},{12,20},{14,22},{16,8},... | collective-permute-start | bytes 393224 | tf_op jit(solution)/shard_map/ppermute | solution.py:522
  235.1 11.6 %collective-permute-start.22 = (bf16[64,1024]{1,0:T(8,128)(2,1)S(1)}, bf16[64,1024]{1,0:T(8,128)(2,1)S(1)}, u32[]{:S(2)}, u32[]{:S(2)}) collective-permute-start(bf16[64,1024]{1,0:T(8,128)(2,1)S(1)} %get-tuple-element.89), channel_id=1, source_target_pairs={{0,16},{2,18},{4,20},{6,22},{8,24},{10,26},{12,28},{14,30},{16,0},... | collective-permute-start | bytes 393224 | tf_op jit(solution)/shard_map/ppermute | solution.py:522
  238.1 8.7 %collective-permute-start.21 = (bf16[64,1024]{1,0:T(8,128)(2,1)S(1)}, bf16[64,1024]{1,0:T(8,128)(2,1)S(1)}, u32[]{:S(2)}, u32[]{:S(2)}) collective-permute-start(bf16[64,1024]{1,0:T(8,128)(2,1)S(1)} %get-tuple-element.90), channel_id=1, source_target_pairs={{0,8},{2,10},{4,12},{6,14},{8,0},{10,2},{12,4},{14,6},{16,24},{18,... | collective-permute-start | bytes 393224 | tf_op jit(solution)/shard_map/ppermute | solution.py:522
  247.6 4.3 %collective-permute-start.26 = (bf16[64,1024]{1,0:T(8,128)(2,1)S(1)}, bf16[64,1024]{1,0:T(8,128)(2,1)S(1)}, u32[]{:S(2)}, u32[]{:S(2)}) collective-permute-start(bf16[64,1024]{1,0:T(8,128)(2,1)S(1)} %get-tuple-element.56), channel_id=1, source_target_pairs={{0,24},{2,26},{4,28},{6,30},{8,16},{10,18},{12,20},{14,22},{16,8},... | collective-permute-start | bytes 393224 | tf_op jit(solution)/shard_map/ppermute | solution.py:522
  248.0 12.4 %collective-permute-start.25 = (bf16[64,1024]{1,0:T(8,128)(2,1)S(1)}, bf16[64,1024]{1,0:T(8,128)(2,1)S(1)}, u32[]{:S(2)}, u32[]{:S(2)}) collective-permute-start(bf16[64,1024]{1,0:T(8,128)(2,1)S(1)} %get-tuple-element.56), channel_id=1, source_target_pairs={{0,16},{2,18},{4,20},{6,22},{8,24},{10,26},{12,28},{14,30},{16,0},... | collective-permute-start | bytes 393224 | tf_op jit(solution)/shard_map/ppermute | solution.py:522
  252.0 8.4 %collective-permute-start.24 = (bf16[64,1024]{1,0:T(8,128)(2,1)S(1)}, bf16[64,1024]{1,0:T(8,128)(2,1)S(1)}, u32[]{:S(2)}, u32[]{:S(2)}) collective-permute-start(bf16[64,1024]{1,0:T(8,128)(2,1)S(1)} %get-tuple-element.56), channel_id=1, source_target_pairs={{0,8},{2,10},{4,12},{6,14},{8,0},{10,2},{12,4},{14,6},{16,24},{18,... | collective-permute-start | bytes 393224 | tf_op jit(solution)/shard_map/ppermute | solution.py:522
  260.5 13.1 %collective-permute-start.32 = (bf16[4,64,1024]{2,1,0:T(8,128)(2,1)S(1)}, bf16[4,64,1024]{2,1,0:T(8,128)(2,1)S(1)}, u32[]{:S(2)}, u32[]{:S(2)}) collective-permute-start(bf16[4,64,1024]{2,1,0:T(8,128)(2,1)S(1)} %pad_maximum_fusion.refs_0_), channel_id=1, source_target_pairs={{0,6},{2,4},{4,2},{6,0},{8,14},{10,12},{12,10},{14,8},{16,22},{18,... | collective-permute-start | bytes 1572872 | tf_op jit(solution)/shard_map/ppermute | solution.py:522
  262.2 24.4 %collective-permute-start.30 = (bf16[4,64,1024]{2,1,0:T(8,128)(2,1)S(1)}, bf16[4,64,1024]{2,1,0:T(8,128)(2,1)}, u32[]{:S(2)}, u32[]{:S(2)}) collective-permute-start(bf16[4,64,1024]{2,1,0:T(8,128)(2,1)S(1)} %pad_maximum_fusion.refs_0_), channel_id=1, source_target_pairs={{0,4},{2,6},{4,0},{6,2},{8,12},{10,14},{12,8},{14,10},{16,20},{18,... | collective-permute-start | bytes 1572872 | tf_op jit(solution)/shard_map/ppermute | solution.py:522
  262.6 24.6 %collective-permute-start.28 = (bf16[4,64,1024]{2,1,0:T(8,128)(2,1)S(1)}, bf16[4,64,1024]{2,1,0:T(8,128)(2,1)}, u32[]{:S(2)}, u32[]{:S(2)}) collective-permute-start(bf16[4,64,1024]{2,1,0:T(8,128)(2,1)S(1)} %pad_maximum_fusion.refs_0_), channel_id=1, source_target_pairs={{0,2},{2,0},{4,6},{6,4},{8,10},{10,8},{12,14},{14,12},{16,18},{18,... | collective-permute-start | bytes 1572872 | tf_op jit(solution)/shard_map/ppermute | solution.py:522
  263.2 24.7 %collective-permute-start.27 = (bf16[4,64,1024]{2,1,0:T(8,128)(2,1)S(1)}, bf16[4,64,1024]{2,1,0:T(8,128)(2,1)}, u32[]{:S(2)}, u32[]{:S(2)}) collective-permute-start(bf16[4,64,1024]{2,1,0:T(8,128)(2,1)S(1)} %pad_maximum_fusion.refs_0_), channel_id=1, source_target_pairs={{0,1},{1,0},{2,3},{3,2},{4,5},{5,4},{6,7},{7,6},{8,9},{9,8},{10,11... | collective-permute-start | bytes 1572872 | tf_op jit(solution)/shard_map/ppermute | solution.py:532
  273.6 14.3 %collective-permute-start.33 = (bf16[4,64,1024]{2,1,0:T(8,128)(2,1)S(1)}, bf16[4,64,1024]{2,1,0:T(8,128)(2,1)}, u32[]{:S(2)}, u32[]{:S(2)}) collective-permute-start(bf16[4,64,1024]{2,1,0:T(8,128)(2,1)S(1)} %collective-permute-done.32.refs_6_), channel_id=1, source_target_pairs={{0,1},{1,0},{2,3},{3,2},{4,5},{5,4},{6,7},{7,6},{8,9},{9,8},{10,11... | collective-permute-start | bytes 1572872 | tf_op jit(solution)/shard_map/ppermute | solution.py:532
  (35 other events, 458.0 us)

commit v8 on v6

--- a/solution.py
+++ b/solution.py
@@ -27,10 +27,9 @@
     return lax.dot_general(a, b, (((ca,), (cb,)), ((), ())), preferred_element_type=jnp.float32)
 
 
-def compose_kernel(store_rows, groups, capacity, place_ref, adj_ref, table_ref, near_ref, ids_ref, column_ref):
+def compose_kernel(adj_ref, table_ref, ids_ref):
     fan, near_rows = adj_ref.shape
     his = table_ref.shape[1]
-    here = place_ref[0]
     table = table_ref[...]
     parts = jnp.concatenate([table // 65536, (table // 256) % 256, table % 256], axis=0)
     parts = parts.astype(jnp.float32).astype(jnp.bfloat16)
@@ -43,43 +42,85 @@
         value = found[:LANES] * 65536.0 + found[LANES : 2 * LANES] * 256.0 + found[2 * LANES :]
         value = jnp.where(row_lo == position % LANES, value, 0.0)
         ids_ref[column : column + 1, :] = jnp.sum(value, axis=0, keepdims=True).astype(jnp.int32)
+
+
+def compose(adjacency, table):
+    near_rows, fan = adjacency.shape
+    return pl.pallas_call(
+        compose_kernel,
+        out_shape=jax.ShapeDtypeStruct((fan, near_rows), jnp.int32),
+        in_specs=[VMEM, VMEM],
+        out_specs=VMEM,
+        compiler_params=pltpu.CompilerParams(vmem_limit_bytes=32 * MIB),
+        name="compose_ids",
+    )(adjacency.T, table)
+
+
+def request_kernel(store_rows, stores, capacity, place_ref, near_ref, request_ref, column_ref):
+    groups = stores // PLANE
+    near_rows = near_ref.shape[1]
+    here, mine = place_ref[0], place_ref[1]
     near = near_ref[...]
-    per_plane = PLANE * store_rows
-    plane, row = near // per_plane, near % per_plane + 1
-    row_plane = lax.broadcasted_iota(jnp.int32, (groups, near_rows), 0)
-    marks = jnp.where(row_plane == plane, 1.0, 0.0)
+    owner, slot = near // store_rows, near % store_rows
+    row_owner = lax.broadcasted_iota(jnp.int32, (stores, near_rows), 0)
+    marks = jnp.where(row_owner == owner, 1.0, 0.0)
     earlier = lax.broadcasted_iota(jnp.int32, (near_rows, near_rows), 0) < lax.broadcasted_iota(
         jnp.int32, (near_rows, near_rows), 1
     )
     counts = dot(marks.astype(jnp.bfloat16), jnp.where(earlier, 1.0, 0.0).astype(jnp.bfloat16))
     rank = jnp.sum(counts * marks, axis=0, keepdims=True).astype(jnp.int32)
-    wanted = lax.broadcasted_iota(jnp.int32, (groups * capacity, near_rows), 0)
-    marks = jnp.where(wanted == plane * capacity + rank, 1.0, 0.0).astype(jnp.bfloat16)
+    wanted = lax.broadcasted_iota(jnp.int32, (stores * capacity, near_rows), 0)
+    marks = jnp.where(wanted == owner * capacity + rank, 1.0, 0.0).astype(jnp.bfloat16)
     line = lax.broadcasted_iota(jnp.int32, (8, near_rows), 0)
-    halves = jnp.where(line == 0, row // 256, jnp.where(line == 1, row % 256, 0))
+    halves = jnp.where(line == 0, slot // 256, jnp.where(line == 1, slot % 256, 0))
     found = dot(halves.astype(jnp.float32).astype(jnp.bfloat16), marks, 1, 1)
-    found = (found[0:1] * 256.0 + found[1:2]).astype(jnp.int32)
-    for line in range(groups * capacity // near_rows):
-        ids_ref[fan + line : fan + line + 1, :] = found[:, line * near_rows : (line + 1) * near_rows]
-    hops = here - plane
+    request_ref[...] = (found[0:1] * 256.0 + found[1:2]).astype(jnp.int32)
+    hops = here - owner // PLANE
     hops = jnp.where(hops < 0, hops + groups, hops)
-    column_ref[...] = hops * capacity + rank
-
-
-def compose(place, adjacency, table, near, store_rows, groups, capacity):
-    near_rows, fan = adjacency.shape
-    rows = fan + groups * capacity // near_rows
+    distance = lax.bitwise_xor(owner % PLANE, mine)
+    column_ref[...] = (distance * groups + hops) * capacity + rank
+
+
+def request_near(place, near, store_rows, stores, capacity):
     return pl.pallas_call(
-        functools.partial(compose_kernel, store_rows, groups, capacity),
+        functools.partial(request_kernel, store_rows, stores, capacity),
         out_shape=(
-            jax.ShapeDtypeStruct((rows, near_rows), jnp.int32),
-            jax.ShapeDtypeStruct((1, near_rows), jnp.int32),
+            jax.ShapeDtypeStruct((1, stores * capacity), jnp.int32),
+            jax.ShapeDtypeStruct(near.shape, jnp.int32),
         ),
-        in_specs=[SMEM, VMEM, VMEM, VMEM],
+        in_specs=[SMEM, VMEM],
         out_specs=(VMEM, VMEM),
         compiler_params=pltpu.CompilerParams(vmem_limit_bytes=32 * MIB),
-        name="compose_ids",
-    )(place, adjacency.T, table, near)
+        name="request_near",
+    )(place, near)
+
+
+def near_kernel(groups, place_ref, request_ref, features_ref, out_ref):
+    here, mine = place_ref[0], place_ref[1]
+    store_rows = features_ref.shape[0]
+    capacity = request_ref.shape[1]
+    slots = lax.broadcasted_iota(jnp.int32, (store_rows, PLANE * capacity), 0)
+    for k in range(groups):
+        plane = here + k
+        plane = jnp.where(plane >= groups, plane - groups, plane)
+        lines = []
+        for d in range(PLANE):
+            trainer = plane * PLANE + lax.bitwise_xor(mine, jnp.int32(d))
+            lines.append(request_ref[pl.ds(trainer, 1), :])
+        marks = jnp.where(slots == jnp.concatenate(lines, axis=1), 1.0, 0.0).astype(jnp.bfloat16)
+        out_ref[k] = dot(marks, features_ref[...], 0, 0).astype(jnp.bfloat16)
+
+
+def near_rows_held(place, requests, features, groups):
+    capacity = requests.shape[1]
+    return pl.pallas_call(
+        functools.partial(near_kernel, groups),
+        out_shape=jax.ShapeDtypeStruct((groups, PLANE * capacity, features.shape[1]), jnp.bfloat16),
+        in_specs=[SMEM, VMEM, VMEM],
+        out_specs=VMEM,
+        compiler_params=pltpu.CompilerParams(vmem_limit_bytes=32 * MIB),
+        name="near_rows",
+    )(place, requests, features)
 
 
 def sort_pairs(count):
@@ -102,11 +143,11 @@
     return [d for d in (2, 3, 4, 5, 6, 8) if d < fan] + [fan]
 
 
-def list_kernel(store_rows, fan, capacity, block, place_ref, *refs):
+def list_kernel(store_rows, block, place_ref, *refs):
     groups = len(refs) // 2
     ids_refs, out_refs = refs[:groups], refs[groups:]
     here, mine, rep = place_ref[0], place_ref[1], place_ref[2]
-    near_rows = ids_refs[0].shape[1]
+    fan, near_rows = ids_refs[0].shape
     per_plane = PLANE * store_rows
     sub = lax.broadcasted_iota(jnp.int32, (near_rows, near_rows), 0)
     lane = lax.broadcasted_iota(jnp.int32, (near_rows, near_rows), 1)
@@ -121,7 +162,7 @@
         return distance * store_rows + jnp.where(distance == 0, slot, turned)
 
     for ids_ref, out_ref in zip(ids_refs, out_refs):
-        gid = ids_ref[:fan, :]
+        gid = ids_ref[...]
         held = gid // per_plane == here
         row = jnp.where(held, turn(gid % per_plane), per_plane)
         count = jnp.sum(jnp.where(held, 1, 0), axis=0, keepdims=True)
@@ -149,22 +190,14 @@
             blocks = (ends[d].astype(jnp.int32) + (block - 1)) // block
             ahead = ahead + jnp.where(nodes == i, blocks, 0)
         out_ref[fan + 1 : fan + 2, :] = ahead
-        lists = jnp.concatenate(
-            [ids_ref[i : i + 1, :] for i in range(fan, ids_ref.shape[0])], axis=1
-        )
-        own = jnp.zeros((1, capacity), jnp.int32)
-        for g in range(groups):
-            own = own + jnp.where(here == g, lists[:, g * capacity : (g + 1) * capacity], 0)
-        own = jnp.where(own == 0, per_plane, turn(own - 1))
-        out_ref[fan + 2 : fan + 3, :capacity] = own * 8
-
-
-def row_lists(place, ids_all, store_rows, fan, capacity, block):
-    near_rows = ids_all[0].shape[1]
+
+
+def row_lists(place, ids_all, store_rows, block):
+    fan, near_rows = ids_all[0].shape
     groups = len(ids_all)
     return pl.pallas_call(
-        functools.partial(list_kernel, store_rows, fan, capacity, block),
-        out_shape=(jax.ShapeDtypeStruct((fan + 3, near_rows), jnp.int32),) * groups,
+        functools.partial(list_kernel, store_rows, block),
+        out_shape=(jax.ShapeDtypeStruct((fan + 2, near_rows), jnp.int32),) * groups,
         in_specs=[SMEM] + [VMEM] * groups,
         out_specs=(VMEM,) * groups,
         compiler_params=pltpu.CompilerParams(vmem_limit_bytes=32 * MIB),
@@ -172,12 +205,12 @@
     )(place, *ids_all)
 
 
-def partial_kernel(count, places, capacity, block, *refs):
+def partial_kernel(count, places, block, *refs):
     index_refs, piece_refs = refs[:count], refs[count : count + len(places)]
-    out_ref, table, sums, kept = refs[-5 - len(places) : -1 - len(places)]
+    out_ref, table, sums = refs[-4 - len(places) : -1 - len(places)]
     buffers = refs[-1 - len(places) : -1]
     arrived = refs[-1]
-    fan, near_rows = index_refs[0].shape[0] - 3, index_refs[0].shape[1]
+    fan, near_rows = index_refs[0].shape[0] - 2, index_refs[0].shape[1]
     units = buffers[0].shape[1] // LANES
     total = table.shape[0] // 8 - 1
     chunk = 256
@@ -212,7 +245,6 @@
 
         lax.fori_loop(0, buffer.shape[0] // chunk, fill, 0)
 
-    near_unroll = 16
     for turn, index_ref in enumerate(index_refs):
         begin = 0
         depths = depths_of(fan)
@@ -230,35 +262,24 @@
             lax.fori_loop(begin, end, step, 0)
             begin = end
 
-        def near(i, carry):
-            for u in range(near_unroll):
-                n = i * near_unroll + u
-                kept[pl.ds(pl.multiple_of(n * 8, 8), 8), :] = row(index_ref[fan + 2, n])
-            return carry
-
-        lax.fori_loop(0, capacity // near_unroll, near, 0)
         for unit in range(units):
             lanes = slice(unit * LANES, (unit + 1) * LANES)
             out_ref[turn, :near_rows, lanes] = sums[
                 pl.ds(unit, near_rows, stride=8), :
             ].astype(jnp.bfloat16)
-            out_ref[turn, near_rows:, lanes] = kept[
-                pl.ds(unit, capacity, stride=8), :
-            ].astype(jnp.bfloat16)
-
-
-def partial_sums(lists, pieces, places, total, capacity, block):
+
+
+def partial_sums(lists, pieces, places, total, block):
     near_rows = lists[0].shape[1]
     width = pieces[0].shape[1]
     return pl.pallas_call(
-        functools.partial(partial_kernel, len(lists), places, capacity, block),
-        out_shape=jax.ShapeDtypeStruct((len(lists), near_rows + capacity, width), jnp.bfloat16),
+        functools.partial(partial_kernel, len(lists), places, block),
+        out_shape=jax.ShapeDtypeStruct((len(lists), near_rows, width), jnp.bfloat16),
         in_specs=[SMEM] * len(lists) + [pl.BlockSpec(memory_space=pl.ANY)] * len(pieces),
         out_specs=VMEM,
         scratch_shapes=[
             pltpu.VMEM(((total + 1) * 8, LANES), jnp.float32),
             pltpu.VMEM(((near_rows + 1) * 8, LANES), jnp.float32),
-            pltpu.VMEM(((capacity + 1) * 8, LANES), jnp.float32),
         ]
         + [pltpu.VMEM(piece.shape, piece.dtype) for piece in pieces]
         + [pltpu.SemaphoreType.DMA((len(pieces),))],
@@ -270,13 +291,13 @@
 def trainer_kernel(sizes, scale, *refs):
     groups, rows_low, rows_top, classes, class_pad = sizes
     place_ref, labels_ref, adj_ref, column_ref, wl_ref, wt_ref = refs[:6]
-    block_refs = refs[6:-10]
+    block_refs, near_refs = refs[6 : 6 + groups], refs[6 + groups : -10]
     logits_ref, keep_ref, send_ref, li, hidden, slope, top_in, wt, weights, arrived = refs[-10:]
     seeds, fan_top = adj_ref.shape
     near_rows, low_width = li.shape
     feat = low_width // 2
     width = hidden.shape[1]
-    capacity = block_refs[0].shape[0] - near_rows
+    capacity = near_refs[0].shape[0]
     here, mine, rep = place_ref[0], place_ref[1], place_ref[2]
     fan_low = place_ref[3].astype(jnp.float32)
 
@@ -284,21 +305,16 @@
     bring.start()
     column = column_ref[...]
     rows_cap = lax.broadcasted_iota(jnp.int32, (capacity, near_rows), 0)
-    marks = [
-        jnp.where(rows_cap + k * capacity == column, 1.0, 0.0).astype(jnp.bfloat16)
-        for k in range(groups)
-    ]
-    for part in range(len(block_refs) // groups):
-        blocks = block_refs[part * groups : (part + 1) * groups]
-        share = blocks[0].shape[1]
-        near = total = None
-        for k in range(groups):
-            term = dot(marks[k], blocks[k][near_rows:, :], 0, 0)
-            near = term if near is None else near + term
-            term = blocks[k][:near_rows, :].astype(jnp.float32)
-            total = term if total is None else total + term
-        li[:, part * share : (part + 1) * share] = near.astype(jnp.bfloat16)
-        li[:, feat + part * share : feat + (part + 1) * share] = (total / fan_low).astype(jnp.bfloat16)
+    near = None
+    for d in range(PLANE):
+        marks = jnp.where(rows_cap + d * capacity == column, 1.0, 0.0).astype(jnp.bfloat16)
+        term = dot(marks, near_refs[d][...], 0, 0)
+        near = term if near is None else near + term
+    total = block_refs[0][...].astype(jnp.float32)
+    for k in range(1, groups):
+        total = total + block_refs[k][...].astype(jnp.float32)
+    li[:, :feat] = near.astype(jnp.bfloat16)
+    li[:, feat:] = (total / fan_low).astype(jnp.bfloat16)
 
     wt[...] = jnp.zeros_like(wt)
     wt[:, :classes] = wt_ref[...].astype(jnp.bfloat16)
@@ -515,7 +531,7 @@
     store_rows = features.shape[0]
     half = store_rows // 2
     near_rows, fan = adjacency_low.shape
-    capacity = min(near_rows, PLANE * (2 * near_rows // stores))
+    capacity = 2 * near_rows // stores
     classes = weights_top.shape[1]
     class_pad = -(-classes // LANES) * LANES
     rows_low, rows_top = first_low.shape[0], first_top.shape[0]
@@ -532,23 +548,34 @@
     def sibling(x):
         return lax.ppermute(x, "rep", [(0, 1), (1, 0)])
 
+    gid_near = owners_near[:, 0] * store_rows + slots_near[:, 0]
+    requests, column = request_near(place, gid_near.reshape(1, near_rows), store_rows, stores, capacity)
+    requests = lax.all_to_all(requests.reshape(stores, capacity), "store", 0, 0, tiled=True)
     quarter = half // 2
     own = lax.dynamic_slice_in_dim(features, rep * half, half, 0)
+    own, requests = lax.optimization_barrier((own, requests))
     from_x, from_y = across(own, 1), across(own, 2)
 
-    gid_near = owners_near[:, 0] * store_rows + slots_near[:, 0]
     gid_far = owners_far[:, 0] * store_rows + slots_far[:, 0]
     table = jnp.concatenate([gid_near, gid_far]).reshape(-1, LANES)
     table = jnp.pad(table, ((0, -table.shape[0] % 16), (0, 0))).T
-    ids, column = compose(
-        place, adjacency_low, table, gid_near.reshape(1, near_rows), store_rows, groups, capacity
-    )
+    ids = compose(adjacency_low, table)
     ids_all = [ids] + [along(ids, -k) for k in range(1, groups)]
     block = 16
-    lists = row_lists(place, ids_all, store_rows, fan, capacity, block)
-
-    from_x, from_y, lists = lax.optimization_barrier((from_x, from_y, lists))
+    lists = row_lists(place, ids_all, store_rows, block)
+
+    held = near_rows_held(place, requests, features, groups)
+    held, lists = lax.optimization_barrier((held, lists))
+    lined = [held[0]] + [along(held[k], k) for k in range(1, groups)]
+
+    far = groups // 2
+    sent = lined.pop(far)
+    from_x, from_y, lined = lax.optimization_barrier((from_x, from_y, lined))
     corner_a, corner_b = across(from_x[:quarter], 2), across(from_y[quarter:], 1)
+    from_x, from_y, corner_a, corner_b, sent = lax.optimization_barrier(
+        (from_x, from_y, corner_a, corner_b, sent)
+    )
+    lined.insert(far, sent)
     pieces = [features, from_x, sibling(from_x), from_y, sibling(from_y)]
     pieces += [corner_a, corner_b, sibling(corner_a), sibling(corner_b)]
     places = [0, store_rows, store_rows + half, 2 * store_rows, 2 * store_rows + half]
@@ -556,8 +583,13 @@
 
     blocks = []
     for k in range(groups):
-        made = partial_sums([lists[k]], pieces, places, PLANE * store_rows, capacity, block)
+        made = partial_sums([lists[k]], pieces, places, PLANE * store_rows, block)
         blocks.append(along(made[0], k) if k else made[0])
+
+    nears = []
+    for d in range(PLANE):
+        sheet = jnp.concatenate([part[d * capacity : (d + 1) * capacity] for part in lined])
+        nears.append(across(sheet, d) if d else sheet)
 
     scale = 1.0 / (labels.shape[0] * members)
     logits, keep, send = trainer_step(
@@ -567,7 +599,7 @@
         column,
         weights_low,
         weights_top,
-        blocks,
+        blocks + nears,
         sizes,
         scale,
     )

time: 305 us -> 292 us (0.957)
  waiting for transfers between devices: 150 us -> 120 us
  other arithmetic: 3.62 us -> 11 us
  local copies, waits for them, and re-layouts: 18.5 us -> 22.9 us
    ppermute x10 -> x13, waiting for transfers between devices: 69.2 us -> 41.6 us  [across(): return lax.ppermute(x, 'store', [(i, i ^ distance) for i in range(stores)])]
    ppermute x9, starting transfers between devices: 15.4 us -> 8.2 us  [sibling(): return lax.ppermute(x, 'rep', [(0, 1), (1, 0)])]
    all_to_all x0 -> x1, starting transfers between devices: none -> 6.66 us  [per_device(): lax.all_to_all(requests.reshape(stores, capacity), 'store', 0, 0, tiled=T...]
    ppermute x12 -> x15, waiting for transfers between devices: 73.6 us -> 67.3 us  [along(): lax.ppermute(x, 'store', [(i, (i + hops * PLANE) % stores) for i in range...]
    concatenate x0 -> x4, other arithmetic: none -> 5.9 us  [per_device(): jnp.concatenate([part[d * capacity:(d + 1) * capacity] for part in lined])]
    pallas_call x6 -> x8, Pallas kernels: 64.9 us -> 68 us  [the longest x4 58.1 us: partial_sums(): pl.pallas_call(functools.partial(partial_kernel, len(lists), places, bloc...]
    ppermute x10 -> x13, starting transfers between devices: 9.59 us -> 11.2 us  [across(): return lax.ppermute(x, 'store', [(i, i ^ distance) for i in range(stores)])]
    ppermute x12 -> x15, starting transfers between devices: 17.8 us -> 18.9 us  [along(): lax.ppermute(x, 'store', [(i, (i + hops * PLANE) % stores) for i in range...]
  transfers between devices with their start and end apart: 31 -> 38, of which waited for: 21 -> 22; matrix products, arithmetic and copies ran while one was open for 2% -> 5% of each run, Pallas kernels for 17% -> 23%
where the time goes in v8:
time: 292 us; the launch traced here: 290 us
  waiting for transfers between devices  120 us (41%)
  Pallas kernels  90.4 us (31%)
  starting transfers between devices  45 us (15%)
  local copies, waits for them, and re-layouts  22.9 us (8%)
  other arithmetic  11 us (4%)
    ppermute x15, waiting for transfers between devices, along(): lax.ppermute(x, 'store', [(i, (i + hops * PLANE) % stores) for i in range...  67.3 us
    pallas_call x4, Pallas kernels, partial_sums(): pl.pallas_call(functools.partial(partial_kernel, len(lists), places, bloc...  58.1 us
    ppermute x13, waiting for transfers between devices, across(): return lax.ppermute(x, 'store', [(i, i ^ distance) for i in range(stores)])  41.6 us
    ppermute x15, starting transfers between devices, along(): lax.ppermute(x, 'store', [(i, (i + hops * PLANE) % stores) for i in range...  18.9 us
    pallas_call x1, Pallas kernels, trainer_step(): pl.pallas_call(functools.partial(trainer_kernel, sizes, scale), out_shape...  14.4 us
    unnamed x76, local copies, waits for them, and re-layouts  13.4 us
    ppermute x13, starting transfers between devices, across(): return lax.ppermute(x, 'store', [(i, i ^ distance) for i in range(stores)])  11.2 us
    ppermute x9, waiting for transfers between devices, sibling(): return lax.ppermute(x, 'rep', [(0, 1), (1, 0)])  8.57 us
  transfers between devices with their start and end apart: 38, of which 22 were waited for; matrix products, arithmetic and copies ran while one was open for 5% of the time, Pallas kernels for 23%

profile of v8, /device:TPU:9, one launch (start us, length us, event | category | flops | bytes accessed | tf_op | source)
XLA Modules:
  0.0 290.3 jit_solution(1700434717684762316)
XLA Ops:
  4.7 6.7 %all-to-all-start = ((s32[16,1,64]{2,1,0:T(1,128)}), s32[16,1,64]{2,1,0:T(1,128)S(1)}, u32[]{:S(2)}, u32[]{:S(2)}) async-start(s32[16,1,64]{2,1,0:T(1,128)} %bitcast.5), calls=%async_computation | async-start | bytes 16384 | tf_op jit(solution)/shard_map/all_to_all | solution.py:553
  11.3 2.7 constant_dynamic-slice_fusion
  14.0 2.3 all-to-all-done
  19.7 2.6 collective-permute-start.1
  22.3 4.1 %near_rows.1 = bf16[4,256,768]{2,1,0:T(8,128)(2,1)S(1)} custom-call(s32[4]{0:T(128)S(1)} %pad_add_fusion.place_ref.refs_0_, s32[16,64]{1,0:T(8,128)S(1)} %bitcast.57, bf16[2048,768]{1,0:T(8,128)(2,1)S(1)} %copy-done), custom_call_target="tpu_custom_call" | custom-call | tf_op jit(solution)/shard_map/near_rows/pallas_call | solution.py:116
  26.4 2.7 row_lists.1
  30.9 6.0 %collective-permute-done.6 = bf16[256,768]{1,0:T(8,128)(2,1)S(1)} collective-permute-done((bf16[256,768]{1,0:T(8,128)(2,1)S(1)}, bf16[256,768]{1,0:T(8,128)(2,1)S(1)}, u32[]{:S(2)}, u32[]{:S(2)}) %collective-permute-start.6) | collective-permute-done | bytes 393248 | tf_op jit(solution)/shard_map/ppermute | solution.py:546
  36.9 11.2 %collective-permute-done.5 = bf16[256,768]{1,0:T(8,128)(2,1)S(1)} collective-permute-done((bf16[256,768]{1,0:T(8,128)(2,1)S(1)}, bf16[256,768]{1,0:T(8,128)(2,1)S(1)}, u32[]{:S(2)}, u32[]{:S(2)}) %collective-permute-start.5) | collective-permute-done | bytes 393248 | tf_op jit(solution)/shard_map/ppermute | solution.py:546
  48.1 2.3 collective-permute-done.4.refs_4_
  56.3 17.1 %collective-permute-done.9 = bf16[256,768]{1,0:T(8,128)(2,1)S(1)} collective-permute-done((bf16[256,768]{1,0:T(8,128)(2,1)S(1)}, bf16[256,768]{1,0:T(8,128)(2,1)S(1)}, u32[]{:S(2)}, u32[]{:S(2)}) %collective-permute-start.9) | collective-permute-done | bytes 393248 | tf_op jit(solution)/shard_map/ppermute | solution.py:546
  79.3 2.2 collective-permute-done.13.refs_9_
  84.7 14.6 %partial_sums.5 = bf16[1,512,768]{2,1,0:T(8,128)(2,1)} custom-call(s32[17,512]{1,0:T(8,128)} %copy-done.11, bf16[2048,768]{1,0:T(8,128)(2,1)} %refs_1_.7, bf16[1024,768]{1,0:T(8,128)(2,1)} %collective-permute-done.3.refs_2_, bf16[1024,768]{1,0:T(8,128)(2,1)} %copy-done.16, bf16[1024,768]{1,0:T(8,128)(2,1)} %collective-permute-done.4.refs_4_, ...), custom_call_target="tpu_custom_call" | custom-call | tf_op jit(solution)/shard_map/partial_sums/pallas_call | solution.py:275
  100.6 14.6 %partial_sums.6 = bf16[1,512,768]{2,1,0:T(8,128)(2,1)} custom-call(s32[17,512]{1,0:T(8,128)} %copy-done.10, bf16[2048,768]{1,0:T(8,128)(2,1)} %refs_1_.7, bf16[1024,768]{1,0:T(8,128)(2,1)} %collective-permute-done.3.refs_2_, bf16[1024,768]{1,0:T(8,128)(2,1)} %copy-done.16, bf16[1024,768]{1,0:T(8,128)(2,1)} %collective-permute-done.4.refs_4_, ...), custom_call_target="tpu_custom_call" | custom-call | tf_op jit(solution)/shard_map/partial_sums/pallas_call | solution.py:275
  115.3 2.7 collective-permute-start.15
  118.1 14.2 %partial_sums.7 = bf16[1,512,768]{2,1,0:T(8,128)(2,1)} custom-call(s32[17,512]{1,0:T(8,128)} %copy-done.9, bf16[2048,768]{1,0:T(8,128)(2,1)} %refs_1_.7, bf16[1024,768]{1,0:T(8,128)(2,1)} %collective-permute-done.3.refs_2_, bf16[1024,768]{1,0:T(8,128)(2,1)} %copy-done.16, bf16[1024,768]{1,0:T(8,128)(2,1)} %collective-permute-done.4.refs_4_, ...), custom_call_target="tpu_custom_call" | custom-call | tf_op jit(solution)/shard_map/partial_sums/pallas_call | solution.py:275
  144.4 14.7 %partial_sums.4 = bf16[1,512,768]{2,1,0:T(8,128)(2,1)} custom-call(s32[17,512]{1,0:T(8,128)} %copy-done.8, bf16[2048,768]{1,0:T(8,128)(2,1)} %refs_1_.7, bf16[1024,768]{1,0:T(8,128)(2,1)} %collective-permute-done.3.refs_2_, bf16[1024,768]{1,0:T(8,128)(2,1)} %copy-done.16, bf16[1024,768]{1,0:T(8,128)(2,1)} %collective-permute-done.4.refs_4_, ...), custom_call_target="tpu_custom_call" | custom-call | tf_op jit(solution)/shard_map/partial_sums/pallas_call | solution.py:275
  159.1 9.3 %collective-permute-done.15.refs_8_ = bf16[512,768]{1,0:T(8,128)(2,1)S(1)} collective-permute-done((bf16[512,768]{1,0:T(8,128)(2,1)}, bf16[512,768]{1,0:T(8,128)(2,1)S(1)}, u32[]{:S(2)}, u32[]{:S(2)}) %collective-permute-start.15) | collective-permute-done | bytes 786464 | tf_op jit(solution)/shard_map/ppermute | solution.py:546
  168.5 4.1 %collective-permute-done.16.refs_9_ = bf16[512,768]{1,0:T(8,128)(2,1)} collective-permute-done((bf16[512,768]{1,0:T(8,128)(2,1)}, bf16[512,768]{1,0:T(8,128)(2,1)}, u32[]{:S(2)}, u32[]{:S(2)}) %collective-permute-start.16) | collective-permute-done | bytes 786464 | tf_op jit(solution)/shard_map/ppermute | solution.py:546
  172.6 14.4 %trainer_step.1 = (f32[128,153]{1,0:T(8,128)}, f32[4,4,64,1024]{3,2,1,0:T(8,128)}, bf16[4,4,64,1024]{3,2,1,0:T(8,128)(2,1)}) custom-call(s32[4]{0:T(128)} %copy-done.13, s32[128,1]{1,0:T(8,128)} %copy.36.refs_1_, s32[128,10]{1,0:T(8,128)} %copy.37.refs_2_, s32[1,512]{1,0:T(1,128)} %copy-done.15, f32[1536,1024]{1,0:T(8,128)} %refs_4_.2, ...), custom_call_target="tpu_custom_call" | custom-call | tf_op jit(solution)/shard_map/trainer_step/pallas_call | solution.py:397
  187.7 4.0 %collective-permute-done.20 = bf16[4,4,64,1024]{3,2,1,0:T(8,128)(2,1)S(1)} collective-permute-done((bf16[4,4,64,1024]{3,2,1,0:T(8,128)(2,1)}, bf16[4,4,64,1024]{3,2,1,0:T(8,128)(2,1)S(1)}, u32[]{:S(2)}, u32[]{:S(2)}) %collective-permute-start.20) | collective-permute-done | bytes 2097184 | tf_op jit(solution)/shard_map/ppermute | solution.py:549
  191.7 3.1 %fusion.3 = (bf16[4,4,64,1024]{3,2,1,0:T(8,128)(2,1)S(1)}, f32[4,4,64,1024]{3,2,1,0:T(8,128)S(1)}) fusion(f32[4,4,64,1024]{3,2,1,0:T(8,128)} %get-tuple-element.64, bf16[4,4,64,1024]{3,2,1,0:T(8,128)(2,1)S(1)} %collective-permute-done.20), kind=kLoop, calls=%fused_computation.26 | loop fusion | flops 3145728 | bytes 12582912 | tf_op jit(solution)/shard_map/convert.5
  197.6 10.5 %collective-permute-done.21 = bf16[4,64,1024]{2,1,0:T(8,128)(2,1)S(1)} collective-permute-done((bf16[4,64,1024]{2,1,0:T(8,128)(2,1)S(1)}, bf16[4,64,1024]{2,1,0:T(8,128)(2,1)S(1)}, u32[]{:S(2)}, u32[]{:S(2)}) %collective-permute-start.21) | collective-permute-done | bytes 524320 | tf_op jit(solution)/shard_map/ppermute | solution.py:543
  208.1 11.0 %collective-permute-done.23 = bf16[4,64,1024]{2,1,0:T(8,128)(2,1)S(1)} collective-permute-done((bf16[4,64,1024]{2,1,0:T(8,128)(2,1)S(1)}, bf16[4,64,1024]{2,1,0:T(8,128)(2,1)S(1)}, u32[]{:S(2)}, u32[]{:S(2)}) %collective-permute-start.23) | collective-permute-done | bytes 524320 | tf_op jit(solution)/shard_map/ppermute | solution.py:543
  220.9 2.3 collective-permute-start.24
  226.2 5.4 %collective-permute-done.24.refs_1_ = bf16[64,1024]{1,0:T(8,128)(2,1)S(1)} collective-permute-done((bf16[64,1024]{1,0:T(8,128)(2,1)S(1)}, bf16[64,1024]{1,0:T(8,128)(2,1)S(1)}, u32[]{:S(2)}, u32[]{:S(2)}) %collective-permute-start.24) | collective-permute-done | bytes 131104 | tf_op jit(solution)/shard_map/ppermute | solution.py:546
  237.3 7.9 %collective-permute-done.28 = bf16[64,1024]{1,0:T(8,128)(2,1)S(1)} collective-permute-done((bf16[64,1024]{1,0:T(8,128)(2,1)S(1)}, bf16[64,1024]{1,0:T(8,128)(2,1)S(1)}, u32[]{:S(2)}, u32[]{:S(2)}) %collective-permute-start.28) | collective-permute-done | bytes 131104 | tf_op jit(solution)/shard_map/ppermute | solution.py:546
  251.9 8.5 %collective-permute-done.35.refs_6_ = bf16[4,64,1024]{2,1,0:T(8,128)(2,1)S(1)} collective-permute-done((bf16[4,64,1024]{2,1,0:T(8,128)(2,1)S(1)}, bf16[4,64,1024]{2,1,0:T(8,128)(2,1)S(1)}, u32[]{:S(2)}, u32[]{:S(2)}) %collective-permute-start.35) | collective-permute-done | bytes 524320 | tf_op jit(solution)/shard_map/ppermute | solution.py:543
  260.5 3.6 %collective-permute-start.36 = (bf16[4,64,1024]{2,1,0:T(8,128)(2,1)S(1)}, bf16[4,64,1024]{2,1,0:T(8,128)(2,1)}, u32[]{:S(2)}, u32[]{:S(2)}) collective-permute-start(bf16[4,64,1024]{2,1,0:T(8,128)(2,1)S(1)} %collective-permute-done.35.refs_6_), channel_id=1, source_target_pairs={{0,1},{1,0},{2,3},{3,2},{4,5},{5,4},{6,7},{7,6},{8,9},{9,8},{10,11... | collective-permute-start | bytes 1572872 | tf_op jit(solution)/shard_map/ppermute | solution.py:549
  264.0 9.2 %collective-permute-done.33.refs_4_ = bf16[4,64,1024]{2,1,0:T(8,128)(2,1)} collective-permute-done((bf16[4,64,1024]{2,1,0:T(8,128)(2,1)S(1)}, bf16[4,64,1024]{2,1,0:T(8,128)(2,1)}, u32[]{:S(2)}, u32[]{:S(2)}) %collective-permute-start.33) | collective-permute-done | bytes 524320 | tf_op jit(solution)/shard_map/ppermute | solution.py:543
  276.4 2.8 copy-done.1
  279.2 7.1 %apply_updates.1 = (f32[4,4,2,48,1024]{4,3,2,1,0:T(8,128)}, f32[4,4,2,64,153]{4,3,2,1,0:T(8,128)S(1)}) custom-call(s32[4]{0:T(128)S(1)} %copy-done.14, f32[4,4,2,48,1024]{4,3,2,1,0:T(8,128)S(1)} %bitcast.53, f32[4,4,2,64,153]{4,3,2,1,0:T(8,128)S(1)} %bitcast.54, bf16[4,64,1024]{2,1,0:T(8,128)(2,1)S(1)} %pad_maximum_fusion.refs_0_, ...), custom_call_target="tpu_custom_call" | custom-call | tf_op jit(solution)/shard_map/apply_updates/pallas_call | solution.py:495
  287.6 2.7 copy.41
  (158 shorter events, 62.3 us)
Async XLA Ops:
  4.7 11.6 %all-to-all-start = ((s32[16,1,64]{2,1,0:T(1,128)}), s32[16,1,64]{2,1,0:T(1,128)S(1)}, u32[]{:S(2)}, u32[]{:S(2)}) async-start(s32[16,1,64]{2,1,0:T(1,128)} %bitcast.5), calls=%async_computation | async-start | bytes 16384 | tf_op jit(solution)/shard_map/all_to_all | solution.py:553
  16.3 34.1 %collective-permute-start.4 = (bf16[1024,768]{1,0:T(8,128)(2,1)}, bf16[1024,768]{1,0:T(8,128)(2,1)}, u32[]{:S(2)}, u32[]{:S(2)}) collective-permute-start(bf16[1024,768]{1,0:T(8,128)(2,1)} %constant_dynamic-slice_fusion), channel_id=1, source_target_pairs={{0,4},{2,6},{4,0},{6,2},{8,12},{10,14},{12,8},{14,10},{16,20},{18,... | collective-permute-start | bytes 4718600 | tf_op jit(solution)/shard_map/ppermute | solution.py:543
  16.6 33.8 %collective-permute-start.3 = (bf16[1024,768]{1,0:T(8,128)(2,1)}, bf16[1024,768]{1,0:T(8,128)(2,1)}, u32[]{:S(2)}, u32[]{:S(2)}) collective-permute-start(bf16[1024,768]{1,0:T(8,128)(2,1)} %constant_dynamic-slice_fusion), channel_id=1, source_target_pairs={{0,2},{2,0},{4,6},{6,4},{8,10},{10,8},{12,14},{14,12},{16,18},{18,... | collective-permute-start | bytes 4718600 | tf_op jit(solution)/shard_map/ppermute | solution.py:543
  19.0 7.4 %collective-permute-start.2 = (s32[15,512]{1,0:T(8,128)S(1)}, s32[15,512]{1,0:T(8,128)S(1)}, u32[]{:S(2)}, u32[]{:S(2)}) collective-permute-start(s32[15,512]{1,0:T(8,128)S(1)} %compose_ids.1.refs_0_), channel_id=1, source_target_pairs={{0,8},{2,10},{4,12},{6,14},{8,16},{10,18},{12,20},{14,22},{16,24},... | collective-permute-start | bytes 92168 | tf_op jit(solution)/shard_map/ppermute | solution.py:546
  19.7 6.7 %collective-permute-start.1 = (s32[15,512]{1,0:T(8,128)S(1)}, s32[15,512]{1,0:T(8,128)S(1)}, u32[]{:S(2)}, u32[]{:S(2)}) collective-permute-start(s32[15,512]{1,0:T(8,128)S(1)} %compose_ids.1.refs_0_), channel_id=1, source_target_pairs={{0,16},{2,18},{4,20},{6,22},{8,24},{10,26},{12,28},{14,30},{16,0},... | collective-permute-start | bytes 92168 | tf_op jit(solution)/shard_map/ppermute | solution.py:546
  29.3 7.5 %collective-permute-start.6 = (bf16[256,768]{1,0:T(8,128)(2,1)S(1)}, bf16[256,768]{1,0:T(8,128)(2,1)S(1)}, u32[]{:S(2)}, u32[]{:S(2)}) collective-permute-start(bf16[256,768]{1,0:T(8,128)(2,1)S(1)} %get-tuple-element.102), channel_id=1, source_target_pairs={{0,24},{2,26},{4,28},{6,30},{8,0},{10,2},{12,4},{14,6},{16,8},{18,... | collective-permute-start | bytes 1179656 | tf_op jit(solution)/shard_map/ppermute | solution.py:546
  30.5 17.5 %collective-permute-start.5 = (bf16[256,768]{1,0:T(8,128)(2,1)S(1)}, bf16[256,768]{1,0:T(8,128)(2,1)S(1)}, u32[]{:S(2)}, u32[]{:S(2)}) collective-permute-start(bf16[256,768]{1,0:T(8,128)(2,1)S(1)} %get-tuple-element.103), channel_id=1, source_target_pairs={{0,8},{2,10},{4,12},{6,14},{8,16},{10,18},{12,20},{14,22},{16,24},... | collective-permute-start | bytes 1179656 | tf_op jit(solution)/shard_map/ppermute | solution.py:546
  52.8 20.6 %collective-permute-start.8 = (bf16[512,768]{1,0:T(8,128)(2,1)S(1)}, bf16[512,768]{1,0:T(8,128)(2,1)S(1)}, u32[]{:S(2)}, u32[]{:S(2)}) collective-permute-start(bf16[512,768]{1,0:T(8,128)(2,1)S(1)} %slice.100), channel_id=1, source_target_pairs={{0,2},{2,0},{4,6},{6,4},{8,10},{10,8},{12,14},{14,12},{16,18},{18,... | collective-permute-start | bytes 2359304 | tf_op jit(solution)/shard_map/ppermute | solution.py:543
  53.2 20.2 %collective-permute-start.7 = (bf16[512,768]{1,0:T(8,128)(2,1)S(1)}, bf16[512,768]{1,0:T(8,128)(2,1)S(1)}, u32[]{:S(2)}, u32[]{:S(2)}) collective-permute-start(bf16[512,768]{1,0:T(8,128)(2,1)S(1)} %slice.99), channel_id=1, source_target_pairs={{0,4},{2,6},{4,0},{6,2},{8,12},{10,14},{12,8},{14,10},{16,20},{18,... | collective-permute-start | bytes 2359304 | tf_op jit(solution)/shard_map/ppermute | solution.py:543
  54.4 19.0 %collective-permute-start.9 = (bf16[256,768]{1,0:T(8,128)(2,1)S(1)}, bf16[256,768]{1,0:T(8,128)(2,1)S(1)}, u32[]{:S(2)}, u32[]{:S(2)}) collective-permute-start(bf16[256,768]{1,0:T(8,128)(2,1)S(1)} %get-tuple-element.101), channel_id=1, source_target_pairs={{0,16},{2,18},{4,20},{6,22},{8,24},{10,26},{12,28},{14,30},{16,0},... | collective-permute-start | bytes 1179656 | tf_op jit(solution)/shard_map/ppermute | solution.py:546
  73.4 8.1 %collective-permute-start.10 = (bf16[1024,768]{1,0:T(8,128)(2,1)}, bf16[1024,768]{1,0:T(8,128)(2,1)S(1)}, u32[]{:S(2)}, u32[]{:S(2)}) collective-permute-start(bf16[1024,768]{1,0:T(8,128)(2,1)} %collective-permute-done.3.refs_2_), channel_id=1, source_target_pairs={{0,1},{1,0},{2,3},{3,2},{4,5},{5,4},{6,7},{7,6},{8,9},{9,8},{10,11... | collective-permute-start | bytes 4718600 | tf_op jit(solution)/shard_map/ppermute | solution.py:549
  74.0 8.5 %collective-permute-start.11 = (bf16[1024,768]{1,0:T(8,128)(2,1)}, bf16[1024,768]{1,0:T(8,128)(2,1)S(1)}, u32[]{:S(2)}, u32[]{:S(2)}) collective-permute-start(bf16[1024,768]{1,0:T(8,128)(2,1)} %collective-permute-done.4.refs_4_), channel_id=1, source_target_pairs={{0,1},{1,0},{2,3},{3,2},{4,5},{5,4},{6,7},{7,6},{8,9},{9,8},{10,11... | collective-permute-start | bytes 4718600 | tf_op jit(solution)/shard_map/ppermute | solution.py:549
  74.5 7.0 %collective-permute-start.13 = (bf16[512,768]{1,0:T(8,128)(2,1)S(1)}, bf16[512,768]{1,0:T(8,128)(2,1)S(1)}, u32[]{:S(2)}, u32[]{:S(2)}) collective-permute-start(bf16[512,768]{1,0:T(8,128)(2,1)S(1)} %collective-permute-done.8.refs_7_), channel_id=1, source_target_pairs={{0,1},{1,0},{2,3},{3,2},{4,5},{5,4},{6,7},{7,6},{8,9},{9,8},{10,11... | collective-permute-start | bytes 2359304 | tf_op jit(solution)/shard_map/ppermute | solution.py:549
  77.5 59.7 %collective-permute-start.17 = (bf16[256,768]{1,0:T(8,128)(2,1)}, bf16[256,768]{1,0:T(8,128)(2,1)S(1)}, u32[]{:S(2)}, u32[]{:S(2)}) collective-permute-start(bf16[256,768]{1,0:T(8,128)(2,1)} %pad_maximum_fusion.2), channel_id=1, source_target_pairs={{0,2},{2,0},{4,6},{6,4},{8,10},{10,8},{12,14},{14,12},{16,18},{18,... | collective-permute-start | bytes 1179656 | tf_op jit(solution)/shard_map/ppermute | solution.py:543
  99.3 59.8 %collective-permute-start.14 = (bf16[512,768]{1,0:T(8,128)(2,1)}, bf16[512,768]{1,0:T(8,128)(2,1)S(1)}, u32[]{:S(2)}, u32[]{:S(2)}) collective-permute-start(bf16[512,768]{1,0:T(8,128)(2,1)} %bitcast.62), channel_id=1, source_target_pairs={{0,8},{2,10},{4,12},{6,14},{8,16},{10,18},{12,20},{14,22},{16,24},... | collective-permute-start | bytes 2359304 | tf_op jit(solution)/shard_map/ppermute | solution.py:546
  115.3 53.2 %collective-permute-start.15 = (bf16[512,768]{1,0:T(8,128)(2,1)}, bf16[512,768]{1,0:T(8,128)(2,1)S(1)}, u32[]{:S(2)}, u32[]{:S(2)}) collective-permute-start(bf16[512,768]{1,0:T(8,128)(2,1)} %bitcast.63), channel_id=1, source_target_pairs={{0,16},{2,18},{4,20},{6,22},{8,24},{10,26},{12,28},{14,30},{16,0},... | collective-permute-start | bytes 2359304 | tf_op jit(solution)/shard_map/ppermute | solution.py:546
  132.3 40.3 %collective-permute-start.16 = (bf16[512,768]{1,0:T(8,128)(2,1)}, bf16[512,768]{1,0:T(8,128)(2,1)}, u32[]{:S(2)}, u32[]{:S(2)}) collective-permute-start(bf16[512,768]{1,0:T(8,128)(2,1)} %bitcast.64), channel_id=1, source_target_pairs={{0,24},{2,26},{4,28},{6,30},{8,0},{10,2},{12,4},{14,6},{16,8},{18,... | collective-permute-start | bytes 2359304 | tf_op jit(solution)/shard_map/ppermute | solution.py:546
  135.1 24.1 %collective-permute-start.18 = (bf16[256,768]{1,0:T(8,128)(2,1)}, bf16[256,768]{1,0:T(8,128)(2,1)}, u32[]{:S(2)}, u32[]{:S(2)}) collective-permute-start(bf16[256,768]{1,0:T(8,128)(2,1)} %pad_maximum_fusion.3), channel_id=1, source_target_pairs={{0,4},{2,6},{4,0},{6,2},{8,12},{10,14},{12,8},{14,10},{16,20},{18,... | collective-permute-start | bytes 1179656 | tf_op jit(solution)/shard_map/ppermute | solution.py:543
  137.2 21.9 %collective-permute-start.19 = (bf16[256,768]{1,0:T(8,128)(2,1)}, bf16[256,768]{1,0:T(8,128)(2,1)}, u32[]{:S(2)}, u32[]{:S(2)}) collective-permute-start(bf16[256,768]{1,0:T(8,128)(2,1)} %pad_maximum_fusion.4), channel_id=1, source_target_pairs={{0,6},{2,4},{4,2},{6,0},{8,14},{10,12},{12,10},{14,8},{16,22},{18,... | collective-permute-start | bytes 1179656 | tf_op jit(solution)/shard_map/ppermute | solution.py:543
  194.9 13.2 %collective-permute-start.21 = (bf16[4,64,1024]{2,1,0:T(8,128)(2,1)S(1)}, bf16[4,64,1024]{2,1,0:T(8,128)(2,1)S(1)}, u32[]{:S(2)}, u32[]{:S(2)}) collective-permute-start(bf16[4,64,1024]{2,1,0:T(8,128)(2,1)S(1)} %get-tuple-element.98), channel_id=1, source_target_pairs={{0,2},{2,0},{4,6},{6,4},{8,10},{10,8},{12,14},{14,12},{16,18},{18,... | collective-permute-start | bytes 1572872 | tf_op jit(solution)/shard_map/ppermute | solution.py:543
  196.1 23.1 %collective-permute-start.23 = (bf16[4,64,1024]{2,1,0:T(8,128)(2,1)S(1)}, bf16[4,64,1024]{2,1,0:T(8,128)(2,1)S(1)}, u32[]{:S(2)}, u32[]{:S(2)}) collective-permute-start(bf16[4,64,1024]{2,1,0:T(8,128)(2,1)S(1)} %get-tuple-element.99), channel_id=1, source_target_pairs={{0,6},{2,4},{4,2},{6,0},{8,14},{10,12},{12,10},{14,8},{16,22},{18,... | collective-permute-start | bytes 1572872 | tf_op jit(solution)/shard_map/ppermute | solution.py:543
  196.2 23.0 %collective-permute-start.22 = (bf16[4,64,1024]{2,1,0:T(8,128)(2,1)S(1)}, bf16[4,64,1024]{2,1,0:T(8,128)(2,1)S(1)}, u32[]{:S(2)}, u32[]{:S(2)}) collective-permute-start(bf16[4,64,1024]{2,1,0:T(8,128)(2,1)S(1)} %get-tuple-element.100), channel_id=1, source_target_pairs={{0,4},{2,6},{4,0},{6,2},{8,12},{10,14},{12,8},{14,10},{16,20},{18,... | collective-permute-start | bytes 1572872 | tf_op jit(solution)/shard_map/ppermute | solution.py:543
  219.6 5.3 %collective-permute-start.26 = (bf16[64,1024]{1,0:T(8,128)(2,1)S(1)}, bf16[64,1024]{1,0:T(8,128)(2,1)S(1)}, u32[]{:S(2)}, u32[]{:S(2)}) collective-permute-start(bf16[64,1024]{1,0:T(8,128)(2,1)S(1)} %get-tuple-element.105), channel_id=1, source_target_pairs={{0,24},{2,26},{4,28},{6,30},{8,0},{10,2},{12,4},{14,6},{16,8},{18,... | collective-permute-start | bytes 393224 | tf_op jit(solution)/shard_map/ppermute | solution.py:546
  219.6 6.6 %collective-permute-start.25 = (bf16[64,1024]{1,0:T(8,128)(2,1)S(1)}, bf16[64,1024]{1,0:T(8,128)(2,1)S(1)}, u32[]{:S(2)}, u32[]{:S(2)}) collective-permute-start(bf16[64,1024]{1,0:T(8,128)(2,1)S(1)} %get-tuple-element.106), channel_id=1, source_target_pairs={{0,16},{2,18},{4,20},{6,22},{8,24},{10,26},{12,28},{14,30},{16,0},... | collective-permute-start | bytes 393224 | tf_op jit(solution)/shard_map/ppermute | solution.py:546
  220.9 10.8 %collective-permute-start.24 = (bf16[64,1024]{1,0:T(8,128)(2,1)S(1)}, bf16[64,1024]{1,0:T(8,128)(2,1)S(1)}, u32[]{:S(2)}, u32[]{:S(2)}) collective-permute-start(bf16[64,1024]{1,0:T(8,128)(2,1)S(1)} %get-tuple-element.107), channel_id=1, source_target_pairs={{0,8},{2,10},{4,12},{6,14},{8,16},{10,18},{12,20},{14,22},{16,24},... | collective-permute-start | bytes 393224 | tf_op jit(solution)/shard_map/ppermute | solution.py:546
  234.8 10.4 %collective-permute-start.28 = (bf16[64,1024]{1,0:T(8,128)(2,1)S(1)}, bf16[64,1024]{1,0:T(8,128)(2,1)S(1)}, u32[]{:S(2)}, u32[]{:S(2)}) collective-permute-start(bf16[64,1024]{1,0:T(8,128)(2,1)S(1)} %get-tuple-element.66), channel_id=1, source_target_pairs={{0,16},{2,18},{4,20},{6,22},{8,24},{10,26},{12,28},{14,30},{16,0},... | collective-permute-start | bytes 393224 | tf_op jit(solution)/shard_map/ppermute | solution.py:546
  235.7 11.3 %collective-permute-start.27 = (bf16[64,1024]{1,0:T(8,128)(2,1)S(1)}, bf16[64,1024]{1,0:T(8,128)(2,1)S(1)}, u32[]{:S(2)}, u32[]{:S(2)}) collective-permute-start(bf16[64,1024]{1,0:T(8,128)(2,1)S(1)} %get-tuple-element.66), channel_id=1, source_target_pairs={{0,24},{2,26},{4,28},{6,30},{8,0},{10,2},{12,4},{14,6},{16,8},{18,... | collective-permute-start | bytes 393224 | tf_op jit(solution)/shard_map/ppermute | solution.py:546
  247.1 13.3 %collective-permute-start.35 = (bf16[4,64,1024]{2,1,0:T(8,128)(2,1)S(1)}, bf16[4,64,1024]{2,1,0:T(8,128)(2,1)S(1)}, u32[]{:S(2)}, u32[]{:S(2)}) collective-permute-start(bf16[4,64,1024]{2,1,0:T(8,128)(2,1)S(1)} %pad_maximum_fusion.refs_0_), channel_id=1, source_target_pairs={{0,6},{2,4},{4,2},{6,0},{8,14},{10,12},{12,10},{14,8},{16,22},{18,... | collective-permute-start | bytes 1572872 | tf_op jit(solution)/shard_map/ppermute | solution.py:543
  249.0 24.3 %collective-permute-start.33 = (bf16[4,64,1024]{2,1,0:T(8,128)(2,1)S(1)}, bf16[4,64,1024]{2,1,0:T(8,128)(2,1)}, u32[]{:S(2)}, u32[]{:S(2)}) collective-permute-start(bf16[4,64,1024]{2,1,0:T(8,128)(2,1)S(1)} %pad_maximum_fusion.refs_0_), channel_id=1, source_target_pairs={{0,4},{2,6},{4,0},{6,2},{8,12},{10,14},{12,8},{14,10},{16,20},{18,... | collective-permute-start | bytes 1572872 | tf_op jit(solution)/shard_map/ppermute | solution.py:543
  250.1 23.6 %collective-permute-start.31 = (bf16[4,64,1024]{2,1,0:T(8,128)(2,1)S(1)}, bf16[4,64,1024]{2,1,0:T(8,128)(2,1)}, u32[]{:S(2)}, u32[]{:S(2)}) collective-permute-start(bf16[4,64,1024]{2,1,0:T(8,128)(2,1)S(1)} %pad_maximum_fusion.refs_0_), channel_id=1, source_target_pairs={{0,2},{2,0},{4,6},{6,4},{8,10},{10,8},{12,14},{14,12},{16,18},{18,... | collective-permute-start | bytes 1572872 | tf_op jit(solution)/shard_map/ppermute | solution.py:543
  250.3 25.0 %collective-permute-start.30 = (bf16[4,64,1024]{2,1,0:T(8,128)(2,1)S(1)}, bf16[4,64,1024]{2,1,0:T(8,128)(2,1)}, u32[]{:S(2)}, u32[]{:S(2)}) collective-permute-start(bf16[4,64,1024]{2,1,0:T(8,128)(2,1)S(1)} %pad_maximum_fusion.refs_0_), channel_id=1, source_target_pairs={{0,1},{1,0},{2,3},{3,2},{4,5},{5,4},{6,7},{7,6},{8,9},{9,8},{10,11... | collective-permute-start | bytes 1572872 | tf_op jit(solution)/shard_map/ppermute | solution.py:549
  260.5 14.8 %collective-permute-start.36 = (bf16[4,64,1024]{2,1,0:T(8,128)(2,1)S(1)}, bf16[4,64,1024]{2,1,0:T(8,128)(2,1)}, u32[]{:S(2)}, u32[]{:S(2)}) collective-permute-start(bf16[4,64,1024]{2,1,0:T(8,128)(2,1)S(1)} %collective-permute-done.35.refs_6_), channel_id=1, source_target_pairs={{0,1},{1,0},{2,3},{3,2},{4,5},{5,4},{6,7},{7,6},{8,9},{9,8},{10,11... | collective-permute-start | bytes 1572872 | tf_op jit(solution)/shard_map/ppermute | solution.py:549
  (42 other events, 634.8 us)

commit v9 on v8

--- a/solution.py
+++ b/solution.py
@@ -283,7 +283,7 @@
         ]
         + [pltpu.VMEM(piece.shape, piece.dtype) for piece in pieces]
         + [pltpu.SemaphoreType.DMA((len(pieces),))],
-        compiler_params=pltpu.CompilerParams(vmem_limit_bytes=60 * MIB),
+        compiler_params=pltpu.CompilerParams(vmem_limit_bytes=50 * MIB),
         name="partial_sums",
     )(*lists, *pieces)
 
@@ -501,7 +501,7 @@
             out_specs=specs,
         ),
         out_shape=[jax.ShapeDtypeStruct(a.shape, jnp.float32) for a in (low, top)],
-        compiler_params=pltpu.CompilerParams(vmem_limit_bytes=32 * MIB),
+        compiler_params=pltpu.CompilerParams(vmem_limit_bytes=60 * MIB),
         name="apply_updates",
     )(place, low, top, *deltas)
     return nl.reshape(wl.shape), nt.reshape(wt.shape)

time: 292 us -> 290 us (level)
  waiting for transfers between devices: 120 us -> 125 us
  local copies, waits for them, and re-layouts: 22.9 us -> 18.1 us
    pallas_call x1, Pallas kernels: 7.12 us -> 11 us  [apply_updates(): pl.pallas_call(functools.partial(apply_kernel, sizes), grid_spec=pltpu.Pr...]
    ppermute x15, waiting for transfers between devices: 67.3 us -> 70.9 us  [along(): lax.ppermute(x, 'store', [(i, (i + hops * PLANE) % stores) for i in range...]
    unnamed x76 -> x48, local copies, waits for them, and re-layouts: 13.4 us -> 9.97 us
  transfers between devices with their start and end apart: 38 -> 38, of which waited for: 22 -> 23; matrix products, arithmetic and copies ran while one was open for 5% -> 4% of each run, Pallas kernels for 23% -> 22%
where the time goes in v9:
time: 290 us; the launch traced here: 288 us
  waiting for transfers between devices  125 us (43%)
  Pallas kernels  91.8 us (32%)
  starting transfers between devices  44 us (15%)
  local copies, waits for them, and re-layouts  18.1 us (6%)
  other arithmetic  8.41 us (3%)
    ppermute x15, waiting for transfers between devices, along(): lax.ppermute(x, 'store', [(i, (i + hops * PLANE) % stores) for i in range...  70.9 us
    pallas_call x4, Pallas kernels, partial_sums(): pl.pallas_call(functools.partial(partial_kernel, len(lists), places, bloc...  55.6 us
    ppermute x13, waiting for transfers between devices, across(): return lax.ppermute(x, 'store', [(i, i ^ distance) for i in range(stores)])  40.7 us
    ppermute x15, starting transfers between devices, along(): lax.ppermute(x, 'store', [(i, (i + hops * PLANE) % stores) for i in range...  18.6 us
    pallas_call x1, Pallas kernels, trainer_step(): pl.pallas_call(functools.partial(trainer_kernel, sizes, scale), out_shape...  14.4 us
    ppermute x9, waiting for transfers between devices, sibling(): return lax.ppermute(x, 'rep', [(0, 1), (1, 0)])  11.2 us
    pallas_call x1, Pallas kernels, apply_updates(): pl.pallas_call(functools.partial(apply_kernel, sizes), grid_spec=pltpu.Pr...  11 us
    unnamed x48, local copies, waits for them, and re-layouts  9.97 us
  transfers between devices with their start and end apart: 38, of which 23 were waited for; matrix products, arithmetic and copies ran while one was open for 4% of the time, Pallas kernels for 22%

profile of v9, /device:TPU:9, one launch (start us, length us, event | category | flops | bytes accessed | tf_op | source)
XLA Modules:
  0.0 288.4 jit_solution(5414030437440054725)
XLA Ops:
  4.7 6.7 %all-to-all-start = ((s32[16,1,64]{2,1,0:T(1,128)}), s32[16,1,64]{2,1,0:T(1,128)S(1)}, u32[]{:S(2)}, u32[]{:S(2)}) async-start(s32[16,1,64]{2,1,0:T(1,128)} %bitcast.5), calls=%async_computation | async-start | bytes 16384 | tf_op jit(solution)/shard_map/all_to_all | solution.py:553
  11.3 2.7 constant_dynamic-slice_fusion
  14.0 2.3 all-to-all-done
  19.7 2.6 collective-permute-start.1
  22.3 4.1 %near_rows.1 = bf16[4,256,768]{2,1,0:T(8,128)(2,1)S(1)} custom-call(s32[4]{0:T(128)S(1)} %pad_add_fusion.place_ref.refs_0_, s32[16,64]{1,0:T(8,128)S(1)} %bitcast.55, bf16[2048,768]{1,0:T(8,128)(2,1)S(1)} %copy-done), custom_call_target="tpu_custom_call" | custom-call | tf_op jit(solution)/shard_map/near_rows/pallas_call | solution.py:116
  26.4 2.7 row_lists.1
  30.8 6.0 %collective-permute-done.6 = bf16[256,768]{1,0:T(8,128)(2,1)S(1)} collective-permute-done((bf16[256,768]{1,0:T(8,128)(2,1)S(1)}, bf16[256,768]{1,0:T(8,128)(2,1)S(1)}, u32[]{:S(2)}, u32[]{:S(2)}) %collective-permute-start.6) | collective-permute-done | bytes 393248 | tf_op jit(solution)/shard_map/ppermute | solution.py:546
  36.8 11.2 %collective-permute-done.5 = bf16[256,768]{1,0:T(8,128)(2,1)S(1)} collective-permute-done((bf16[256,768]{1,0:T(8,128)(2,1)S(1)}, bf16[256,768]{1,0:T(8,128)(2,1)S(1)}, u32[]{:S(2)}, u32[]{:S(2)}) %collective-permute-start.5) | collective-permute-done | bytes 393248 | tf_op jit(solution)/shard_map/ppermute | solution.py:546
  48.0 2.4 collective-permute-done.4.refs_4_
  56.2 17.1 %collective-permute-done.9 = bf16[256,768]{1,0:T(8,128)(2,1)S(1)} collective-permute-done((bf16[256,768]{1,0:T(8,128)(2,1)S(1)}, bf16[256,768]{1,0:T(8,128)(2,1)S(1)}, u32[]{:S(2)}, u32[]{:S(2)}) %collective-permute-start.9) | collective-permute-done | bytes 393248 | tf_op jit(solution)/shard_map/ppermute | solution.py:546
  75.8 3.3 %collective-permute-done.12.refs_8_ = bf16[512,768]{1,0:T(8,128)(2,1)S(1)} collective-permute-done((bf16[512,768]{1,0:T(8,128)(2,1)S(1)}, bf16[512,768]{1,0:T(8,128)(2,1)S(1)}, u32[]{:S(2)}, u32[]{:S(2)}) %collective-permute-start.12) | collective-permute-done | bytes 786464 | tf_op jit(solution)/shard_map/ppermute | solution.py:549
  83.6 14.4 %partial_sums.5 = bf16[1,512,768]{2,1,0:T(8,128)(2,1)} custom-call(s32[17,512]{1,0:T(8,128)S(1)} %get-tuple-element.56.refs_0_, bf16[2048,768]{1,0:T(8,128)(2,1)} %refs_1_.7, bf16[1024,768]{1,0:T(8,128)(2,1)} %collective-permute-done.3.refs_2_, bf16[1024,768]{1,0:T(8,128)(2,1)} %copy-done.9, bf16[1024,768]{1,0:T(8,128)(2,1)} %collective-permute-done.4.refs_4_, ...), custom_call_target="tpu_custom_call" | custom-call | tf_op jit(solution)/shard_map/partial_sums/pallas_call | solution.py:275
  99.5 13.9 %partial_sums.6 = bf16[1,512,768]{2,1,0:T(8,128)(2,1)} custom-call(s32[17,512]{1,0:T(8,128)S(1)} %get-tuple-element.57.refs_0_, bf16[2048,768]{1,0:T(8,128)(2,1)} %refs_1_.7, bf16[1024,768]{1,0:T(8,128)(2,1)} %collective-permute-done.3.refs_2_, bf16[1024,768]{1,0:T(8,128)(2,1)} %copy-done.9, bf16[1024,768]{1,0:T(8,128)(2,1)} %collective-permute-done.4.refs_4_, ...), custom_call_target="tpu_custom_call" | custom-call | tf_op jit(solution)/shard_map/partial_sums/pallas_call | solution.py:275
  113.5 3.8 %collective-permute-start.15 = (bf16[512,768]{1,0:T(8,128)(2,1)}, bf16[512,768]{1,0:T(8,128)(2,1)}, u32[]{:S(2)}, u32[]{:S(2)}) collective-permute-start(bf16[512,768]{1,0:T(8,128)(2,1)} %bitcast.18), channel_id=1, source_target_pairs={{0,16},{2,18},{4,20},{6,22},{8,24},{10,26},{12,28},{14,30},{16,0},... | collective-permute-start | bytes 2359304 | tf_op jit(solution)/shard_map/ppermute | solution.py:546
  117.2 14.1 %partial_sums.7 = bf16[1,512,768]{2,1,0:T(8,128)(2,1)} custom-call(s32[17,512]{1,0:T(8,128)S(1)} %get-tuple-element.58.refs_0_, bf16[2048,768]{1,0:T(8,128)(2,1)} %refs_1_.7, bf16[1024,768]{1,0:T(8,128)(2,1)} %collective-permute-done.3.refs_2_, bf16[1024,768]{1,0:T(8,128)(2,1)} %copy-done.9, bf16[1024,768]{1,0:T(8,128)(2,1)} %collective-permute-done.4.refs_4_, ...), custom_call_target="tpu_custom_call" | custom-call | tf_op jit(solution)/shard_map/partial_sums/pallas_call | solution.py:275
  136.9 2.8 copy.38.refs_5_
  141.4 13.2 %partial_sums.4 = bf16[1,512,768]{2,1,0:T(8,128)(2,1)S(1)} custom-call(s32[17,512]{1,0:T(8,128)S(1)} %get-tuple-element.47.refs_0_, bf16[2048,768]{1,0:T(8,128)(2,1)} %refs_1_.7, bf16[1024,768]{1,0:T(8,128)(2,1)} %collective-permute-done.3.refs_2_, bf16[1024,768]{1,0:T(8,128)(2,1)} %copy-done.9, bf16[1024,768]{1,0:T(8,128)(2,1)} %collective-permute-done.4.refs_4_, ...), custom_call_target="tpu_custom_call" | custom-call | tf_op jit(solution)/shard_map/partial_sums/pallas_call | solution.py:275
  155.5 12.7 %collective-permute-done.15.refs_8_ = bf16[512,768]{1,0:T(8,128)(2,1)} collective-permute-done((bf16[512,768]{1,0:T(8,128)(2,1)}, bf16[512,768]{1,0:T(8,128)(2,1)}, u32[]{:S(2)}, u32[]{:S(2)}) %collective-permute-start.15) | collective-permute-done | bytes 786464 | tf_op jit(solution)/shard_map/ppermute | solution.py:546
  168.2 3.8 %collective-permute-done.16.refs_9_ = bf16[512,768]{1,0:T(8,128)(2,1)} collective-permute-done((bf16[512,768]{1,0:T(8,128)(2,1)}, bf16[512,768]{1,0:T(8,128)(2,1)}, u32[]{:S(2)}, u32[]{:S(2)}) %collective-permute-start.16) | collective-permute-done | bytes 786464 | tf_op jit(solution)/shard_map/ppermute | solution.py:546
  172.0 14.4 %trainer_step.1 = (f32[128,153]{1,0:T(8,128)}, f32[4,4,64,1024]{3,2,1,0:T(8,128)}, bf16[4,4,64,1024]{3,2,1,0:T(8,128)(2,1)}) custom-call(s32[4]{0:T(128)} %copy-done.7, s32[128,1]{1,0:T(8,128)} %copy.36.refs_1_, s32[128,10]{1,0:T(8,128)} %copy.37.refs_2_, s32[1,512]{1,0:T(1,128)} %copy-done.8, f32[1536,1024]{1,0:T(8,128)} %refs_4_.2, ...), custom_call_target="tpu_custom_call" | custom-call | tf_op jit(solution)/shard_map/trainer_step/pallas_call | solution.py:397
  187.0 4.0 %collective-permute-done.20 = bf16[4,4,64,1024]{3,2,1,0:T(8,128)(2,1)S(1)} collective-permute-done((bf16[4,4,64,1024]{3,2,1,0:T(8,128)(2,1)}, bf16[4,4,64,1024]{3,2,1,0:T(8,128)(2,1)S(1)}, u32[]{:S(2)}, u32[]{:S(2)}) %collective-permute-start.20) | collective-permute-done | bytes 2097184 | tf_op jit(solution)/shard_map/ppermute | solution.py:549
  191.0 3.1 %fusion.3 = (bf16[4,4,64,1024]{3,2,1,0:T(8,128)(2,1)S(1)}, f32[4,4,64,1024]{3,2,1,0:T(8,128)S(1)}) fusion(f32[4,4,64,1024]{3,2,1,0:T(8,128)} %get-tuple-element.64, bf16[4,4,64,1024]{3,2,1,0:T(8,128)(2,1)S(1)} %collective-permute-done.20), kind=kLoop, calls=%fused_computation.26 | loop fusion | flops 3145728 | bytes 12582912 | tf_op jit(solution)/shard_map/convert.5
  197.0 10.5 %collective-permute-done.21 = bf16[4,64,1024]{2,1,0:T(8,128)(2,1)S(1)} collective-permute-done((bf16[4,64,1024]{2,1,0:T(8,128)(2,1)S(1)}, bf16[4,64,1024]{2,1,0:T(8,128)(2,1)S(1)}, u32[]{:S(2)}, u32[]{:S(2)}) %collective-permute-start.21) | collective-permute-done | bytes 524320 | tf_op jit(solution)/shard_map/ppermute | solution.py:543
  207.5 11.1 %collective-permute-done.23 = bf16[4,64,1024]{2,1,0:T(8,128)(2,1)S(1)} collective-permute-done((bf16[4,64,1024]{2,1,0:T(8,128)(2,1)S(1)}, bf16[4,64,1024]{2,1,0:T(8,128)(2,1)S(1)}, u32[]{:S(2)}, u32[]{:S(2)}) %collective-permute-start.23) | collective-permute-done | bytes 524320 | tf_op jit(solution)/shard_map/ppermute | solution.py:543
  221.2 3.2 %collective-permute-done.26.refs_3_ = bf16[64,1024]{1,0:T(8,128)(2,1)S(1)} collective-permute-done((bf16[64,1024]{1,0:T(8,128)(2,1)S(1)}, bf16[64,1024]{1,0:T(8,128)(2,1)S(1)}, u32[]{:S(2)}, u32[]{:S(2)}) %collective-permute-start.26) | collective-permute-done | bytes 131104 | tf_op jit(solution)/shard_map/ppermute | solution.py:546
  226.4 4.3 %collective-permute-done.24.refs_1_ = bf16[64,1024]{1,0:T(8,128)(2,1)S(1)} collective-permute-done((bf16[64,1024]{1,0:T(8,128)(2,1)S(1)}, bf16[64,1024]{1,0:T(8,128)(2,1)S(1)}, u32[]{:S(2)}, u32[]{:S(2)}) %collective-permute-start.24) | collective-permute-done | bytes 131104 | tf_op jit(solution)/shard_map/ppermute | solution.py:546
  237.1 7.4 %collective-permute-done.28 = bf16[64,1024]{1,0:T(8,128)(2,1)S(1)} collective-permute-done((bf16[64,1024]{1,0:T(8,128)(2,1)S(1)}, bf16[64,1024]{1,0:T(8,128)(2,1)S(1)}, u32[]{:S(2)}, u32[]{:S(2)}) %collective-permute-start.28) | collective-permute-done | bytes 131104 | tf_op jit(solution)/shard_map/ppermute | solution.py:546
  250.8 8.0 %collective-permute-done.35.refs_6_ = bf16[4,64,1024]{2,1,0:T(8,128)(2,1)S(1)} collective-permute-done((bf16[4,64,1024]{2,1,0:T(8,128)(2,1)S(1)}, bf16[4,64,1024]{2,1,0:T(8,128)(2,1)S(1)}, u32[]{:S(2)}, u32[]{:S(2)}) %collective-permute-start.35) | collective-permute-done | bytes 524320 | tf_op jit(solution)/shard_map/ppermute | solution.py:543
  258.7 4.4 %collective-permute-start.36 = (bf16[4,64,1024]{2,1,0:T(8,128)(2,1)S(1)}, bf16[4,64,1024]{2,1,0:T(8,128)(2,1)S(1)}, u32[]{:S(2)}, u32[]{:S(2)}) collective-permute-start(bf16[4,64,1024]{2,1,0:T(8,128)(2,1)S(1)} %collective-permute-done.35.refs_6_), channel_id=1, source_target_pairs={{0,1},{1,0},{2,3},{3,2},{4,5},{5,4},{6,7},{7,6},{8,9},{9,8},{10,11... | collective-permute-start | bytes 1572872 | tf_op jit(solution)/shard_map/ppermute | solution.py:549
  263.1 8.7 %collective-permute-done.33.refs_4_ = bf16[4,64,1024]{2,1,0:T(8,128)(2,1)S(1)} collective-permute-done((bf16[4,64,1024]{2,1,0:T(8,128)(2,1)S(1)}, bf16[4,64,1024]{2,1,0:T(8,128)(2,1)S(1)}, u32[]{:S(2)}, u32[]{:S(2)}) %collective-permute-start.33) | collective-permute-done | bytes 524320 | tf_op jit(solution)/shard_map/ppermute | solution.py:543
  274.8 11.0 %apply_updates.1 = (f32[4,4,2,48,1024]{4,3,2,1,0:T(8,128)}, f32[4,4,2,64,153]{4,3,2,1,0:T(8,128)}) custom-call(s32[4]{0:T(128)} %copy-done.7, f32[4,4,2,48,1024]{4,3,2,1,0:T(8,128)} %bitcast.59, f32[4,4,2,64,153]{4,3,2,1,0:T(8,128)} %bitcast.60, bf16[4,64,1024]{2,1,0:T(8,128)(2,1)} %copy-done.11, bf16[4,64,1024]{2,1,0:T(8,128)(2,1)} %copy-done.15, ...), custom_call_target="tpu_custom_call" | custom-call | tf_op jit(solution)/shard_map/apply_updates/pallas_call | solution.py:495
  285.7 2.7 copy.41
  (130 shorter events, 55.0 us)
Async XLA Ops:
  4.7 11.6 %all-to-all-start = ((s32[16,1,64]{2,1,0:T(1,128)}), s32[16,1,64]{2,1,0:T(1,128)S(1)}, u32[]{:S(2)}, u32[]{:S(2)}) async-start(s32[16,1,64]{2,1,0:T(1,128)} %bitcast.5), calls=%async_computation | async-start | bytes 16384 | tf_op jit(solution)/shard_map/all_to_all | solution.py:553
  16.3 34.1 %collective-permute-start.4 = (bf16[1024,768]{1,0:T(8,128)(2,1)}, bf16[1024,768]{1,0:T(8,128)(2,1)}, u32[]{:S(2)}, u32[]{:S(2)}) collective-permute-start(bf16[1024,768]{1,0:T(8,128)(2,1)} %constant_dynamic-slice_fusion), channel_id=1, source_target_pairs={{0,4},{2,6},{4,0},{6,2},{8,12},{10,14},{12,8},{14,10},{16,20},{18,... | collective-permute-start | bytes 4718600 | tf_op jit(solution)/shard_map/ppermute | solution.py:543
  16.6 33.8 %collective-permute-start.3 = (bf16[1024,768]{1,0:T(8,128)(2,1)}, bf16[1024,768]{1,0:T(8,128)(2,1)}, u32[]{:S(2)}, u32[]{:S(2)}) collective-permute-start(bf16[1024,768]{1,0:T(8,128)(2,1)} %constant_dynamic-slice_fusion), channel_id=1, source_target_pairs={{0,2},{2,0},{4,6},{6,4},{8,10},{10,8},{12,14},{14,12},{16,18},{18,... | collective-permute-start | bytes 4718600 | tf_op jit(solution)/shard_map/ppermute | solution.py:543
  19.0 7.4 %collective-permute-start.2 = (s32[15,512]{1,0:T(8,128)S(1)}, s32[15,512]{1,0:T(8,128)S(1)}, u32[]{:S(2)}, u32[]{:S(2)}) collective-permute-start(s32[15,512]{1,0:T(8,128)S(1)} %compose_ids.1.refs_0_), channel_id=1, source_target_pairs={{0,8},{2,10},{4,12},{6,14},{8,16},{10,18},{12,20},{14,22},{16,24},... | collective-permute-start | bytes 92168 | tf_op jit(solution)/shard_map/ppermute | solution.py:546
  19.7 6.7 %collective-permute-start.1 = (s32[15,512]{1,0:T(8,128)S(1)}, s32[15,512]{1,0:T(8,128)S(1)}, u32[]{:S(2)}, u32[]{:S(2)}) collective-permute-start(s32[15,512]{1,0:T(8,128)S(1)} %compose_ids.1.refs_0_), channel_id=1, source_target_pairs={{0,16},{2,18},{4,20},{6,22},{8,24},{10,26},{12,28},{14,30},{16,0},... | collective-permute-start | bytes 92168 | tf_op jit(solution)/shard_map/ppermute | solution.py:546
  29.3 7.5 %collective-permute-start.6 = (bf16[256,768]{1,0:T(8,128)(2,1)S(1)}, bf16[256,768]{1,0:T(8,128)(2,1)S(1)}, u32[]{:S(2)}, u32[]{:S(2)}) collective-permute-start(bf16[256,768]{1,0:T(8,128)(2,1)S(1)} %get-tuple-element.102), channel_id=1, source_target_pairs={{0,24},{2,26},{4,28},{6,30},{8,0},{10,2},{12,4},{14,6},{16,8},{18,... | collective-permute-start | bytes 1179656 | tf_op jit(solution)/shard_map/ppermute | solution.py:546
  30.5 17.5 %collective-permute-start.5 = (bf16[256,768]{1,0:T(8,128)(2,1)S(1)}, bf16[256,768]{1,0:T(8,128)(2,1)S(1)}, u32[]{:S(2)}, u32[]{:S(2)}) collective-permute-start(bf16[256,768]{1,0:T(8,128)(2,1)S(1)} %get-tuple-element.103), channel_id=1, source_target_pairs={{0,8},{2,10},{4,12},{6,14},{8,16},{10,18},{12,20},{14,22},{16,24},... | collective-permute-start | bytes 1179656 | tf_op jit(solution)/shard_map/ppermute | solution.py:546
  52.8 20.5 %collective-permute-start.8 = (bf16[512,768]{1,0:T(8,128)(2,1)S(1)}, bf16[512,768]{1,0:T(8,128)(2,1)S(1)}, u32[]{:S(2)}, u32[]{:S(2)}) collective-permute-start(bf16[512,768]{1,0:T(8,128)(2,1)S(1)} %slice.100), channel_id=1, source_target_pairs={{0,2},{2,0},{4,6},{6,4},{8,10},{10,8},{12,14},{14,12},{16,18},{18,... | collective-permute-start | bytes 2359304 | tf_op jit(solution)/shard_map/ppermute | solution.py:543
  53.2 20.2 %collective-permute-start.7 = (bf16[512,768]{1,0:T(8,128)(2,1)S(1)}, bf16[512,768]{1,0:T(8,128)(2,1)S(1)}, u32[]{:S(2)}, u32[]{:S(2)}) collective-permute-start(bf16[512,768]{1,0:T(8,128)(2,1)S(1)} %slice.99), channel_id=1, source_target_pairs={{0,4},{2,6},{4,0},{6,2},{8,12},{10,14},{12,8},{14,10},{16,20},{18,... | collective-permute-start | bytes 2359304 | tf_op jit(solution)/shard_map/ppermute | solution.py:543
  54.3 19.0 %collective-permute-start.9 = (bf16[256,768]{1,0:T(8,128)(2,1)S(1)}, bf16[256,768]{1,0:T(8,128)(2,1)S(1)}, u32[]{:S(2)}, u32[]{:S(2)}) collective-permute-start(bf16[256,768]{1,0:T(8,128)(2,1)S(1)} %get-tuple-element.101), channel_id=1, source_target_pairs={{0,16},{2,18},{4,20},{6,22},{8,24},{10,26},{12,28},{14,30},{16,0},... | collective-permute-start | bytes 1179656 | tf_op jit(solution)/shard_map/ppermute | solution.py:546
  73.3 8.0 %collective-permute-start.10 = (bf16[1024,768]{1,0:T(8,128)(2,1)}, bf16[1024,768]{1,0:T(8,128)(2,1)S(1)}, u32[]{:S(2)}, u32[]{:S(2)}) collective-permute-start(bf16[1024,768]{1,0:T(8,128)(2,1)} %collective-permute-done.3.refs_2_), channel_id=1, source_target_pairs={{0,1},{1,0},{2,3},{3,2},{4,5},{5,4},{6,7},{7,6},{8,9},{9,8},{10,11... | collective-permute-start | bytes 4718600 | tf_op jit(solution)/shard_map/ppermute | solution.py:549
  73.8 7.7 %collective-permute-start.11 = (bf16[1024,768]{1,0:T(8,128)(2,1)}, bf16[1024,768]{1,0:T(8,128)(2,1)S(1)}, u32[]{:S(2)}, u32[]{:S(2)}) collective-permute-start(bf16[1024,768]{1,0:T(8,128)(2,1)} %collective-permute-done.4.refs_4_), channel_id=1, source_target_pairs={{0,1},{1,0},{2,3},{3,2},{4,5},{5,4},{6,7},{7,6},{8,9},{9,8},{10,11... | collective-permute-start | bytes 4718600 | tf_op jit(solution)/shard_map/ppermute | solution.py:549
  74.3 7.0 %collective-permute-start.13 = (bf16[512,768]{1,0:T(8,128)(2,1)S(1)}, bf16[512,768]{1,0:T(8,128)(2,1)S(1)}, u32[]{:S(2)}, u32[]{:S(2)}) collective-permute-start(bf16[512,768]{1,0:T(8,128)(2,1)S(1)} %collective-permute-done.8.refs_7_), channel_id=1, source_target_pairs={{0,1},{1,0},{2,3},{3,2},{4,5},{5,4},{6,7},{7,6},{8,9},{9,8},{10,11... | collective-permute-start | bytes 2359304 | tf_op jit(solution)/shard_map/ppermute | solution.py:549
  75.2 59.2 %collective-permute-start.17 = (bf16[256,768]{1,0:T(8,128)(2,1)S(1)}, bf16[256,768]{1,0:T(8,128)(2,1)}, u32[]{:S(2)}, u32[]{:S(2)}) collective-permute-start(bf16[256,768]{1,0:T(8,128)(2,1)S(1)} %pad_maximum_fusion.2), channel_id=1, source_target_pairs={{0,2},{2,0},{4,6},{6,4},{8,10},{10,8},{12,14},{14,12},{16,18},{18,... | collective-permute-start | bytes 1179656 | tf_op jit(solution)/shard_map/ppermute | solution.py:543
  98.0 57.5 %collective-permute-start.14 = (bf16[512,768]{1,0:T(8,128)(2,1)}, bf16[512,768]{1,0:T(8,128)(2,1)}, u32[]{:S(2)}, u32[]{:S(2)}) collective-permute-start(bf16[512,768]{1,0:T(8,128)(2,1)} %bitcast.17), channel_id=1, source_target_pairs={{0,8},{2,10},{4,12},{6,14},{8,16},{10,18},{12,20},{14,22},{16,24},... | collective-permute-start | bytes 2359304 | tf_op jit(solution)/shard_map/ppermute | solution.py:546
  113.5 54.7 %collective-permute-start.15 = (bf16[512,768]{1,0:T(8,128)(2,1)}, bf16[512,768]{1,0:T(8,128)(2,1)}, u32[]{:S(2)}, u32[]{:S(2)}) collective-permute-start(bf16[512,768]{1,0:T(8,128)(2,1)} %bitcast.18), channel_id=1, source_target_pairs={{0,16},{2,18},{4,20},{6,22},{8,24},{10,26},{12,28},{14,30},{16,0},... | collective-permute-start | bytes 2359304 | tf_op jit(solution)/shard_map/ppermute | solution.py:546
  131.4 40.6 %collective-permute-start.16 = (bf16[512,768]{1,0:T(8,128)(2,1)}, bf16[512,768]{1,0:T(8,128)(2,1)}, u32[]{:S(2)}, u32[]{:S(2)}) collective-permute-start(bf16[512,768]{1,0:T(8,128)(2,1)} %bitcast.19), channel_id=1, source_target_pairs={{0,24},{2,26},{4,28},{6,30},{8,0},{10,2},{12,4},{14,6},{16,8},{18,... | collective-permute-start | bytes 2359304 | tf_op jit(solution)/shard_map/ppermute | solution.py:546
  133.1 22.4 %collective-permute-start.18 = (bf16[256,768]{1,0:T(8,128)(2,1)}, bf16[256,768]{1,0:T(8,128)(2,1)}, u32[]{:S(2)}, u32[]{:S(2)}) collective-permute-start(bf16[256,768]{1,0:T(8,128)(2,1)} %pad_maximum_fusion.3), channel_id=1, source_target_pairs={{0,4},{2,6},{4,0},{6,2},{8,12},{10,14},{12,8},{14,10},{16,20},{18,... | collective-permute-start | bytes 1179656 | tf_op jit(solution)/shard_map/ppermute | solution.py:543
  134.4 21.1 %collective-permute-start.19 = (bf16[256,768]{1,0:T(8,128)(2,1)}, bf16[256,768]{1,0:T(8,128)(2,1)}, u32[]{:S(2)}, u32[]{:S(2)}) collective-permute-start(bf16[256,768]{1,0:T(8,128)(2,1)} %pad_maximum_fusion.4), channel_id=1, source_target_pairs={{0,6},{2,4},{4,2},{6,0},{8,14},{10,12},{12,10},{14,8},{16,22},{18,... | collective-permute-start | bytes 1179656 | tf_op jit(solution)/shard_map/ppermute | solution.py:543
  194.3 13.2 %collective-permute-start.21 = (bf16[4,64,1024]{2,1,0:T(8,128)(2,1)S(1)}, bf16[4,64,1024]{2,1,0:T(8,128)(2,1)S(1)}, u32[]{:S(2)}, u32[]{:S(2)}) collective-permute-start(bf16[4,64,1024]{2,1,0:T(8,128)(2,1)S(1)} %get-tuple-element.98), channel_id=1, source_target_pairs={{0,2},{2,0},{4,6},{6,4},{8,10},{10,8},{12,14},{14,12},{16,18},{18,... | collective-permute-start | bytes 1572872 | tf_op jit(solution)/shard_map/ppermute | solution.py:543
  195.4 23.2 %collective-permute-start.23 = (bf16[4,64,1024]{2,1,0:T(8,128)(2,1)S(1)}, bf16[4,64,1024]{2,1,0:T(8,128)(2,1)S(1)}, u32[]{:S(2)}, u32[]{:S(2)}) collective-permute-start(bf16[4,64,1024]{2,1,0:T(8,128)(2,1)S(1)} %get-tuple-element.99), channel_id=1, source_target_pairs={{0,6},{2,4},{4,2},{6,0},{8,14},{10,12},{12,10},{14,8},{16,22},{18,... | collective-permute-start | bytes 1572872 | tf_op jit(solution)/shard_map/ppermute | solution.py:543
  195.7 23.0 %collective-permute-start.22 = (bf16[4,64,1024]{2,1,0:T(8,128)(2,1)S(1)}, bf16[4,64,1024]{2,1,0:T(8,128)(2,1)S(1)}, u32[]{:S(2)}, u32[]{:S(2)}) collective-permute-start(bf16[4,64,1024]{2,1,0:T(8,128)(2,1)S(1)} %get-tuple-element.100), channel_id=1, source_target_pairs={{0,4},{2,6},{4,0},{6,2},{8,12},{10,14},{12,8},{14,10},{16,20},{18,... | collective-permute-start | bytes 1572872 | tf_op jit(solution)/shard_map/ppermute | solution.py:543
  219.1 7.3 %collective-permute-start.25 = (bf16[64,1024]{1,0:T(8,128)(2,1)S(1)}, bf16[64,1024]{1,0:T(8,128)(2,1)S(1)}, u32[]{:S(2)}, u32[]{:S(2)}) collective-permute-start(bf16[64,1024]{1,0:T(8,128)(2,1)S(1)} %get-tuple-element.106), channel_id=1, source_target_pairs={{0,16},{2,18},{4,20},{6,22},{8,24},{10,26},{12,28},{14,30},{16,0},... | collective-permute-start | bytes 393224 | tf_op jit(solution)/shard_map/ppermute | solution.py:546
  219.5 11.2 %collective-permute-start.24 = (bf16[64,1024]{1,0:T(8,128)(2,1)S(1)}, bf16[64,1024]{1,0:T(8,128)(2,1)S(1)}, u32[]{:S(2)}, u32[]{:S(2)}) collective-permute-start(bf16[64,1024]{1,0:T(8,128)(2,1)S(1)} %get-tuple-element.107), channel_id=1, source_target_pairs={{0,8},{2,10},{4,12},{6,14},{8,16},{10,18},{12,20},{14,22},{16,24},... | collective-permute-start | bytes 393224 | tf_op jit(solution)/shard_map/ppermute | solution.py:546
  231.6 5.5 %collective-permute-start.29 = (bf16[64,1024]{1,0:T(8,128)(2,1)S(1)}, bf16[64,1024]{1,0:T(8,128)(2,1)S(1)}, u32[]{:S(2)}, u32[]{:S(2)}) collective-permute-start(bf16[64,1024]{1,0:T(8,128)(2,1)S(1)} %get-tuple-element.66), channel_id=1, source_target_pairs={{0,8},{2,10},{4,12},{6,14},{8,16},{10,18},{12,20},{14,22},{16,24},... | collective-permute-start | bytes 393224 | tf_op jit(solution)/shard_map/ppermute | solution.py:546
  233.8 10.7 %collective-permute-start.28 = (bf16[64,1024]{1,0:T(8,128)(2,1)S(1)}, bf16[64,1024]{1,0:T(8,128)(2,1)S(1)}, u32[]{:S(2)}, u32[]{:S(2)}) collective-permute-start(bf16[64,1024]{1,0:T(8,128)(2,1)S(1)} %get-tuple-element.66), channel_id=1, source_target_pairs={{0,16},{2,18},{4,20},{6,22},{8,24},{10,26},{12,28},{14,30},{16,0},... | collective-permute-start | bytes 393224 | tf_op jit(solution)/shard_map/ppermute | solution.py:546
  235.2 10.5 %collective-permute-start.27 = (bf16[64,1024]{1,0:T(8,128)(2,1)S(1)}, bf16[64,1024]{1,0:T(8,128)(2,1)S(1)}, u32[]{:S(2)}, u32[]{:S(2)}) collective-permute-start(bf16[64,1024]{1,0:T(8,128)(2,1)S(1)} %get-tuple-element.66), channel_id=1, source_target_pairs={{0,24},{2,26},{4,28},{6,30},{8,0},{10,2},{12,4},{14,6},{16,8},{18,... | collective-permute-start | bytes 393224 | tf_op jit(solution)/shard_map/ppermute | solution.py:546
  245.8 13.0 %collective-permute-start.35 = (bf16[4,64,1024]{2,1,0:T(8,128)(2,1)S(1)}, bf16[4,64,1024]{2,1,0:T(8,128)(2,1)S(1)}, u32[]{:S(2)}, u32[]{:S(2)}) collective-permute-start(bf16[4,64,1024]{2,1,0:T(8,128)(2,1)S(1)} %pad_maximum_fusion.refs_0_), channel_id=1, source_target_pairs={{0,6},{2,4},{4,2},{6,0},{8,14},{10,12},{12,10},{14,8},{16,22},{18,... | collective-permute-start | bytes 1572872 | tf_op jit(solution)/shard_map/ppermute | solution.py:543
  247.9 23.9 %collective-permute-start.33 = (bf16[4,64,1024]{2,1,0:T(8,128)(2,1)S(1)}, bf16[4,64,1024]{2,1,0:T(8,128)(2,1)S(1)}, u32[]{:S(2)}, u32[]{:S(2)}) collective-permute-start(bf16[4,64,1024]{2,1,0:T(8,128)(2,1)S(1)} %pad_maximum_fusion.refs_0_), channel_id=1, source_target_pairs={{0,4},{2,6},{4,0},{6,2},{8,12},{10,14},{12,8},{14,10},{16,20},{18,... | collective-permute-start | bytes 1572872 | tf_op jit(solution)/shard_map/ppermute | solution.py:543
  248.3 24.0 %collective-permute-start.31 = (bf16[4,64,1024]{2,1,0:T(8,128)(2,1)S(1)}, bf16[4,64,1024]{2,1,0:T(8,128)(2,1)S(1)}, u32[]{:S(2)}, u32[]{:S(2)}) collective-permute-start(bf16[4,64,1024]{2,1,0:T(8,128)(2,1)S(1)} %pad_maximum_fusion.refs_0_), channel_id=1, source_target_pairs={{0,2},{2,0},{4,6},{6,4},{8,10},{10,8},{12,14},{14,12},{16,18},{18,... | collective-permute-start | bytes 1572872 | tf_op jit(solution)/shard_map/ppermute | solution.py:543
  248.5 24.8 %collective-permute-start.30 = (bf16[4,64,1024]{2,1,0:T(8,128)(2,1)S(1)}, bf16[4,64,1024]{2,1,0:T(8,128)(2,1)S(1)}, u32[]{:S(2)}, u32[]{:S(2)}) collective-permute-start(bf16[4,64,1024]{2,1,0:T(8,128)(2,1)S(1)} %pad_maximum_fusion.refs_0_), channel_id=1, source_target_pairs={{0,1},{1,0},{2,3},{3,2},{4,5},{5,4},{6,7},{7,6},{8,9},{9,8},{10,11... | collective-permute-start | bytes 1572872 | tf_op jit(solution)/shard_map/ppermute | solution.py:549
  258.7 14.5 %collective-permute-start.36 = (bf16[4,64,1024]{2,1,0:T(8,128)(2,1)S(1)}, bf16[4,64,1024]{2,1,0:T(8,128)(2,1)S(1)}, u32[]{:S(2)}, u32[]{:S(2)}) collective-permute-start(bf16[4,64,1024]{2,1,0:T(8,128)(2,1)S(1)} %collective-permute-done.35.refs_6_), channel_id=1, source_target_pairs={{0,1},{1,0},{2,3},{3,2},{4,5},{5,4},{6,7},{7,6},{8,9},{9,8},{10,11... | collective-permute-start | bytes 1572872 | tf_op jit(solution)/shard_map/ppermute | solution.py:549
  (28 other events, 323.9 us)

commit v10 on v9

--- a/solution.py
+++ b/solution.py
@@ -373,7 +373,7 @@
             even = grad[s * pair : s * pair + rows_low]
             odd = grad[s * pair + rows_low : (s + 1) * pair]
             a, b = slot(m * (tile // pair) + s)
-            keep_ref[a, b, :rows_low, :] = jnp.where(first, even, odd)
+            keep_ref[a, b, :rows_low, :] = jnp.where(first, even, odd).astype(jnp.bfloat16)
             send_ref[a, b, :rows_low, :] = jnp.where(first, odd, even).astype(jnp.bfloat16)
     grad = dot(top_in[...], dlogits, 0, 0)
     for s in range(stores):
@@ -384,7 +384,7 @@
         a, b = slot(s)
         own = jnp.concatenate([own[g * sub : (g + 1) * sub] for g in range(lane_groups)], axis=1)
         other = jnp.concatenate([other[g * sub : (g + 1) * sub] for g in range(lane_groups)], axis=1)
-        keep_ref[a, b, rows_low:, :] = own
+        keep_ref[a, b, rows_low:, :] = own.astype(jnp.bfloat16)
         send_ref[a, b, rows_low:, :] = other.astype(jnp.bfloat16)
 
 
@@ -398,7 +398,7 @@
         functools.partial(trainer_kernel, sizes, scale),
         out_shape=(
             jax.ShapeDtypeStruct((seeds, classes), jnp.float32),
-            jax.ShapeDtypeStruct((PLANE, groups, rows, width), jnp.float32),
+            jax.ShapeDtypeStruct((PLANE, groups, rows, width), jnp.bfloat16),
             jax.ShapeDtypeStruct((PLANE, groups, rows, width), jnp.bfloat16),
         ),
         in_specs=[SMEM] + [VMEM] * 3 + [pl.BlockSpec(memory_space=pl.ANY)] + [VMEM] * (1 + len(blocks)),
@@ -603,7 +603,7 @@
         sizes,
         scale,
     )
-    total = keep + sibling(send).astype(jnp.float32)
+    total = keep.astype(jnp.float32) + sibling(send).astype(jnp.float32)
     arrived = [across(total[d].astype(bf16), d) for d in range(1, PLANE)]
     total = total[0] + sum(a.astype(jnp.float32) for a in arrived)
     shares = [total[0]] + [along(total[k].astype(bf16), k) for k in range(1, groups)]

time: 290 us -> 288 us (level)
    another operation x2 -> x1, other arithmetic: 3.44 us -> 0.35 us
  transfers between devices with their start and end apart: 38 -> 38, of which waited for: 23 -> 23; matrix products, arithmetic and copies ran while one was open for 4% -> 4% of each run, Pallas kernels for 22% -> 23%
where the time goes in v10:
time: 288 us; the launch traced here: 287 us
  waiting for transfers between devices  124 us (43%)
  Pallas kernels  93.2 us (32%)
  starting transfers between devices  43.5 us (15%)
  local copies, waits for them, and re-layouts  18.1 us (6%)
  other arithmetic  7.95 us (3%)
    ppermute x15, waiting for transfers between devices, along(): lax.ppermute(x, 'store', [(i, (i + hops * PLANE) % stores) for i in range...  69.3 us
    pallas_call x4, Pallas kernels, partial_sums(): pl.pallas_call(functools.partial(partial_kernel, len(lists), places, bloc...  57.8 us
    ppermute x13, waiting for transfers between devices, across(): return lax.ppermute(x, 'store', [(i, i ^ distance) for i in range(stores)])  40.7 us
    ppermute x15, starting transfers between devices, along(): lax.ppermute(x, 'store', [(i, (i + hops * PLANE) % stores) for i in range...  17.8 us
    pallas_call x1, Pallas kernels, trainer_step(): pl.pallas_call(functools.partial(trainer_kernel, sizes, scale), out_shape...  13.7 us
    ppermute x9, waiting for transfers between devices, sibling(): return lax.ppermute(x, 'rep', [(0, 1), (1, 0)])  11.2 us
    pallas_call x1, Pallas kernels, apply_updates(): pl.pallas_call(functools.partial(apply_kernel, sizes), grid_spec=pltpu.Pr...  11 us
    ppermute x13, starting transfers between devices, across(): return lax.ppermute(x, 'store', [(i, i ^ distance) for i in range(stores)])  10 us
  transfers between devices with their start and end apart: 38, of which 23 were waited for; matrix products, arithmetic and copies ran while one was open for 4% of the time, Pallas kernels for 23%

profile of v10, /device:TPU:9, one launch (start us, length us, event | category | flops | bytes accessed | tf_op | source)
XLA Modules:
  0.0 287.3 jit_solution(4386984495920407266)
XLA Ops:
  4.7 6.7 %all-to-all-start = ((s32[16,1,64]{2,1,0:T(1,128)}), s32[16,1,64]{2,1,0:T(1,128)S(1)}, u32[]{:S(2)}, u32[]{:S(2)}) async-start(s32[16,1,64]{2,1,0:T(1,128)} %bitcast.5), calls=%async_computation | async-start | bytes 16384 | tf_op jit(solution)/shard_map/all_to_all | solution.py:553
  11.3 2.7 constant_dynamic-slice_fusion
  14.0 2.3 all-to-all-done
  19.7 2.6 collective-permute-start.1
  22.3 4.1 %near_rows.1 = bf16[4,256,768]{2,1,0:T(8,128)(2,1)S(1)} custom-call(s32[4]{0:T(128)S(1)} %pad_add_fusion.place_ref.refs_0_, s32[16,64]{1,0:T(8,128)S(1)} %bitcast.55, bf16[2048,768]{1,0:T(8,128)(2,1)S(1)} %copy-done), custom_call_target="tpu_custom_call" | custom-call | tf_op jit(solution)/shard_map/near_rows/pallas_call | solution.py:116
  26.4 2.7 row_lists.1
  30.8 6.0 %collective-permute-done.6 = bf16[256,768]{1,0:T(8,128)(2,1)S(1)} collective-permute-done((bf16[256,768]{1,0:T(8,128)(2,1)S(1)}, bf16[256,768]{1,0:T(8,128)(2,1)S(1)}, u32[]{:S(2)}, u32[]{:S(2)}) %collective-permute-start.6) | collective-permute-done | bytes 393248 | tf_op jit(solution)/shard_map/ppermute | solution.py:546
  36.8 11.2 %collective-permute-done.5 = bf16[256,768]{1,0:T(8,128)(2,1)S(1)} collective-permute-done((bf16[256,768]{1,0:T(8,128)(2,1)S(1)}, bf16[256,768]{1,0:T(8,128)(2,1)S(1)}, u32[]{:S(2)}, u32[]{:S(2)}) %collective-permute-start.5) | collective-permute-done | bytes 393248 | tf_op jit(solution)/shard_map/ppermute | solution.py:546
  48.0 2.4 collective-permute-done.4.refs_4_
  56.2 17.1 %collective-permute-done.9 = bf16[256,768]{1,0:T(8,128)(2,1)S(1)} collective-permute-done((bf16[256,768]{1,0:T(8,128)(2,1)S(1)}, bf16[256,768]{1,0:T(8,128)(2,1)S(1)}, u32[]{:S(2)}, u32[]{:S(2)}) %collective-permute-start.9) | collective-permute-done | bytes 393248 | tf_op jit(solution)/shard_map/ppermute | solution.py:546
  75.8 3.3 %collective-permute-done.12.refs_8_ = bf16[512,768]{1,0:T(8,128)(2,1)S(1)} collective-permute-done((bf16[512,768]{1,0:T(8,128)(2,1)S(1)}, bf16[512,768]{1,0:T(8,128)(2,1)S(1)}, u32[]{:S(2)}, u32[]{:S(2)}) %collective-permute-start.12) | collective-permute-done | bytes 786464 | tf_op jit(solution)/shard_map/ppermute | solution.py:549
  83.6 14.8 %partial_sums.5 = bf16[1,512,768]{2,1,0:T(8,128)(2,1)} custom-call(s32[17,512]{1,0:T(8,128)S(1)} %get-tuple-element.56.refs_0_, bf16[2048,768]{1,0:T(8,128)(2,1)} %refs_1_.7, bf16[1024,768]{1,0:T(8,128)(2,1)} %collective-permute-done.3.refs_2_, bf16[1024,768]{1,0:T(8,128)(2,1)} %copy-done.9, bf16[1024,768]{1,0:T(8,128)(2,1)} %collective-permute-done.4.refs_4_, ...), custom_call_target="tpu_custom_call" | custom-call | tf_op jit(solution)/shard_map/partial_sums/pallas_call | solution.py:275
  98.5 14.7 %partial_sums.6 = bf16[1,512,768]{2,1,0:T(8,128)(2,1)} custom-call(s32[17,512]{1,0:T(8,128)S(1)} %get-tuple-element.57.refs_0_, bf16[2048,768]{1,0:T(8,128)(2,1)} %refs_1_.7, bf16[1024,768]{1,0:T(8,128)(2,1)} %collective-permute-done.3.refs_2_, bf16[1024,768]{1,0:T(8,128)(2,1)} %copy-done.9, bf16[1024,768]{1,0:T(8,128)(2,1)} %collective-permute-done.4.refs_4_, ...), custom_call_target="tpu_custom_call" | custom-call | tf_op jit(solution)/shard_map/partial_sums/pallas_call | solution.py:275
  113.2 5.0 %collective-permute-start.15 = (bf16[512,768]{1,0:T(8,128)(2,1)}, bf16[512,768]{1,0:T(8,128)(2,1)}, u32[]{:S(2)}, u32[]{:S(2)}) collective-permute-start(bf16[512,768]{1,0:T(8,128)(2,1)} %bitcast.18), channel_id=1, source_target_pairs={{0,16},{2,18},{4,20},{6,22},{8,24},{10,26},{12,28},{14,30},{16,0},... | collective-permute-start | bytes 2359304 | tf_op jit(solution)/shard_map/ppermute | solution.py:546
  118.1 14.7 %partial_sums.7 = bf16[1,512,768]{2,1,0:T(8,128)(2,1)} custom-call(s32[17,512]{1,0:T(8,128)S(1)} %get-tuple-element.58.refs_0_, bf16[2048,768]{1,0:T(8,128)(2,1)} %refs_1_.7, bf16[1024,768]{1,0:T(8,128)(2,1)} %collective-permute-done.3.refs_2_, bf16[1024,768]{1,0:T(8,128)(2,1)} %copy-done.9, bf16[1024,768]{1,0:T(8,128)(2,1)} %collective-permute-done.4.refs_4_, ...), custom_call_target="tpu_custom_call" | custom-call | tf_op jit(solution)/shard_map/partial_sums/pallas_call | solution.py:275
  137.9 2.8 copy.38.refs_5_
  142.4 13.6 %partial_sums.4 = bf16[1,512,768]{2,1,0:T(8,128)(2,1)S(1)} custom-call(s32[17,512]{1,0:T(8,128)S(1)} %get-tuple-element.47.refs_0_, bf16[2048,768]{1,0:T(8,128)(2,1)} %refs_1_.7, bf16[1024,768]{1,0:T(8,128)(2,1)} %collective-permute-done.3.refs_2_, bf16[1024,768]{1,0:T(8,128)(2,1)} %copy-done.9, bf16[1024,768]{1,0:T(8,128)(2,1)} %collective-permute-done.4.refs_4_, ...), custom_call_target="tpu_custom_call" | custom-call | tf_op jit(solution)/shard_map/partial_sums/pallas_call | solution.py:275
  156.9 12.1 %collective-permute-done.15.refs_8_ = bf16[512,768]{1,0:T(8,128)(2,1)} collective-permute-done((bf16[512,768]{1,0:T(8,128)(2,1)}, bf16[512,768]{1,0:T(8,128)(2,1)}, u32[]{:S(2)}, u32[]{:S(2)}) %collective-permute-start.15) | collective-permute-done | bytes 786464 | tf_op jit(solution)/shard_map/ppermute | solution.py:546
  169.0 3.2 %collective-permute-done.16.refs_9_ = bf16[512,768]{1,0:T(8,128)(2,1)} collective-permute-done((bf16[512,768]{1,0:T(8,128)(2,1)}, bf16[512,768]{1,0:T(8,128)(2,1)}, u32[]{:S(2)}, u32[]{:S(2)}) %collective-permute-start.16) | collective-permute-done | bytes 786464 | tf_op jit(solution)/shard_map/ppermute | solution.py:546
  172.2 13.7 %trainer_step.1 = (f32[128,153]{1,0:T(8,128)}, bf16[4,4,64,1024]{3,2,1,0:T(8,128)(2,1)}, bf16[4,4,64,1024]{3,2,1,0:T(8,128)(2,1)}) custom-call(s32[4]{0:T(128)} %copy-done.7, s32[128,1]{1,0:T(8,128)} %copy.36.refs_1_, s32[128,10]{1,0:T(8,128)} %copy.37.refs_2_, s32[1,512]{1,0:T(1,128)} %copy-done.8, f32[1536,1024]{1,0:T(8,128)} %refs_4_.2, ...), custom_call_target="tpu_custom_call" | custom-call | tf_op jit(solution)/shard_map/trainer_step/pallas_call | solution.py:397
  186.4 4.0 %collective-permute-done.20 = bf16[4,4,64,1024]{3,2,1,0:T(8,128)(2,1)S(1)} collective-permute-done((bf16[4,4,64,1024]{3,2,1,0:T(8,128)(2,1)}, bf16[4,4,64,1024]{3,2,1,0:T(8,128)(2,1)S(1)}, u32[]{:S(2)}, u32[]{:S(2)}) %collective-permute-start.20) | collective-permute-done | bytes 2097184 | tf_op jit(solution)/shard_map/ppermute | solution.py:549
  190.4 2.6 convert_add_fusion
  195.9 10.5 %collective-permute-done.21 = bf16[4,64,1024]{2,1,0:T(8,128)(2,1)S(1)} collective-permute-done((bf16[4,64,1024]{2,1,0:T(8,128)(2,1)S(1)}, bf16[4,64,1024]{2,1,0:T(8,128)(2,1)S(1)}, u32[]{:S(2)}, u32[]{:S(2)}) %collective-permute-start.21) | collective-permute-done | bytes 524320 | tf_op jit(solution)/shard_map/ppermute | solution.py:543
  206.4 11.1 %collective-permute-done.23 = bf16[4,64,1024]{2,1,0:T(8,128)(2,1)S(1)} collective-permute-done((bf16[4,64,1024]{2,1,0:T(8,128)(2,1)S(1)}, bf16[4,64,1024]{2,1,0:T(8,128)(2,1)S(1)}, u32[]{:S(2)}, u32[]{:S(2)}) %collective-permute-start.23) | collective-permute-done | bytes 524320 | tf_op jit(solution)/shard_map/ppermute | solution.py:543
  220.3 2.9 collective-permute-done.26.refs_3_
  224.9 4.7 %collective-permute-done.24.refs_1_ = bf16[64,1024]{1,0:T(8,128)(2,1)S(1)} collective-permute-done((bf16[64,1024]{1,0:T(8,128)(2,1)S(1)}, bf16[64,1024]{1,0:T(8,128)(2,1)S(1)}, u32[]{:S(2)}, u32[]{:S(2)}) %collective-permute-start.24) | collective-permute-done | bytes 131104 | tf_op jit(solution)/shard_map/ppermute | solution.py:546
  235.9 7.4 %collective-permute-done.28 = bf16[64,1024]{1,0:T(8,128)(2,1)S(1)} collective-permute-done((bf16[64,1024]{1,0:T(8,128)(2,1)S(1)}, bf16[64,1024]{1,0:T(8,128)(2,1)S(1)}, u32[]{:S(2)}, u32[]{:S(2)}) %collective-permute-start.28) | collective-permute-done | bytes 131104 | tf_op jit(solution)/shard_map/ppermute | solution.py:546
  249.7 8.0 %collective-permute-done.35.refs_6_ = bf16[4,64,1024]{2,1,0:T(8,128)(2,1)S(1)} collective-permute-done((bf16[4,64,1024]{2,1,0:T(8,128)(2,1)S(1)}, bf16[4,64,1024]{2,1,0:T(8,128)(2,1)S(1)}, u32[]{:S(2)}, u32[]{:S(2)}) %collective-permute-start.35) | collective-permute-done | bytes 524320 | tf_op jit(solution)/shard_map/ppermute | solution.py:543
  257.6 4.4 %collective-permute-start.36 = (bf16[4,64,1024]{2,1,0:T(8,128)(2,1)S(1)}, bf16[4,64,1024]{2,1,0:T(8,128)(2,1)S(1)}, u32[]{:S(2)}, u32[]{:S(2)}) collective-permute-start(bf16[4,64,1024]{2,1,0:T(8,128)(2,1)S(1)} %collective-permute-done.35.refs_6_), channel_id=1, source_target_pairs={{0,1},{1,0},{2,3},{3,2},{4,5},{5,4},{6,7},{7,6},{8,9},{9,8},{10,11... | collective-permute-start | bytes 1572872 | tf_op jit(solution)/shard_map/ppermute | solution.py:549
  262.0 8.7 %collective-permute-done.33.refs_4_ = bf16[4,64,1024]{2,1,0:T(8,128)(2,1)S(1)} collective-permute-done((bf16[4,64,1024]{2,1,0:T(8,128)(2,1)S(1)}, bf16[4,64,1024]{2,1,0:T(8,128)(2,1)S(1)}, u32[]{:S(2)}, u32[]{:S(2)}) %collective-permute-start.33) | collective-permute-done | bytes 524320 | tf_op jit(solution)/shard_map/ppermute | solution.py:543
  273.6 11.0 %apply_updates.1 = (f32[4,4,2,48,1024]{4,3,2,1,0:T(8,128)}, f32[4,4,2,64,153]{4,3,2,1,0:T(8,128)}) custom-call(s32[4]{0:T(128)} %copy-done.7, f32[4,4,2,48,1024]{4,3,2,1,0:T(8,128)} %bitcast.59, f32[4,4,2,64,153]{4,3,2,1,0:T(8,128)} %bitcast.60, bf16[4,64,1024]{2,1,0:T(8,128)(2,1)} %copy-done.11, bf16[4,64,1024]{2,1,0:T(8,128)(2,1)} %copy-done.15, ...), custom_call_target="tpu_custom_call" | custom-call | tf_op jit(solution)/shard_map/apply_updates/pallas_call | solution.py:495
  284.6 2.7 copy.41
  (130 shorter events, 52.9 us)
Async XLA Ops:
  4.7 11.6 %all-to-all-start = ((s32[16,1,64]{2,1,0:T(1,128)}), s32[16,1,64]{2,1,0:T(1,128)S(1)}, u32[]{:S(2)}, u32[]{:S(2)}) async-start(s32[16,1,64]{2,1,0:T(1,128)} %bitcast.5), calls=%async_computation | async-start | bytes 16384 | tf_op jit(solution)/shard_map/all_to_all | solution.py:553
  16.3 34.1 %collective-permute-start.4 = (bf16[1024,768]{1,0:T(8,128)(2,1)}, bf16[1024,768]{1,0:T(8,128)(2,1)}, u32[]{:S(2)}, u32[]{:S(2)}) collective-permute-start(bf16[1024,768]{1,0:T(8,128)(2,1)} %constant_dynamic-slice_fusion), channel_id=1, source_target_pairs={{0,4},{2,6},{4,0},{6,2},{8,12},{10,14},{12,8},{14,10},{16,20},{18,... | collective-permute-start | bytes 4718600 | tf_op jit(solution)/shard_map/ppermute | solution.py:543
  16.6 33.8 %collective-permute-start.3 = (bf16[1024,768]{1,0:T(8,128)(2,1)}, bf16[1024,768]{1,0:T(8,128)(2,1)}, u32[]{:S(2)}, u32[]{:S(2)}) collective-permute-start(bf16[1024,768]{1,0:T(8,128)(2,1)} %constant_dynamic-slice_fusion), channel_id=1, source_target_pairs={{0,2},{2,0},{4,6},{6,4},{8,10},{10,8},{12,14},{14,12},{16,18},{18,... | collective-permute-start | bytes 4718600 | tf_op jit(solution)/shard_map/ppermute | solution.py:543
  19.0 7.4 %collective-permute-start.2 = (s32[15,512]{1,0:T(8,128)S(1)}, s32[15,512]{1,0:T(8,128)S(1)}, u32[]{:S(2)}, u32[]{:S(2)}) collective-permute-start(s32[15,512]{1,0:T(8,128)S(1)} %compose_ids.1.refs_0_), channel_id=1, source_target_pairs={{0,8},{2,10},{4,12},{6,14},{8,16},{10,18},{12,20},{14,22},{16,24},... | collective-permute-start | bytes 92168 | tf_op jit(solution)/shard_map/ppermute | solution.py:546
  19.7 6.7 %collective-permute-start.1 = (s32[15,512]{1,0:T(8,128)S(1)}, s32[15,512]{1,0:T(8,128)S(1)}, u32[]{:S(2)}, u32[]{:S(2)}) collective-permute-start(s32[15,512]{1,0:T(8,128)S(1)} %compose_ids.1.refs_0_), channel_id=1, source_target_pairs={{0,16},{2,18},{4,20},{6,22},{8,24},{10,26},{12,28},{14,30},{16,0},... | collective-permute-start | bytes 92168 | tf_op jit(solution)/shard_map/ppermute | solution.py:546
  29.3 7.5 %collective-permute-start.6 = (bf16[256,768]{1,0:T(8,128)(2,1)S(1)}, bf16[256,768]{1,0:T(8,128)(2,1)S(1)}, u32[]{:S(2)}, u32[]{:S(2)}) collective-permute-start(bf16[256,768]{1,0:T(8,128)(2,1)S(1)} %get-tuple-element.102), channel_id=1, source_target_pairs={{0,24},{2,26},{4,28},{6,30},{8,0},{10,2},{12,4},{14,6},{16,8},{18,... | collective-permute-start | bytes 1179656 | tf_op jit(solution)/shard_map/ppermute | solution.py:546
  30.5 17.5 %collective-permute-start.5 = (bf16[256,768]{1,0:T(8,128)(2,1)S(1)}, bf16[256,768]{1,0:T(8,128)(2,1)S(1)}, u32[]{:S(2)}, u32[]{:S(2)}) collective-permute-start(bf16[256,768]{1,0:T(8,128)(2,1)S(1)} %get-tuple-element.103), channel_id=1, source_target_pairs={{0,8},{2,10},{4,12},{6,14},{8,16},{10,18},{12,20},{14,22},{16,24},... | collective-permute-start | bytes 1179656 | tf_op jit(solution)/shard_map/ppermute | solution.py:546
  52.8 20.5 %collective-permute-start.8 = (bf16[512,768]{1,0:T(8,128)(2,1)S(1)}, bf16[512,768]{1,0:T(8,128)(2,1)S(1)}, u32[]{:S(2)}, u32[]{:S(2)}) collective-permute-start(bf16[512,768]{1,0:T(8,128)(2,1)S(1)} %slice.100), channel_id=1, source_target_pairs={{0,2},{2,0},{4,6},{6,4},{8,10},{10,8},{12,14},{14,12},{16,18},{18,... | collective-permute-start | bytes 2359304 | tf_op jit(solution)/shard_map/ppermute | solution.py:543
  53.2 20.2 %collective-permute-start.7 = (bf16[512,768]{1,0:T(8,128)(2,1)S(1)}, bf16[512,768]{1,0:T(8,128)(2,1)S(1)}, u32[]{:S(2)}, u32[]{:S(2)}) collective-permute-start(bf16[512,768]{1,0:T(8,128)(2,1)S(1)} %slice.99), channel_id=1, source_target_pairs={{0,4},{2,6},{4,0},{6,2},{8,12},{10,14},{12,8},{14,10},{16,20},{18,... | collective-permute-start | bytes 2359304 | tf_op jit(solution)/shard_map/ppermute | solution.py:543
  54.3 19.0 %collective-permute-start.9 = (bf16[256,768]{1,0:T(8,128)(2,1)S(1)}, bf16[256,768]{1,0:T(8,128)(2,1)S(1)}, u32[]{:S(2)}, u32[]{:S(2)}) collective-permute-start(bf16[256,768]{1,0:T(8,128)(2,1)S(1)} %get-tuple-element.101), channel_id=1, source_target_pairs={{0,16},{2,18},{4,20},{6,22},{8,24},{10,26},{12,28},{14,30},{16,0},... | collective-permute-start | bytes 1179656 | tf_op jit(solution)/shard_map/ppermute | solution.py:546
  73.3 8.0 %collective-permute-start.10 = (bf16[1024,768]{1,0:T(8,128)(2,1)}, bf16[1024,768]{1,0:T(8,128)(2,1)S(1)}, u32[]{:S(2)}, u32[]{:S(2)}) collective-permute-start(bf16[1024,768]{1,0:T(8,128)(2,1)} %collective-permute-done.3.refs_2_), channel_id=1, source_target_pairs={{0,1},{1,0},{2,3},{3,2},{4,5},{5,4},{6,7},{7,6},{8,9},{9,8},{10,11... | collective-permute-start | bytes 4718600 | tf_op jit(solution)/shard_map/ppermute | solution.py:549
  73.8 7.7 %collective-permute-start.11 = (bf16[1024,768]{1,0:T(8,128)(2,1)}, bf16[1024,768]{1,0:T(8,128)(2,1)S(1)}, u32[]{:S(2)}, u32[]{:S(2)}) collective-permute-start(bf16[1024,768]{1,0:T(8,128)(2,1)} %collective-permute-done.4.refs_4_), channel_id=1, source_target_pairs={{0,1},{1,0},{2,3},{3,2},{4,5},{5,4},{6,7},{7,6},{8,9},{9,8},{10,11... | collective-permute-start | bytes 4718600 | tf_op jit(solution)/shard_map/ppermute | solution.py:549
  74.3 7.0 %collective-permute-start.13 = (bf16[512,768]{1,0:T(8,128)(2,1)S(1)}, bf16[512,768]{1,0:T(8,128)(2,1)S(1)}, u32[]{:S(2)}, u32[]{:S(2)}) collective-permute-start(bf16[512,768]{1,0:T(8,128)(2,1)S(1)} %collective-permute-done.8.refs_7_), channel_id=1, source_target_pairs={{0,1},{1,0},{2,3},{3,2},{4,5},{5,4},{6,7},{7,6},{8,9},{9,8},{10,11... | collective-permute-start | bytes 2359304 | tf_op jit(solution)/shard_map/ppermute | solution.py:549
  75.2 59.3 %collective-permute-start.17 = (bf16[256,768]{1,0:T(8,128)(2,1)S(1)}, bf16[256,768]{1,0:T(8,128)(2,1)}, u32[]{:S(2)}, u32[]{:S(2)}) collective-permute-start(bf16[256,768]{1,0:T(8,128)(2,1)S(1)} %pad_maximum_fusion.2), channel_id=1, source_target_pairs={{0,2},{2,0},{4,6},{6,4},{8,10},{10,8},{12,14},{14,12},{16,18},{18,... | collective-permute-start | bytes 1179656 | tf_op jit(solution)/shard_map/ppermute | solution.py:543
  98.4 58.5 %collective-permute-start.14 = (bf16[512,768]{1,0:T(8,128)(2,1)}, bf16[512,768]{1,0:T(8,128)(2,1)}, u32[]{:S(2)}, u32[]{:S(2)}) collective-permute-start(bf16[512,768]{1,0:T(8,128)(2,1)} %bitcast.17), channel_id=1, source_target_pairs={{0,8},{2,10},{4,12},{6,14},{8,16},{10,18},{12,20},{14,22},{16,24},... | collective-permute-start | bytes 2359304 | tf_op jit(solution)/shard_map/ppermute | solution.py:546
  113.2 55.8 %collective-permute-start.15 = (bf16[512,768]{1,0:T(8,128)(2,1)}, bf16[512,768]{1,0:T(8,128)(2,1)}, u32[]{:S(2)}, u32[]{:S(2)}) collective-permute-start(bf16[512,768]{1,0:T(8,128)(2,1)} %bitcast.18), channel_id=1, source_target_pairs={{0,16},{2,18},{4,20},{6,22},{8,24},{10,26},{12,28},{14,30},{16,0},... | collective-permute-start | bytes 2359304 | tf_op jit(solution)/shard_map/ppermute | solution.py:546
  132.9 39.3 %collective-permute-start.16 = (bf16[512,768]{1,0:T(8,128)(2,1)}, bf16[512,768]{1,0:T(8,128)(2,1)}, u32[]{:S(2)}, u32[]{:S(2)}) collective-permute-start(bf16[512,768]{1,0:T(8,128)(2,1)} %bitcast.19), channel_id=1, source_target_pairs={{0,24},{2,26},{4,28},{6,30},{8,0},{10,2},{12,4},{14,6},{16,8},{18,... | collective-permute-start | bytes 2359304 | tf_op jit(solution)/shard_map/ppermute | solution.py:546
  133.7 23.2 %collective-permute-start.18 = (bf16[256,768]{1,0:T(8,128)(2,1)}, bf16[256,768]{1,0:T(8,128)(2,1)}, u32[]{:S(2)}, u32[]{:S(2)}) collective-permute-start(bf16[256,768]{1,0:T(8,128)(2,1)} %pad_maximum_fusion.3), channel_id=1, source_target_pairs={{0,4},{2,6},{4,0},{6,2},{8,12},{10,14},{12,8},{14,10},{16,20},{18,... | collective-permute-start | bytes 1179656 | tf_op jit(solution)/shard_map/ppermute | solution.py:543
  134.5 22.4 %collective-permute-start.19 = (bf16[256,768]{1,0:T(8,128)(2,1)}, bf16[256,768]{1,0:T(8,128)(2,1)}, u32[]{:S(2)}, u32[]{:S(2)}) collective-permute-start(bf16[256,768]{1,0:T(8,128)(2,1)} %pad_maximum_fusion.4), channel_id=1, source_target_pairs={{0,6},{2,4},{4,2},{6,0},{8,14},{10,12},{12,10},{14,8},{16,22},{18,... | collective-permute-start | bytes 1179656 | tf_op jit(solution)/shard_map/ppermute | solution.py:543
  193.2 13.2 %collective-permute-start.21 = (bf16[4,64,1024]{2,1,0:T(8,128)(2,1)S(1)}, bf16[4,64,1024]{2,1,0:T(8,128)(2,1)S(1)}, u32[]{:S(2)}, u32[]{:S(2)}) collective-permute-start(bf16[4,64,1024]{2,1,0:T(8,128)(2,1)S(1)} %get-tuple-element.98), channel_id=1, source_target_pairs={{0,2},{2,0},{4,6},{6,4},{8,10},{10,8},{12,14},{14,12},{16,18},{18,... | collective-permute-start | bytes 1572872 | tf_op jit(solution)/shard_map/ppermute | solution.py:543
  194.3 23.1 %collective-permute-start.23 = (bf16[4,64,1024]{2,1,0:T(8,128)(2,1)S(1)}, bf16[4,64,1024]{2,1,0:T(8,128)(2,1)S(1)}, u32[]{:S(2)}, u32[]{:S(2)}) collective-permute-start(bf16[4,64,1024]{2,1,0:T(8,128)(2,1)S(1)} %get-tuple-element.99), channel_id=1, source_target_pairs={{0,6},{2,4},{4,2},{6,0},{8,14},{10,12},{12,10},{14,8},{16,22},{18,... | collective-permute-start | bytes 1572872 | tf_op jit(solution)/shard_map/ppermute | solution.py:543
  194.5 23.0 %collective-permute-start.22 = (bf16[4,64,1024]{2,1,0:T(8,128)(2,1)S(1)}, bf16[4,64,1024]{2,1,0:T(8,128)(2,1)S(1)}, u32[]{:S(2)}, u32[]{:S(2)}) collective-permute-start(bf16[4,64,1024]{2,1,0:T(8,128)(2,1)S(1)} %get-tuple-element.100), channel_id=1, source_target_pairs={{0,4},{2,6},{4,0},{6,2},{8,12},{10,14},{12,8},{14,10},{16,20},{18,... | collective-permute-start | bytes 1572872 | tf_op jit(solution)/shard_map/ppermute | solution.py:543
  218.0 6.9 %collective-permute-start.25 = (bf16[64,1024]{1,0:T(8,128)(2,1)S(1)}, bf16[64,1024]{1,0:T(8,128)(2,1)S(1)}, u32[]{:S(2)}, u32[]{:S(2)}) collective-permute-start(bf16[64,1024]{1,0:T(8,128)(2,1)S(1)} %get-tuple-element.106), channel_id=1, source_target_pairs={{0,16},{2,18},{4,20},{6,22},{8,24},{10,26},{12,28},{14,30},{16,0},... | collective-permute-start | bytes 393224 | tf_op jit(solution)/shard_map/ppermute | solution.py:546
  218.4 11.2 %collective-permute-start.24 = (bf16[64,1024]{1,0:T(8,128)(2,1)S(1)}, bf16[64,1024]{1,0:T(8,128)(2,1)S(1)}, u32[]{:S(2)}, u32[]{:S(2)}) collective-permute-start(bf16[64,1024]{1,0:T(8,128)(2,1)S(1)} %get-tuple-element.107), channel_id=1, source_target_pairs={{0,8},{2,10},{4,12},{6,14},{8,16},{10,18},{12,20},{14,22},{16,24},... | collective-permute-start | bytes 393224 | tf_op jit(solution)/shard_map/ppermute | solution.py:546
  230.5 5.5 %collective-permute-start.29 = (bf16[64,1024]{1,0:T(8,128)(2,1)S(1)}, bf16[64,1024]{1,0:T(8,128)(2,1)S(1)}, u32[]{:S(2)}, u32[]{:S(2)}) collective-permute-start(bf16[64,1024]{1,0:T(8,128)(2,1)S(1)} %get-tuple-element.66), channel_id=1, source_target_pairs={{0,8},{2,10},{4,12},{6,14},{8,16},{10,18},{12,20},{14,22},{16,24},... | collective-permute-start | bytes 393224 | tf_op jit(solution)/shard_map/ppermute | solution.py:546
  232.7 10.7 %collective-permute-start.28 = (bf16[64,1024]{1,0:T(8,128)(2,1)S(1)}, bf16[64,1024]{1,0:T(8,128)(2,1)S(1)}, u32[]{:S(2)}, u32[]{:S(2)}) collective-permute-start(bf16[64,1024]{1,0:T(8,128)(2,1)S(1)} %get-tuple-element.66), channel_id=1, source_target_pairs={{0,16},{2,18},{4,20},{6,22},{8,24},{10,26},{12,28},{14,30},{16,0},... | collective-permute-start | bytes 393224 | tf_op jit(solution)/shard_map/ppermute | solution.py:546
  234.1 10.5 %collective-permute-start.27 = (bf16[64,1024]{1,0:T(8,128)(2,1)S(1)}, bf16[64,1024]{1,0:T(8,128)(2,1)S(1)}, u32[]{:S(2)}, u32[]{:S(2)}) collective-permute-start(bf16[64,1024]{1,0:T(8,128)(2,1)S(1)} %get-tuple-element.66), channel_id=1, source_target_pairs={{0,24},{2,26},{4,28},{6,30},{8,0},{10,2},{12,4},{14,6},{16,8},{18,... | collective-permute-start | bytes 393224 | tf_op jit(solution)/shard_map/ppermute | solution.py:546
  244.7 13.0 %collective-permute-start.35 = (bf16[4,64,1024]{2,1,0:T(8,128)(2,1)S(1)}, bf16[4,64,1024]{2,1,0:T(8,128)(2,1)S(1)}, u32[]{:S(2)}, u32[]{:S(2)}) collective-permute-start(bf16[4,64,1024]{2,1,0:T(8,128)(2,1)S(1)} %pad_maximum_fusion.refs_0_), channel_id=1, source_target_pairs={{0,6},{2,4},{4,2},{6,0},{8,14},{10,12},{12,10},{14,8},{16,22},{18,... | collective-permute-start | bytes 1572872 | tf_op jit(solution)/shard_map/ppermute | solution.py:543
  246.9 23.8 %collective-permute-start.33 = (bf16[4,64,1024]{2,1,0:T(8,128)(2,1)S(1)}, bf16[4,64,1024]{2,1,0:T(8,128)(2,1)S(1)}, u32[]{:S(2)}, u32[]{:S(2)}) collective-permute-start(bf16[4,64,1024]{2,1,0:T(8,128)(2,1)S(1)} %pad_maximum_fusion.refs_0_), channel_id=1, source_target_pairs={{0,4},{2,6},{4,0},{6,2},{8,12},{10,14},{12,8},{14,10},{16,20},{18,... | collective-permute-start | bytes 1572872 | tf_op jit(solution)/shard_map/ppermute | solution.py:543
  247.0 24.2 %collective-permute-start.31 = (bf16[4,64,1024]{2,1,0:T(8,128)(2,1)S(1)}, bf16[4,64,1024]{2,1,0:T(8,128)(2,1)S(1)}, u32[]{:S(2)}, u32[]{:S(2)}) collective-permute-start(bf16[4,64,1024]{2,1,0:T(8,128)(2,1)S(1)} %pad_maximum_fusion.refs_0_), channel_id=1, source_target_pairs={{0,2},{2,0},{4,6},{6,4},{8,10},{10,8},{12,14},{14,12},{16,18},{18,... | collective-permute-start | bytes 1572872 | tf_op jit(solution)/shard_map/ppermute | solution.py:543
  247.4 24.8 %collective-permute-start.30 = (bf16[4,64,1024]{2,1,0:T(8,128)(2,1)S(1)}, bf16[4,64,1024]{2,1,0:T(8,128)(2,1)S(1)}, u32[]{:S(2)}, u32[]{:S(2)}) collective-permute-start(bf16[4,64,1024]{2,1,0:T(8,128)(2,1)S(1)} %pad_maximum_fusion.refs_0_), channel_id=1, source_target_pairs={{0,1},{1,0},{2,3},{3,2},{4,5},{5,4},{6,7},{7,6},{8,9},{9,8},{10,11... | collective-permute-start | bytes 1572872 | tf_op jit(solution)/shard_map/ppermute | solution.py:549
  257.6 14.5 %collective-permute-start.36 = (bf16[4,64,1024]{2,1,0:T(8,128)(2,1)S(1)}, bf16[4,64,1024]{2,1,0:T(8,128)(2,1)S(1)}, u32[]{:S(2)}, u32[]{:S(2)}) collective-permute-start(bf16[4,64,1024]{2,1,0:T(8,128)(2,1)S(1)} %collective-permute-done.35.refs_6_), channel_id=1, source_target_pairs={{0,1},{1,0},{2,3},{3,2},{4,5},{5,4},{6,7},{7,6},{8,9},{9,8},{10,11... | collective-permute-start | bytes 1572872 | tf_op jit(solution)/shard_map/ppermute | solution.py:549
  (28 other events, 326.5 us)
